TPU v7x, 32 devices: a whole 2x2x4 slice. The times are simulated.
32 devices in a mesh: expert: 8 (over z, x), hidden: 4 (over y, core).
Axes of the slice: x: 2, y: 2, z: 4, core: 2. Of those that a mesh axis runs over, the one named last changes fastest.
Arguments:
- token_ids: int32 [8, 1024], P('expert'), may hold values from 0 to 50303
- target_ids: int32 [8, 1024], P('expert'), may hold values from 0 to 50303
- doc_segments: int32 [8, 1024], P('expert'), may hold values from 0 to 7, never falling along the last dimension, each value on 1 to 512 neighbouring positions
- hash_experts: int32 [50304], replicated, may hold values from 0 to 7
- embed_table: float32 [50304, 768], P(('expert', 'hidden')), may hold values from -0.3 to 0.3
- embed_first: float32 [50304, 768], P(('expert', 'hidden')), may hold values from -3.5762787e-07 to 3.5762787e-07
- embed_second: float32 [50304, 768], P(('expert', 'hidden')), may hold values from 1.6509235e-14 to 1.4790959e-10
- attn_in: float32 [768, 3, 768], P('expert', None, 'hidden'), may hold values from -0.21875 to 0.21875
- attn_in_first: float32 [768, 3, 768], P('expert', None, 'hidden'), may hold values from -3.5762787e-07 to 3.5762787e-07
- attn_in_second: float32 [768, 3, 768], P('expert', None, 'hidden'), may hold values from 1.6509235e-14 to 6.730688e-14
- attn_out: float32 [768, 768], P('expert', 'hidden'), may hold values from -0.875 to 0.875
- attn_out_first: float32 [768, 768], P('expert', 'hidden'), may hold values from -3.5762787e-07 to 3.5762787e-07
- attn_out_second: float32 [768, 768], P('expert', 'hidden'), may hold values from 1.6509235e-14 to 6.730688e-14
- expert_in: float32 [8, 768, 3072], P('expert', None, 'hidden'), may hold values from -0.21875 to 0.21875
- expert_in_first: float32 [8, 768, 3072], P('expert', None, 'hidden'), may hold values from -3.5762787e-07 to 3.5762787e-07
- expert_in_second: float32 [8, 768, 3072], P('expert', None, 'hidden'), may hold values from 1.6509235e-14 to 6.730688e-14
- expert_out: float32 [8, 3072, 768], P('expert', 'hidden'), may hold values from -0.109375 to 0.109375
- expert_out_first: float32 [8, 3072, 768], P('expert', 'hidden'), may hold values from -3.5762787e-07 to 3.5762787e-07
- expert_out_second: float32 [8, 3072, 768], P('expert', 'hidden'), may hold values from 1.6509235e-14 to 6.730688e-14
- norm_gains: float32 [768, 3], P('expert'), may hold values from 0.5 to 1.5
- gains_first: float32 [768, 3], P('expert'), may hold values from -3.8146973e-06 to 3.8146973e-06
- gains_second: float32 [768, 3], P('expert'), may hold values from 1.6509234e-12 to 6.730688e-12
Outputs:
- loss_value: float32 [], replicated
- clip_norm: float32 [], replicated
- embed_new: float32 [50304, 768], P(('expert', 'hidden'))
- embed_first_new: float32 [50304, 768], P(('expert', 'hidden'))
- embed_second_new: float32 [50304, 768], P(('expert', 'hidden'))
- attn_in_new: float32 [768, 3, 768], P('expert', None, 'hidden')
- attn_in_first_new: float32 [768, 3, 768], P('expert', None, 'hidden')
- attn_in_second_new: float32 [768, 3, 768], P('expert', None, 'hidden')
- attn_out_new: float32 [768, 768], P('expert', 'hidden')
- attn_out_first_new: float32 [768, 768], P('expert', 'hidden')
- attn_out_second_new: float32 [768, 768], P('expert', 'hidden')
- expert_in_new: float32 [8, 768, 3072], P('expert', None, 'hidden')
- expert_in_first_new: float32 [8, 768, 3072], P('expert', None, 'hidden')
- expert_in_second_new: float32 [8, 768, 3072], P('expert', None, 'hidden')
- expert_out_new: float32 [8, 3072, 768], P('expert', 'hidden')
- expert_out_first_new: float32 [8, 3072, 768], P('expert', 'hidden')
- expert_out_second_new: float32 [8, 3072, 768], P('expert', 'hidden')
- gains_new: float32 [768, 3], P('expert')
- gains_first_new: float32 [768, 3], P('expert')
- gains_second_new: float32 [768, 3], P('expert')
All inputs are finite; a program needn't handle non-finite values.
Results may differ from a plain program's by a relative error of at most 0.0025.
The roundings to bfloat16 on the way count: a program that leaves them out, or rounds other values in their place, can miss the bound.
Values may be sent and summed in bfloat16 or wider, within the bound.
No kernel may reach another device: no remote copies, remote signals or barrier semaphores. Data moves between devices by JAX's collectives and lax.ppermute only.
A program may use at most 256 MiB of HBM per device.

v0:
```python
from functools import partial

import jax
import jax.numpy as jnp
from jax import lax
from jax.sharding import PartitionSpec as P

HD = 64
DOCS_ROW = 8
STEP = 7


EPS_NORM = 1e-06
BETA_ONE = 0.9
BETA_TWO = 0.95
ADAM_EPS = 1e-08
RATE_MATRIX = 0.05
RATE_GAIN = 0.3
DECAY = 0.1
CLIP_AT = 0.005


def joined(x, axis, combine):
    everything = jax.tree.map(lambda part: lax.all_gather(part, axis), x)
    leading = jax.tree.map(lambda part: part[0], everything)

    def step(k, so_far):
        return combine(so_far, jax.tree.map(lambda part: part[k], everything))

    return lax.fori_loop(1, lax.axis_size(axis), step, leading)


def rms_norm(rows_in, gain):
    return (
        rows_in * lax.rsqrt(jnp.mean(rows_in * rows_in, axis=-1, keepdims=True) + EPS_NORM) * gain
    )


def norm_back(rows_in, gain, gradient):
    normed, pullback = jax.vjp(rms_norm, rows_in, gain)
    return pullback(gradient)


def places(expert_ids, experts, capacity):
    onehot = (expert_ids[:, None] == jnp.arange(experts, dtype=jnp.int32)).astype(jnp.int32)
    before = jnp.cumsum(onehot, axis=0) - onehot
    slot_rank = jnp.sum(before * onehot, axis=1)
    return jnp.where(slot_rank < capacity, expert_ids * capacity + slot_rank, experts * capacity)


def row_scores(queries, key_rows, segment):
    scores = jnp.einsum(
        "qhd,khd->hqk", queries, key_rows, preferred_element_type=jnp.float32
    ) * queries.shape[-1] ** (-0.5)
    position = jnp.arange(scores.shape[-1])
    allowed = (position[:, None] >= position[None, :]) & (segment[:, None] == segment[None, :])
    return jnp.where(allowed[None], scores, -1e30)


def attend(inputs):
    queries, key_rows, value_rows, segment = inputs
    scores = row_scores(queries, key_rows, segment)
    row_peak = jnp.max(scores, axis=-1, keepdims=True)
    exponent = jnp.exp(scores - row_peak)
    totals = jnp.sum(exponent, axis=-1, keepdims=True)
    probability = (exponent / totals).astype(jnp.bfloat16)
    attended = jnp.einsum(
        "hqk,khd->qhd", probability, value_rows, preferred_element_type=jnp.float32
    )
    return (attended.astype(jnp.bfloat16), (row_peak + jnp.log(totals))[..., 0])


def attend_back(inputs):
    queries, key_rows, value_rows, segment, log_total, grad_rows = inputs
    scores = row_scores(queries, key_rows, segment)
    probability = jnp.exp(scores - log_total[..., None])
    d_prob = jnp.einsum("qhd,khd->hqk", grad_rows, value_rows, preferred_element_type=jnp.float32)
    centre = jnp.sum(probability * d_prob, axis=-1, keepdims=True)
    d_score = (probability * (d_prob - centre)).astype(jnp.bfloat16)
    factor = queries.shape[-1] ** (-0.5)
    d_query = (
        jnp.einsum("hqk,khd->qhd", d_score, key_rows, preferred_element_type=jnp.float32) * factor
    )
    d_key = (
        jnp.einsum("hqk,qhd->khd", d_score, queries, preferred_element_type=jnp.float32) * factor
    )
    d_value = jnp.einsum(
        "hqk,qhd->khd",
        probability.astype(jnp.bfloat16),
        grad_rows,
        preferred_element_type=jnp.float32,
    )
    return (d_query, d_key, d_value)


def combine_stats(left, right):
    peak_both = jnp.maximum(left[0], right[0])
    summed = left[1] * jnp.exp(left[0] - peak_both) + right[1] * jnp.exp(right[0] - peak_both)
    return (peak_both, summed, left[2] + right[2])


def adam_step(weight, first_moment, second_moment, gradient, step_rate, weight_decay):
    first_moment = BETA_ONE * first_moment + (1.0 - BETA_ONE) * gradient
    second_moment = BETA_TWO * second_moment + (1.0 - BETA_TWO) * gradient * gradient
    update = (
        first_moment
        / (1.0 - BETA_ONE**STEP)
        / (jnp.sqrt(second_moment / (1.0 - BETA_TWO**STEP)) + ADAM_EPS)
    )
    return (weight - step_rate * (update + weight_decay * weight), first_moment, second_moment)


def widen(block):
    return lax.all_gather(block, "hidden", axis=2, tiled=True)


def split_sum(rows_in):
    return lax.psum_scatter(rows_in, "hidden", scatter_dimension=1, tiled=True)


def on_device(
    token_ids,
    target_ids,
    doc_segments,
    hash_experts,
    embed_table,
    embed_first,
    embed_second,
    attn_in,
    attn_in_first,
    attn_in_second,
    attn_out,
    attn_out_first,
    attn_out_second,
    expert_in,
    expert_in_first,
    expert_in_second,
    expert_out,
    expert_out_first,
    expert_out_second,
    norm_gains,
    gains_first,
    gains_second,
):
    n_expert = lax.axis_size("expert")
    n_hidden = lax.axis_size("hidden")
    hidden_index = lax.axis_index("hidden")
    rows_dev, seq_len = token_ids.shape
    tok_count = rows_dev * seq_len
    vocab_rows, model_width = embed_table.shape
    heads_dev = attn_in.shape[2] // HD
    embed_scale = model_width**0.5
    share_width = model_width // n_hidden
    table_all, attn_in_all, attn_out_all, gains_all = (
        lax.all_gather(embed_table.astype(jnp.bfloat16), "expert", axis=0, tiled=True),
        lax.all_gather(attn_in.astype(jnp.bfloat16), "expert", axis=0, tiled=True),
        lax.all_gather(attn_out.astype(jnp.bfloat16), "expert", axis=0, tiled=True),
        lax.all_gather(norm_gains.astype(jnp.bfloat16), "expert", axis=0, tiled=True),
    )
    gain_full = gains_all.astype(jnp.float32)
    flat_ids = token_ids.reshape(tok_count)
    block_index = flat_ids // vocab_rows
    is_owned = block_index % n_hidden == hidden_index
    local_index = jnp.where(
        is_owned, block_index // n_hidden * vocab_rows + flat_ids % vocab_rows, 0
    )
    looked_up = jnp.where(is_owned[:, None], table_all[local_index], jnp.zeros((), jnp.bfloat16))
    embedded = lax.psum(looked_up, "hidden").astype(jnp.float32) * embed_scale
    normed_one = rms_norm(embedded, gain_full[:, 0]).astype(jnp.bfloat16)
    qkv = jnp.einsum(
        "td,dcf->tcf", normed_one, attn_in_all, preferred_element_type=jnp.float32
    ).astype(jnp.bfloat16)
    shaped = qkv.reshape(rows_dev, seq_len, 3, heads_dev, HD)
    queries = shaped[:, :, 0]
    key_rows = shaped[:, :, 1]
    value_rows = shaped[:, :, 2]
    attended, attn_totals = lax.map(attend, (queries, key_rows, value_rows, doc_segments))
    attended_flat = attended.reshape(tok_count, heads_dev * HD)
    attn_part = jnp.einsum(
        "tf,df->td", attended_flat, attn_out_all, preferred_element_type=jnp.float32
    )
    after_attn = embedded + lax.psum(attn_part, "hidden")
    normed_two = rms_norm(after_attn, gain_full[:, 1]).astype(jnp.bfloat16)
    capacity = 3 * tok_count // (2 * n_expert)
    slot_index = places(hash_experts[flat_ids], n_expert, capacity)

    def fill_slots(rows_in):
        buffer = (
            jnp.zeros((n_expert * capacity + 1, model_width), rows_in.dtype)
            .at[slot_index]
            .set(rows_in)
        )
        block = buffer[:-1].reshape(n_expert, capacity, model_width)
        block = lax.dynamic_slice_in_dim(block, hidden_index * share_width, share_width, 2)
        return block

    def arrive(block):
        block = widen(block)
        return block.reshape(n_expert * capacity, model_width)

    def pick_slots(buffer):
        buffer = widen(buffer)
        flat_rows = buffer.reshape(n_expert * capacity, model_width)
        padded = jnp.concatenate([flat_rows, jnp.zeros((1, model_width), flat_rows.dtype)], axis=0)
        return padded[slot_index].astype(jnp.float32)

    def as_blocks(rows_in):
        return rows_in.reshape(n_expert, capacity, rows_in.shape[1])

    received = arrive(
        lax.all_to_all(fill_slots(normed_two), "expert", split_axis=0, concat_axis=0, tiled=True)
    )
    w_in = expert_in[0].astype(jnp.bfloat16)
    w_out = expert_out[0].astype(jnp.bfloat16)
    pre_act = jnp.dot(received, w_in, preferred_element_type=jnp.float32)
    active = jax.nn.gelu(pre_act, approximate=False).astype(jnp.bfloat16)
    expert_part = jnp.dot(active, w_out, preferred_element_type=jnp.float32)
    expert_result = split_sum(expert_part).astype(jnp.bfloat16)
    moe_rows = pick_slots(
        lax.all_to_all(as_blocks(expert_result), "expert", split_axis=0, concat_axis=0, tiled=True)
    )
    after_moe = after_attn + moe_rows
    final_rows = rms_norm(after_moe, gain_full[:, 2]).astype(jnp.bfloat16)
    flat_targets = target_ids.reshape(tok_count)
    target_block = flat_targets // vocab_rows
    target_owned = target_block % n_hidden == hidden_index
    target_local = jnp.where(
        target_owned, target_block // n_hidden * vocab_rows + flat_targets % vocab_rows, 0
    )
    logits = jnp.einsum("td,vd->tv", final_rows, table_all, preferred_element_type=jnp.float32)
    row_peak = jnp.max(logits, axis=1)
    row_total = jnp.sum(jnp.exp(logits - row_peak[:, None]), axis=1)
    target_logit = jnp.where(
        target_owned, jnp.take_along_axis(logits, target_local[:, None], axis=1)[:, 0], 0.0
    )
    row_peak, row_total, target_logit = joined(
        (row_peak, row_total, target_logit), "hidden", combine_stats
    )
    log_total = row_peak + jnp.log(row_total)

    def row_counts(segment):
        return jnp.sum((segment[:, None] == segment[None, :]).astype(jnp.float32), axis=1)

    counts = lax.map(row_counts, doc_segments).reshape(tok_count)
    weights = 1.0 / counts / (rows_dev * n_expert * DOCS_ROW)
    loss_part = jnp.sum((log_total - target_logit) * weights)
    vocab_local = jnp.arange(logits.shape[1])
    target_hit = vocab_local[None, :] == jnp.where(target_owned, target_local, -1)[:, None]
    d_logits = (
        (jnp.exp(logits - log_total[:, None]) - target_hit.astype(jnp.float32)) * weights[:, None]
    ).astype(jnp.bfloat16)
    d_final = lax.psum(jnp.dot(d_logits, table_all, preferred_element_type=jnp.float32), "hidden")
    d_table = jnp.einsum("tv,td->vd", d_logits, final_rows, preferred_element_type=jnp.float32)
    d_after_moe, d_gain_three = norm_back(after_moe, gain_full[:, 2], d_final)
    grad_in = arrive(
        lax.all_to_all(
            fill_slots(d_after_moe.astype(jnp.bfloat16)),
            "expert",
            split_axis=0,
            concat_axis=0,
            tiled=True,
        )
    )
    d_w_out = jnp.einsum("rf,rd->fd", active, grad_in, preferred_element_type=jnp.float32)
    d_active = jnp.einsum("rd,fd->rf", grad_in, w_out, preferred_element_type=jnp.float32)
    gelu_value, gelu_pull = jax.vjp(partial(jax.nn.gelu, approximate=False), pre_act)
    d_pre = gelu_pull(d_active)[0].astype(jnp.bfloat16)
    d_w_in = jnp.einsum("rd,rf->df", received, d_pre, preferred_element_type=jnp.float32)
    d_recv_part = jnp.einsum("rf,df->rd", d_pre, w_in, preferred_element_type=jnp.float32)
    d_received = split_sum(d_recv_part).astype(jnp.bfloat16)
    d_normed_two = pick_slots(
        lax.all_to_all(as_blocks(d_received), "expert", split_axis=0, concat_axis=0, tiled=True)
    )
    d_after_norm, d_gain_two = norm_back(after_attn, gain_full[:, 1], d_normed_two)
    d_after_attn = d_after_moe + d_after_norm
    d_branch = d_after_attn.astype(jnp.bfloat16)
    d_attn_out = jnp.einsum(
        "td,tf->df", d_branch, attended_flat, preferred_element_type=jnp.float32
    )
    d_attended = jnp.einsum(
        "td,df->tf", d_branch, attn_out_all, preferred_element_type=jnp.float32
    ).astype(jnp.bfloat16)
    d_query, d_key, d_value = lax.map(
        attend_back,
        (
            queries,
            key_rows,
            value_rows,
            doc_segments,
            attn_totals,
            d_attended.reshape(rows_dev, seq_len, heads_dev, HD),
        ),
    )
    d_qkv = (
        jnp.stack([d_query, d_key, d_value], axis=2)
        .astype(jnp.bfloat16)
        .reshape(tok_count, 3, heads_dev * HD)
    )
    d_attn_in = jnp.einsum("td,tcf->dcf", normed_one, d_qkv, preferred_element_type=jnp.float32)
    d_normed_one = lax.psum(
        jnp.einsum("tcf,dcf->td", d_qkv, attn_in_all, preferred_element_type=jnp.float32), "hidden"
    )
    d_embed_norm, d_gain_one = norm_back(embedded, gain_full[:, 0], d_normed_one)
    d_embedded = d_after_attn + d_embed_norm
    d_table = d_table.at[local_index].add(
        jnp.where(is_owned[:, None], d_embedded * embed_scale, 0.0)
    )
    d_gains = jnp.stack([d_gain_one, d_gain_two, d_gain_three], axis=1)
    g_table, g_attn_in, g_attn_out, g_gains = (
        lax.psum_scatter(d_table, "expert", scatter_dimension=0, tiled=True),
        lax.psum_scatter(d_attn_in, "expert", scatter_dimension=0, tiled=True),
        lax.psum_scatter(d_attn_out, "expert", scatter_dimension=0, tiled=True),
        lax.psum_scatter(d_gains, "expert", scatter_dimension=0, tiled=True),
    )
    g_expert_in = d_w_in[None]
    g_expert_out = d_w_out[None]
    squares = (
        jnp.sum(g_table * g_table)
        + jnp.sum(g_attn_in * g_attn_in)
        + jnp.sum(g_attn_out * g_attn_out)
    )
    squares = (
        squares
        + jnp.sum(g_expert_in * g_expert_in)
        + jnp.sum(g_expert_out * g_expert_out)
        + jnp.sum(g_gains * g_gains) / n_hidden
    )
    total_squares, loss_value = lax.psum((squares, loss_part / n_hidden), ("expert", "hidden"))
    clip_norm = jnp.sqrt(total_squares)
    clip_scale = jnp.minimum(1.0, CLIP_AT / clip_norm)
    table_up = adam_step(
        embed_table, embed_first, embed_second, g_table * clip_scale, RATE_MATRIX, DECAY
    )
    attn_in_up = adam_step(
        attn_in, attn_in_first, attn_in_second, g_attn_in * clip_scale, RATE_MATRIX, DECAY
    )
    attn_out_up = adam_step(
        attn_out, attn_out_first, attn_out_second, g_attn_out * clip_scale, RATE_MATRIX, DECAY
    )
    expert_in_up = adam_step(
        expert_in, expert_in_first, expert_in_second, g_expert_in * clip_scale, RATE_MATRIX, DECAY
    )
    expert_out_up = adam_step(
        expert_out,
        expert_out_first,
        expert_out_second,
        g_expert_out * clip_scale,
        RATE_MATRIX,
        DECAY,
    )
    gains_up = adam_step(
        norm_gains, gains_first, gains_second, g_gains * clip_scale, RATE_GAIN, 0.0
    )
    return (
        loss_value,
        clip_norm,
        table_up[0],
        table_up[1],
        table_up[2],
        attn_in_up[0],
        attn_in_up[1],
        attn_in_up[2],
        attn_out_up[0],
        attn_out_up[1],
        attn_out_up[2],
        expert_in_up[0],
        expert_in_up[1],
        expert_in_up[2],
        expert_out_up[0],
        expert_out_up[1],
        expert_out_up[2],
        gains_up[0],
        gains_up[1],
        gains_up[2],
    )


def solution(mesh):
    placed = (
        P("expert", None),
        P("expert", None),
        P("expert", None),
        P(),
        P(("expert", "hidden"), None),
        P(("expert", "hidden"), None),
        P(("expert", "hidden"), None),
        P("expert", None, "hidden"),
        P("expert", None, "hidden"),
        P("expert", None, "hidden"),
        P("expert", "hidden"),
        P("expert", "hidden"),
        P("expert", "hidden"),
        P("expert", None, "hidden"),
        P("expert", None, "hidden"),
        P("expert", None, "hidden"),
        P("expert", "hidden", None),
        P("expert", "hidden", None),
        P("expert", "hidden", None),
        P("expert", None),
        P("expert", None),
        P("expert", None),
    )
    return jax.shard_map(
        on_device,
        mesh=mesh,
        in_specs=placed,
        out_specs=(
            P(),
            P(),
            P(("expert", "hidden"), None),
            P(("expert", "hidden"), None),
            P(("expert", "hidden"), None),
            P("expert", None, "hidden"),
            P("expert", None, "hidden"),
            P("expert", None, "hidden"),
            P("expert", "hidden"),
            P("expert", "hidden"),
            P("expert", "hidden"),
            P("expert", None, "hidden"),
            P("expert", None, "hidden"),
            P("expert", None, "hidden"),
            P("expert", "hidden", None),
            P("expert", "hidden", None),
            P("expert", "hidden", None),
            P("expert", None),
            P("expert", None),
            P("expert", None),
        ),
        check_vma=False,
    )
```

profile of v0, /device:TPU:0, one launch (start us, length us, event | category | flops | bytes accessed | tf_op | source)
XLA Modules:
  0.0 2310.2 jit_solution(7883150780198685969)
XLA Ops:
  11.5 44.6 %all-gather.3 = bf16[8,96,3]{1,2,0:T(4,128)(2,1)S(1)} all-gather(bf16[1,96,3]{1,2,0:T(4,128)(2,1)S(1)} %convert_bitcast_fusion.1), channel_id=1, replica_groups=mesh['expert'=8,'hidden'=4] {'expert'}, dimensions={0}, use_global_device_ids=true | all-gather | bytes 5184 | tf_op jit(solution)/shard_map/all_gather | solution.py:158
  56.6 329.4 %all-gather.19.cloned.1.call-done = bf16[8,1572,768]{2,1,0:T(8,128)(2,1)} async-done(((bf16[1,1572,768]{2,1,0:T(8,128)(2,1)}), bf16[8,1572,768]{2,1,0:T(8,128)(2,1)}) %all-gather.19.cloned.1.call-update) | async-done | bytes 19316752 | tf_op jit(solution)/shard_map/all_gather | solution.py:155
  386.0 21.9 reshape.808
  407.9 13.4 gather_fusion
  422.8 36.8 %all_gather.42 = bf16[768,3,192]{2,1,0:T(4,128)(2,1)S(1)} all-gather(bf16[96,3,192]{2,1,0:T(4,128)(2,1)S(1)} %copy.96), channel_id=1, replica_groups=mesh['expert'=8,'hidden'=4] {'expert'}, dimensions={0}, use_global_device_ids=true | all-gather | bytes 995328 | tf_op jit(solution)/shard_map/all_gather | solution.py:156
  460.6 31.3 %all_gather.43 = bf16[768,192]{1,0:T(8,128)(2,1)S(1)} all-gather(bf16[96,192]{1,0:T(8,128)(2,1)S(1)} %convert_element_type.121), channel_id=1, replica_groups=mesh['expert'=8,'hidden'=4] {'expert'}, dimensions={0}, use_global_device_ids=true | all-gather | bytes 331776 | tf_op jit(solution)/shard_map/all_gather | solution.py:157
  511.0 6.2 gather_fusion.1
  520.1 59.0 %all-reduce.12.cloned.1.call-done = f32[1024,768]{1,0:T(8,128)} async-done(((f32[1024,768]{1,0:T(8,128)}), f32[1024,768]{1,0:T(8,128)}) %all-reduce.12.cloned.1.call-update) | async-done | bytes 3145744 | tf_op jit(solution)/shard_map/psum | solution.py:182
  582.0 7.3 scatter_custom_fusion
  591.4 25.5 %all_to_all.20 = bf16[8,192,192]{2,1,0:T(8,128)(2,1)} all-to-all(bf16[8,192,192]{2,1,0:T(8,128)(2,1)S(1)} %constant_dynamic-slice_fusion.4), channel_id=1, replica_groups=mesh['expert'=8,'hidden'=4] {'expert'}, dimensions={0} | all-to-all | bytes 1179648 | tf_op jit(solution)/shard_map/all_to_all | solution.py:211
  620.1 26.4 %all-gather.11.cloned.1.call-done = bf16[8,192,768]{1,0,2:T(8,128)(2,1)} async-done(((bf16[8,192,192]{1,0,2:T(8,128)(2,1)}), bf16[8,192,768]{1,0,2:T(8,128)(2,1)}) %all-gather.11.cloned.1.call-update) | async-done | bytes 2359312 | tf_op jit(solution)/shard_map/all_gather | solution.py:114
  646.6 4.8 copy.100
  651.4 15.3 multiply_convert_fusion.2
  672.4 47.9 %reduce-scatter.10.cloned.1.call-done = f32[1536,192]{0,1:T(8,128)} async-done(((f32[1536,768]{0,1:T(8,128)}), f32[1536,192]{0,1:T(8,128)}) %reduce-scatter.10.cloned.1.call-update) | async-done | bytes 1179664 | tf_op jit(solution)/shard_map/reduce_scatter | solution.py:118
  726.2 25.5 %all_to_all.21 = bf16[8,192,192]{1,2,0:T(8,128)(2,1)S(1)} all-to-all(bf16[8,192,192]{1,2,0:T(8,128)(2,1)S(1)} %copy.101), channel_id=1, replica_groups=mesh['expert'=8,'hidden'=4] {'expert'}, dimensions={0} | all-to-all | bytes 1179648 | tf_op jit(solution)/shard_map/all_to_all | solution.py:220
  753.9 25.8 %all-gather.13.cloned.1.call-done = bf16[8,192,768]{1,0,2:T(8,128)(2,1)} async-done(((bf16[8,192,192]{1,0,2:T(8,128)(2,1)}), bf16[8,192,768]{1,0,2:T(8,128)(2,1)}) %all-gather.13.cloned.1.call-update) | async-done | bytes 2359312 | tf_op jit(solution)/shard_map/all_gather | solution.py:114
  779.8 4.8 copy.103
  787.8 7.5 gather_fusion.2
  799.1 31.0 %fusion.111 = (f32[1024]{0:T(1024)S(1)}, f32[1024,12576]{0,1:T(8,128)}) fusion(bf16[1024,768]{1,0:T(8,128)(2,1)} %multiply_convert_fusion.3, bf16[12576,768]{1,0:T(8,128)(2,1)} %reshape.808), kind=kOutput, calls=%fused_computation.262 | convolution fusion | flops 19793215488 | bytes 72404992 | tf_op jit(solution)/shard_map/td,vd->tv/dot_general | solution.py:230
  830.0 39.3 %gather_fusion.4 = f32[1024]{0:T(1024)S(1)} fusion(f32[1024,12576]{0,1:T(8,128)} %get-tuple-element.325, s32[1024]{0:T(1024)S(1)} %bitcast.196), kind=kCustom, calls=%fused_computation.4 | custom fusion | bytes 16384 | tf_op jit(solution)/shard_map/jit(take_along_axis)/gather | solution.py:234
  869.4 5.2 all-gather.4
  874.6 19.7 exponential_reduce_fusion
  894.2 5.2 all-gather.1
  899.4 5.6 all-gather
  905.9 33.0 %fusion.100 = f32[1024,768]{1,0:T(8,128)} fusion(bf16[12576,768]{1,0:T(8,128)(2,1)} %reshape.808, f32[1024,12576]{0,1:T(8,128)} %get-tuple-element.325, f32[1024]{0:T(1024)S(1)} %get-tuple-element.318, s32[1024]{0:T(1024)S(1)} %select_select_fusion, f32[1024]{0:T(1024)S(1)} %get-tuple-element.307), kind=kOutput, calls=%fused_computation.259 | convolution fusion | flops 19857604608 | bytes 73986048 | tf_op jit(solution)/shard_map/dot_general | solution.py:252
  938.9 67.7 %all-reduce.14.cloned.1.call-done = f32[1024,768]{1,0:T(8,128)} async-done(((f32[1024,768]{1,0:T(8,128)}), f32[1024,768]{1,0:T(8,128)}) %all-reduce.14.cloned.1.call-update) | async-done | bytes 3145744 | tf_op jit(solution)/shard_map/psum | solution.py:252
  1010.1 8.1 scatter_custom_fusion.1
  1020.3 25.5 %all_to_all.22 = bf16[8,192,192]{2,1,0:T(8,128)(2,1)} all-to-all(bf16[8,192,192]{2,1,0:T(8,128)(2,1)S(1)} %constant_dynamic-slice_fusion.3), channel_id=1, replica_groups=mesh['expert'=8,'hidden'=4] {'expert'}, dimensions={0} | all-to-all | bytes 1179648 | tf_op jit(solution)/shard_map/all_to_all | solution.py:256
  1048.5 27.0 %all-gather.15.cloned.1.call-done = bf16[8,192,768]{1,0,2:T(8,128)(2,1)} async-done(((bf16[8,192,192]{1,0,2:T(8,128)(2,1)}), bf16[8,192,768]{1,0,2:T(8,128)(2,1)}) %all-gather.15.cloned.1.call-update) | async-done | bytes 2359312 | tf_op jit(solution)/shard_map/all_gather | solution.py:114
  1075.5 4.8 copy.105
  1080.3 8.4 add_convert_fusion
  1094.4 47.9 %reduce-scatter.12.cloned.1.call-done = f32[1536,192]{0,1:T(8,128)} async-done(((f32[1536,768]{0,1:T(8,128)}), f32[1536,192]{0,1:T(8,128)}) %reduce-scatter.12.cloned.1.call-update) | async-done | bytes 1179664 | tf_op jit(solution)/shard_map/reduce_scatter | solution.py:118
  1148.2 25.5 %all_to_all.23 = bf16[8,192,192]{1,2,0:T(8,128)(2,1)S(1)} all-to-all(bf16[8,192,192]{1,2,0:T(8,128)(2,1)S(1)} %copy.106), channel_id=1, replica_groups=mesh['expert'=8,'hidden'=4] {'expert'}, dimensions={0} | all-to-all | bytes 1179648 | tf_op jit(solution)/shard_map/all_to_all | solution.py:272
  1176.5 25.3 %all-gather.17.cloned.1.call-done = bf16[8,192,768]{1,0,2:T(8,128)(2,1)} async-done(((bf16[8,192,192]{1,0,2:T(8,128)(2,1)}), bf16[8,192,768]{1,0,2:T(8,128)(2,1)}) %all-gather.17.cloned.1.call-update) | async-done | bytes 2359312 | tf_op jit(solution)/shard_map/all_gather | solution.py:114
  1209.8 7.6 gather_fusion.3
  1225.2 6.3 multiply_reduce_fusion
  1233.1 5.2 multiply_convert_fusion.1
  1251.1 39.2 %fusion.101 = f32[12576,768]{1,0:T(8,128)} fusion(bf16[1024,768]{1,0:T(8,128)(2,1)} %multiply_convert_fusion.3, f32[1024,12576]{0,1:T(8,128)} %get-tuple-element.325, f32[1024]{0:T(1024)S(1)} %get-tuple-element.318, s32[1024]{0:T(1024)S(1)} %select_select_fusion, f32[1024]{0:T(1024)S(1)} %get-tuple-element.307), kind=kOutput, calls=%fused_computation.260 | convolution fusion | flops 19857604608 | bytes 91729920 | tf_op jit(solution)/shard_map/tv,td->vd/dot_general | solution.py:253
  1294.1 6.6 multiply_reduce_fusion.7
  1304.8 14.6 all-reduce.16.cloned.1.call-done
  1324.0 4.8 fusion.37
  1328.8 56.9 %reduce-scatter.16.cloned.1.call-done = f32[96,192]{1,0:T(8,128)} async-done(((f32[768,192]{1,0:T(8,128)}), f32[96,192]{1,0:T(8,128)}) %reduce-scatter.16.cloned.1.call-update) | async-done | bytes 73744 | tf_op jit(solution)/shard_map/reduce_scatter | solution.py:312
  1391.5 32.9 %scatter_fusion = f32[12576,768]{1,0:T(8,128)} fusion(f32[12576,768]{1,0:T(8,128)} %fusion.101, s32[1024]{0:T(1024)S(1)} %bitcast.232, f32[1024,768]{1,0:T(8,128)} %fusion.31), kind=kCustom, calls=%fused_computation.7 | custom fusion | flops 786432 | bytes 9441280 | tf_op jit(solution)/shard_map/scatter-add | solution.py:305
  1424.4 782.2 %fusion = f32[1576,768]{1,0:T(8,128)} fusion(f32[12576,768]{1,0:T(8,128)} %scatter_fusion), kind=kCustom, calls=%all-reduce-scatter | all-reduce-scatter fusion | flops 9682945 | bytes 43475456
  2211.2 13.4 concatenate.15
  2233.7 41.7 %all-reduce.4 = (f32[]{:T(128)}, f32[]{:T(128)}) all-reduce(f32[]{:T(128)S(6)} %div.270, f32[]{:T(128)S(6)} %add.574), channel_id=1, replica_groups=mesh['expert'=8,'hidden'=4] {'expert','hidden'}, use_global_device_ids=true, to_apply=%region_18.19 | all-reduce | flops 2 | bytes 16 | tf_op jit(solution)/shard_map/psum | solution.py:328
  2276.8 13.5 multiply_subtract_fusion
  2294.1 6.4 multiply_subtract_fusion.1
  (304 shorter events, 144.5 us)
Async XLA Ops:
  7.2 503.8 %copy-start = (s32[50304]{0:T(1024)S(1)}, s32[50304]{0:T(1024)}, u32[]{:S(2)}) copy-start(s32[50304]{0:T(1024)} %param.27) | copy-start | bytes 603652
  7.2 49.0 %copy-start.28 = (f32[96,3,192]{2,0,1:T(8,128)S(1)}, f32[96,3,192]{2,0,1:T(8,128)}, u32[]{:S(2)}) copy-start(f32[96,3,192]{2,0,1:T(8,128)} %param.31) | copy-start | bytes 663556
  7.2 378.8 %all-gather.19.cloned.1.call-start = ((), (), s32[]{:S(2)}) async-start(), calls=%async_computation.21 | async-start | bytes 21786624 | tf_op jit(solution)/shard_map/all_gather | solution.py:155
  11.4 45.0 %copy-start.59 = (s32[1,1024]{1,0:T(1,128)S(1)}, s32[1,1024]{1,0:T(1,128)}, u32[]{:S(2)}) copy-start(s32[1,1024]{1,0:T(1,128)} %param.24) | copy-start | bytes 12292
  11.4 481.0 %all-reduce.10.cloned.1.call-start = ((), (), s32[]{:S(2)}) async-start(), calls=%async_computation.9 | async-start | bytes 3145728 | tf_op jit(solution)/shard_map/psum | solution.py:168
  56.5 364.9 %copy-start.65 = (pred[1024]{0:T(1024)(128)(4,1)}, pred[1024]{0:T(1024)(128)(4,1)S(1)}, u32[]{:S(2)}) copy-start(pred[1024]{0:T(1024)(128)(4,1)S(1)} %fusion.83) | copy-start | bytes 3076
  56.6 351.3 %copy-start.60 = (s32[1024,1]{0,1:T(1,128)}, s32[1024,1]{0,1:T(1,128)S(1)}, u32[]{:S(2)}) copy-start(s32[1024,1]{0,1:T(1,128)S(1)} %get-tuple-element.320) | copy-start | bytes 12292
  422.7 37.7 %copy-start.36 = (f32[96,192]{1,0:T(8,128)S(1)}, f32[96,192]{1,0:T(8,128)}, u32[]{:S(2)}) copy-start(f32[96,192]{1,0:T(8,128)} %param.34) | copy-start | bytes 221188
  422.7 69.1 %copy-start.51 = (s32[1,1024]{1,0:T(1,128)S(1)}, s32[1,1024]{1,0:T(1,128)}, u32[]{:S(2)}) copy-start(s32[1,1024]{1,0:T(1,128)} %param.26) | copy-start | bytes 12292
  422.8 156.3 %all-reduce.12.cloned.1.call-start = ((), (), s32[]{:S(2)}) async-start(), calls=%async_computation.10 | async-start | bytes 6291456 | tf_op jit(solution)/shard_map/psum | solution.py:182
  460.5 37.1 %copy-start.31 = (bf16[768,3,192]{0,2,1:T(8,128)(2,1)}, bf16[768,3,192]{0,2,1:T(8,128)(2,1)S(1)}, u32[]{:S(2)}) copy-start(bf16[768,3,192]{0,2,1:T(8,128)(2,1)S(1)} %copy.97) | copy-start | bytes 2654212
  460.5 37.1 %copy-start.55 = (f32[768]{0:T(1024)}, f32[768]{0:T(1024)S(1)}, u32[]{:S(2)}) copy-start(f32[768]{0:T(1024)S(1)} %get-tuple-element.269) | copy-start | bytes 9220
  460.5 121.5 %copy-start.45 = (f32[768]{0:T(1024)}, f32[768]{0:T(1024)S(1)}, u32[]{:S(2)}) copy-start(f32[768]{0:T(1024)S(1)} %get-tuple-element.267) | copy-start | bytes 9220
  491.8 15.7 copy-start.14
  510.6 136.0 %all-gather.11.cloned.1.call-start = ((), (), s32[]{:S(2)}) async-start(), calls=%async_computation.11 | async-start | bytes 3932160 | tf_op jit(solution)/shard_map/all_gather | solution.py:114
  619.5 100.8 %reduce-scatter.10.cloned.1.call-start = ((), (), s32[]{:S(2)}) async-start(), calls=%async_computation.12 | async-start | bytes 5898240 | tf_op jit(solution)/shard_map/reduce_scatter | solution.py:118
  651.4 16.7 copy-start.18
  672.3 107.4 %all-gather.13.cloned.1.call-start = ((), (), s32[]{:S(2)}) async-start(), calls=%async_computation.13 | async-start | bytes 3932160 | tf_op jit(solution)/shard_map/all_gather | solution.py:114
  722.5 30.8 %copy-start.52 = (s32[1,1024]{1,0:T(1,128)S(1)}, s32[1,1024]{1,0:T(1,128)}, u32[]{:S(2)}) copy-start(s32[1,1024]{1,0:T(1,128)} %param.25) | copy-start | bytes 12292
  753.0 253.6 %all-reduce.14.cloned.1.call-start = ((), (), s32[]{:S(2)}) async-start(), calls=%async_computation.14 | async-start | bytes 6291456 | tf_op jit(solution)/shard_map/psum | solution.py:252
  938.9 136.6 %all-gather.15.cloned.1.call-start = ((), (), s32[]{:S(2)}) async-start(), calls=%async_computation.15 | async-start | bytes 3932160 | tf_op jit(solution)/shard_map/all_gather | solution.py:114
  1048.4 93.9 %reduce-scatter.12.cloned.1.call-start = ((), (), s32[]{:S(2)}) async-start(), calls=%async_computation.16 | async-start | bytes 5898240 | tf_op jit(solution)/shard_map/reduce_scatter | solution.py:118
  1094.3 107.5 %all-gather.17.cloned.1.call-start = ((), (), s32[]{:S(2)}) async-start(), calls=%async_computation.17 | async-start | bytes 3932160 | tf_op jit(solution)/shard_map/all_gather | solution.py:114
  1144.5 30.8 %copy-start.71 = (u32[32]{0:T(128)S(1)}, u32[32]{0:T(128)}, u32[]{:S(2)}) copy-start(u32[32]{0:T(128)} %constant.380) | copy-start | bytes 388
  1144.5 32.0 %copy-start.48 = (f32[3,1024]{1,0:T(4,128)S(1)}, f32[3,1024]{1,0:T(4,128)}, u32[]{:S(2)}) copy-start(f32[3,1024]{1,0:T(4,128)} %copy-done.47) | copy-start | bytes 36868
  1144.5 32.0 %copy-start.50 = (f32[3,1024]{1,0:T(4,128)S(1)}, f32[3,1024]{1,0:T(4,128)}, u32[]{:S(2)}) copy-start(f32[3,1024]{1,0:T(4,128)} %copy-done.49) | copy-start | bytes 36868
  1175.0 144.4 %all-reduce.16.cloned.1.call-start = ((), (), s32[]{:S(2)}) async-start(), calls=%async_computation.18 | async-start | bytes 6291456 | tf_op jit(solution)/shard_map/psum | solution.py:300
  1250.8 40.2 %copy-start.7 = (f32[1024,768]{1,0:T(8,128)S(1)}, f32[1024,768]{1,0:T(8,128)}, u32[]{:S(2)}) copy-start(f32[1024,768]{1,0:T(8,128)} %copy-done.6) | copy-start | bytes 9437188
  1250.9 134.9 %reduce-scatter.16.cloned.1.call-start = ((), (), s32[]{:S(2)}) async-start(), calls=%async_computation.20 | async-start | bytes 884736 | tf_op jit(solution)/shard_map/reduce_scatter | solution.py:312
  1293.6 915.4 %reduce-scatter.18.cloned.1.call-start = ((), (), s32[]{:S(2)}) async-start(), calls=%async_computation.22 | async-start | bytes 442368
  1300.7 18.7 copy-start.56
  1300.7 18.7 copy-start.64
  1323.9 63.3 %copy-start.58 = (f32[1024]{0:T(1024)S(1)}, f32[1024]{0:T(1024)}, u32[]{:S(2)}) copy-start(f32[1024]{0:T(1024)} %copy-done.57) | copy-start | bytes 12292
  1324.0 63.3 %copy-start.62 = (f32[1024]{0:T(1024)S(1)}, f32[1024]{0:T(1024)}, u32[]{:S(2)}) copy-start(f32[1024]{0:T(1024)} %get-tuple-element.316) | copy-start | bytes 12292
  1324.0 63.3 %copy-start.66 = (pred[1024]{0:T(1024)(128)(4,1)S(1)}, pred[1024]{0:T(1024)(128)(4,1)}, u32[]{:S(2)}) copy-start(pred[1024]{0:T(1024)(128)(4,1)} %copy-done.65) | copy-start | bytes 3076
  1324.0 904.9 %reduce-scatter.14.cloned.1.call-start = ((), (), s32[]{:S(2)}) async-start(), calls=%async_computation.19 | async-start | bytes 2654208 | tf_op jit(solution)/shard_map/reduce_scatter | solution.py:311
  2207.5 3.6 collective-permute-start
  2224.6 51.6 %copy-start.68 = (f32[96,3]{0,1:T(4,128)S(1)}, f32[96,3]{0,1:T(4,128)}, u32[]{:S(2)}) copy-start(f32[96,3]{0,1:T(4,128)} %param.43) | copy-start | bytes 3460
  2224.6 51.6 %copy-start.69 = (f32[96,3]{0,1:T(4,128)S(1)}, f32[96,3]{0,1:T(4,128)}, u32[]{:S(2)}) copy-start(f32[96,3]{0,1:T(4,128)} %param.44) | copy-start | bytes 3460
  2224.6 51.6 %copy-start.70 = (f32[96,3]{0,1:T(4,128)S(1)}, f32[96,3]{0,1:T(4,128)}, u32[]{:S(2)}) copy-start(f32[96,3]{0,1:T(4,128)} %param.45) | copy-start | bytes 3460
  2276.8 13.6 copy-start.9
  2276.8 13.6 copy-start.10
  2276.8 13.6 copy-start.17
  2276.8 14.6 copy-start.19
  2276.8 15.3 copy-start.20
  2276.8 15.9 copy-start.21
  2276.8 16.6 copy-start.22
  2276.8 17.2 copy-start.23
  (44 other events, 205.9 us)
Sparse Core Ops, SparseCore 0:
  11.5 374.4 all-gather.18
  422.9 42.7 all-reduce.9
  510.8 68.2 all-reduce.11
  619.6 26.9 all-gather.10
  672.5 47.8 reduce-scatter.9
  753.1 26.6 all-gather.12
  939.0 67.5 all-reduce.13
  1048.5 26.9 all-gather.14
  1094.4 47.8 reduce-scatter.11
  1175.1 26.6 all-gather.16
  1251.0 68.4 all-reduce.15
  1323.2 62.5 reduce-scatter.15
  1389.9 157.3 reduce-scatter.17
  1551.7 121.3 reduce-scatter.13
where the time goes:
time: 2320 us; the launch traced here: 2310 us
  blocking collectives  1050 us (45%)
  waiting for transfers between devices  728 us (31%)
  matrix products  182 us (8%)
  local copies, waits for them, and re-layouts  174 us (8%)
  other arithmetic  146 us (6%)
    unnamed x1, blocking collectives  782 us
    all_gather x1, waiting for transfers between devices, on_device(): lax.all_gather(embed_table.astype(jnp.bfloat16), 'expert', axis=0, tiled=...  329 us
    all_gather x4, waiting for transfers between devices, widen(): return lax.all_gather(block, 'hidden', axis=2, tiled=True)  105 us
    reduce_scatter x2, waiting for transfers between devices, split_sum(): return lax.psum_scatter(rows_in, 'hidden', scatter_dimension=1, tiled=True)  95.9 us
    psum x1, waiting for transfers between devices, on_device(): lax.psum(jnp.dot(d_logits, table_all, preferred_element_type=jnp.float32)...  67.7 us
    psum x1, waiting for transfers between devices, on_device(): after_attn = embedded + lax.psum(attn_part, 'hidden')  59 us
    reduce_scatter x1, waiting for transfers between devices, on_device(): lax.psum_scatter(d_attn_out, 'expert', scatter_dimension=0, tiled=True)  56.9 us
    unnamed x158, local copies, waits for them, and re-layouts  53.3 us
  transfers between devices with their start and end apart: 15, of which 11 were waited for; matrix products, arithmetic and copies ran while one was open for 40% of the time, Pallas kernels for 0%

commit v1 on v0

v1 whole, which is shorter than its diff:
```python
from functools import partial

import jax
import jax.numpy as jnp
from jax import lax
from jax.experimental import pallas as pl
from jax.experimental.pallas import tpu as pltpu
from jax.sharding import PartitionSpec as P

HD = 64
DOCS_ROW = 8
STEP = 7


EPS_NORM = 1e-06
BETA_ONE = 0.9
BETA_TWO = 0.95
ADAM_EPS = 1e-08
RATE_MATRIX = 0.05
RATE_GAIN = 0.3
DECAY = 0.1
CLIP_AT = 0.005
NEVER = -1e30
BF = jnp.bfloat16
F32 = jnp.float32
VMEM = 56 * 1024 * 1024


def flip(x, axis, k):
    return lax.ppermute(x, axis, [(j, j ^ k) for j in range(lax.axis_size(axis))])


def hidden_gather(x):
    two = jnp.stack([x, flip(x, "hidden", 2)])
    return jnp.concatenate([two, flip(two, "hidden", 1)])


def piece_of(bits):
    return (bits >> 1) + 2 * (bits & 1)


def round_up(n, m):
    return -(-n // m) * m


def rms_norm(rows_in, gain):
    return (
        rows_in * lax.rsqrt(jnp.mean(rows_in * rows_in, axis=-1, keepdims=True) + EPS_NORM) * gain
    )


def norm_back(rows_in, gain, gradient):
    normed, pullback = jax.vjp(rms_norm, rows_in, gain)
    return pullback(gradient)


def dot(a, b, ca=1, cb=0):
    return lax.dot_general(a, b, (((ca,), (cb,)), ((), ())), preferred_element_type=F32)


def hot_rows(place, count):
    return (jnp.arange(count, dtype=jnp.int32)[:, None] == place[None, :]).astype(BF)


def hot_columns(place, count):
    return (place[:, None] == jnp.arange(count, dtype=jnp.int32)[None, :]).astype(BF)


QB = 256
SPAN = 2


def mask_of(seg_a, seg_b, pos_a, pos_b):
    return (pos_a >= pos_b) & (seg_a == seg_b)


def attend_kernel(q_ref, k_ref, v_ref, segr_ref, segc_ref, o_ref):
    seq = q_ref.shape[0]
    factor = HD**-0.5
    for b in range(seq // QB):
        lo, hi = max(0, b - SPAN) * QB, (b + 1) * QB
        width = hi - lo
        seg_q = segc_ref[b * QB : hi, :]
        seg_k = segr_ref[:, lo:hi]
        pos_q = lax.broadcasted_iota(jnp.int32, (QB, width), 0) + b * QB
        pos_k = lax.broadcasted_iota(jnp.int32, (QB, width), 1) + lo
        allowed = (pos_q >= pos_k) & (seg_q == seg_k)
        for p in range(2):
            cols = slice(p * HD, (p + 1) * HD)
            q = q_ref[b * QB : hi, cols]
            k = k_ref[lo:hi, cols]
            v = v_ref[lo:hi, cols]
            s = jnp.where(allowed, dot(q, k, 1, 1) * factor, NEVER)
            e = jnp.exp(s - jnp.max(s, axis=1, keepdims=True))
            prob = (e / jnp.sum(e, axis=1, keepdims=True)).astype(BF)
            o_ref[b * QB : hi, cols] = dot(prob, v).astype(BF)


def attend(qkv, seg):
    seq, width = qkv.shape
    pairs = width // 3 // 128

    def part(c):
        return pl.BlockSpec((seq, 128), lambda i: (0, c * pairs + i))

    return pl.pallas_call(
        attend_kernel,
        grid=(pairs,),
        in_specs=[
            part(0),
            part(1),
            part(2),
            pl.BlockSpec((1, seq), lambda i: (0, 0)),
            pl.BlockSpec((seq, 1), lambda i: (0, 0)),
        ],
        out_specs=pl.BlockSpec((seq, 128), lambda i: (0, i)),
        out_shape=jax.ShapeDtypeStruct((seq, width // 3), BF),
        compiler_params=pltpu.CompilerParams(vmem_limit_bytes=VMEM),
        name="attend",
    )(qkv, qkv, qkv, seg[None, :], seg[:, None])


def attend_back_kernel(q_ref, k_ref, v_ref, g_ref, segr_ref, segc_ref, dq_ref, dk_ref, dv_ref, dk_acc, dv_acc):
    seq = q_ref.shape[0]
    factor = HD**-0.5
    dk_acc[...] = jnp.zeros_like(dk_acc)
    dv_acc[...] = jnp.zeros_like(dv_acc)
    for b in range(seq // QB):
        lo, hi = max(0, b - SPAN) * QB, (b + 1) * QB
        width = hi - lo
        seg_q = segr_ref[:, b * QB : hi]
        seg_k = segc_ref[lo:hi, :]
        pos_q = lax.broadcasted_iota(jnp.int32, (width, QB), 1) + b * QB
        pos_k = lax.broadcasted_iota(jnp.int32, (width, QB), 0) + lo
        allowed = (pos_q >= pos_k) & (seg_q == seg_k)
        for p in range(2):
            cols = slice(p * HD, (p + 1) * HD)
            q = q_ref[b * QB : hi, cols]
            k = k_ref[lo:hi, cols]
            v = v_ref[lo:hi, cols]
            g = g_ref[b * QB : hi, cols]
            s = jnp.where(allowed, dot(k, q, 1, 1) * factor, NEVER)
            e = jnp.exp(s - jnp.max(s, axis=0, keepdims=True))
            prob = e / jnp.sum(e, axis=0, keepdims=True)
            d_prob = dot(v, g, 1, 1)
            centre = jnp.sum(prob * d_prob, axis=0, keepdims=True)
            d_score = (prob * (d_prob - centre)).astype(BF)
            dq_ref[b * QB : hi, cols] = (dot(d_score, k, 0, 0) * factor).astype(BF)
            dk_acc[lo:hi, cols] += dot(d_score, q) * factor
            dv_acc[lo:hi, cols] += dot(prob.astype(BF), g)
    dk_ref[...] = dk_acc[...].astype(BF)
    dv_ref[...] = dv_acc[...].astype(BF)


def attend_back(qkv, seg, grad):
    seq, width = qkv.shape
    pairs = width // 3 // 128

    def part(c):
        return pl.BlockSpec((seq, 128), lambda i: (0, c * pairs + i))

    return pl.pallas_call(
        attend_back_kernel,
        grid=(pairs,),
        in_specs=[
            part(0),
            part(1),
            part(2),
            part(0),
            pl.BlockSpec((1, seq), lambda i: (0, 0)),
            pl.BlockSpec((seq, 1), lambda i: (0, 0)),
        ],
        out_specs=[part(0)] * 3,
        out_shape=[jax.ShapeDtypeStruct((seq, width // 3), BF)] * 3,
        scratch_shapes=[pltpu.VMEM((seq, 128), F32)] * 2,
        compiler_params=pltpu.CompilerParams(vmem_limit_bytes=VMEM),
        name="attend_back",
    )(qkv, qkv, qkv, grad, seg[None, :], seg[:, None])


def vocab_block(count):
    for parts in (5, 4, 3, 2):
        if count % (128 * parts) == 0 and count // parts >= 640:
            return count // parts
    return count


def logits_kernel(block, padded, real, table_ref, rows_ref, col_ref, out_ref, stat_ref):
    j = pl.program_id(0)
    logits = dot(table_ref[...], rows_ref[...], 1, 1)
    first = j * block
    row = lax.broadcasted_iota(jnp.int32, (block, 1), 0) + first
    pad = jnp.zeros((block, 1), F32)
    for q in range(4):
        pad = jnp.where((row >= q * padded + real) & (row < (q + 1) * padded), NEVER, pad)
    logits = logits + pad
    out_ref[...] = logits

    @pl.when(j == 0)
    def _():
        stat_ref[0:1, :] = jnp.full((1, stat_ref.shape[1]), NEVER, F32)
        stat_ref[1:8, :] = jnp.zeros((7, stat_ref.shape[1]), F32)

    before = stat_ref[0:1, :]
    peak = jnp.maximum(before, jnp.max(logits, axis=0, keepdims=True))
    total = jnp.sum(jnp.exp(logits - peak), axis=0, keepdims=True)
    rows = lax.broadcasted_iota(jnp.int32, logits.shape, 0)
    hit = rows == (col_ref[...] - first)
    stat_ref[0:1, :] = peak
    stat_ref[1:2, :] = stat_ref[1:2, :] * jnp.exp(before - peak) + total
    stat_ref[2:3, :] += jnp.sum(jnp.where(hit, logits, 0.0), axis=0, keepdims=True)


def head_logits(table, rows, col, padded, real):
    vocab, width = table.shape
    tokens = rows.shape[0]
    block = vocab_block(vocab)
    return pl.pallas_call(
        partial(logits_kernel, block, padded, real),
        grid=(vocab // block,),
        in_specs=[
            pl.BlockSpec((block, width), lambda j: (j, 0)),
            pl.BlockSpec((tokens, width), lambda j: (0, 0)),
            pl.BlockSpec((1, tokens), lambda j: (0, 0)),
        ],
        out_specs=[
            pl.BlockSpec((block, tokens), lambda j: (j, 0)),
            pl.BlockSpec((8, tokens), lambda j: (0, 0)),
        ],
        out_shape=[
            jax.ShapeDtypeStruct((vocab, tokens), F32),
            jax.ShapeDtypeStruct((8, tokens), F32),
        ],
        compiler_params=pltpu.CompilerParams(vmem_limit_bytes=VMEM),
        cost_estimate=pl.CostEstimate(
            flops=2 * vocab * tokens * width,
            bytes_accessed=4 * vocab * tokens + 2 * vocab * width,
            transcendentals=vocab * tokens,
        ),
        name="head_logits",
    )(table, rows, col)


def head_back_kernel(block, table_ref, logits_ref, col_ref, side_ref, d_ref, out_ref, acc):
    j = pl.program_id(0)
    logits = logits_ref[...]
    rows = lax.broadcasted_iota(jnp.int32, logits.shape, 0)
    hit = rows == (col_ref[...] - j * block)
    prob = jnp.exp(logits - side_ref[0:1, :])
    d = (jnp.where(hit, prob - 1.0, prob) * side_ref[1:2, :]).astype(BF)
    d_ref[...] = d
    part = dot(table_ref[...], d)

    @pl.when(j == 0)
    def _():
        acc[...] = part

    @pl.when(j > 0)
    def _():
        acc[...] += part

    @pl.when(j == pl.num_programs(0) - 1)
    def _():
        out_ref[...] = acc[...].T.astype(out_ref.dtype)


def head_back(table_t, logits, col, side):
    width, vocab = table_t.shape
    tokens = logits.shape[1]
    block = vocab_block(vocab)
    return pl.pallas_call(
        partial(head_back_kernel, block),
        grid=(vocab // block,),
        in_specs=[
            pl.BlockSpec((width, block), lambda j: (0, j)),
            pl.BlockSpec((block, tokens), lambda j: (j, 0)),
            pl.BlockSpec((1, tokens), lambda j: (0, 0)),
            pl.BlockSpec((8, tokens), lambda j: (0, 0)),
        ],
        out_specs=[
            pl.BlockSpec((block, tokens), lambda j: (j, 0)),
            pl.BlockSpec((tokens, width), lambda j: (0, 0)),
        ],
        out_shape=[
            jax.ShapeDtypeStruct((vocab, tokens), BF),
            jax.ShapeDtypeStruct((tokens, width), BF),
        ],
        scratch_shapes=[pltpu.VMEM((width, tokens), F32)],
        compiler_params=pltpu.CompilerParams(vmem_limit_bytes=VMEM),
        cost_estimate=pl.CostEstimate(
            flops=2 * vocab * tokens * width,
            bytes_accessed=6 * vocab * tokens + 2 * vocab * width,
            transcendentals=vocab * tokens,
        ),
        name="head_back",
    )(table_t, logits, col, side)


def table_grad_kernel(count, *refs):
    d_refs, row_refs, out_ref = refs[:count], refs[count : 2 * count], refs[2 * count]
    total = dot(d_refs[0][...], row_refs[0][...])
    for k in range(1, count):
        total += dot(d_refs[k][...], row_refs[k][...])
    out_ref[...] = total


def table_grad(ds, rows):
    vocab, tokens = ds[0].shape
    width = rows[0].shape[1]
    count = len(ds)
    block = vocab // 10 if vocab % 160 == 0 else vocab // 4 if vocab % 64 == 0 else vocab
    return pl.pallas_call(
        partial(table_grad_kernel, count),
        grid=(vocab // block,),
        in_specs=[pl.BlockSpec((block, tokens), lambda j: (j, 0))] * count
        + [pl.BlockSpec((tokens, width), lambda j: (0, 0))] * count,
        out_specs=pl.BlockSpec((block, width), lambda j: (j, 0)),
        out_shape=jax.ShapeDtypeStruct((vocab, width), F32),
        compiler_params=pltpu.CompilerParams(vmem_limit_bytes=VMEM),
        cost_estimate=pl.CostEstimate(
            flops=2 * vocab * tokens * width * count,
            bytes_accessed=2 * vocab * tokens * count + 4 * vocab * width,
            transcendentals=0,
        ),
        name="table_grad",
    )(*ds, *rows)


def adam_step(weight, first_moment, second_moment, gradient, step_rate, weight_decay):
    first_moment = BETA_ONE * first_moment + (1.0 - BETA_ONE) * gradient
    second_moment = BETA_TWO * second_moment + (1.0 - BETA_TWO) * gradient * gradient
    update = (
        first_moment
        / (1.0 - BETA_ONE**STEP)
        / (jnp.sqrt(second_moment / (1.0 - BETA_TWO**STEP)) + ADAM_EPS)
    )
    return (weight - step_rate * (update + weight_decay * weight), first_moment, second_moment)


def combine_stats(left, right):
    peak = jnp.maximum(left[0], right[0])
    total = left[1] * jnp.exp(left[0] - peak) + right[1] * jnp.exp(right[0] - peak)
    return jnp.stack([peak, total, left[2] + right[2]])


def on_device(
    token_ids,
    target_ids,
    doc_segments,
    hash_experts,
    embed_table,
    embed_first,
    embed_second,
    attn_in,
    attn_in_first,
    attn_in_second,
    attn_out,
    attn_out_first,
    attn_out_second,
    expert_in,
    expert_in_first,
    expert_in_second,
    expert_out,
    expert_out_first,
    expert_out_second,
    norm_gains,
    gains_first,
    gains_second,
):
    n_expert = lax.axis_size("expert")
    n_hidden = lax.axis_size("hidden")
    assert n_hidden == 4 and token_ids.shape[0] == 1
    e_index = lax.axis_index("expert")
    h_index = lax.axis_index("hidden")
    tok_count = token_ids.shape[1]
    vocab_rows, model_width = embed_table.shape
    embed_scale = model_width**0.5
    ids = token_ids[0]
    targets = target_ids[0]
    segment = doc_segments[0]
    token_at = jnp.arange(tok_count, dtype=jnp.int32)

    padded = round_up(vocab_rows, 32)
    table_own = jnp.pad(embed_table.astype(BF), ((0, padded - vocab_rows), (0, 0)))
    own_rows = attn_in.shape[0]
    head_width = attn_in.shape[2]
    packed = jnp.concatenate(
        [
            attn_in.reshape(own_rows, 3 * head_width),
            attn_out,
            jnp.pad(norm_gains, ((0, 0), (0, 125))),
        ],
        axis=1,
    ).astype(BF)
    packed = jnp.stack([packed, flip(packed, "hidden", 2)])
    packed = lax.all_gather(packed, "expert", axis=1, tiled=True)
    w_qkv = (
        packed[:, :, : 3 * head_width]
        .reshape(2, model_width, 3, head_width)
        .transpose(1, 2, 0, 3)
        .reshape(model_width, 6 * head_width)
    )
    w_proj = (
        packed[:, :, 3 * head_width : 4 * head_width]
        .transpose(1, 0, 2)
        .reshape(model_width, 2 * head_width)
    )
    gain_full = packed[0, :, 4 * head_width : 4 * head_width + 3].astype(F32)

    slots = round_up(3 * tok_count // (2 * n_expert * n_hidden), 16)
    shard = ids // vocab_rows
    shard_e, shard_h = shard // n_hidden, shard % n_hidden
    same_id = ids[:, None] == ids[None, :]
    first_at = jnp.min(jnp.where(same_id, token_at[None, :], tok_count), axis=1)
    is_first = first_at == token_at
    rank = jnp.sum(
        (
            (shard[:, None] == shard[None, :])
            & is_first[None, :]
            & (token_at[None, :] < first_at[:, None])
        ).astype(jnp.int32),
        axis=1,
    )
    overflow = jnp.max(rank) >= slots
    place_own = jnp.where(
        (shard_h == h_index) & (rank < slots), shard_e * slots + rank, -1
    )
    wanted = jnp.max(
        jnp.where(
            jnp.arange(n_expert * slots, dtype=jnp.int32)[:, None] == place_own[None, :],
            (ids % vocab_rows)[None, :],
            -1,
        ),
        axis=1,
    )
    asked = jnp.concatenate(
        [
            wanted.reshape(n_expert, slots),
            jnp.broadcast_to(overflow.astype(jnp.int32), (n_expert, 128 - slots)),
        ],
        axis=1,
    )
    asked = lax.all_to_all(asked, "expert", split_axis=0, concat_axis=0, tiled=True)
    any_overflow = jnp.max(asked[:, slots:]) > 0
    asked_rows = asked[:, :slots].reshape(n_expert * slots)
    answer = dot(hot_columns(asked_rows, padded), table_own).astype(BF)
    answer = lax.all_to_all(answer, "expert", split_axis=0, concat_axis=0, tiled=True)
    answers = hidden_gather(answer).reshape(4 * n_expert * slots, model_width)
    place_all = piece_of(shard_h ^ h_index) * (n_expert * slots) + shard_e * slots + rank
    looked_up = dot(hot_columns(place_all, 4 * n_expert * slots), answers).astype(BF)

    def look_up_all():
        table_all = lax.all_gather(embed_table.astype(BF), "expert", axis=0, tiled=True)
        is_owned = shard_h == h_index
        local = jnp.where(is_owned, shard_e * vocab_rows + ids % vocab_rows, 0)
        found = jnp.where(is_owned[:, None], table_all[local], jnp.zeros((), BF))
        return lax.psum(found, "hidden")

    looked_up = lax.cond(any_overflow, look_up_all, lambda: looked_up)
    embedded = looked_up.astype(F32) * embed_scale

    normed_one = rms_norm(embedded, gain_full[:, 0]).astype(BF)
    qkv = dot(normed_one, w_qkv).astype(BF)
    attended = attend(qkv, segment)
    attn_part = dot(attended, w_proj, 1, 1)
    after_attn = embedded + (attn_part + flip(attn_part, "hidden", 1))
    normed_two = rms_norm(after_attn, gain_full[:, 1]).astype(BF)

    capacity = 3 * tok_count // (2 * n_expert)
    quarter = capacity // n_hidden
    expert_ids = hash_experts[ids]
    onehot = (expert_ids[:, None] == jnp.arange(n_expert, dtype=jnp.int32)).astype(jnp.int32)
    before = jnp.cumsum(onehot, axis=0) - onehot
    slot_rank = jnp.sum(before * onehot, axis=1)
    kept = slot_rank < capacity
    slot_h = slot_rank // quarter
    slot_in = expert_ids * quarter + slot_rank % quarter
    rows_dev = n_expert * quarter
    fill_place = jnp.where(kept & (slot_h == h_index), slot_in, -1)
    pick_place = jnp.where(kept, piece_of(slot_h ^ h_index) * rows_dev + slot_in, -1)
    fill_hot = hot_rows(fill_place, rows_dev)
    pick_hot = hot_columns(pick_place, 4 * rows_dev)

    def to_expert(rows_in):
        block = dot(fill_hot, rows_in).astype(BF)
        return lax.all_to_all(block, "expert", split_axis=0, concat_axis=0, tiled=True)

    def from_expert(rows_in):
        block = lax.all_to_all(rows_in, "expert", split_axis=0, concat_axis=0, tiled=True)
        return dot(pick_hot, hidden_gather(block).reshape(4 * rows_dev, model_width))

    weights_own = jnp.stack([expert_in[0], expert_out[0]]).astype(BF)
    expert_w = hidden_gather(weights_own)
    received = to_expert(normed_two)
    pre_act = [dot(received, expert_w[p, 0]) for p in range(4)]
    active = [jax.nn.gelu(pre, approximate=False).astype(BF) for pre in pre_act]
    expert_result = sum(dot(active[p], expert_w[p, 1]) for p in range(4)).astype(BF)
    moe_rows = from_expert(expert_result)
    after_moe = after_attn + moe_rows
    final_rows = rms_norm(after_moe, gain_full[:, 2]).astype(BF)

    half, fourth = tok_count // 2, tok_count // 4
    own_at = (h_index & 1) * half + (h_index >> 1) * fourth
    other_at = (h_index & 1) * half + (1 - (h_index >> 1)) * fourth
    n_far = n_expert // 2

    def own_order(x):
        return jnp.concatenate(
            [
                lax.dynamic_slice_in_dim(x, own_at, fourth, x.ndim - 1),
                lax.dynamic_slice_in_dim(x, other_at, fourth, x.ndim - 1),
            ],
            axis=-1,
        )

    counts = jnp.sum((segment[:, None] == segment[None, :]).astype(F32), axis=1)
    weights = 1.0 / counts / (n_expert * DOCS_ROW)
    about = own_order(jnp.stack([targets.astype(F32), weights]))
    about_all = [about] + [flip(about, "expert", 2 * k) for k in range(1, n_far)]
    slice_two = jnp.concatenate([table_own, flip(table_own, "expert", 1)])
    table = jnp.concatenate([slice_two, flip(slice_two, "hidden", 1)])
    table_t = table.T

    own_part = lax.dynamic_slice_in_dim(final_rows, own_at, fourth, 0)
    other_part = lax.dynamic_slice_in_dim(final_rows, other_at, fourth, 0)
    head_rows = [jnp.concatenate([own_part, other_part])]
    for k in range(1, n_far):
        far = flip(own_part, "expert", 2 * k)
        head_rows.append(jnp.concatenate([far, flip(far, "hidden", 2)]))

    columns = []
    for k in range(n_far):
        target = about_all[k][0].astype(jnp.int32)
        block_of = target // vocab_rows
        away_e = (block_of // n_hidden) ^ e_index
        away_h = (block_of % n_hidden) ^ h_index
        mine = (away_e < 2) & (away_h < 2)
        column = (away_e + 2 * away_h) * padded + target % vocab_rows
        columns.append(jnp.where(mine, column, -1)[None, :])
    logits, stats = [], []
    for k in range(n_far):
        one, stat = head_logits(table, head_rows[k], columns[k], padded, vocab_rows)
        logits.append(one)
        stats.append(stat[:3])
    stat = jnp.stack(stats, axis=1)
    across = flip(stat, "hidden", 2)
    stat = combine_stats(stat, jnp.concatenate([across[..., fourth:], across[..., :fourth]], axis=2))
    far_stats = [flip(stat, "expert", 2 * k) for k in range(1, n_far)]
    for k in range(1, n_far):
        far = jnp.stack([far_stats[k - 1][:, j ^ k] for j in range(n_far)], axis=1)
        stat = combine_stats(stat, far)
    log_total = stat[0] + jnp.log(stat[1])
    loss_part = jnp.sum((log_total[0] - stat[2, 0]) * about[1])

    d_logits, d_parts = [None] * n_far, [None] * n_far
    for k in list(range(1, n_far)) + [0]:
        side = jnp.concatenate(
            [log_total[k][None, :], about_all[k][1:2], jnp.zeros((6, half), F32)]
        )
        d_logits[k], part = head_back(table_t, logits[k], columns[k], side)
        gathered = part[:fourth].astype(F32) + flip(part[fourth:], "hidden", 2).astype(F32)
        if k:
            gathered = flip(gathered.astype(BF), "expert", 2 * k).astype(F32)
        d_parts[k] = gathered
    d_quarter = sum(d_parts)
    d_four = hidden_gather(d_quarter.astype(BF))
    low_half = jnp.where(h_index & 1, d_four[2:], d_four[:2])
    high_half = jnp.where(h_index & 1, d_four[:2], d_four[2:])
    both = jnp.stack([low_half, high_half])
    both = jnp.where(h_index >> 1, both[:, ::-1], both)
    d_final = both.reshape(tok_count, model_width).astype(F32)

    d_slices = table_grad(d_logits, head_rows)
    d_after_moe, d_gain_three = norm_back(after_moe, gain_full[:, 2], d_final)

    d_slices = d_slices.reshape(2, 2, padded, model_width)
    d_two = d_slices[0] + flip(d_slices[1], "hidden", 1)
    d_table = d_two[0] + flip(d_two[1].astype(BF), "expert", 1).astype(F32)

    grad_in = to_expert(d_after_moe.astype(BF))
    d_received = 0.0
    d_w = []
    for p in range(4):
        d_active = dot(grad_in, expert_w[p, 1], 1, 1)
        gelu_pull = jax.vjp(partial(jax.nn.gelu, approximate=False), pre_act[p])[1]
        d_pre = gelu_pull(d_active)[0].astype(BF)
        d_received = d_received + dot(d_pre, expert_w[p, 0], 1, 1)
        d_w.append(jnp.stack([dot(received, d_pre, 0, 0), dot(active[p], grad_in, 0, 0)]))
    d_normed_two = from_expert(d_received.astype(BF))
    w_near = flip(jnp.stack([d_w[2], d_w[3]]), "hidden", 1)
    g_expert = (d_w[0] + w_near[0]) + flip((d_w[1] + w_near[1]).astype(BF), "hidden", 2).astype(F32)
    d_after_norm, d_gain_two = norm_back(after_attn, gain_full[:, 1], d_normed_two)
    d_after_attn = d_after_moe + d_after_norm

    d_branch = d_after_attn.astype(BF)
    d_proj = dot(d_branch, attended[:, :head_width], 0, 0)
    d_attended = dot(d_branch, w_proj).astype(BF)
    d_qkv = jnp.concatenate(attend_back(qkv, segment, d_attended), axis=1)
    d_norm_part = dot(d_qkv, w_qkv, 1, 1)
    d_own = d_qkv.reshape(tok_count, 3, 2, head_width)[:, :, 0].reshape(tok_count, 3 * head_width)
    d_in = dot(normed_one, d_own, 0, 0)
    d_normed_one = d_norm_part + flip(d_norm_part, "hidden", 1)
    d_embed_norm, d_gain_one = norm_back(embedded, gain_full[:, 0], d_normed_one)
    d_embedded = (d_after_attn + d_embed_norm) * embed_scale

    d_high = lax.reduce_precision(d_embedded, 8, 7)
    d_low = (d_embedded - d_high).astype(BF)
    row_hot = hot_rows(place_own, n_expert * slots)
    d_rows = dot(row_hot, d_high.astype(BF)) + dot(row_hot, d_low)
    d_gains = jnp.stack([d_gain_one, d_gain_two, d_gain_three], axis=1).reshape(n_expert, 1, -1)
    gains_high = lax.reduce_precision(d_gains, 8, 7)
    gains_two = jnp.concatenate([gains_high, d_gains - gains_high], axis=1).astype(BF)
    gains_two = jnp.pad(gains_two, ((0, 0), (0, 14), (0, model_width - gains_two.shape[2])))
    sent = jnp.concatenate(
        [
            d_rows.astype(BF).reshape(n_expert, slots, model_width),
            gains_two,
            jnp.concatenate([d_in, d_proj], axis=1)
            .astype(BF)
            .reshape(n_expert, own_rows, 4 * head_width),
        ],
        axis=1,
    )
    got = lax.all_to_all(sent, "expert", split_axis=0, concat_axis=0, tiled=True)
    got_rows = got[:, :slots].reshape(n_expert * slots, model_width)
    d_scattered = dot(hot_rows(asked_rows, padded), got_rows)

    def scatter_all():
        def step(k, carry):
            d_far, ids_far, total = carry
            shard_far = ids_far // vocab_rows
            is_owned = shard_far == e_index * n_hidden + h_index
            local = jnp.where(is_owned, ids_far % vocab_rows, 0)
            total = total.at[local].add(jnp.where(is_owned[:, None], d_far, 0.0))
            ring = [(j, (j + 1) % n_expert) for j in range(n_expert)]
            return lax.ppermute(d_far, "expert", ring), lax.ppermute(ids_far, "expert", ring), total

        start = (d_embedded, ids, jnp.zeros((padded, model_width), F32))
        return lax.fori_loop(0, n_expert, step, start)[2]

    d_scattered = lax.cond(any_overflow, scatter_all, lambda: d_scattered)
    g_table = (d_table + d_scattered)[:vocab_rows]
    g_attn = jnp.sum(got[:, slots + 16 :].astype(F32), axis=0)
    g_attn_in = g_attn[:, : 3 * head_width].reshape(own_rows, 3, head_width)
    g_attn_out = g_attn[:, 3 * head_width :]
    g_gains = jnp.sum(got[:, slots : slots + 2, : 3 * own_rows].astype(F32), axis=(0, 1)).reshape(
        own_rows, 3
    )
    g_expert_in = g_expert[0][None]
    g_expert_out = g_expert[1][None]

    squares = (
        jnp.sum(g_table * g_table)
        + jnp.sum(g_attn * g_attn)
        + jnp.sum(g_expert * g_expert)
        + jnp.sum(g_gains * g_gains) / n_hidden
    )
    both_sums = jnp.stack([squares, loss_part * (2.0 / n_hidden)])
    both_sums = jnp.broadcast_to(jnp.pad(both_sums, (0, 126))[None], (n_expert, 128))
    both_sums = lax.all_to_all(both_sums, "expert", split_axis=0, concat_axis=0, tiled=True)
    both_sums = lax.all_gather(jnp.sum(both_sums, axis=0), "hidden", axis=0)
    both_sums = jnp.sum(both_sums, axis=0)
    clip_norm = jnp.sqrt(both_sums[0])
    loss_value = both_sums[1]
    clip_scale = jnp.minimum(1.0, CLIP_AT / clip_norm)
    table_up = adam_step(
        embed_table, embed_first, embed_second, g_table * clip_scale, RATE_MATRIX, DECAY
    )
    attn_in_up = adam_step(
        attn_in, attn_in_first, attn_in_second, g_attn_in * clip_scale, RATE_MATRIX, DECAY
    )
    attn_out_up = adam_step(
        attn_out, attn_out_first, attn_out_second, g_attn_out * clip_scale, RATE_MATRIX, DECAY
    )
    expert_in_up = adam_step(
        expert_in, expert_in_first, expert_in_second, g_expert_in * clip_scale, RATE_MATRIX, DECAY
    )
    expert_out_up = adam_step(
        expert_out,
        expert_out_first,
        expert_out_second,
        g_expert_out * clip_scale,
        RATE_MATRIX,
        DECAY,
    )
    gains_up = adam_step(
        norm_gains, gains_first, gains_second, g_gains * clip_scale, RATE_GAIN, 0.0
    )
    return (
        loss_value,
        clip_norm,
        *table_up,
        *attn_in_up,
        *attn_out_up,
        *expert_in_up,
        *expert_out_up,
        *gains_up,
    )


def solution(mesh):
    rows = P("expert", None)
    table = P(("expert", "hidden"), None)
    wide = P("expert", None, "hidden")
    flat = P("expert", "hidden")
    tall = P("expert", "hidden", None)
    groups = (table, wide, flat, wide, tall, rows)
    each = tuple(spec for spec in groups for _ in range(3))
    return jax.shard_map(
        on_device,
        mesh=mesh,
        in_specs=(rows, rows, rows, P(), *each),
        out_specs=(P(), P(), *each),
        check_vma=False,
    )
```

time: 2320 us -> 937 us (0.40)
  blocking collectives: 1050 us -> 48.3 us
  waiting for transfers between devices: 728 us -> 240 us
  Pallas kernels: 0 us -> 181 us
  matrix products: 182 us -> 96.3 us
  starting transfers between devices: 3.93 us -> 69 us
  local copies, waits for them, and re-layouts: 174 us -> 133 us
    unnamed x1 -> x0, blocking collectives: 782 us -> none
    all_gather x5 -> x1, waiting for transfers between devices: 434 us -> 53.9 us  [on_device(): packed = lax.all_gather(packed, 'expert', axis=1, tiled=True)]
    pallas_call x0 -> x11, Pallas kernels: none -> 181 us  [the longest x4 59.8 us: head_back(): pl.pallas_call(partial(head_back_kernel, block), grid=(vocab // block,),...]
    reduce_scatter x4 -> x0, waiting for transfers between devices: 153 us -> none  [the longest x2 95.9 us: split_sum(): return lax.psum_scatter(rows_in, 'hidden', scatter_dimension=1, tiled=True)]
    ppermute x0 -> x39, waiting for transfers between devices: none -> 145 us  [flip(): lax.ppermute(x, axis, [(j, j ^ k) for j in range(lax.axis_size(axis))])]
    psum x4 -> x0, waiting for transfers between devices: 141 us -> none  [the longest x1 67.7 us: on_device(): lax.psum(jnp.dot(d_logits, table_all, preferred_element_type=jnp.float32)...]
    all_gather x6 -> x1, blocking collectives: 129 us -> 5.03 us  [on_device(): both_sums = lax.all_gather(jnp.sum(both_sums, axis=0), 'hidden', axis=0)]
    dot_general x20 -> x39, matrix products: 179 us -> 96.3 us  [dot(): lax.dot_general(a, b, (((ca,), (cb,)), ((), ())), preferred_element_type=...]
  transfers between devices with their start and end apart: 15 -> 46, of which waited for: 11 -> 21; matrix products, arithmetic and copies ran while one was open for 40% -> 25% of each run, Pallas kernels for 0% -> 15%
where the time goes in v1:
time: 937 us; the launch traced here: 927 us
  waiting for transfers between devices  240 us (26%)
  Pallas kernels  181 us (19%)
  local copies, waits for them, and re-layouts  133 us (14%)
  other arithmetic  127 us (14%)
  matrix products  96.3 us (10%)
  starting transfers between devices  69 us (7%)
  blocking collectives  48.3 us (5%)
  between operations  23.8 us (3%)
    ppermute x39, waiting for transfers between devices, flip(): lax.ppermute(x, axis, [(j, j ^ k) for j in range(lax.axis_size(axis))])  145 us
    dot_general x39, matrix products, dot(): lax.dot_general(a, b, (((ca,), (cb,)), ((), ())), preferred_element_type=...  96.3 us
    pallas_call x4, Pallas kernels, head_back(): pl.pallas_call(partial(head_back_kernel, block), grid=(vocab // block,),...  59.8 us
    pallas_call x4, Pallas kernels, head_logits(): pl.pallas_call(partial(logits_kernel, block, padded, real), grid=(vocab /...  55.2 us
    all_gather x1, waiting for transfers between devices, on_device(): packed = lax.all_gather(packed, 'expert', axis=1, tiled=True)  53.9 us
    ppermute x39, starting transfers between devices, flip(): lax.ppermute(x, axis, [(j, j ^ k) for j in range(lax.axis_size(axis))])  38.4 us
    unnamed x240, local copies, waits for them, and re-layouts  33.5 us
    concatenate x2, local copies, waits for them, and re-layouts, on_device(): table = jnp.concatenate([slice_two, flip(slice_two, 'hidden', 1)])  28.9 us
  transfers between devices with their start and end apart: 46, of which 21 were waited for; matrix products, arithmetic and copies ran while one was open for 25% of the time, Pallas kernels for 15%

profile of v1, /device:TPU:0, one launch (start us, length us, event | category | flops | bytes accessed | tf_op | source)
XLA Modules:
  0.0 927.0 jit_solution(2008335309111458246)
XLA Ops:
  14.1 7.3 all-to-all-start
  30.2 21.9 %all_to_all.83 = bf16[8,48,768]{2,1,0:T(8,128)(2,1)S(1)} all-to-all(bf16[8,48,768]{2,1,0:T(8,128)(2,1)S(1)} %bitcast.401), channel_id=1, replica_groups=mesh['expert'=8,'hidden'=4] {'expert'}, dimensions={0} | all-to-all | bytes 1179648 | tf_op jit(solution)/shard_map/all_to_all | solution.py:447
  53.6 12.2 %collective-permute-done.4 = bf16[384,768]{1,0:T(8,128)(2,1)S(1)} collective-permute-done((bf16[384,768]{1,0:T(8,128)(2,1)S(1)}, bf16[384,768]{1,0:T(8,128)(2,1)S(1)}, u32[]{:S(2)}, u32[]{:S(2)}) %collective-permute-start.4) | collective-permute-done | bytes 589856 | tf_op jit(solution)/shard_map/ppermute | solution.py:30
  69.5 5.0 collective-permute-done.6
  83.0 9.0 conditional.2
  96.8 53.9 %all-gather.8.cloned.1.call-done = bf16[2,768,896]{2,0,1:T(2,128)(2,1)} async-done(((bf16[2,96,896]{2,0,1:T(2,128)(2,1)}), bf16[2,768,896]{2,0,1:T(2,128)(2,1)}) %all-gather.8.cloned.1.call-update) | async-done | bytes 2752528 | tf_op jit(solution)/shard_map/all_gather | solution.py:396
  162.1 5.3 convolution_convert_fusion.q_ref.k_ref.v_ref
  167.4 15.0 %attend.1 = bf16[1024,384]{1,0:T(8,128)(2,1)} custom-call(bf16[1024,1152]{1,0:T(8,128)(2,1)} %convolution_convert_fusion.q_ref.k_ref.v_ref, bf16[1024,1152]{1,0:T(8,128)(2,1)} %convolution_convert_fusion.q_ref.k_ref.v_ref, bf16[1024,1152]{1,0:T(8,128)(2,1)} %convolution_convert_fusion.q_ref.k_ref.v_ref, s32[1,1024]{1,0:T(1,128)} %segr_ref.3, ...), custom_call_target="tpu_custom_call" | custom-call | tf_op jit(solution)/shard_map/attend/pallas_call | solution.py:106
  195.9 6.2 gather_fusion.1
  207.4 35.9 %collective-permute-done.8 = bf16[2,768,768]{2,1,0:T(8,128)(2,1)} collective-permute-done((bf16[2,768,768]{2,1,0:T(8,128)(2,1)}, bf16[2,768,768]{2,1,0:T(8,128)(2,1)}, u32[]{:S(2)}, u32[]{:S(2)}) %collective-permute-start.8) | collective-permute-done | bytes 2359328 | tf_op jit(solution)/shard_map/ppermute | solution.py:30
  261.9 12.1 %all-to-all-done.2 = bf16[8,48,768]{2,1,0:T(8,128)(2,1)S(1)} async-done(((bf16[8,48,768]{2,1,0:T(8,128)(2,1)}), bf16[8,48,768]{2,1,0:T(8,128)(2,1)S(1)}, u32[]{:S(2)}, u32[]{:S(2)}) %all-to-all-start.2) | async-done | bytes 589856 | tf_op jit(solution)/shard_map/all_to_all | solution.py:486
  274.0 5.5 multiply_convert_fusion.8
  280.2 5.3 multiply_convert_fusion.7
  287.6 5.3 multiply_convert_fusion.5
  292.9 5.5 multiply_convert_fusion.6
  307.7 5.3 pad_maximum_fusion.1
  313.0 10.4 %all-to-all-done.3 = bf16[8,48,768]{2,1,0:T(8,128)(2,1)} async-done(((bf16[8,48,768]{2,1,0:T(8,128)(2,1)}), bf16[8,48,768]{2,1,0:T(8,128)(2,1)}, u32[]{:S(2)}, u32[]{:S(2)}) %all-to-all-start.3) | async-done | bytes 589856 | tf_op jit(solution)/shard_map/all_to_all | solution.py:489
  324.7 12.3 %collective-permute-done.10 = bf16[384,768]{1,0:T(8,128)(2,1)S(1)} collective-permute-done((bf16[384,768]{1,0:T(8,128)(2,1)}, bf16[384,768]{1,0:T(8,128)(2,1)S(1)}, u32[]{:S(2)}, u32[]{:S(2)}) %collective-permute-start.10) | collective-permute-done | bytes 589856 | tf_op jit(solution)/shard_map/ppermute | solution.py:30
  358.3 15.1 %concatenate.98 = bf16[6400,768]{0,1:T(8,128)(2,1)} concatenate(bf16[1600,768]{0,1:T(8,128)(2,1)S(1)} %pad.17, bf16[1600,768]{0,1:T(8,128)(2,1)} %copy.245, bf16[3200,768]{0,1:T(8,128)(2,1)} %collective-permute-done.3), dimensions={0} | concatenate | bytes 19660800 | tf_op jit(solution)/shard_map/concatenate | solution.py:521
  373.4 13.8 %copy.256.table_ref = bf16[6400,768]{1,0:T(8,128)(2,1)} copy(bf16[6400,768]{0,1:T(8,128)(2,1)} %concatenate.98) | data formatting | bytes 19660800 | tf_op jit(solution)/shard_map/concatenate | solution.py:521
  392.9 13.8 %head_logits.4 = (f32[6400,512]{1,0:T(8,128)}, f32[8,512]{1,0:T(8,128)}) custom-call(bf16[6400,768]{1,0:T(8,128)(2,1)} %copy.256.table_ref, bf16[512,768]{1,0:T(8,128)(2,1)} %pad_maximum_fusion.11.rows_ref.refs_4_, s32[1,512]{1,0:T(1,128)} %and_select_fusion.21.col_ref), custom_call_target="tpu_custom_call" | custom-call | flops 5033164800 | bytes 22937600 | tf_op jit(solution)/shard_map/head_logits/pallas_call | solution.py:218
  411.5 13.8 %head_logits.7 = (f32[6400,512]{1,0:T(8,128)}, f32[8,512]{1,0:T(8,128)}) custom-call(bf16[6400,768]{1,0:T(8,128)(2,1)} %copy.256.table_ref, bf16[512,768]{1,0:T(8,128)(2,1)} %copy-done.72, s32[1,512]{1,0:T(1,128)} %and_select_fusion.6.col_ref), custom_call_target="tpu_custom_call" | custom-call | flops 5033164800 | bytes 22937600 | tf_op jit(solution)/shard_map/head_logits/pallas_call | solution.py:218
  427.0 14.0 %head_logits.6 = (f32[6400,512]{1,0:T(8,128)}, f32[8,512]{1,0:T(8,128)}) custom-call(bf16[6400,768]{1,0:T(8,128)(2,1)} %copy.256.table_ref, bf16[512,768]{1,0:T(8,128)(2,1)} %copy-done.71, s32[1,512]{1,0:T(1,128)} %and_select_fusion.11.col_ref), custom_call_target="tpu_custom_call" | custom-call | flops 5033164800 | bytes 22937600 | tf_op jit(solution)/shard_map/head_logits/pallas_call | solution.py:218
  442.6 13.8 %head_logits.5 = (f32[6400,512]{1,0:T(8,128)}, f32[8,512]{1,0:T(8,128)}) custom-call(bf16[6400,768]{1,0:T(8,128)(2,1)} %copy.256.table_ref, bf16[512,768]{1,0:T(8,128)(2,1)} %copy-done.70, s32[1,512]{1,0:T(1,128)} %and_select_fusion.16.col_ref), custom_call_target="tpu_custom_call" | custom-call | flops 5033164800 | bytes 22937600 | tf_op jit(solution)/shard_map/head_logits/pallas_call | solution.py:218
  468.9 14.8 %head_back.7 = (bf16[6400,512]{1,0:T(8,128)(2,1)}, bf16[512,768]{1,0:T(8,128)(2,1)}) custom-call(bf16[768,6400]{1,0:T(8,128)(2,1)} %bitcast.333, f32[6400,512]{1,0:T(8,128)} %get-tuple-element.170.logits_ref, s32[1,512]{1,0:T(1,128)} %and_select_fusion.6.col_ref, f32[8,512]{1,0:T(8,128)} %get-tuple-element.382.side_ref), custom_call_target="tpu_custom_call" | custom-call | flops 5033164800 | bytes 29491200 | tf_op jit(solution)/shard_map/head_back/pallas_call | solution.py:271
  485.5 14.9 %head_back.6 = (bf16[6400,512]{1,0:T(8,128)(2,1)}, bf16[512,768]{1,0:T(8,128)(2,1)}) custom-call(bf16[768,6400]{1,0:T(8,128)(2,1)} %bitcast.334, f32[6400,512]{1,0:T(8,128)} %get-tuple-element.168.logits_ref, s32[1,512]{1,0:T(1,128)} %and_select_fusion.11.col_ref, f32[8,512]{1,0:T(8,128)} %get-tuple-element.381.side_ref), custom_call_target="tpu_custom_call" | custom-call | flops 5033164800 | bytes 29491200 | tf_op jit(solution)/shard_map/head_back/pallas_call | solution.py:271
  502.8 14.8 %head_back.5 = (bf16[6400,512]{1,0:T(8,128)(2,1)}, bf16[512,768]{1,0:T(8,128)(2,1)}) custom-call(bf16[768,6400]{1,0:T(8,128)(2,1)} %bitcast.335, f32[6400,512]{1,0:T(8,128)} %get-tuple-element.166.logits_ref, s32[1,512]{1,0:T(1,128)} %and_select_fusion.16.col_ref, f32[8,512]{1,0:T(8,128)} %get-tuple-element.380.side_ref), custom_call_target="tpu_custom_call" | custom-call | flops 5033164800 | bytes 29491200 | tf_op jit(solution)/shard_map/head_back/pallas_call | solution.py:271
  519.4 15.3 %head_back.4 = (bf16[6400,512]{1,0:T(8,128)(2,1)}, bf16[512,768]{1,0:T(8,128)(2,1)}) custom-call(bf16[768,6400]{1,0:T(8,128)(2,1)} %bitcast.336, f32[6400,512]{1,0:T(8,128)} %get-tuple-element.160.logits_ref, s32[1,512]{1,0:T(1,128)} %and_select_fusion.21.col_ref, f32[8,512]{1,0:T(8,128)} %get-tuple-element.379.side_ref), custom_call_target="tpu_custom_call" | custom-call | flops 5033164800 | bytes 29491200 | tf_op jit(solution)/shard_map/head_back/pallas_call | solution.py:271
  543.7 7.6 collective-permute-done.33
  551.3 17.1 %collective-permute-done.31 = bf16[256,768]{1,0:T(8,128)(2,1)S(1)} collective-permute-done((bf16[256,768]{1,0:T(8,128)(2,1)S(1)}, bf16[256,768]{1,0:T(8,128)(2,1)S(1)}, u32[]{:S(2)}, u32[]{:S(2)}) %collective-permute-start.31) | collective-permute-done | bytes 393248 | tf_op jit(solution)/shard_map/ppermute | solution.py:30
  570.0 8.0 collective-permute-done.34
  587.6 21.3 %all_to_all.84 = bf16[8,48,768]{2,1,0:T(8,128)(2,1)S(1)} all-to-all(bf16[8,48,768]{2,1,0:T(8,128)(2,1)S(1)} %bitcast.400), channel_id=1, replica_groups=mesh['expert'=8,'hidden'=4] {'expert'}, dimensions={0} | all-to-all | bytes 1179648 | tf_op jit(solution)/shard_map/all_to_all | solution.py:486
  629.8 27.1 %table_grad.1 = f32[6400,768]{1,0:T(8,128)} custom-call(bf16[6400,512]{1,0:T(8,128)(2,1)} %get-tuple-element.165.refs_0_, bf16[6400,512]{1,0:T(8,128)(2,1)} %get-tuple-element.167.refs_1_, bf16[6400,512]{1,0:T(8,128)(2,1)} %get-tuple-element.169.refs_2_, bf16[6400,512]{1,0:T(8,128)(2,1)} %get-tuple-element.171.refs_3_, ...), custom_call_target="tpu_custom_call" | custom-call | flops 20132659200 | bytes 45875200 | tf_op jit(solution)/shard_map/table_grad/pallas_call | solution.py:312
  658.4 14.8 %fusion.189 = (f32[3200,768]{1,0:T(8,128)}, f32[3200,768]{1,0:T(8,128)}) fusion(f32[6400,768]{1,0:T(8,128)} %table_grad.1), kind=kLoop, calls=%fused_computation.483 | loop fusion | bytes 39321600 | tf_op jit(solution)/shard_map/slice | solution.py:577
  683.3 7.2 collective-permute-done.37
  698.3 23.3 %attend_back.1 = (bf16[1024,384]{1,0:T(8,128)(2,1)}, bf16[1024,384]{1,0:T(8,128)(2,1)}, bf16[1024,384]{1,0:T(8,128)(2,1)}) custom-call(bf16[1024,1152]{1,0:T(8,128)(2,1)} %convolution_convert_fusion.q_ref.k_ref.v_ref, bf16[1024,1152]{1,0:T(8,128)(2,1)} %convolution_convert_fusion.q_ref.k_ref.v_ref, ...), custom_call_target="tpu_custom_call" | custom-call | tf_op jit(solution)/shard_map/attend_back/pallas_call | solution.py:162
  739.4 5.8 fusion.33
  750.2 6.0 fusion.37
  765.3 6.0 all-to-all-start.6
  772.6 11.5 %add.562 = f32[2,1600,768]{2,1,0:T(8,128)} add(f32[2,1600,768]{2,1,0:T(8,128)} %bitcast.337, f32[2,1600,768]{2,1,0:T(8,128)} %collective-permute-done.25) | non-fusion elementwise | flops 2457600 | bytes 29491200 | tf_op jit(solution)/shard_map/add | solution.py:577
  804.4 12.9 %all-to-all-done.6 = bf16[8,160,768]{2,1,0:T(8,128)(2,1)S(1)} async-done(((bf16[8,160,768]{2,1,0:T(8,128)(2,1)}), bf16[8,160,768]{2,1,0:T(8,128)(2,1)S(1)}, u32[]{:S(2)}, u32[]{:S(2)}) %all-to-all-start.6) | async-done | bytes 1966112 | tf_op jit(solution)/shard_map/all_to_all | solution.py:624
  823.3 29.1 %collective-permute-done.26 = bf16[1600,768]{1,0:T(8,128)(2,1)} collective-permute-done((bf16[1600,768]{1,0:T(8,128)(2,1)}, bf16[1600,768]{1,0:T(8,128)(2,1)}, u32[]{:S(2)}, u32[]{:S(2)}) %collective-permute-start.26) | collective-permute-done | bytes 2457632 | tf_op jit(solution)/shard_map/ppermute | solution.py:30
  852.5 8.6 multiply_reduce_fusion
  864.5 6.4 multiply_reduce_fusion.1
  872.3 5.2 all-to-all-start.7
  883.9 5.0 all-gather.2
  894.6 13.7 %multiply_subtract_fusion = (f32[1572,768]{1,0:T(8,128)}, f32[1572,768]{1,0:T(8,128)}, f32[1572,768]{1,0:T(8,128)}) fusion(f32[1572,768]{1,0:T(8,128)} %param.32, f32[1572,768]{1,0:T(8,128)} %get-tuple-element.321, f32[]{:T(128)S(6)} %min.3, f32[1572,768]{1,0:T(8,128)} %param.33, f32[1572,768]{1,0:T(8,128)} %param.34), kind=kLoop, calls=%fused_computation.38 | loop fusion | flops 19316736 | bytes 33804292 | tf_op jit(solution)/shard_map/sub | solution.py:337
  911.8 6.4 multiply_subtract_fusion.1
  (511 shorter events, 282.8 us)
Async XLA Ops:
  8.0 187.8 %copy-start = (s32[50304]{0:T(1024)S(1)}, s32[50304]{0:T(1024)}, u32[]{:S(2)}) copy-start(s32[50304]{0:T(1024)} %param.31) | copy-start | bytes 603652
  14.1 14.6 %all-to-all-start = ((s32[8,1,128]{2,1,0:T(1,128)}), s32[8,1,128]{2,1,0:T(1,128)S(1)}, u32[]{:S(2)}, u32[]{:S(2)}) async-start(s32[8,1,128]{2,1,0:T(1,128)} %bitcast.7), calls=%async_computation | async-start | bytes 8192 | tf_op jit(solution)/shard_map/all_to_all | solution.py:443
  52.1 13.7 %collective-permute-start.4 = (bf16[384,768]{1,0:T(8,128)(2,1)S(1)}, bf16[384,768]{1,0:T(8,128)(2,1)S(1)}, u32[]{:S(2)}, u32[]{:S(2)}) collective-permute-start(bf16[384,768]{1,0:T(8,128)(2,1)S(1)} %bitcast.365), channel_id=1, source_target_pairs={{0,2},{1,3},{2,0},{3,1},{4,6},{5,7},{6,4},{7,5},{8,10},{9,11},{10,... | collective-permute-start | bytes 1769480 | tf_op jit(solution)/shard_map/ppermute | solution.py:30
  66.0 11.5 %collective-permute-start.5 = (bf16[2,384,768]{2,1,0:T(8,128)(2,1)S(1)}, bf16[2,384,768]{2,1,0:T(8,128)(2,1)}, u32[]{:S(2)}, u32[]{:S(2)}) collective-permute-start(bf16[2,384,768]{2,1,0:T(8,128)(2,1)S(1)} %pad_maximum_fusion.8), channel_id=1, source_target_pairs={{0,1},{1,0},{2,3},{3,2},{4,5},{5,4},{6,7},{7,6},{8,9},{9,8},{10,11... | collective-permute-start | bytes 3538952 | tf_op jit(solution)/shard_map/ppermute | solution.py:30
  66.6 7.9 collective-permute-start.6
  92.0 58.6 %all-gather.8.cloned.1.call-start = ((), (), s32[]{:S(2)}) async-start(), calls=%async_computation.10 | async-start | bytes 3096576 | tf_op jit(solution)/shard_map/all_gather | solution.py:396
  186.4 61.2 %collective-permute-start.7 = (f32[1024,768]{1,0:T(8,128)}, f32[1024,768]{1,0:T(8,128)}, u32[]{:S(2)}, u32[]{:S(2)}) collective-permute-start(f32[1024,768]{1,0:T(8,128)} %fusion.197), channel_id=1, source_target_pairs={{0,1},{1,0},{2,3},{3,2},{4,5},{5,4},{6,7},{7,6},{8,9},{9,8},{10,11... | collective-permute-start | bytes 9437192 | tf_op jit(solution)/shard_map/ppermute | solution.py:30
  190.9 52.4 %collective-permute-start.8 = (bf16[2,768,768]{2,1,0:T(8,128)(2,1)}, bf16[2,768,768]{2,1,0:T(8,128)(2,1)}, u32[]{:S(2)}, u32[]{:S(2)}) collective-permute-start(bf16[2,768,768]{2,1,0:T(8,128)(2,1)} %pad_maximum_fusion.4), channel_id=1, source_target_pairs={{0,2},{1,3},{2,0},{3,1},{4,6},{5,7},{6,4},{7,5},{8,10},{9,11},{10,... | collective-permute-start | bytes 7077896 | tf_op jit(solution)/shard_map/ppermute | solution.py:30
  195.3 62.2 %collective-permute-start.2 = (bf16[1600,768]{1,0:T(8,128)(2,1)}, bf16[1600,768]{1,0:T(8,128)(2,1)}, u32[]{:S(2)}, u32[]{:S(2)}) collective-permute-start(bf16[1600,768]{1,0:T(8,128)(2,1)} %copy.243), channel_id=1, source_target_pairs={{0,4},{4,0},{8,12},{12,8},{16,20},{20,16},{24,28},{28,24},{1,5},{5... | collective-permute-start | bytes 7372808 | tf_op jit(solution)/shard_map/ppermute | solution.py:30
  247.4 40.2 %collective-permute-start.9 = (bf16[2,2,768,768]{3,2,1,0:T(8,128)(2,1)}, bf16[2,2,768,768]{3,2,1,0:T(8,128)(2,1)}, u32[]{:S(2)}, u32[]{:S(2)}) collective-permute-start(bf16[2,2,768,768]{3,2,1,0:T(8,128)(2,1)} %pad_maximum_fusion.2), channel_id=1, source_target_pairs={{0,1},{1,0},{2,3},{3,2},{4,5},{5,4},{6,7},{7,6},{8,9},{9,8},{10,11... | collective-permute-start | bytes 14155784 | tf_op jit(solution)/shard_map/ppermute | solution.py:30
  253.4 20.6 %all-to-all-start.2 = ((bf16[8,48,768]{2,1,0:T(8,128)(2,1)}), bf16[8,48,768]{2,1,0:T(8,128)(2,1)S(1)}, u32[]{:S(2)}, u32[]{:S(2)}) async-start(bf16[8,48,768]{2,1,0:T(8,128)(2,1)} %bitcast.399), calls=%async_computation.2 | async-start | bytes 1179648 | tf_op jit(solution)/shard_map/all_to_all | solution.py:486
  274.0 403.3 %copy-start.9 = (bf16[8,48,768]{2,1,0:T(8,128)(2,1)}, bf16[8,48,768]{2,1,0:T(8,128)(2,1)S(1)}, u32[]{:S(2)}) copy-start(bf16[8,48,768]{2,1,0:T(8,128)(2,1)S(1)} %all-to-all-done.2) | copy-start | bytes 1769476
  303.3 20.1 %all-to-all-start.3 = ((bf16[8,48,768]{2,1,0:T(8,128)(2,1)}), bf16[8,48,768]{2,1,0:T(8,128)(2,1)}, u32[]{:S(2)}, u32[]{:S(2)}) async-start(bf16[8,48,768]{2,1,0:T(8,128)(2,1)} %bitcast.372), calls=%async_computation.3 | async-start | bytes 1179648 | tf_op jit(solution)/shard_map/all_to_all | solution.py:489
  313.0 45.3 %collective-permute-start.3 = (bf16[3200,768]{0,1:T(8,128)(2,1)}, bf16[3200,768]{0,1:T(8,128)(2,1)}, u32[]{:S(2)}, u32[]{:S(2)}) collective-permute-start(bf16[3200,768]{0,1:T(8,128)(2,1)} %pad_maximum_fusion.1), channel_id=1, source_target_pairs={{0,1},{1,0},{2,3},{3,2},{4,5},{5,4},{6,7},{7,6},{8,9},{9,8},{10,11... | collective-permute-start | bytes 14745608 | tf_op jit(solution)/shard_map/ppermute | solution.py:30
  323.4 13.6 %collective-permute-start.10 = (bf16[384,768]{1,0:T(8,128)(2,1)}, bf16[384,768]{1,0:T(8,128)(2,1)S(1)}, u32[]{:S(2)}, u32[]{:S(2)}) collective-permute-start(bf16[384,768]{1,0:T(8,128)(2,1)} %bitcast.45), channel_id=1, source_target_pairs={{0,2},{1,3},{2,0},{3,1},{4,6},{5,7},{6,4},{7,5},{8,10},{9,11},{10,... | collective-permute-start | bytes 1769480 | tf_op jit(solution)/shard_map/ppermute | solution.py:30
  340.0 6.7 collective-permute-start.11
  340.7 5.4 collective-permute-start.20
  342.7 14.3 %collective-permute-start.17 = (f32[2,512]{1,0:T(2,128)S(1)}, f32[2,512]{1,0:T(2,128)S(1)}, u32[]{:S(2)}, u32[]{:S(2)}) collective-permute-start(f32[2,512]{1,0:T(2,128)S(1)} %pad_maximum_fusion.22), channel_id=1, source_target_pairs={{0,16},{4,20},{8,24},{12,28},{16,0},{20,4},{24,8},{28,12},{1,17},{... | collective-permute-start | bytes 12296 | tf_op jit(solution)/shard_map/ppermute | solution.py:30
  342.7 14.9 %collective-permute-start.14 = (f32[2,512]{1,0:T(2,128)S(1)}, f32[2,512]{1,0:T(2,128)S(1)}, u32[]{:S(2)}, u32[]{:S(2)}) collective-permute-start(f32[2,512]{1,0:T(2,128)S(1)} %pad_maximum_fusion.22), channel_id=1, source_target_pairs={{0,8},{4,12},{8,0},{12,4},{16,24},{20,28},{24,16},{28,20},{1,9},{5... | collective-permute-start | bytes 12296 | tf_op jit(solution)/shard_map/ppermute | solution.py:30
  355.0 36.6 %collective-permute-start.18 = (bf16[256,768]{1,0:T(8,128)(2,1)}, bf16[256,768]{1,0:T(8,128)(2,1)}, u32[]{:S(2)}, u32[]{:S(2)}) collective-permute-start(bf16[256,768]{1,0:T(8,128)(2,1)} %get-tuple-element.343), channel_id=1, source_target_pairs={{0,24},{4,28},{8,16},{12,20},{16,8},{20,12},{24,0},{28,4},{1,25},{... | collective-permute-start | bytes 1179656 | tf_op jit(solution)/shard_map/ppermute | solution.py:30
  387.2 20.2 %collective-permute-start.15 = (bf16[256,768]{1,0:T(8,128)(2,1)}, bf16[256,768]{1,0:T(8,128)(2,1)S(1)}, u32[]{:S(2)}, u32[]{:S(2)}) collective-permute-start(bf16[256,768]{1,0:T(8,128)(2,1)} %get-tuple-element.343), channel_id=1, source_target_pairs={{0,16},{4,20},{8,24},{12,28},{16,0},{20,4},{24,8},{28,12},{1,17},{... | collective-permute-start | bytes 1179656 | tf_op jit(solution)/shard_map/ppermute | solution.py:30
  387.2 20.9 %collective-permute-start.12 = (bf16[256,768]{1,0:T(8,128)(2,1)}, bf16[256,768]{1,0:T(8,128)(2,1)S(1)}, u32[]{:S(2)}, u32[]{:S(2)}) collective-permute-start(bf16[256,768]{1,0:T(8,128)(2,1)} %get-tuple-element.343), channel_id=1, source_target_pairs={{0,8},{4,12},{8,0},{12,4},{16,24},{20,28},{24,16},{28,20},{1,9},{5... | collective-permute-start | bytes 1179656 | tf_op jit(solution)/shard_map/ppermute | solution.py:30
  391.6 19.0 %collective-permute-start.19 = (bf16[256,768]{1,0:T(8,128)(2,1)}, bf16[256,768]{1,0:T(8,128)(2,1)S(1)}, u32[]{:S(2)}, u32[]{:S(2)}) collective-permute-start(bf16[256,768]{1,0:T(8,128)(2,1)} %collective-permute-done.18), channel_id=1, source_target_pairs={{0,2},{1,3},{2,0},{3,1},{4,6},{5,7},{6,4},{7,5},{8,10},{9,11},{10,... | collective-permute-start | bytes 1179656 | tf_op jit(solution)/shard_map/ppermute | solution.py:30
  407.4 18.6 %collective-permute-start.16 = (bf16[256,768]{1,0:T(8,128)(2,1)S(1)}, bf16[256,768]{1,0:T(8,128)(2,1)S(1)}, u32[]{:S(2)}, u32[]{:S(2)}) collective-permute-start(bf16[256,768]{1,0:T(8,128)(2,1)S(1)} %collective-permute-done.15), channel_id=1, source_target_pairs={{0,2},{1,3},{2,0},{3,1},{4,6},{5,7},{6,4},{7,5},{8,10},{9,11},{10,... | collective-permute-start | bytes 1179656 | tf_op jit(solution)/shard_map/ppermute | solution.py:30
  408.1 33.5 %collective-permute-start.13 = (bf16[256,768]{1,0:T(8,128)(2,1)S(1)}, bf16[256,768]{1,0:T(8,128)(2,1)S(1)}, u32[]{:S(2)}, u32[]{:S(2)}) collective-permute-start(bf16[256,768]{1,0:T(8,128)(2,1)S(1)} %collective-permute-done.12), channel_id=1, source_target_pairs={{0,2},{1,3},{2,0},{3,1},{4,6},{5,7},{6,4},{7,5},{8,10},{9,11},{10,... | collective-permute-start | bytes 1179656 | tf_op jit(solution)/shard_map/ppermute | solution.py:30
  457.1 3.9 collective-permute-start.21
  461.1 3.9 collective-permute-start.22
  461.3 5.7 collective-permute-start.24
  463.4 4.7 collective-permute-start.23
  484.7 52.5 %collective-permute-start.32 = (bf16[256,768]{1,0:T(8,128)(2,1)S(1)}, bf16[256,768]{1,0:T(8,128)(2,1)S(1)}, u32[]{:S(2)}, u32[]{:S(2)}) collective-permute-start(bf16[256,768]{1,0:T(8,128)(2,1)S(1)} %slice.352), channel_id=1, source_target_pairs={{0,2},{1,3},{2,0},{3,1},{4,6},{5,7},{6,4},{7,5},{8,10},{9,11},{10,... | collective-permute-start | bytes 1179656 | tf_op jit(solution)/shard_map/ppermute | solution.py:30
  501.3 37.9 %collective-permute-start.30 = (bf16[256,768]{1,0:T(8,128)(2,1)S(1)}, bf16[256,768]{1,0:T(8,128)(2,1)S(1)}, u32[]{:S(2)}, u32[]{:S(2)}) collective-permute-start(bf16[256,768]{1,0:T(8,128)(2,1)S(1)} %slice.350), channel_id=1, source_target_pairs={{0,2},{1,3},{2,0},{3,1},{4,6},{5,7},{6,4},{7,5},{8,10},{9,11},{10,... | collective-permute-start | bytes 1179656 | tf_op jit(solution)/shard_map/ppermute | solution.py:30
  518.6 21.5 %collective-permute-start.28 = (bf16[256,768]{1,0:T(8,128)(2,1)S(1)}, bf16[256,768]{1,0:T(8,128)(2,1)S(1)}, u32[]{:S(2)}, u32[]{:S(2)}) collective-permute-start(bf16[256,768]{1,0:T(8,128)(2,1)S(1)} %slice.348), channel_id=1, source_target_pairs={{0,2},{1,3},{2,0},{3,1},{4,6},{5,7},{6,4},{7,5},{8,10},{9,11},{10,... | collective-permute-start | bytes 1179656 | tf_op jit(solution)/shard_map/ppermute | solution.py:30
  535.9 7.8 collective-permute-start.27
  537.4 13.9 %collective-permute-start.33 = (bf16[256,768]{1,0:T(8,128)(2,1)S(1)}, bf16[256,768]{1,0:T(8,128)(2,1)S(1)}, u32[]{:S(2)}, u32[]{:S(2)}) collective-permute-start(bf16[256,768]{1,0:T(8,128)(2,1)S(1)} %add_convert_fusion.5), channel_id=1, source_target_pairs={{0,24},{4,28},{8,16},{12,20},{16,8},{20,12},{24,0},{28,4},{1,25},{... | collective-permute-start | bytes 1179656 | tf_op jit(solution)/shard_map/ppermute | solution.py:30
  539.3 29.0 %collective-permute-start.31 = (bf16[256,768]{1,0:T(8,128)(2,1)S(1)}, bf16[256,768]{1,0:T(8,128)(2,1)S(1)}, u32[]{:S(2)}, u32[]{:S(2)}) collective-permute-start(bf16[256,768]{1,0:T(8,128)(2,1)S(1)} %add_convert_fusion.6), channel_id=1, source_target_pairs={{0,16},{4,20},{8,24},{12,28},{16,0},{20,4},{24,8},{28,12},{1,17},{... | collective-permute-start | bytes 1179656 | tf_op jit(solution)/shard_map/ppermute | solution.py:30
  540.3 28.0 %collective-permute-start.29 = (bf16[256,768]{1,0:T(8,128)(2,1)S(1)}, bf16[256,768]{1,0:T(8,128)(2,1)S(1)}, u32[]{:S(2)}, u32[]{:S(2)}) collective-permute-start(bf16[256,768]{1,0:T(8,128)(2,1)S(1)} %add_convert_fusion.7), channel_id=1, source_target_pairs={{0,8},{4,12},{8,0},{12,4},{16,24},{20,28},{24,16},{28,20},{1,9},{5... | collective-permute-start | bytes 1179656 | tf_op jit(solution)/shard_map/ppermute | solution.py:30
  568.6 9.4 %collective-permute-start.34 = (bf16[256,768]{1,0:T(8,128)(2,1)S(1)}, bf16[256,768]{1,0:T(8,128)(2,1)S(1)}, u32[]{:S(2)}, u32[]{:S(2)}) collective-permute-start(bf16[256,768]{1,0:T(8,128)(2,1)S(1)} %add_convert_fusion.4), channel_id=1, source_target_pairs={{0,2},{1,3},{2,0},{3,1},{4,6},{5,7},{6,4},{7,5},{8,10},{9,11},{10,... | collective-permute-start | bytes 1179656 | tf_op jit(solution)/shard_map/ppermute | solution.py:30
  578.1 2.5 collective-permute-start.35
  626.1 30.9 %all-to-all-start.5 = ((bf16[8,48,768]{2,1,0:T(8,128)(2,1)}), bf16[8,48,768]{2,1,0:T(8,128)(2,1)S(1)}, u32[]{:S(2)}, u32[]{:S(2)}) async-start(bf16[8,48,768]{2,1,0:T(8,128)(2,1)} %bitcast.371), calls=%async_computation.5 | async-start | bytes 1179648 | tf_op jit(solution)/shard_map/all_to_all | solution.py:489
  657.0 18.2 %collective-permute-start.36 = (bf16[384,768]{1,0:T(8,128)(2,1)S(1)}, bf16[384,768]{1,0:T(8,128)(2,1)S(1)}, u32[]{:S(2)}, u32[]{:S(2)}) collective-permute-start(bf16[384,768]{1,0:T(8,128)(2,1)S(1)} %bitcast.362), channel_id=1, source_target_pairs={{0,2},{1,3},{2,0},{3,1},{4,6},{5,7},{6,4},{7,5},{8,10},{9,11},{10,... | collective-permute-start | bytes 1769480 | tf_op jit(solution)/shard_map/ppermute | solution.py:30
  673.2 99.3 %collective-permute-start.25 = (f32[2,1600,768]{2,1,0:T(8,128)}, f32[2,1600,768]{2,1,0:T(8,128)}, u32[]{:S(2)}, u32[]{:S(2)}) collective-permute-start(f32[2,1600,768]{2,1,0:T(8,128)} %bitcast.61), channel_id=1, source_target_pairs={{0,1},{1,0},{2,3},{3,2},{4,5},{5,4},{6,7},{7,6},{8,9},{9,8},{10,11... | collective-permute-start | bytes 29491208 | tf_op jit(solution)/shard_map/ppermute | solution.py:30
  676.3 14.2 %collective-permute-start.37 = (bf16[2,384,768]{2,1,0:T(8,128)(2,1)}, bf16[2,384,768]{2,1,0:T(8,128)(2,1)}, u32[]{:S(2)}, u32[]{:S(2)}) collective-permute-start(bf16[2,384,768]{2,1,0:T(8,128)(2,1)} %pad_maximum_fusion.10), channel_id=1, source_target_pairs={{0,1},{1,0},{2,3},{3,2},{4,5},{5,4},{6,7},{7,6},{8,9},{9,8},{10,11... | collective-permute-start | bytes 3538952 | tf_op jit(solution)/shard_map/ppermute | solution.py:30
  683.0 111.4 %collective-permute-start.39 = (f32[2,2,768,768]{3,2,1,0:T(8,128)}, f32[2,2,768,768]{3,2,1,0:T(8,128)}, u32[]{:S(2)}, u32[]{:S(2)}) collective-permute-start(f32[2,2,768,768]{3,2,1,0:T(8,128)} %pad_maximum_fusion), channel_id=1, source_target_pairs={{0,1},{1,0},{2,3},{3,2},{4,5},{5,4},{6,7},{7,6},{8,9},{9,8},{10,11... | collective-permute-start | bytes 28311560 | tf_op jit(solution)/shard_map/ppermute | solution.py:30
  728.4 11.0 %collective-permute-start.38 = (f32[1024,768]{1,0:T(8,128)}, f32[1024,768]{1,0:T(8,128)}, u32[]{:S(2)}, u32[]{:S(2)}) collective-permute-start(f32[1024,768]{1,0:T(8,128)} %fusion.198), channel_id=1, source_target_pairs={{0,1},{1,0},{2,3},{3,2},{4,5},{5,4},{6,7},{7,6},{8,9},{9,8},{10,11... | collective-permute-start | bytes 9437192 | tf_op jit(solution)/shard_map/ppermute | solution.py:30
  765.3 52.0 %all-to-all-start.6 = ((bf16[8,160,768]{2,1,0:T(8,128)(2,1)}), bf16[8,160,768]{2,1,0:T(8,128)(2,1)S(1)}, u32[]{:S(2)}, u32[]{:S(2)}) async-start(bf16[8,160,768]{2,1,0:T(8,128)(2,1)} %fusion.47), calls=%async_computation.6 | async-start | bytes 3932160 | tf_op jit(solution)/shard_map/all_to_all | solution.py:624
  788.2 64.2 %collective-permute-start.26 = (bf16[1600,768]{1,0:T(8,128)(2,1)}, bf16[1600,768]{1,0:T(8,128)(2,1)}, u32[]{:S(2)}, u32[]{:S(2)}) collective-permute-start(bf16[1600,768]{1,0:T(8,128)(2,1)} %fusion.42), channel_id=1, source_target_pairs={{0,4},{4,0},{8,12},{12,8},{16,20},{20,16},{24,28},{28,24},{1,5},{5... | collective-permute-start | bytes 7372808 | tf_op jit(solution)/shard_map/ppermute | solution.py:30
  798.9 65.7 %collective-permute-start.40 = (bf16[2,768,768]{2,1,0:T(8,128)(2,1)}, bf16[2,768,768]{2,1,0:T(8,128)(2,1)}, u32[]{:S(2)}, u32[]{:S(2)}) collective-permute-start(bf16[2,768,768]{2,1,0:T(8,128)(2,1)} %fusion.15), channel_id=1, source_target_pairs={{0,2},{1,3},{2,0},{3,1},{4,6},{5,7},{6,4},{7,5},{8,10},{9,11},{10,... | collective-permute-start | bytes 7077896 | tf_op jit(solution)/shard_map/ppermute | solution.py:30
  872.3 11.6 %all-to-all-start.7 = ((f32[8,1,128]{2,1,0:T(1,128)}), f32[8,1,128]{2,1,0:T(1,128)S(1)}, u32[]{:S(2)}, u32[]{:S(2)}) async-start(f32[8,1,128]{2,1,0:T(1,128)} %broadcast_in_dim.134), calls=%async_computation.7 | async-start | bytes 8192 | tf_op jit(solution)/shard_map/all_to_all | solution.py:660
  (111 other events, 1201.1 us)
Sparse Core Ops, SparseCore 1:
  95.3 55.3 all-gather.7

commit v2 on v1

v2 whole, which is shorter than its diff:
```python
from functools import partial

import jax
import jax.numpy as jnp
from jax import lax
from jax.experimental import pallas as pl
from jax.experimental.pallas import tpu as pltpu
from jax.sharding import PartitionSpec as P

HD = 64
DOCS_ROW = 8
STEP = 7


EPS_NORM = 1e-06
BETA_ONE = 0.9
BETA_TWO = 0.95
ADAM_EPS = 1e-08
RATE_MATRIX = 0.05
RATE_GAIN = 0.3
DECAY = 0.1
CLIP_AT = 0.005
NEVER = -1e30
BF = jnp.bfloat16
F32 = jnp.float32
VMEM = 56 * 1024 * 1024
SHORT = pl.CostEstimate(flops=1024, bytes_accessed=1024, transcendentals=0)


def flip(x, axis, k):
    return lax.ppermute(x, axis, [(j, j ^ k) for j in range(lax.axis_size(axis))])


def behind(x, after):
    return jnp.where(after == after, x, 0)


def far_flip(x, axis, k, after=None):
    pairs = [[j, j ^ k] for j in range(lax.axis_size(axis)) if not j & k]
    both = lax.all_gather(x, axis, axis_index_groups=pairs)
    upper = (lax.axis_index(axis) // k) % 2
    if after is not None:
        upper = behind(upper, after)
    return lax.dynamic_index_in_dim(both, 1 - upper, 0, keepdims=False)


def hidden_gather(x):
    far = flip(x, "hidden", 2)
    return [x, far, flip(x, "hidden", 1), flip(far, "hidden", 1)]


def piece_of(bits):
    return (bits >> 1) + 2 * (bits & 1)


def round_up(n, m):
    return -(-n // m) * m


def dot(a, b, ca=1, cb=0):
    return lax.dot_general(a, b, (((ca,), (cb,)), ((), ())), preferred_element_type=F32)


def hot_rows(place, count):
    return (jnp.arange(count, dtype=jnp.int32)[:, None] == place[None, :]).astype(BF)


def hot_columns(place, count):
    return (place[:, None] == jnp.arange(count, dtype=jnp.int32)[None, :]).astype(BF)


QB = 256
SPAN = 2


ANY = pl.BlockSpec(memory_space=pl.ANY)
WHOLE = pl.BlockSpec(memory_space=pltpu.VMEM)


def bias_of(first, second, axis, at_first, at_second):
    shape = (first.shape[0], second.shape[1])
    pos_a = lax.broadcasted_iota(jnp.int32, shape, 0) + at_first
    pos_b = lax.broadcasted_iota(jnp.int32, shape, 1) + at_second
    seen = (pos_a >= pos_b) if axis == 0 else (pos_b >= pos_a)
    return jnp.where(seen & (first == second), 0.0, NEVER)


def pack_kernel(in_ref, out_ref, gains_ref, *rest):
    o_ref = rest[-1]
    o_ref[...] = jnp.zeros_like(o_ref)
    width = out_ref.shape[1]
    for c in range(3):
        o_ref[:, c * width : (c + 1) * width] = in_ref[c].astype(BF)
    wide = round_up(3 * width, 128)
    o_ref[:, wide : wide + width] = out_ref[...].astype(BF)
    o_ref[:, wide + width : wide + width + 3] = gains_ref[...].astype(BF)


def pack(attn_in, attn_out, gains, ready):
    rows, width = attn_out.shape
    return pl.pallas_call(
        pack_kernel,
        in_specs=[WHOLE] * 3 + [ANY] * len(ready),
        out_specs=WHOLE,
        out_shape=jax.ShapeDtypeStruct((rows, round_up(round_up(3 * width, 128) + width + 3, 128)), BF),
        name="pack",
    )(attn_in.transpose(1, 0, 2), attn_out, gains, *ready)


def attend_kernel(rows_ref, w_ref, segr_ref, segc_ref, *rest):
    qkv_ref, o_ref, part_ref = rest[-3:]
    pieces, seq, width = o_ref.shape
    wide = round_up(3 * width, 128)
    factor = jnp.asarray(HD**-0.5, BF)
    heads = [(p, c) for p in range(pieces) for c in range(0, width, HD)]
    for p in range(pieces):
        qkv_ref[p] = dot(rows_ref[...], w_ref[p, :, : 3 * width]).astype(BF)
    for b in range(seq // QB):
        lo, at, hi = max(0, b - SPAN) * QB, b * QB, (b + 1) * QB
        bias = bias_of(segc_ref[at:hi, :], segr_ref[:, lo:hi], 0, at, lo)
        scores = []
        for p, c in heads:
            q = qkv_ref[p, at:hi, c : c + HD] * factor
            scores.append(dot(q, qkv_ref[p, lo:hi, width + c : width + c + HD], 1, 1))
        probs = []
        for s in scores:
            s = s + bias
            e = jnp.exp(s - jnp.max(s, axis=1, keepdims=True))
            probs.append((e * (1.0 / jnp.sum(e, axis=1, keepdims=True))).astype(BF))
        outs = [
            dot(prob, qkv_ref[p, lo:hi, 2 * width + c : 2 * width + c + HD])
            for prob, (p, c) in zip(probs, heads, strict=True)
        ]
        for out, (p, c) in zip(outs, heads, strict=True):
            o_ref[p, at:hi, c : c + HD] = out.astype(BF)
    total = dot(o_ref[0], w_ref[0, :, wide : wide + width], 1, 1)
    for p in range(1, pieces):
        total += dot(o_ref[p], w_ref[p, :, wide : wide + width], 1, 1)
    part_ref[...] = total


def attend(rows, packed, width, seg, ready):
    seq, model = rows.shape
    pieces = packed.shape[0]
    return pl.pallas_call(
        attend_kernel,
        in_specs=[WHOLE] * 4 + [ANY] * len(ready),
        out_specs=[WHOLE] * 3,
        out_shape=[
            jax.ShapeDtypeStruct((pieces, seq, 3 * width), BF),
            jax.ShapeDtypeStruct((pieces, seq, width), BF),
            jax.ShapeDtypeStruct((seq, model), F32),
        ],
        compiler_params=pltpu.CompilerParams(vmem_limit_bytes=VMEM),
        cost_estimate=SHORT,
        name="attend",
    )(rows, packed, seg[None, :], seg[:, None], *ready)


def attend_back_kernel(branch_ref, w_ref, qkv_ref, segr_ref, segc_ref, *rest):
    d_ref, part_ref, g_ref, dk_acc, dv_acc = rest[-5:]
    pieces, seq, width = g_ref.shape
    wide = round_up(3 * width, 128)
    scale = HD**-0.5
    factor = jnp.asarray(scale, BF)
    heads = [(p, c) for p in range(pieces) for c in range(0, width, HD)]
    for p in range(pieces):
        g_ref[p] = dot(branch_ref[...], w_ref[p, :, wide : wide + width]).astype(BF)
    dk_acc[...] = jnp.zeros_like(dk_acc)
    dv_acc[...] = jnp.zeros_like(dv_acc)
    for b in range(seq // QB):
        lo, at, hi = max(0, b - SPAN) * QB, b * QB, (b + 1) * QB
        bias = bias_of(segc_ref[lo:hi, :], segr_ref[:, at:hi], 1, lo, at)
        for group in (heads[: len(heads) // 2], heads[len(heads) // 2 :]):
            qs = [qkv_ref[p, at:hi, c : c + HD] * factor for p, c in group]
            ks = [qkv_ref[p, lo:hi, width + c : width + c + HD] for p, c in group]
            gs = [g_ref[p, at:hi, c : c + HD] for p, c in group]
            scores = [dot(k, q, 1, 1) for k, q in zip(ks, qs, strict=True)]
            d_probs = [
                dot(qkv_ref[p, lo:hi, 2 * width + c : 2 * width + c + HD], g, 1, 1)
                for (p, c), g in zip(group, gs, strict=True)
            ]
            probs, d_scores = [], []
            for s, d_prob in zip(scores, d_probs, strict=True):
                s = s + bias
                e = jnp.exp(s - jnp.max(s, axis=0, keepdims=True))
                prob = e * (1.0 / jnp.sum(e, axis=0, keepdims=True))
                centre = jnp.sum(prob * d_prob, axis=0, keepdims=True)
                d_scores.append((prob * (d_prob - centre)).astype(BF))
                probs.append(prob.astype(BF))
            dqs = [dot(d, k, 0, 0) for d, k in zip(d_scores, ks, strict=True)]
            dks = [dot(d, q) for d, q in zip(d_scores, qs, strict=True)]
            dvs = [dot(prob, g) for prob, g in zip(probs, gs, strict=True)]
            for i, (p, c) in enumerate(group):
                d_ref[p, at:hi, c : c + HD] = (dqs[i] * scale).astype(BF)
                dk_acc[p, lo:hi, c : c + HD] += dks[i]
                dv_acc[p, lo:hi, c : c + HD] += dvs[i]
    d_ref[:, :, width : 2 * width] = dk_acc[...].astype(BF)
    d_ref[:, :, 2 * width :] = dv_acc[...].astype(BF)
    total = dot(d_ref[0], w_ref[0, :, : 3 * width], 1, 1)
    for p in range(1, pieces):
        total += dot(d_ref[p], w_ref[p, :, : 3 * width], 1, 1)
    part_ref[...] = total


def attend_back(branch, packed, qkv, seg, ready):
    seq, model = branch.shape
    pieces, _, width = qkv.shape
    return pl.pallas_call(
        attend_back_kernel,
        in_specs=[WHOLE] * 5 + [ANY] * len(ready),
        out_specs=[WHOLE] * 2,
        out_shape=[
            jax.ShapeDtypeStruct((pieces, seq, width), BF),
            jax.ShapeDtypeStruct((seq, model), F32),
        ],
        scratch_shapes=[
            pltpu.VMEM((pieces, seq, width // 3), BF),
            pltpu.VMEM((pieces, seq, width // 3), F32),
            pltpu.VMEM((pieces, seq, width // 3), F32),
        ],
        compiler_params=pltpu.CompilerParams(vmem_limit_bytes=VMEM),
        cost_estimate=SHORT,
        name="attend_back",
    )(branch, packed, qkv, seg[None, :], seg[:, None], *ready)


def attn_grad_kernel(rows_ref, d_ref, branch_ref, o_ref, *rest):
    out_ref = rest[-1]
    width = d_ref.shape[2]
    out_ref[:, :width] = dot(rows_ref[...], d_ref[0], 0, 0).astype(BF)
    out_ref[:, width:] = dot(branch_ref[...], o_ref[0], 0, 0).astype(BF)


def attn_grad(rows, d_qkv, branch, attended, ready):
    model = rows.shape[1]
    seq, third = attended.shape[1:]
    one = pl.BlockSpec((1, seq, 3 * third), lambda i: (0, 0, 0))
    two = pl.BlockSpec((1, seq, third), lambda i: (0, 0, 0))
    full = pl.BlockSpec((seq, model), lambda i: (0, 0))
    return pl.pallas_call(
        attn_grad_kernel,
        grid=(1,),
        in_specs=[full, one, full, two] + [ANY] * len(ready),
        out_specs=pl.BlockSpec((model, 4 * third), lambda i: (0, 0)),
        out_shape=jax.ShapeDtypeStruct((model, 4 * third), BF),
        compiler_params=pltpu.CompilerParams(vmem_limit_bytes=VMEM),
        cost_estimate=SHORT,
        name="attn_grad",
    )(rows, d_qkv, branch, attended, *ready)


def picked(place_ref, *row_refs):
    count = row_refs[0].shape[0]
    at = lax.broadcasted_iota(jnp.int32, (place_ref.shape[0], count), 1)
    total = None
    for q, ref in enumerate(row_refs):
        part = dot((at == place_ref[...] - q * count).astype(BF), ref[...])
        total = part if total is None else total + part
    return total


def pick_norm_kernel(scale, pick, parts, base, *refs):
    first_refs, refs = refs[:parts], refs[parts:]
    if base:
        base_ref, refs = refs[0], refs[1:]
    gain_ref, sum_ref, norm_ref = refs[0], refs[-2], refs[-1]
    if pick:
        x = picked(*first_refs)
    else:
        x = first_refs[0][...]
        for ref in first_refs[1:]:
            x = x + ref[...]
    if base:
        x = base_ref[...] + x
    if scale != 1.0:
        x = x * scale
    sum_ref[...] = x
    root = lax.rsqrt(jnp.mean(x * x, axis=1, keepdims=True) + EPS_NORM)
    norm_ref[...] = (x * root * gain_ref[...]).astype(BF)


def pick_norm(first, base, gain, scale=1.0, pick=True, ready=()):
    tokens = first[0].shape[0]
    width = gain.shape[1]
    block = min(tokens, 256)
    by_rows = pl.BlockSpec((block, width), lambda i: (i, 0))
    if pick:
        first = (first[0][:, None], *first[1:])
        specs = [pl.BlockSpec((block, 1), lambda i: (i, 0))]
        specs += [pl.BlockSpec(r.shape, lambda i: (0, 0)) for r in first[1:]]
    else:
        specs = [by_rows] * len(first)
    has_base = base is not None
    return pl.pallas_call(
        partial(pick_norm_kernel, scale, pick, len(first), has_base),
        grid=(tokens // block,),
        in_specs=specs
        + [by_rows] * has_base
        + [pl.BlockSpec((1, width), lambda i: (0, 0))]
        + [ANY] * len(ready),
        out_specs=[by_rows, by_rows],
        out_shape=[
            jax.ShapeDtypeStruct((tokens, width), F32),
            jax.ShapeDtypeStruct((tokens, width), BF),
        ],
        compiler_params=pltpu.CompilerParams(vmem_limit_bytes=VMEM),
        cost_estimate=SHORT,
        name="pick_norm",
    )(*first, *((base,) if has_base else ()), gain, *ready)


def norm_back_kernel(scale, parts, pick, rest, split, x_ref, gain_ref, *refs):
    g_refs, refs = refs[:parts], refs[parts:]
    if rest:
        rest_ref, refs = refs[0], refs[1:]
    gain_out, one_ref, two_ref = refs[-3:]
    x = x_ref[...]
    if pick == "rows":
        g = picked(*g_refs)
    elif pick == "blocks":
        which = g_refs[0][pl.program_id(0)]
        g = g_refs[1][...].astype(F32)
        for q, ref in enumerate(g_refs[2:], 1):
            g = jnp.where(which == q, ref[...].astype(F32), g)
    else:
        g = g_refs[0][...].astype(F32)
        for ref in g_refs[1:]:
            g = g + ref[...].astype(F32)
    root = lax.rsqrt(jnp.mean(x * x, axis=1, keepdims=True) + EPS_NORM)
    scaled = x * root
    d_gain = jnp.sum(g * scaled, axis=0, keepdims=True)
    g = g * gain_ref[...]
    dx = root * (g - scaled * jnp.mean(g * scaled, axis=1, keepdims=True))
    if rest:
        dx = rest_ref[...] + dx
    if scale != 1.0:
        dx = dx * scale
    high = dx.astype(BF)
    one_ref[...] = high
    two_ref[...] = (dx - high.astype(F32)).astype(BF) if split else dx

    @pl.when(pl.program_id(0) == 0)
    def _():
        gain_out[...] = d_gain

    @pl.when(pl.program_id(0) > 0)
    def _():
        gain_out[...] += d_gain


def norm_back(x, gain, gradients, rest=None, scale=1.0, split=False, pick="", ready=()):
    tokens, width = x.shape
    block = min(tokens, 256)
    by_rows = pl.BlockSpec((block, width), lambda i: (i, 0))
    one_row = pl.BlockSpec((1, width), lambda i: (0, 0))
    has_rest = rest is not None
    whole = [pl.BlockSpec(g.shape, lambda i: (0, 0)) for g in gradients[1:]]
    if pick == "rows":
        gradients = (gradients[0][:, None], *gradients[1:])
        specs = [pl.BlockSpec((block, 1), lambda i: (i, 0)), *whole]
    elif pick == "blocks":
        specs = [pl.BlockSpec(memory_space=pltpu.SMEM), *whole]
    else:
        specs = [by_rows] * len(gradients)
    return pl.pallas_call(
        partial(norm_back_kernel, scale, len(gradients), pick, has_rest, split),
        grid=(tokens // block,),
        in_specs=[by_rows, one_row] + specs + [by_rows] * has_rest + [ANY] * len(ready),
        out_specs=[one_row, by_rows, by_rows],
        out_shape=[
            jax.ShapeDtypeStruct((1, width), F32),
            jax.ShapeDtypeStruct((tokens, width), BF),
            jax.ShapeDtypeStruct((tokens, width), BF if split else F32),
        ],
        compiler_params=pltpu.CompilerParams(vmem_limit_bytes=VMEM),
        cost_estimate=SHORT,
        name="norm_back",
    )(x, gain, *gradients, *((rest,) if has_rest else ()), *ready)


ERFC = (
    -1.26551223,
    1.00002368,
    0.37409196,
    0.09678418,
    -0.18628806,
    0.27886807,
    -1.13520398,
    1.48851587,
    -0.82215223,
    0.17087277,
)


def gelu_and_slope(x):
    t = 1.0 / (1.0 + 0.35355339059327373 * jnp.abs(x))
    poly = jnp.full_like(t, ERFC[-1])
    for c in ERFC[-2::-1]:
        poly = poly * t + c
    square = 0.5 * x * x
    half = 0.5 * t * jnp.exp(poly - square)
    below = jnp.where(x >= 0.0, 1.0 - half, half)
    return x * below, below + x * jnp.exp(-square) * 0.3989422804014327


def expert_back_kernel(grad_ref, *refs):
    w_refs, slope_refs, refs = refs[:4], refs[4:8], refs[8:]
    out_ref, d_refs = refs[-5], refs[-4:]
    grad = grad_ref[...]
    total = None
    for w_ref, slope_ref, d_ref in zip(w_refs, slope_refs, d_refs, strict=True):
        d_pre = (dot(grad, w_ref[1], 1, 1) * slope_ref[...]).astype(BF)
        d_ref[...] = d_pre
        product = dot(d_pre, w_ref[0], 1, 1)
        total = product if total is None else total + product
    out_ref[...] = total.astype(BF)


def expert_back(grad, weights, slopes, ready):
    return pl.pallas_call(
        expert_back_kernel,
        in_specs=[WHOLE] * 9 + [ANY] * len(ready),
        out_specs=[WHOLE] * 5,
        out_shape=[jax.ShapeDtypeStruct(grad.shape, BF)]
        + [jax.ShapeDtypeStruct(slope.shape, BF) for slope in slopes],
        compiler_params=pltpu.CompilerParams(vmem_limit_bytes=VMEM),
        cost_estimate=SHORT,
        name="expert_back",
    )(grad, *weights, *slopes, *ready)


def part_rows(padded):
    return max(r for r in range(32, 385, 32) if padded % r == 0)


def cast_pick_kernel(real, place_ref, x_ref, table_ref, o_ref, acc):
    j = pl.program_id(0)
    rows = x_ref.shape[0]
    at = lax.broadcasted_iota(jnp.int32, x_ref.shape, 0) + j * rows
    table_ref[...] = jnp.where(at < real, x_ref[...], 0.0).astype(BF)
    column = lax.broadcasted_iota(jnp.int32, (place_ref.shape[0], rows), 1) + j * rows
    found = dot((column == place_ref[...]).astype(BF), table_ref[...])

    @pl.when(j == 0)
    def _():
        acc[...] = found

    @pl.when(j > 0)
    def _():
        acc[...] += found

    @pl.when(j == pl.num_programs(0) - 1)
    def _():
        o_ref[...] = acc[...].astype(BF)


def cast_pick(place, x, padded):
    real, width = x.shape
    rows = part_rows(padded)
    count = place.shape[0]
    return pl.pallas_call(
        partial(cast_pick_kernel, real),
        grid=(padded // rows,),
        in_specs=[
            pl.BlockSpec((count, 1), lambda j: (0, 0)),
            pl.BlockSpec((rows, width), lambda j: (j, 0)),
        ],
        out_specs=[
            pl.BlockSpec((rows, width), lambda j: (j, 0)),
            pl.BlockSpec((count, width), lambda j: (0, 0)),
        ],
        out_shape=[
            jax.ShapeDtypeStruct((padded, width), BF),
            jax.ShapeDtypeStruct((count, width), BF),
        ],
        scratch_shapes=[pltpu.VMEM((count, width), F32)],
        compiler_params=pltpu.CompilerParams(vmem_limit_bytes=VMEM),
        cost_estimate=SHORT,
        name="cast_pick",
    )(place[:, None], x)


def turn_kernel(a_ref, b_ref, c_ref, d_ref, o_ref):
    o_ref[...] = jnp.concatenate([a_ref[...], b_ref[...], c_ref[...], d_ref[...]], axis=0).T


def turned(slices):
    padded, width = slices[0].shape
    rows = part_rows(padded)
    return pl.pallas_call(
        turn_kernel,
        grid=(padded // rows,),
        in_specs=[pl.BlockSpec((rows, width), lambda j: (j, 0))] * 4,
        out_specs=pl.BlockSpec((width, 4 * rows), lambda j: (0, j)),
        out_shape=jax.ShapeDtypeStruct((width, 4 * padded), BF),
        compiler_params=pltpu.CompilerParams(vmem_limit_bytes=VMEM),
        cost_estimate=pl.CostEstimate(flops=0, bytes_accessed=24 * padded * width, transcendentals=0),
        name="turned",
    )(*slices)


def logits_kernel(
    real, a_ref, b_ref, c_ref, d_ref, rows_ref, col_ref, *rest
):
    out_ref, peak_ref, stat_ref, peak_s, sum_s, hit_s = rest[-6:]
    j = pl.program_id(0)
    tokens = rows_ref.shape[0]
    part = a_ref.shape[0]

    @pl.when(j == 0)
    def _():
        peak_s[...] = jnp.full((8, tokens), NEVER, F32)
        sum_s[...] = jnp.zeros((8, tokens), F32)
        hit_s[...] = jnp.zeros((8, tokens), F32)

    away = col_ref[...] - j * (4 * part) - lax.broadcasted_iota(jnp.int32, (8, tokens), 0)
    peak, total, hit = peak_s[...], sum_s[...], hit_s[...]
    rows = rows_ref[...]
    tail = round_up(part * (-(-real // part)) - real, 8)
    for q, ref in enumerate((a_ref, b_ref, c_ref, d_ref)):
        logits = dot(ref[...], rows, 1, 1)
        if tail:
            at = lax.broadcasted_iota(jnp.int32, (tail, tokens), 0) + (j + 1) * part - tail
            end = jnp.where(at < real, logits[part - tail :], NEVER)
            logits = jnp.concatenate([logits[: part - tail], end], axis=0)
        tiles = logits.reshape(part // 8, 8, tokens)
        new = jnp.maximum(peak, jnp.max(tiles, axis=0))
        powers = jnp.exp(tiles - new[None])
        out_ref[q * part : (q + 1) * part, :] = powers.reshape(part, tokens)
        peak_ref[q * 8 : (q + 1) * 8, :] = new
        total = total * jnp.exp(peak - new) + jnp.sum(powers, axis=0)
        for i in range(part // 8):
            hit = hit + jnp.where(away == q * part + 8 * i, tiles[i], 0.0)
        peak = new
    peak_s[...], sum_s[...], hit_s[...] = peak, total, hit

    @pl.when(j == pl.num_programs(0) - 1)
    def _():
        top = jnp.max(peak, axis=0, keepdims=True)
        stat_ref[0:1, :] = top
        stat_ref[1:2, :] = jnp.sum(total * jnp.exp(peak - top), axis=0, keepdims=True)
        stat_ref[2:3, :] = jnp.sum(hit, axis=0, keepdims=True)
        stat_ref[3:8, :] = jnp.zeros((5, tokens), F32)


def head_logits(slices, rows, col, real, ready=()):
    padded, width = slices[0].shape
    tokens = rows.shape[0]
    part = part_rows(padded)
    steps = padded // part
    return pl.pallas_call(
        partial(logits_kernel, real),
        grid=(steps,),
        in_specs=[pl.BlockSpec((part, width), lambda j: (j, 0))] * 4
        + [
            pl.BlockSpec((tokens, width), lambda j: (0, 0)),
            pl.BlockSpec((1, tokens), lambda j: (0, 0)),
        ]
        + [ANY] * len(ready),
        out_specs=[
            pl.BlockSpec((4 * part, tokens), lambda j: (j, 0)),
            pl.BlockSpec((32, tokens), lambda j: (j, 0)),
            pl.BlockSpec((8, tokens), lambda j: (0, 0)),
        ],
        out_shape=[
            jax.ShapeDtypeStruct((4 * padded, tokens), F32),
            jax.ShapeDtypeStruct((32 * steps, tokens), F32),
            jax.ShapeDtypeStruct((8, tokens), F32),
        ],
        scratch_shapes=[pltpu.VMEM((8, tokens), F32)] * 3,
        compiler_params=pltpu.CompilerParams(vmem_limit_bytes=VMEM),
        cost_estimate=pl.CostEstimate(flops=16 * padded * tokens * width, bytes_accessed=16 * padded * tokens, transcendentals=0),
        name="head_logits",
    )(*slices, rows, col, *ready)


def head_back_kernel(table_ref, power_ref, peak_ref, col_ref, side_ref, *rest):
    d_ref, out_ref, acc = rest[-3:]
    j = pl.program_id(0)
    block, tokens = power_ref.shape
    part = block // 4
    away = col_ref[...] - j * block - lax.broadcasted_iota(jnp.int32, (8, tokens), 0)
    log_total, weight = side_ref[0:1, :], side_ref[1:2, :]
    pieces = []
    for q in range(4):
        factor = jnp.exp(peak_ref[q * 8 : (q + 1) * 8, :] - log_total) * weight
        for i in range(part // 8):
            at = q * part + 8 * i
            less = jnp.where(away == at, weight, 0.0)
            pieces.append(power_ref[at : at + 8, :] * factor - less)
    d = jnp.concatenate(pieces, axis=0).astype(BF)
    d_ref[...] = d
    product = dot(table_ref[...], d)

    @pl.when(j == 0)
    def _():
        acc[...] = product

    @pl.when(j > 0)
    def _():
        acc[...] += product

    @pl.when(j == pl.num_programs(0) - 1)
    def _():
        out_ref[...] = acc[...].T.astype(out_ref.dtype)


def head_back(table_t, powers, peaks, at, col, side, ready=()):
    width, vocab = table_t.shape
    tokens = col.shape[1]
    steps = peaks.shape[0] // 32
    block = vocab // steps
    return pl.pallas_call(
        head_back_kernel,
        grid=(steps,),
        in_specs=[
            pl.BlockSpec((width, block), lambda j: (0, j)),
            pl.BlockSpec((block, tokens), lambda j: (j, at)),
            pl.BlockSpec((32, tokens), lambda j: (j, at)),
            pl.BlockSpec((1, tokens), lambda j: (0, 0)),
            pl.BlockSpec((8, tokens), lambda j: (0, 0)),
        ]
        + [ANY] * len(ready),
        out_specs=[
            pl.BlockSpec((block, tokens), lambda j: (j, 0)),
            pl.BlockSpec((tokens, width), lambda j: (0, 0)),
        ],
        out_shape=[
            jax.ShapeDtypeStruct((vocab, tokens), BF),
            jax.ShapeDtypeStruct((tokens, width), BF),
        ],
        scratch_shapes=[pltpu.VMEM((width, tokens), F32)],
        compiler_params=pltpu.CompilerParams(vmem_limit_bytes=VMEM),
        cost_estimate=pl.CostEstimate(flops=4 * vocab * tokens * width, bytes_accessed=6 * vocab * tokens, transcendentals=0),
        name="head_back",
    )(table_t, powers, peaks, col, side, *ready)


def table_grad_kernel(count, *refs):
    d_refs, row_refs, out_refs = refs[: 2 * count], refs[2 * count : 3 * count], refs[-2:]
    total = None
    for k in range(count):
        both = jnp.concatenate([d_refs[2 * k][...], d_refs[2 * k + 1][...]], axis=0)
        product = dot(both, row_refs[k][...])
        total = product if total is None else total + product
    part = out_refs[0].shape[0]
    for q in range(2):
        out_refs[q][...] = total[q * part : (q + 1) * part]


def table_grad(ds, rows, padded, which, ready):
    width = rows[0].shape[1]
    part = part_rows(padded)

    def spec(tokens, q):
        return pl.BlockSpec((part, tokens), lambda j: (4 * j + q, 0))

    return pl.pallas_call(
        partial(table_grad_kernel, len(ds)),
        grid=(padded // part,),
        in_specs=[spec(d.shape[1], q) for d in ds for q in which]
        + [pl.BlockSpec(r.shape, lambda j: (0, 0)) for r in rows]
        + [ANY] * len(ready),
        out_specs=[pl.BlockSpec((part, width), lambda j: (j, 0))] * 2,
        out_shape=[jax.ShapeDtypeStruct((padded, width), F32)] * 2,
        compiler_params=pltpu.CompilerParams(vmem_limit_bytes=VMEM),
        cost_estimate=pl.CostEstimate(
            flops=4 * padded * width * sum(d.shape[1] for d in ds),
            bytes_accessed=8 * padded * width,
            transcendentals=0,
        ),
        name="table_grad",
    )(*[d for d in ds for _ in which], *rows, *ready)


def finish_kernel(real, base_ref, place_ref, rows_ref, out_ref, square_ref):
    rows = base_ref.shape[0]
    first = pl.program_id(0) * rows
    at = lax.broadcasted_iota(jnp.int32, (rows, place_ref.shape[1]), 0) + first
    spread = dot((at == place_ref[...]).astype(BF), rows_ref[...])
    g = base_ref[...] + spread
    out_ref[...] = g
    inside = lax.broadcasted_iota(jnp.int32, g.shape, 0) + first < real
    g = jnp.where(inside, g, 0.0)
    squares = jnp.sum(g * g, axis=0, keepdims=True)

    @pl.when(pl.program_id(0) == 0)
    def _():
        square_ref[...] = squares

    @pl.when(pl.program_id(0) > 0)
    def _():
        square_ref[...] += squares


def finish(base, place, rows, real):
    padded, width = base.shape
    part = part_rows(padded)
    block = pl.BlockSpec((part, width), lambda j: (j, 0))
    return pl.pallas_call(
        partial(finish_kernel, real),
        grid=(padded // part,),
        in_specs=[
            block,
            pl.BlockSpec((1, place.shape[0]), lambda j: (0, 0)),
            pl.BlockSpec(rows.shape, lambda j: (0, 0)),
        ],
        out_specs=[block, pl.BlockSpec((1, width), lambda j: (0, 0))],
        out_shape=[
            jax.ShapeDtypeStruct((real, width), F32),
            jax.ShapeDtypeStruct((1, width), F32),
        ],
        compiler_params=pltpu.CompilerParams(vmem_limit_bytes=VMEM),
        cost_estimate=SHORT,
        name="finish",
    )(base, place[None, :], rows)


def adam_step(weight, first_moment, second_moment, gradient, step_rate, weight_decay):
    first_moment = BETA_ONE * first_moment + (1.0 - BETA_ONE) * gradient
    second_moment = BETA_TWO * second_moment + (1.0 - BETA_TWO) * gradient * gradient
    update = (
        first_moment
        / (1.0 - BETA_ONE**STEP)
        / (jnp.sqrt(second_moment / (1.0 - BETA_TWO**STEP)) + ADAM_EPS)
    )
    return (weight - step_rate * (update + weight_decay * weight), first_moment, second_moment)


def combine_stats(left, right):
    peak = jnp.maximum(left[0], right[0])
    total = left[1] * jnp.exp(left[0] - peak) + right[1] * jnp.exp(right[0] - peak)
    return jnp.stack([peak, total, left[2] + right[2]])


def on_device(
    token_ids,
    target_ids,
    doc_segments,
    hash_experts,
    embed_table,
    embed_first,
    embed_second,
    attn_in,
    attn_in_first,
    attn_in_second,
    attn_out,
    attn_out_first,
    attn_out_second,
    expert_in,
    expert_in_first,
    expert_in_second,
    expert_out,
    expert_out_first,
    expert_out_second,
    norm_gains,
    gains_first,
    gains_second,
):
    n_expert = lax.axis_size("expert")
    n_hidden = lax.axis_size("hidden")
    assert n_hidden == 4 and token_ids.shape[0] == 1
    e_index = lax.axis_index("expert")
    h_index = lax.axis_index("hidden")
    tok_count = token_ids.shape[1]
    vocab_rows, model_width = embed_table.shape
    embed_scale = model_width**0.5
    ids = token_ids[0]
    targets = target_ids[0]
    segment = doc_segments[0]
    token_at = jnp.arange(tok_count, dtype=jnp.int32)

    padded = round_up(vocab_rows, 32)
    own_rows = attn_in.shape[0]
    head_width = attn_in.shape[2]

    slots = round_up(5 * tok_count // (4 * n_expert * n_hidden), 8)
    shard = ids // vocab_rows
    shard_e, shard_h = shard // n_hidden, shard % n_hidden
    same_id = ids[:, None] == ids[None, :]
    first_at = jnp.min(jnp.where(same_id, token_at[None, :], tok_count), axis=1)
    is_first = first_at == token_at
    rank = jnp.sum(
        (
            (shard[:, None] == shard[None, :])
            & is_first[None, :]
            & (token_at[None, :] < first_at[:, None])
        ).astype(jnp.int32),
        axis=1,
    )
    overflow = jnp.max(rank) >= slots
    place_own = jnp.where(
        (shard_h == h_index) & (rank < slots), shard_e * slots + rank, -1
    )
    wanted = jnp.max(
        jnp.where(
            jnp.arange(n_expert * slots, dtype=jnp.int32)[:, None] == place_own[None, :],
            (ids % vocab_rows)[None, :],
            -1,
        ),
        axis=1,
    )
    asked = jnp.concatenate(
        [
            wanted.reshape(n_expert, slots),
            jnp.broadcast_to(overflow.astype(jnp.int32), (n_expert, 128 - slots)),
        ],
        axis=1,
    )

    asked = lax.all_to_all(asked, "expert", split_axis=0, concat_axis=0, tiled=True)
    any_overflow = jnp.max(asked[:, slots:]) > 0
    asked_rows = asked[:, :slots].reshape(n_expert * slots)

    capacity = 3 * tok_count // (2 * n_expert)
    quarter = capacity // n_hidden
    expert_ids = hash_experts[ids]
    onehot = (expert_ids[:, None] == jnp.arange(n_expert, dtype=jnp.int32)).astype(jnp.int32)
    before = jnp.cumsum(onehot, axis=0) - onehot
    slot_rank = jnp.sum(before * onehot, axis=1)
    kept = slot_rank < capacity
    slot_h = slot_rank // quarter
    slot_in = expert_ids * quarter + slot_rank % quarter
    rows_dev = n_expert * quarter
    fill_place = jnp.where(kept & (slot_h == h_index), slot_in, -1)
    pick_place = jnp.where(kept, piece_of(slot_h ^ h_index) * rows_dev + slot_in, -1)

    asked_rows = jnp.where(any_overflow, -1, asked_rows)
    table_own, answer = cast_pick(asked_rows, embed_table, padded)
    wide = round_up(3 * head_width, 128)
    packed = pack(attn_in, attn_out, norm_gains, (asked_rows,))
    packed = jnp.stack([packed, flip(packed, "hidden", 2)])
    packed = lax.all_gather(packed, "expert", axis=1, tiled=True)
    gain_full = packed[0, :, wide + head_width : wide + head_width + 3].astype(F32).T
    weights_own = jnp.stack([expert_in[0], expert_out[0]]).astype(BF)
    weights_y = far_flip(weights_own, "hidden", 2)

    n_all = n_expert * n_hidden
    own_shard = e_index * n_hidden + h_index
    everyone = [(j, (j + 1) % n_all) for j in range(n_all)]

    answer = lax.all_to_all(
        answer.reshape(n_expert, slots, model_width),
        "expert",
        split_axis=0,
        concat_axis=0,
        tiled=True,
    )
    answers = hidden_gather(answer.reshape(n_expert * slots, model_width))
    place_all = piece_of(shard_h ^ h_index) * (n_expert * slots) + shard_e * slots + rank

    def look_up_step(k, carry):
        table_far, found = carry
        here = (own_shard - k + n_all) % n_all
        place = jnp.where(shard == here, ids % vocab_rows, -1)
        row = dot(hot_columns(place, padded), table_far).astype(BF)
        row = jnp.pad(row, ((0, 4 * n_expert * slots - tok_count), (0, 0)))
        parts = row.reshape(4, n_expert * slots, model_width)
        found = [jnp.where(k == 0, 0, found[q]) + parts[q] for q in range(4)]
        return lax.ppermute(table_far, ("expert", "hidden"), everyone), found

    answers = lax.fori_loop(
        0, jnp.where(any_overflow, n_all, 0), look_up_step, (table_own, answers)
    )[1]
    place_all = jnp.where(any_overflow, token_at, place_all)
    embedded, normed_one = pick_norm(
        (place_all, *answers), None, gain_full[0:1], embed_scale, ready=(fill_place, pick_place)
    )

    qkv, attended, attn_part = attend(normed_one, packed, head_width, segment, ())
    after_attn, normed_two = pick_norm(
        (attn_part, flip(attn_part, "hidden", 1)),
        embedded,
        gain_full[1:2],
        pick=False,
    )

    fill_hot = hot_rows(fill_place, rows_dev)

    def to_expert(rows_in):
        block = dot(fill_hot, rows_in).astype(BF)
        return lax.all_to_all(block, "expert", split_axis=0, concat_axis=0, tiled=True)

    def from_expert(rows_in):
        block = lax.all_to_all(rows_in, "expert", split_axis=0, concat_axis=0, tiled=True)
        return hidden_gather(block.reshape(rows_dev, model_width))

    expert_w = [
        weights_own,
        weights_y,
        flip(weights_own, "hidden", 1),
        flip(weights_y, "hidden", 1),
    ]
    received = to_expert(normed_two)
    active, slope = [None] * 4, [None] * 4
    expert_sum = 0.0
    for p in (0, 2, 1, 3):
        value, slope[p] = gelu_and_slope(dot(received, expert_w[p][0]))
        active[p] = value.astype(BF)
        expert_sum = expert_sum + dot(active[p], expert_w[p][1])
    after_moe, final_rows = pick_norm(
        (pick_place, *from_expert(expert_sum.astype(BF))),
        after_attn,
        gain_full[2:3],
    )

    slice_x = far_flip(table_own, "expert", 1, final_rows[0, 0])
    slices = [table_own, slice_x, flip(table_own, "hidden", 1), flip(slice_x, "hidden", 1)]
    table_t = turned(slices)
    part = part_rows(padded)

    half, fourth = tok_count // 2, tok_count // 4
    own_at = (h_index & 1) * half + (h_index >> 1) * fourth
    other_at = (h_index & 1) * half + (1 - (h_index >> 1)) * fourth
    n_far = n_expert // 2

    def own_order(x):
        return jnp.concatenate(
            [
                lax.dynamic_slice_in_dim(x, own_at, fourth, x.ndim - 1),
                lax.dynamic_slice_in_dim(x, other_at, fourth, x.ndim - 1),
            ],
            axis=-1,
        )

    counts = jnp.sum((segment[:, None] == segment[None, :]).astype(F32), axis=1)
    weights = 1.0 / counts / (n_expert * DOCS_ROW)
    about = own_order(jnp.stack([targets.astype(F32), weights]))
    about_all = [about] + [flip(about, "expert", 2 * k) for k in range(1, n_far)]
    own_part = lax.dynamic_slice_in_dim(final_rows, own_at, fourth, 0)
    other_part = lax.dynamic_slice_in_dim(final_rows, other_at, fourth, 0)
    far_rows = [flip(own_part, "expert", 2 * k) for k in range(1, n_far)]

    columns = []
    for k in range(n_far):
        target = about_all[k][0].astype(jnp.int32)
        block_of = target // vocab_rows
        away_e = (block_of // n_hidden) ^ e_index
        away_h = (block_of % n_hidden) ^ h_index
        mine = (away_e < 2) & (away_h < 2)
        row_of = target % vocab_rows
        column = (row_of // part) * (4 * part) + (away_e + 2 * away_h) * part + row_of % part
        columns.append(jnp.where(mine, column, -1)[None, :])
    head_rows = [jnp.concatenate([own_part, other_part])]
    powers, stats = [], []
    for k in range(0, n_far, 2):
        for far in far_rows[max(k - 1, 0) : k + 1]:
            far = behind(far, stats[-1][0, 0]) if stats else far
            head_rows.append(jnp.concatenate([far, flip(far, "hidden", 2)]))
        one, two, stat = head_logits(
            slices,
            jnp.concatenate(head_rows[k : k + 2]),
            jnp.concatenate(columns[k : k + 2], axis=1),
            vocab_rows,
            () if k else (table_t,),
        )
        powers.append((one, two))
        stats += [stat[:3, :half], stat[:3, half:]]
    stat = jnp.stack(stats, axis=1)
    across = flip(stat, "hidden", 2)
    stat = combine_stats(stat, jnp.concatenate([across[..., fourth:], across[..., :fourth]], axis=2))
    far_stats = [flip(stat, "expert", 2 * k) for k in range(1, n_far)]
    for k in range(1, n_far):
        far = jnp.stack([far_stats[k - 1][:, j ^ k] for j in range(n_far)], axis=1)
        stat = combine_stats(stat, far)
    log_total = stat[0] + jnp.log(stat[1])
    loss_part = jnp.sum((log_total[0] - stat[2, 0]) * about[1])

    groups = [[0], [1]] + [[k, k + 1] for k in range(2, n_far, 2)]
    group_rows = [jnp.concatenate([head_rows[k] for k in group]) for group in groups]
    d_logits, d_parts, on_y = [None] * len(groups), [None] * n_far, []
    for i in range(len(groups) - 1, -1, -1):
        group = groups[i]
        wide_weights = jnp.concatenate([about_all[k][1] for k in group])
        wide_totals = jnp.concatenate([log_total[k] for k in group])
        side = jnp.stack([wide_totals, wide_weights] + [jnp.zeros_like(wide_totals)] * 6)
        d_logits[i], product = head_back(
            table_t,
            *powers[group[0] // 2],
            group[0] % 2,
            jnp.concatenate([columns[k] for k in group], axis=1),
            side,
            on_y[-3:-2] if i == 0 else (),
        )
        for g in reversed(range(len(group))):
            k, one = group[g], product[g * half : (g + 1) * half]
            gathered = one[:fourth].astype(F32) + flip(one[fourth:], "hidden", 2).astype(F32)
            if k:
                on_y.append(gathered.astype(BF))
                gathered = flip(on_y[-1], "expert", 2 * k).astype(F32)
            d_parts[k] = gathered
    d_quarter = sum(d_parts)
    d_four = hidden_gather(d_quarter.astype(BF))
    quarter_h = jnp.array([0, 2, 1, 3], jnp.int32)

    d_gain_three, d_result, d_after_moe = norm_back(
        after_moe,
        gain_full[2:3],
        (piece_of(quarter_h ^ h_index), *d_four),
        pick="blocks",
    )
    d_across = table_grad(d_logits, group_rows, padded, (1, 3), (d_result,))
    across_x = (d_across[0] + flip(d_across[1], "hidden", 1)).astype(BF)
    grad_in = to_expert(d_result)
    d_received, *d_pre = expert_back(grad_in, expert_w, slope, (across_x,))
    d_w = [
        jnp.stack([dot(received, d_pre[p], 0, 0), dot(active[p], grad_in, 0, 0)]) for p in range(4)
    ]
    d_same = table_grad(d_logits, group_rows, padded, (0, 2), (d_received,))

    d_base = (
        d_same[0] + flip(d_same[1], "hidden", 1) + far_flip(across_x, "expert", 1).astype(F32)
    )

    w_near = flip(d_w[3], "hidden", 1), flip(d_w[2], "hidden", 1)
    w_sent = (d_w[1] + w_near[0]).astype(BF)
    w_far = far_flip(w_sent, "hidden", 2)
    d_gain_two, d_branch, d_after_attn = norm_back(
        after_attn,
        gain_full[1:2],
        (pick_place, *from_expert(d_received)),
        d_after_moe,
        pick="rows",
    )

    d_qkv, d_norm_part = attend_back(d_branch, packed, qkv, segment, (w_sent,))
    d_gain_one, d_high, d_low = norm_back(
        embedded,
        gain_full[0:1],
        [d_norm_part, flip(d_norm_part, "hidden", 1)],
        d_after_attn,
        scale=embed_scale,
        split=True,
    )

    attn_sent = attn_grad(normed_one, d_qkv, d_branch, attended, (d_high,))

    row_hot = hot_rows(place_own, n_expert * slots)
    d_rows = dot(row_hot, d_high) + dot(row_hot, d_low)
    d_gains = jnp.concatenate([d_gain_one, d_gain_two, d_gain_three])
    d_gains = d_gains.reshape(3, n_expert, own_rows).transpose(1, 0, 2).reshape(n_expert, 1, -1)
    gains_high = lax.reduce_precision(d_gains, 8, 7)
    gains_two = jnp.concatenate([gains_high, d_gains - gains_high], axis=1).astype(BF)
    gains_two = jnp.pad(gains_two, ((0, 0), (0, 14), (0, model_width - gains_two.shape[2])))
    attn_got = lax.all_to_all(
        attn_sent.reshape(n_expert, own_rows, 4 * head_width),
        "expert",
        split_axis=0,
        concat_axis=0,
        tiled=True,
    )
    sent = jnp.concatenate(
        [d_rows.astype(BF).reshape(n_expert, slots, model_width), gains_two], axis=1
    )
    got = lax.all_to_all(sent, "expert", split_axis=0, concat_axis=0, tiled=True)
    got_rows = got[:, :slots].reshape(n_expert * slots, model_width)

    def scatter_step(k, carry):
        d_far, ids_far, total = carry
        here = ids_far // vocab_rows == own_shard
        local = jnp.where(here, ids_far % vocab_rows, 0)
        d_sum = d_far[0].astype(F32) + d_far[1].astype(F32)
        total = total.at[local].add(jnp.where(here[:, None], d_sum, 0.0))
        ring = [(j, (j + 1) % n_expert) for j in range(n_expert)]
        return lax.ppermute(d_far, "expert", ring), lax.ppermute(ids_far, "expert", ring), total

    d_base = lax.fori_loop(
        0,
        jnp.where(any_overflow, n_expert, 0),
        scatter_step,
        ((d_high, d_low), ids, d_base),
    )[2]
    g_table, table_squares = finish(d_base, asked_rows, got_rows, vocab_rows)
    g_attn = jnp.sum(attn_got.astype(F32), axis=0)
    g_attn_in = g_attn[:, : 3 * head_width].reshape(own_rows, 3, head_width)
    g_attn_out = g_attn[:, 3 * head_width :]
    g_gains = jnp.sum(got[:, slots : slots + 2, : 3 * own_rows].astype(F32), axis=(0, 1))
    g_gains = g_gains.reshape(3, own_rows).T
    g_expert = d_w[0] + w_near[1] + w_far.astype(F32)
    g_expert_in = g_expert[0][None]
    g_expert_out = g_expert[1][None]

    squares = (
        jnp.sum(table_squares)
        + jnp.sum(g_attn * g_attn)
        + jnp.sum(g_expert * g_expert)
        + jnp.sum(g_gains * g_gains) / n_hidden
    )
    both_sums = jnp.stack([squares, loss_part * (2.0 / n_hidden)])
    both_sums = jnp.broadcast_to(jnp.pad(both_sums, (0, 126))[None], (n_expert, 128))
    both_sums = lax.all_to_all(both_sums, "expert", split_axis=0, concat_axis=0, tiled=True)
    both_sums = lax.all_gather(jnp.sum(both_sums, axis=0), "hidden", axis=0)
    both_sums = jnp.sum(both_sums, axis=0)
    clip_norm = jnp.sqrt(both_sums[0])
    loss_value = both_sums[1]
    clip_scale = jnp.minimum(1.0, CLIP_AT / clip_norm)
    table_up = adam_step(
        embed_table, embed_first, embed_second, g_table * clip_scale, RATE_MATRIX, DECAY
    )
    attn_in_up = adam_step(
        attn_in, attn_in_first, attn_in_second, g_attn_in * clip_scale, RATE_MATRIX, DECAY
    )
    attn_out_up = adam_step(
        attn_out, attn_out_first, attn_out_second, g_attn_out * clip_scale, RATE_MATRIX, DECAY
    )
    expert_in_up = adam_step(
        expert_in, expert_in_first, expert_in_second, g_expert_in * clip_scale, RATE_MATRIX, DECAY
    )
    expert_out_up = adam_step(
        expert_out,
        expert_out_first,
        expert_out_second,
        g_expert_out * clip_scale,
        RATE_MATRIX,
        DECAY,
    )
    gains_up = adam_step(
        norm_gains, gains_first, gains_second, g_gains * clip_scale, RATE_GAIN, 0.0
    )
    return (
        loss_value,
        clip_norm,
        *table_up,
        *attn_in_up,
        *attn_out_up,
        *expert_in_up,
        *expert_out_up,
        *gains_up,
    )


def solution(mesh):
    rows = P("expert", None)
    table = P(("expert", "hidden"), None)
    wide = P("expert", None, "hidden")
    flat = P("expert", "hidden")
    tall = P("expert", "hidden", None)
    groups = (table, wide, flat, wide, tall, rows)
    each = tuple(spec for spec in groups for _ in range(3))
    return jax.shard_map(
        on_device,
        mesh=mesh,
        in_specs=(rows, rows, rows, P(), *each),
        out_specs=(P(), P(), *each),
        check_vma=False,
    )
```

time: 937 us -> 747 us (0.80)
  waiting for transfers between devices: 240 us -> 139 us
  local copies, waits for them, and re-layouts: 133 us -> 54.5 us
  Pallas kernels: 181 us -> 252 us
  matrix products: 96.3 us -> 47.7 us
  other arithmetic: 127 us -> 81.9 us
  blocking collectives: 48.3 us -> 72 us
    pallas_call x11 -> x21, Pallas kernels: 181 us -> 252 us  [the longest x3 55.5 us: head_back(): pl.pallas_call(head_back_kernel, grid=(steps,), in_specs=[pl.BlockSpec((w...]
    ppermute x39 -> x43, waiting for transfers between devices: 145 us -> 95 us  [flip(): lax.ppermute(x, axis, [(j, j ^ k) for j in range(lax.axis_size(axis))])]
    dot_general x39 -> x20, matrix products: 96.3 us -> 47.7 us  [dot(): lax.dot_general(a, b, (((ca,), (cb,)), ((), ())), preferred_element_type=...]
    all_gather x1, waiting for transfers between devices: 53.9 us -> 11.8 us  [on_device(): packed = lax.all_gather(packed, 'expert', axis=1, tiled=True)]
    concatenate x6 -> x0, local copies, waits for them, and re-layouts: 33.4 us -> none  [the longest x2 28.9 us: on_device(): table = jnp.concatenate([slice_two, flip(slice_two, 'hidden', 1)])]
    all_to_all x1 -> x2, blocking collectives: 21.9 us -> 42.7 us  [from_expert(): lax.all_to_all(rows_in, 'expert', split_axis=0, concat_axis=0, tiled=True)]
    reduce_sum x6 -> x2, other arithmetic: 23 us -> 2.75 us  [the longest x1 1.46 us: on_device(): g_attn = jnp.sum(attn_got.astype(F32), axis=0)]
    slice x19 -> x14, local copies, waits for them, and re-layouts: 28 us -> 8.82 us  [the longest x3 3.21 us: on_device(): one[fourth:]]
  transfers between devices with their start and end apart: 46 -> 54, of which waited for: 21 -> 26; matrix products, arithmetic and copies ran while one was open for 25% -> 17% of each run, Pallas kernels for 15% -> 24%
where the time goes in v2:
time: 747 us; the launch traced here: 736 us
  Pallas kernels  252 us (34%)
  waiting for transfers between devices  139 us (19%)
  other arithmetic  81.9 us (11%)
  blocking collectives  72 us (10%)
  starting transfers between devices  64.6 us (9%)
  local copies, waits for them, and re-layouts  54.5 us (7%)
  matrix products  47.7 us (6%)
  between operations  24.5 us (3%)
    ppermute x43, waiting for transfers between devices, flip(): lax.ppermute(x, axis, [(j, j ^ k) for j in range(lax.axis_size(axis))])  95 us
    pallas_call x3, Pallas kernels, head_back(): pl.pallas_call(head_back_kernel, grid=(steps,), in_specs=[pl.BlockSpec((w...  55.5 us
    dot_general x20, matrix products, dot(): lax.dot_general(a, b, (((ca,), (cb,)), ((), ())), preferred_element_type=...  47.7 us
    all_to_all x2, blocking collectives, from_expert(): lax.all_to_all(rows_in, 'expert', split_axis=0, concat_axis=0, tiled=True)  42.7 us
    pallas_call x2, Pallas kernels, head_logits(): pl.pallas_call(partial(logits_kernel, real), grid=(steps,), in_specs=[pl....  36.9 us
    pallas_call x2, Pallas kernels, table_grad(): pl.pallas_call(partial(table_grad_kernel, len(ds)), grid=(padded // part,...  31 us
    ppermute x43, starting transfers between devices, flip(): lax.ppermute(x, axis, [(j, j ^ k) for j in range(lax.axis_size(axis))])  28.6 us
    pallas_call x1, Pallas kernels, attend_back(): pl.pallas_call(attend_back_kernel, in_specs=[WHOLE] * 5 + [ANY] * len(rea...  26.3 us
  transfers between devices with their start and end apart: 54, of which 26 were waited for; matrix products, arithmetic and copies ran while one was open for 17% of the time, Pallas kernels for 24%

profile of v2, /device:TPU:0, one launch (start us, length us, event | category | flops | bytes accessed | tf_op | source)
XLA Modules:
  0.0 736.1 jit_solution(5616242061125051467)
XLA Ops:
  12.6 7.3 all-to-all-start
  21.3 4.9 all-to-all-done
  43.8 6.7 cast_pick.1
  55.8 6.1 gather_fusion
  71.4 10.5 %collective-permute-done.4 = bf16[320,768]{1,0:T(8,128)(2,1)} collective-permute-done((bf16[320,768]{1,0:T(8,128)(2,1)S(1)}, bf16[320,768]{1,0:T(8,128)(2,1)}, u32[]{:S(2)}, u32[]{:S(2)}) %collective-permute-start.4) | collective-permute-done | bytes 491552 | tf_op jit(solution)/shard_map/ppermute | solution.py:31
  84.2 11.8 %all-gather.11.cloned.1.call-done = bf16[2,768,896]{2,0,1:T(2,128)(2,1)} async-done(((bf16[2,96,896]{2,0,1:T(2,128)(2,1)}), bf16[2,768,896]{2,0,1:T(2,128)(2,1)}) %all-gather.11.cloned.1.call-update) | async-done | bytes 2752528 | tf_op jit(solution)/shard_map/all_gather | solution.py:834
  98.4 7.4 %pick_norm.3 = (f32[1024,768]{1,0:T(8,128)}, bf16[1024,768]{1,0:T(8,128)(2,1)}) custom-call(s32[1024,1]{1,0:T(8,128)} %get-tuple-element.549.refs_0_, bf16[320,768]{1,0:T(8,128)(2,1)S(1)} %get-tuple-element.329.refs_1_, bf16[320,768]{1,0:T(8,128)(2,1)} %get-tuple-element.330.refs_2_, bf16[320,768]{1,0:T(8,128)(2,1)} %get-tuple-element.331.refs_3_, ...), custom_call_target="tpu_custom_call" | custom-call | flops 1024 | bytes 1024 | tf_op jit(solution)/shard_map/pick_norm/pallas_call | solution.py:295
  109.8 14.7 %attend.1 = (bf16[2,1024,576]{2,1,0:T(8,128)(2,1)}, bf16[2,1024,192]{2,1,0:T(8,128)(2,1)}, f32[1024,768]{1,0:T(8,128)}) custom-call(bf16[1024,768]{1,0:T(8,128)(2,1)} %get-tuple-element.334.rows_ref, bf16[2,768,896]{2,1,0:T(8,128)(2,1)} %copy.208.w_ref, s32[1,1024]{1,0:T(1,128)} %segr_ref.3, s32[1024,1]{1,0:T(8,128)} %copy.209.segc_ref), custom_call_target="tpu_custom_call" | custom-call | flops 1024 | bytes 1024 | tf_op jit(solution)/shard_map/attend/pallas_call | solution.py:145
  130.5 6.4 pick_norm.4
  144.4 8.8 %all-gather.17.cloned.1.call-start = ((), (), s32[]{:S(2)}) async-start(), calls=%async_computation.12 | async-start | bytes 7372800 | tf_op jit(solution)/shard_map/all_gather | solution.py:40
  153.2 6.2 all-gather.13.cloned.1.call-done
  187.1 22.7 %all_to_all.78 = bf16[8,48,768]{2,1,0:T(8,128)(2,1)} all-to-all(bf16[8,48,768]{2,1,0:T(8,128)(2,1)S(1)} %bitcast.308), channel_id=1, replica_groups=mesh['expert'=8,'hidden'=4] {'expert'}, dimensions={0} | all-to-all | bytes 1179648 | tf_op jit(solution)/shard_map/all_to_all | solution.py:886
  210.3 13.9 %collective-permute-done.11.refs_2_ = bf16[384,768]{1,0:T(8,128)(2,1)} collective-permute-done((bf16[384,768]{1,0:T(8,128)(2,1)}, bf16[384,768]{1,0:T(8,128)(2,1)}, u32[]{:S(2)}, u32[]{:S(2)}) %collective-permute-start.11) | collective-permute-done | bytes 589856 | tf_op jit(solution)/shard_map/ppermute | solution.py:31
  230.4 7.9 %pick_norm.5 = (f32[1024,768]{1,0:T(8,128)}, bf16[1024,768]{1,0:T(8,128)(2,1)}) custom-call(s32[1024,1]{1,0:T(8,128)} %fusion.49.refs_0_, bf16[384,768]{1,0:T(8,128)(2,1)} %bitcast.37.refs_1_, bf16[384,768]{1,0:T(8,128)(2,1)} %collective-permute-done.11.refs_2_, bf16[384,768]{1,0:T(8,128)(2,1)} %collective-permute-done.12.refs_3_, ...), custom_call_target="tpu_custom_call" | custom-call | flops 1024 | bytes 1024 | tf_op jit(solution)/shard_map/pick_norm/pallas_call | solution.py:295
  250.5 6.9 collective-permute-done.16
  262.3 5.8 collective-permute-done.17
  271.2 10.3 %turned.1.rest_0_.table_ref = bf16[768,6400]{1,0:T(8,128)(2,1)} custom-call(bf16[1600,768]{1,0:T(8,128)(2,1)} %get-tuple-element.714.a_ref, bf16[1600,768]{1,0:T(8,128)(2,1)} %dynamic-slice_bitcast_fusion.b_ref, bf16[1600,768]{1,0:T(8,128)(2,1)} %collective-permute-done.14.c_ref, bf16[1600,768]{1,0:T(8,128)(2,1)} %collective-permute-done.15.d_ref), custom_call_target="tpu_custom_call" | custom-call | bytes 29491200 | tf_op jit(solution)/shard_map/turned/pallas_call | solution.py:491
  281.5 18.5 %head_logits.2 = (f32[6400,1024]{1,0:T(8,128)}, f32[160,1024]{1,0:T(8,128)}, f32[8,1024]{1,0:T(8,128)}) custom-call(bf16[1600,768]{1,0:T(8,128)(2,1)} %get-tuple-element.714.a_ref, bf16[1600,768]{1,0:T(8,128)(2,1)} %dynamic-slice_bitcast_fusion.b_ref, bf16[1600,768]{1,0:T(8,128)(2,1)} %collective-permute-done.14.c_ref, ...), custom_call_target="tpu_custom_call" | custom-call | flops 20132659200 | bytes 26214400 | tf_op jit(solution)/shard_map/head_logits/pallas_call | solution.py:552
  305.5 9.2 %collective-permute-done.22 = bf16[256,768]{1,0:T(8,128)(2,1)S(1)} collective-permute-done((bf16[256,768]{1,0:T(8,128)(2,1)S(1)}, bf16[256,768]{1,0:T(8,128)(2,1)S(1)}, u32[]{:S(2)}, u32[]{:S(2)}) %collective-permute-start.22) | collective-permute-done | bytes 393248 | tf_op jit(solution)/shard_map/ppermute | solution.py:31
  314.7 5.9 collective-permute-done.20
  321.8 18.5 %head_logits.3 = (f32[6400,1024]{1,0:T(8,128)}, f32[160,1024]{1,0:T(8,128)}, f32[8,1024]{1,0:T(8,128)}) custom-call(bf16[1600,768]{1,0:T(8,128)(2,1)} %get-tuple-element.714.a_ref, bf16[1600,768]{1,0:T(8,128)(2,1)} %dynamic-slice_bitcast_fusion.b_ref, bf16[1600,768]{1,0:T(8,128)(2,1)} %collective-permute-done.14.c_ref, ...), custom_call_target="tpu_custom_call" | custom-call | flops 20132659200 | bytes 26214400 | tf_op jit(solution)/shard_map/head_logits/pallas_call | solution.py:552
  353.3 24.9 %head_back.3 = (bf16[6400,1024]{1,0:T(8,128)(2,1)}, bf16[1024,768]{1,0:T(8,128)(2,1)}) custom-call(bf16[768,6400]{1,0:T(8,128)(2,1)} %turned.1.rest_0_.table_ref, f32[6400,1024]{1,0:T(8,128)} %get-tuple-element.344.power_ref, f32[160,1024]{1,0:T(8,128)} %get-tuple-element.345.peak_ref, s32[1,1024]{1,0:T(1,128)} %pad_add_fusion.1.col_ref, ...), custom_call_target="tpu_custom_call" | custom-call | flops 20132659200 | bytes 39321600 | tf_op jit(solution)/shard_map/head_back/pallas_call | solution.py:614
  382.2 15.4 %head_back.5 = (bf16[6400,512]{1,0:T(8,128)(2,1)}, bf16[512,768]{1,0:T(8,128)(2,1)}) custom-call(bf16[768,6400]{1,0:T(8,128)(2,1)} %turned.1.rest_0_.table_ref, f32[6400,1024]{1,0:T(8,128)} %get-tuple-element.340.power_ref, f32[160,1024]{1,0:T(8,128)} %get-tuple-element.341.peak_ref, s32[1,512]{1,0:T(1,128)} %copy-done.55, f32[8,512]{1,0:T(8,128)} %get-tuple-element.588.side_ref), custom_call_target="tpu_custom_call" | custom-call | flops 10066329600 | bytes 19660800 | tf_op jit(solution)/shard_map/head_back/pallas_call | solution.py:614
  401.8 4.7 collective-permute-done.31
  406.9 15.2 %head_back.4 = (bf16[6400,512]{1,0:T(8,128)(2,1)}, bf16[512,768]{1,0:T(8,128)(2,1)}) custom-call(bf16[768,6400]{1,0:T(8,128)(2,1)} %turned.1.rest_0_.table_ref, f32[6400,1024]{1,0:T(8,128)} %get-tuple-element.340.power_ref, f32[160,1024]{1,0:T(8,128)} %get-tuple-element.341.peak_ref, s32[1,512]{1,0:T(1,128)} %copy-done.54, ...), custom_call_target="tpu_custom_call" | custom-call | flops 10066329600 | bytes 19660800 | tf_op jit(solution)/shard_map/head_back/pallas_call | solution.py:614
  423.7 6.0 collective-permute-done.34
  432.8 7.3 collective-permute-done.36.refs_2_
  442.7 6.0 norm_back.3
  448.7 15.5 %table_grad.2 = (f32[1600,768]{1,0:T(8,128)}, f32[1600,768]{1,0:T(8,128)}) custom-call(bf16[6400,512]{1,0:T(8,128)(2,1)} %get-tuple-element.350.refs_0_.refs_1_, bf16[6400,512]{1,0:T(8,128)(2,1)} %get-tuple-element.350.refs_0_.refs_1_, bf16[6400,512]{1,0:T(8,128)(2,1)} %get-tuple-element.351.refs_2_.refs_3_, ...), custom_call_target="tpu_custom_call" | custom-call | flops 10066329600 | bytes 9830400 | tf_op jit(solution)/shard_map/table_grad/pallas_call | solution.py:659
  465.5 24.0 %all_to_all.79 = bf16[8,48,768]{2,1,0:T(8,128)(2,1)S(1)} all-to-all(bf16[8,48,768]{2,1,0:T(8,128)(2,1)S(1)} %bitcast.307), channel_id=1, replica_groups=mesh['expert'=8,'hidden'=4] {'expert'}, dimensions={0} | all-to-all | bytes 1179648 | tf_op jit(solution)/shard_map/all_to_all | solution.py:883
  494.7 10.4 %expert_back.1 = (bf16[384,768]{1,0:T(8,128)(2,1)}, bf16[384,768]{1,0:T(8,128)(2,1)}, bf16[384,768]{1,0:T(8,128)(2,1)}, bf16[384,768]{1,0:T(8,128)(2,1)}, bf16[384,768]{1,0:T(8,128)(2,1)}) custom-call(bf16[384,768]{1,0:T(8,128)(2,1)} %bitcast.284, bf16[2,768,768]{2,1,0:T(8,128)(2,1)} %pad_maximum_fusion.2.refs_0_, ...), custom_call_target="tpu_custom_call" | custom-call | flops 1024 | bytes 1024 | tf_op jit(solution)/shard_map/expert_back/pallas_call | solution.py:421
  509.6 20.0 %all_to_all.80 = bf16[8,48,768]{2,1,0:T(8,128)(2,1)S(1)} all-to-all(bf16[8,48,768]{2,1,0:T(8,128)(2,1)S(1)} %bitcast.294), channel_id=1, replica_groups=mesh['expert'=8,'hidden'=4] {'expert'}, dimensions={0} | all-to-all | bytes 1179648 | tf_op jit(solution)/shard_map/all_to_all | solution.py:886
  534.1 9.6 %collective-permute-done.40.refs_2_ = bf16[384,768]{1,0:T(8,128)(2,1)S(1)} collective-permute-done((bf16[384,768]{1,0:T(8,128)(2,1)S(1)}, bf16[384,768]{1,0:T(8,128)(2,1)S(1)}, u32[]{:S(2)}, u32[]{:S(2)}) %collective-permute-start.40) | collective-permute-done | bytes 589856 | tf_op jit(solution)/shard_map/ppermute | solution.py:31
  543.7 15.5 %table_grad.3 = (f32[1600,768]{1,0:T(8,128)}, f32[1600,768]{1,0:T(8,128)}) custom-call(bf16[6400,512]{1,0:T(8,128)(2,1)} %get-tuple-element.350.refs_0_.refs_1_, bf16[6400,512]{1,0:T(8,128)(2,1)} %get-tuple-element.350.refs_0_.refs_1_, bf16[6400,512]{1,0:T(8,128)(2,1)} %get-tuple-element.351.refs_2_.refs_3_, ...), custom_call_target="tpu_custom_call" | custom-call | flops 10066329600 | bytes 9830400 | tf_op jit(solution)/shard_map/table_grad/pallas_call | solution.py:659
  560.5 9.4 %norm_back.4 = (f32[1,768]{1,0:T(1,128)}, bf16[1024,768]{1,0:T(8,128)(2,1)}, f32[1024,768]{1,0:T(8,128)}) custom-call(f32[1024,768]{1,0:T(8,128)} %get-tuple-element.336.refs_5_.x_ref, f32[1,768]{1,0:T(1,128)} %get-tuple-element.573.refs_3_.gain_ref, s32[1024,1]{1,0:T(8,128)} %fusion.49.refs_0_, bf16[384,768]{1,0:T(8,128)(2,1)} %bitcast.293, ...), custom_call_target="tpu_custom_call" | custom-call | flops 1024 | bytes 1024 | tf_op jit(solution)/shard_map/norm_back/pallas_call | solution.py:366
  569.9 4.5 fusion.16.rest_0_
  574.4 26.3 %attend_back.1 = (bf16[2,1024,576]{2,1,0:T(8,128)(2,1)}, f32[1024,768]{1,0:T(8,128)}) custom-call(bf16[1024,768]{1,0:T(8,128)(2,1)} %get-tuple-element.357.branch_ref, bf16[2,768,896]{2,1,0:T(8,128)(2,1)} %copy.208.w_ref, bf16[2,1024,576]{2,1,0:T(8,128)(2,1)} %get-tuple-element.358.qkv_ref, s32[1,1024]{1,0:T(1,128)} %segr_ref.3, s32[1024,1]{1,0:T(8,128)} %copy.209.segc_ref, ...), custom_call_target="tpu_custom_call" | custom-call | flops 1024 | bytes 1024 | tf_op jit(solution)/shard_map/attend_back/pallas_call | solution.py:209
  608.4 8.4 %norm_back.5 = (f32[1,768]{1,0:T(1,128)}, bf16[1024,768]{1,0:T(8,128)(2,1)}, bf16[1024,768]{1,0:T(8,128)(2,1)}) custom-call(f32[1024,768]{1,0:T(8,128)} %get-tuple-element.333.refs_2_.x_ref, f32[1,768]{1,0:T(1,128)} %get-tuple-element.574.refs_5_.gain_ref, f32[1024,768]{1,0:T(8,128)} %get-tuple-element.361.refs_0_, ...), custom_call_target="tpu_custom_call" | custom-call | flops 1024 | bytes 1024 | tf_op jit(solution)/shard_map/norm_back/pallas_call | solution.py:366
  631.5 7.6 %convert_add_fusion = f32[1600,768]{1,0:T(8,128)} fusion(f32[1600,768]{1,0:T(8,128)} %get-tuple-element.365, f32[1600,768]{1,0:T(8,128)} %collective-permute-done.45, bf16[2,1600,768]{2,1,0:T(8,128)(2,1)} %bitcast.297, s32[]{:T(128)S(6)} %select_n.541), kind=kLoop, calls=%fused_computation.29 | loop fusion | flops 3686400 | bytes 17203204 | tf_op jit(solution)/shard_map/add | solution.py:1013
  639.1 5.3 attn_grad.1
  645.4 5.0 all-to-all-start.7
  651.2 7.6 %finish.1 = (f32[1572,768]{1,0:T(8,128)}, f32[1,768]{1,0:T(1,128)}) custom-call(f32[1600,768]{1,0:T(8,128)} %get-tuple-element.367.base_ref, s32[1,320]{1,0:T(1,128)} %select_n.543.place_ref, bf16[320,768]{1,0:T(8,128)(2,1)} %bitcast.295), custom_call_target="tpu_custom_call" | custom-call | flops 1024 | bytes 1024 | tf_op jit(solution)/shard_map/finish/pallas_call | solution.py:701
  662.2 6.4 all-gather.19.cloned.1.call-done
  668.6 7.7 %multiply_reduce_fusion = (f32[]{:T(128)}, f32[2,768,768]{2,1,0:T(8,128)}) fusion(bf16[2,2,768,768]{3,2,1,0:T(8,128)(2,1)} %bitcast.304, s32[]{:T(128)S(6)} %select_n.502, f32[2,768,768]{2,1,0:T(8,128)} %collective-permute-done.46, f32[1,768,768]{2,1,0:T(8,128)S(1)} %copy-done.9, f32[1,768,768]{2,1,0:T(8,128)} %convolution_bitcast_fusion.3), kind=kLoop, calls=%fused_computation.40 | loop fusion | flops 7077887 | bytes 16515080 | tf_op jit(solution)/shard_map/reduce_sum | solution.py:1087
  687.7 5.9 all-to-all-done.8
  693.6 5.3 all-gather.4
  704.4 13.7 %multiply_subtract_fusion = (f32[1572,768]{1,0:T(8,128)}, f32[1572,768]{1,0:T(8,128)}, f32[1572,768]{1,0:T(8,128)}) fusion(f32[1572,768]{1,0:T(8,128)} %x_ref.1, f32[1572,768]{1,0:T(8,128)} %get-tuple-element.376, f32[]{:T(128)S(6)} %min.3, f32[1572,768]{1,0:T(8,128)} %param.32, f32[1572,768]{1,0:T(8,128)} %param.33), kind=kLoop, calls=%fused_computation.32 | loop fusion | flops 19316736 | bytes 33804292 | tf_op jit(solution)/shard_map/sub | solution.py:728
  721.6 6.4 multiply_subtract_fusion.1
  (409 shorter events, 207.3 us)
Async XLA Ops:
  12.6 13.6 %all-to-all-start = ((s32[8,1,128]{2,1,0:T(1,128)}), s32[8,1,128]{2,1,0:T(1,128)S(1)}, u32[]{:S(2)}, u32[]{:S(2)}) async-start(s32[8,1,128]{2,1,0:T(1,128)} %bitcast.5), calls=%async_computation | async-start | bytes 8192 | tf_op jit(solution)/shard_map/all_to_all | solution.py:812
  19.9 76.1 %all-gather.11.cloned.1.call-start = ((), (), s32[]{:S(2)}) async-start(), calls=%async_computation.9 | async-start | bytes 3096576 | tf_op jit(solution)/shard_map/all_gather | solution.py:834
  37.7 121.7 %all-gather.13.cloned.1.call-start = ((), (), s32[]{:S(2)}) async-start(), calls=%async_computation.10 | async-start | bytes 7077888 | tf_op jit(solution)/shard_map/all_gather | solution.py:40
  50.5 18.7 %all-to-all-start.1 = ((bf16[8,40,768]{2,1,0:T(8,128)(2,1)}), bf16[8,40,768]{2,1,0:T(8,128)(2,1)S(1)}, u32[]{:S(2)}, u32[]{:S(2)}) async-start(bf16[8,40,768]{2,1,0:T(8,128)(2,1)} %bitcast.310), calls=%async_computation.1 | async-start | bytes 983040 | tf_op jit(solution)/shard_map/all_to_all | solution.py:843
  69.2 12.7 %collective-permute-start.4 = (bf16[320,768]{1,0:T(8,128)(2,1)S(1)}, bf16[320,768]{1,0:T(8,128)(2,1)}, u32[]{:S(2)}, u32[]{:S(2)}) collective-permute-start(bf16[320,768]{1,0:T(8,128)(2,1)S(1)} %bitcast.270), channel_id=1, source_target_pairs={{0,2},{1,3},{2,0},{3,1},{4,6},{5,7},{6,4},{7,5},{8,10},{9,11},{10,... | collective-permute-start | bytes 1474568 | tf_op jit(solution)/shard_map/ppermute | solution.py:31
  71.4 27.0 %collective-permute-start.5 = (bf16[320,768]{1,0:T(8,128)(2,1)S(1)}, bf16[320,768]{1,0:T(8,128)(2,1)}, u32[]{:S(2)}, u32[]{:S(2)}) collective-permute-start(bf16[320,768]{1,0:T(8,128)(2,1)S(1)} %bitcast.271), channel_id=1, source_target_pairs={{0,1},{1,0},{2,3},{3,2},{4,5},{5,4},{6,7},{7,6},{8,9},{9,8},{10,11... | collective-permute-start | bytes 1474568 | tf_op jit(solution)/shard_map/ppermute | solution.py:31
  81.9 16.5 %collective-permute-start.6 = (bf16[320,768]{1,0:T(8,128)(2,1)}, bf16[320,768]{1,0:T(8,128)(2,1)}, u32[]{:S(2)}, u32[]{:S(2)}) collective-permute-start(bf16[320,768]{1,0:T(8,128)(2,1)} %collective-permute-done.4), channel_id=1, source_target_pairs={{0,1},{1,0},{2,3},{3,2},{4,5},{5,4},{6,7},{7,6},{8,9},{9,8},{10,11... | collective-permute-start | bytes 1474568 | tf_op jit(solution)/shard_map/ppermute | solution.py:31
  124.5 6.0 collective-permute-start.8
  127.9 34.8 %collective-permute-start.9 = (bf16[2,768,768]{2,1,0:T(8,128)(2,1)}, bf16[2,768,768]{2,1,0:T(8,128)(2,1)}, u32[]{:S(2)}, u32[]{:S(2)}) collective-permute-start(bf16[2,768,768]{2,1,0:T(8,128)(2,1)} %pad_maximum_fusion.2.refs_0_), channel_id=1, source_target_pairs={{0,1},{1,0},{2,3},{3,2},{4,5},{5,4},{6,7},{7,6},{8,9},{9,8},{10,11... | collective-permute-start | bytes 7077896 | tf_op jit(solution)/shard_map/ppermute | solution.py:31
  139.9 22.8 %all-to-all-start.2 = ((bf16[8,48,768]{2,1,0:T(8,128)(2,1)}), bf16[8,48,768]{2,1,0:T(8,128)(2,1)S(1)}, u32[]{:S(2)}, u32[]{:S(2)}) async-start(bf16[8,48,768]{2,1,0:T(8,128)(2,1)} %bitcast.306), calls=%async_computation.2 | async-start | bytes 1179648 | tf_op jit(solution)/shard_map/all_to_all | solution.py:883
  143.7 97.1 %all-gather.15.cloned.1.call-start = ((), (), s32[]{:S(2)}) async-start(), calls=%async_computation.11 | async-start | bytes 7372800 | tf_op jit(solution)/shard_map/all_gather | solution.py:40
  144.4 487.0 %all-gather.17.cloned.1.call-start = ((), (), s32[]{:S(2)}) async-start(), calls=%async_computation.12 | async-start | bytes 7372800 | tf_op jit(solution)/shard_map/all_gather | solution.py:40
  162.7 16.5 %collective-permute-start.10 = (bf16[2,768,768]{2,1,0:T(8,128)(2,1)}, bf16[2,768,768]{2,1,0:T(8,128)(2,1)}, u32[]{:S(2)}, u32[]{:S(2)}) collective-permute-start(bf16[2,768,768]{2,1,0:T(8,128)(2,1)} %dynamic-slice_bitcast_fusion.1.refs_1_), channel_id=1, source_target_pairs={{0,1},{1,0},{2,3},{3,2},{4,5},{5,4},{6,7},{7,6},{8,9},{9,8},{10,11... | collective-permute-start | bytes 7077896 | tf_op jit(solution)/shard_map/ppermute | solution.py:31
  209.8 14.4 %collective-permute-start.11 = (bf16[384,768]{1,0:T(8,128)(2,1)}, bf16[384,768]{1,0:T(8,128)(2,1)}, u32[]{:S(2)}, u32[]{:S(2)}) collective-permute-start(bf16[384,768]{1,0:T(8,128)(2,1)} %bitcast.37.refs_1_), channel_id=1, source_target_pairs={{0,2},{1,3},{2,0},{3,1},{4,6},{5,7},{6,4},{7,5},{8,10},{9,11},{10,... | collective-permute-start | bytes 1769480 | tf_op jit(solution)/shard_map/ppermute | solution.py:31
  210.3 20.1 %collective-permute-start.12 = (bf16[384,768]{1,0:T(8,128)(2,1)}, bf16[384,768]{1,0:T(8,128)(2,1)}, u32[]{:S(2)}, u32[]{:S(2)}) collective-permute-start(bf16[384,768]{1,0:T(8,128)(2,1)} %bitcast.37.refs_1_), channel_id=1, source_target_pairs={{0,1},{1,0},{2,3},{3,2},{4,5},{5,4},{6,7},{7,6},{8,9},{9,8},{10,11... | collective-permute-start | bytes 1769480 | tf_op jit(solution)/shard_map/ppermute | solution.py:31
  224.2 6.2 collective-permute-start.13
  224.2 47.0 %collective-permute-start.14 = (bf16[1600,768]{1,0:T(8,128)(2,1)S(1)}, bf16[1600,768]{1,0:T(8,128)(2,1)}, u32[]{:S(2)}, u32[]{:S(2)}) collective-permute-start(bf16[1600,768]{1,0:T(8,128)(2,1)S(1)} %copy-done.2), channel_id=1, source_target_pairs={{0,1},{1,0},{2,3},{3,2},{4,5},{5,4},{6,7},{7,6},{8,9},{9,8},{10,11... | collective-permute-start | bytes 7372808 | tf_op jit(solution)/shard_map/ppermute | solution.py:31
  244.1 27.1 %collective-permute-start.15 = (bf16[1600,768]{1,0:T(8,128)(2,1)}, bf16[1600,768]{1,0:T(8,128)(2,1)}, u32[]{:S(2)}, u32[]{:S(2)}) collective-permute-start(bf16[1600,768]{1,0:T(8,128)(2,1)} %dynamic-slice_bitcast_fusion.b_ref), channel_id=1, source_target_pairs={{0,1},{1,0},{2,3},{3,2},{4,5},{5,4},{6,7},{7,6},{8,9},{9,8},{10,11... | collective-permute-start | bytes 7372808 | tf_op jit(solution)/shard_map/ppermute | solution.py:31
  245.8 11.6 %collective-permute-start.16 = (bf16[256,768]{1,0:T(8,128)(2,1)S(1)}, bf16[256,768]{1,0:T(8,128)(2,1)S(1)}, u32[]{:S(2)}, u32[]{:S(2)}) collective-permute-start(bf16[256,768]{1,0:T(8,128)(2,1)S(1)} %get-tuple-element.546), channel_id=1, source_target_pairs={{0,8},{4,12},{8,0},{12,4},{16,24},{20,28},{24,16},{28,20},{1,9},{5... | collective-permute-start | bytes 1179656 | tf_op jit(solution)/shard_map/ppermute | solution.py:31
  247.2 10.7 %collective-permute-start.18 = (f32[2,512]{1,0:T(2,128)S(1)}, f32[2,512]{1,0:T(2,128)S(1)}, u32[]{:S(2)}, u32[]{:S(2)}) collective-permute-start(f32[2,512]{1,0:T(2,128)S(1)} %pad_maximum_fusion.15), channel_id=1, source_target_pairs={{0,8},{4,12},{8,0},{12,4},{16,24},{20,28},{24,16},{28,20},{1,9},{5... | collective-permute-start | bytes 12296 | tf_op jit(solution)/shard_map/ppermute | solution.py:31
  248.1 12.3 %collective-permute-start.24 = (f32[2,512]{1,0:T(2,128)S(1)}, f32[2,512]{1,0:T(2,128)S(1)}, u32[]{:S(2)}, u32[]{:S(2)}) collective-permute-start(f32[2,512]{1,0:T(2,128)S(1)} %pad_maximum_fusion.15), channel_id=1, source_target_pairs={{0,24},{4,28},{8,16},{12,20},{16,8},{20,12},{24,0},{28,4},{1,25},{... | collective-permute-start | bytes 12296 | tf_op jit(solution)/shard_map/ppermute | solution.py:31
  257.5 10.7 %collective-permute-start.17 = (bf16[256,768]{1,0:T(8,128)(2,1)S(1)}, bf16[256,768]{1,0:T(8,128)(2,1)S(1)}, u32[]{:S(2)}, u32[]{:S(2)}) collective-permute-start(bf16[256,768]{1,0:T(8,128)(2,1)S(1)} %collective-permute-done.16), channel_id=1, source_target_pairs={{0,2},{1,3},{2,0},{3,1},{4,6},{5,7},{6,4},{7,5},{8,10},{9,11},{10,... | collective-permute-start | bytes 1179656 | tf_op jit(solution)/shard_map/ppermute | solution.py:31
  258.6 46.2 %collective-permute-start.23 = (f32[2,512]{1,0:T(2,128)S(1)}, f32[2,512]{1,0:T(2,128)S(1)}, u32[]{:S(2)}, u32[]{:S(2)}) collective-permute-start(f32[2,512]{1,0:T(2,128)S(1)} %pad_maximum_fusion.15), channel_id=1, source_target_pairs={{0,16},{4,20},{8,24},{12,28},{16,0},{20,4},{24,8},{28,12},{1,17},{... | collective-permute-start | bytes 12296 | tf_op jit(solution)/shard_map/ppermute | solution.py:31
  260.5 42.0 %collective-permute-start.21 = (bf16[256,768]{1,0:T(8,128)(2,1)S(1)}, bf16[256,768]{1,0:T(8,128)(2,1)S(1)}, u32[]{:S(2)}, u32[]{:S(2)}) collective-permute-start(bf16[256,768]{1,0:T(8,128)(2,1)S(1)} %get-tuple-element.546), channel_id=1, source_target_pairs={{0,24},{4,28},{8,16},{12,20},{16,8},{20,12},{24,0},{28,4},{1,25},{... | collective-permute-start | bytes 1179656 | tf_op jit(solution)/shard_map/ppermute | solution.py:31
  269.4 33.7 %collective-permute-start.19 = (bf16[256,768]{1,0:T(8,128)(2,1)S(1)}, bf16[256,768]{1,0:T(8,128)(2,1)S(1)}, u32[]{:S(2)}, u32[]{:S(2)}) collective-permute-start(bf16[256,768]{1,0:T(8,128)(2,1)S(1)} %get-tuple-element.546), channel_id=1, source_target_pairs={{0,16},{4,20},{8,24},{12,28},{16,0},{20,4},{24,8},{28,12},{1,17},{... | collective-permute-start | bytes 1179656 | tf_op jit(solution)/shard_map/ppermute | solution.py:31
  302.6 12.1 %collective-permute-start.22 = (bf16[256,768]{1,0:T(8,128)(2,1)S(1)}, bf16[256,768]{1,0:T(8,128)(2,1)S(1)}, u32[]{:S(2)}, u32[]{:S(2)}) collective-permute-start(bf16[256,768]{1,0:T(8,128)(2,1)S(1)} %broadcast_select_fusion), channel_id=1, source_target_pairs={{0,2},{1,3},{2,0},{3,1},{4,6},{5,7},{6,4},{7,5},{8,10},{9,11},{10,... | collective-permute-start | bytes 1179656 | tf_op jit(solution)/shard_map/ppermute | solution.py:31
  303.2 17.4 %collective-permute-start.20 = (bf16[256,768]{1,0:T(8,128)(2,1)S(1)}, bf16[256,768]{1,0:T(8,128)(2,1)S(1)}, u32[]{:S(2)}, u32[]{:S(2)}) collective-permute-start(bf16[256,768]{1,0:T(8,128)(2,1)S(1)} %broadcast_select_fusion.1), channel_id=1, source_target_pairs={{0,2},{1,3},{2,0},{3,1},{4,6},{5,7},{6,4},{7,5},{8,10},{9,11},{10,... | collective-permute-start | bytes 1179656 | tf_op jit(solution)/shard_map/ppermute | solution.py:31
  379.4 19.7 %collective-permute-start.33 = (bf16[256,768]{1,0:T(8,128)(2,1)S(1)}, bf16[256,768]{1,0:T(8,128)(2,1)S(1)}, u32[]{:S(2)}, u32[]{:S(2)}) collective-permute-start(bf16[256,768]{1,0:T(8,128)(2,1)S(1)} %get-tuple-element.543), channel_id=1, source_target_pairs={{0,2},{1,3},{2,0},{3,1},{4,6},{5,7},{6,4},{7,5},{8,10},{9,11},{10,... | collective-permute-start | bytes 1179656 | tf_op jit(solution)/shard_map/ppermute | solution.py:31
  379.9 19.2 %collective-permute-start.29 = (bf16[256,768]{1,0:T(8,128)(2,1)S(1)}, bf16[256,768]{1,0:T(8,128)(2,1)S(1)}, u32[]{:S(2)}, u32[]{:S(2)}) collective-permute-start(bf16[256,768]{1,0:T(8,128)(2,1)S(1)} %get-tuple-element.544), channel_id=1, source_target_pairs={{0,2},{1,3},{2,0},{3,1},{4,6},{5,7},{6,4},{7,5},{8,10},{9,11},{10,... | collective-permute-start | bytes 1179656 | tf_op jit(solution)/shard_map/ppermute | solution.py:31
  398.6 7.8 %collective-permute-start.31 = (bf16[256,768]{1,0:T(8,128)(2,1)S(1)}, bf16[256,768]{1,0:T(8,128)(2,1)S(1)}, u32[]{:S(2)}, u32[]{:S(2)}) collective-permute-start(bf16[256,768]{1,0:T(8,128)(2,1)S(1)} %slice.356), channel_id=1, source_target_pairs={{0,2},{1,3},{2,0},{3,1},{4,6},{5,7},{6,4},{7,5},{8,10},{9,11},{10,... | collective-permute-start | bytes 1179656 | tf_op jit(solution)/shard_map/ppermute | solution.py:31
  399.3 24.3 %collective-permute-start.35 = (bf16[256,768]{1,0:T(8,128)(2,1)S(1)}, bf16[256,768]{1,0:T(8,128)(2,1)S(1)}, u32[]{:S(2)}, u32[]{:S(2)}) collective-permute-start(bf16[256,768]{1,0:T(8,128)(2,1)S(1)} %get-tuple-element.542.rest_0_), channel_id=1, source_target_pairs={{0,24},{4,28},{8,16},{12,20},{16,8},{20,12},{24,0},{28,4},{1,25},{... | collective-permute-start | bytes 1179656 | tf_op jit(solution)/shard_map/ppermute | solution.py:31
  401.8 27.9 %collective-permute-start.34 = (bf16[256,768]{1,0:T(8,128)(2,1)S(1)}, bf16[256,768]{1,0:T(8,128)(2,1)S(1)}, u32[]{:S(2)}, u32[]{:S(2)}) collective-permute-start(bf16[256,768]{1,0:T(8,128)(2,1)S(1)} %get-tuple-element.541), channel_id=1, source_target_pairs={{0,16},{4,20},{8,24},{12,28},{16,0},{20,4},{24,8},{28,12},{1,17},{... | collective-permute-start | bytes 1179656 | tf_op jit(solution)/shard_map/ppermute | solution.py:31
  406.5 23.1 %collective-permute-start.32 = (bf16[256,768]{1,0:T(8,128)(2,1)S(1)}, bf16[256,768]{1,0:T(8,128)(2,1)S(1)}, u32[]{:S(2)}, u32[]{:S(2)}) collective-permute-start(bf16[256,768]{1,0:T(8,128)(2,1)S(1)} %add_convert_fusion.3), channel_id=1, source_target_pairs={{0,8},{4,12},{8,0},{12,4},{16,24},{20,28},{24,16},{28,20},{1,9},{5... | collective-permute-start | bytes 1179656 | tf_op jit(solution)/shard_map/ppermute | solution.py:31
  423.1 7.8 %collective-permute-start.30 = (bf16[256,768]{1,0:T(8,128)(2,1)S(1)}, bf16[256,768]{1,0:T(8,128)(2,1)S(1)}, u32[]{:S(2)}, u32[]{:S(2)}) collective-permute-start(bf16[256,768]{1,0:T(8,128)(2,1)S(1)} %slice.352), channel_id=1, source_target_pairs={{0,2},{1,3},{2,0},{3,1},{4,6},{5,7},{6,4},{7,5},{8,10},{9,11},{10,... | collective-permute-start | bytes 1179656 | tf_op jit(solution)/shard_map/ppermute | solution.py:31
  432.3 7.8 %collective-permute-start.36 = (bf16[256,768]{1,0:T(8,128)(2,1)S(1)}, bf16[256,768]{1,0:T(8,128)(2,1)S(1)}, u32[]{:S(2)}, u32[]{:S(2)}) collective-permute-start(bf16[256,768]{1,0:T(8,128)(2,1)S(1)} %add_convert_fusion.1.refs_1_), channel_id=1, source_target_pairs={{0,2},{1,3},{2,0},{3,1},{4,6},{5,7},{6,4},{7,5},{8,10},{9,11},{10,... | collective-permute-start | bytes 1179656 | tf_op jit(solution)/shard_map/ppermute | solution.py:31
  432.8 8.9 %collective-permute-start.37 = (bf16[256,768]{1,0:T(8,128)(2,1)S(1)}, bf16[256,768]{1,0:T(8,128)(2,1)S(1)}, u32[]{:S(2)}, u32[]{:S(2)}) collective-permute-start(bf16[256,768]{1,0:T(8,128)(2,1)S(1)} %add_convert_fusion.1.refs_1_), channel_id=1, source_target_pairs={{0,1},{1,0},{2,3},{3,2},{4,5},{5,4},{6,7},{7,6},{8,9},{9,8},{10,11... | collective-permute-start | bytes 1179656 | tf_op jit(solution)/shard_map/ppermute | solution.py:31
  464.2 28.5 %collective-permute-start.39 = (f32[1600,768]{1,0:T(8,128)}, f32[1600,768]{1,0:T(8,128)S(1)}, u32[]{:S(2)}, u32[]{:S(2)}) collective-permute-start(f32[1600,768]{1,0:T(8,128)} %get-tuple-element.354), channel_id=1, source_target_pairs={{0,1},{1,0},{2,3},{3,2},{4,5},{5,4},{6,7},{7,6},{8,9},{9,8},{10,11... | collective-permute-start | bytes 14745608 | tf_op jit(solution)/shard_map/ppermute | solution.py:31
  509.6 60.2 %collective-permute-start.43 = (f32[2,768,768]{2,1,0:T(8,128)}, f32[2,768,768]{2,1,0:T(8,128)}, u32[]{:S(2)}, u32[]{:S(2)}) collective-permute-start(f32[2,768,768]{2,1,0:T(8,128)} %pad_maximum_fusion), channel_id=1, source_target_pairs={{0,1},{1,0},{2,3},{3,2},{4,5},{5,4},{6,7},{7,6},{8,9},{9,8},{10,11... | collective-permute-start | bytes 14155784 | tf_op jit(solution)/shard_map/ppermute | solution.py:31
  529.6 14.1 %collective-permute-start.40 = (bf16[384,768]{1,0:T(8,128)(2,1)S(1)}, bf16[384,768]{1,0:T(8,128)(2,1)S(1)}, u32[]{:S(2)}, u32[]{:S(2)}) collective-permute-start(bf16[384,768]{1,0:T(8,128)(2,1)S(1)} %bitcast.291), channel_id=1, source_target_pairs={{0,2},{1,3},{2,0},{3,1},{4,6},{5,7},{6,4},{7,5},{8,10},{9,11},{10,... | collective-permute-start | bytes 1769480 | tf_op jit(solution)/shard_map/ppermute | solution.py:31
  529.7 138.9 %all-gather.19.cloned.1.call-start = ((), (), s32[]{:S(2)}) async-start(), calls=%async_computation.13 | async-start | bytes 7077888 | tf_op jit(solution)/shard_map/all_gather | solution.py:40
  534.0 26.5 %collective-permute-start.41 = (bf16[384,768]{1,0:T(8,128)(2,1)S(1)}, bf16[384,768]{1,0:T(8,128)(2,1)}, u32[]{:S(2)}, u32[]{:S(2)}) collective-permute-start(bf16[384,768]{1,0:T(8,128)(2,1)S(1)} %bitcast.292), channel_id=1, source_target_pairs={{0,1},{1,0},{2,3},{3,2},{4,5},{5,4},{6,7},{7,6},{8,9},{9,8},{10,11... | collective-permute-start | bytes 1769480 | tf_op jit(solution)/shard_map/ppermute | solution.py:31
  543.7 16.8 %collective-permute-start.42 = (bf16[384,768]{1,0:T(8,128)(2,1)S(1)}, bf16[384,768]{1,0:T(8,128)(2,1)}, u32[]{:S(2)}, u32[]{:S(2)}) collective-permute-start(bf16[384,768]{1,0:T(8,128)(2,1)S(1)} %collective-permute-done.40.refs_2_), channel_id=1, source_target_pairs={{0,1},{1,0},{2,3},{3,2},{4,5},{5,4},{6,7},{7,6},{8,9},{9,8},{10,11... | collective-permute-start | bytes 1769480 | tf_op jit(solution)/shard_map/ppermute | solution.py:31
  559.3 72.2 %collective-permute-start.45 = (f32[1600,768]{1,0:T(8,128)}, f32[1600,768]{1,0:T(8,128)}, u32[]{:S(2)}, u32[]{:S(2)}) collective-permute-start(f32[1600,768]{1,0:T(8,128)} %get-tuple-element.366), channel_id=1, source_target_pairs={{0,1},{1,0},{2,3},{3,2},{4,5},{5,4},{6,7},{7,6},{8,9},{9,8},{10,11... | collective-permute-start | bytes 14745608 | tf_op jit(solution)/shard_map/ppermute | solution.py:31
  600.7 7.6 %collective-permute-start.44 = (f32[1024,768]{1,0:T(8,128)}, f32[1024,768]{1,0:T(8,128)}, u32[]{:S(2)}, u32[]{:S(2)}) collective-permute-start(f32[1024,768]{1,0:T(8,128)} %get-tuple-element.361.refs_0_), channel_id=1, source_target_pairs={{0,1},{1,0},{2,3},{3,2},{4,5},{5,4},{6,7},{7,6},{8,9},{9,8},{10,11... | collective-permute-start | bytes 9437192 | tf_op jit(solution)/shard_map/ppermute | solution.py:31
  606.7 55.5 %collective-permute-start.46 = (f32[2,768,768]{2,1,0:T(8,128)}, f32[2,768,768]{2,1,0:T(8,128)}, u32[]{:S(2)}, u32[]{:S(2)}) collective-permute-start(f32[2,768,768]{2,1,0:T(8,128)} %pad_maximum_fusion.1), channel_id=1, source_target_pairs={{0,1},{1,0},{2,3},{3,2},{4,5},{5,4},{6,7},{7,6},{8,9},{9,8},{10,11... | collective-permute-start | bytes 14155784 | tf_op jit(solution)/shard_map/ppermute | solution.py:31
  623.0 22.4 %all-to-all-start.6 = ((bf16[8,56,768]{2,1,0:T(8,128)(2,1)}), bf16[8,56,768]{2,1,0:T(8,128)(2,1)S(1)}, u32[]{:S(2)}, u32[]{:S(2)}) async-start(bf16[8,56,768]{2,1,0:T(8,128)(2,1)} %fusion.38), calls=%async_computation.6 | async-start | bytes 1376256 | tf_op jit(solution)/shard_map/all_to_all | solution.py:1056
  645.4 33.5 %all-to-all-start.7 = ((bf16[8,96,768]{2,1,0:T(8,128)(2,1)}), bf16[8,96,768]{2,1,0:T(8,128)(2,1)}, u32[]{:S(2)}, u32[]{:S(2)}) async-start(bf16[8,96,768]{2,1,0:T(8,128)(2,1)} %bitcast.290), calls=%async_computation.7 | async-start | bytes 2359296 | tf_op jit(solution)/shard_map/all_to_all | solution.py:1046
  683.6 10.0 %all-to-all-start.8 = ((f32[8,1,128]{2,1,0:T(1,128)}), f32[8,1,128]{2,1,0:T(1,128)S(1)}, u32[]{:S(2)}, u32[]{:S(2)}) async-start(f32[8,1,128]{2,1,0:T(1,128)} %broadcast_in_dim.129), calls=%async_computation.8 | async-start | bytes 8192 | tf_op jit(solution)/shard_map/all_to_all | solution.py:1092
  (77 other events, 781.4 us)
Sparse Core Ops, SparseCore 0:
  37.9 58.1 all-gather.10
  98.1 61.3 all-gather.12
  161.0 71.1 all-gather.14
  529.8 63.8 all-gather.16
  607.2 61.3 all-gather.18

commit v3 on v2

--- a/solution.py
+++ b/solution.py
@@ -41,11 +41,13 @@
     upper = (lax.axis_index(axis) // k) % 2
     if after is not None:
         upper = behind(upper, after)
-    return lax.dynamic_index_in_dim(both, 1 - upper, 0, keepdims=False)
-
-
-def hidden_gather(x):
+    return lax.dynamic_index_in_dim(both, 1 - upper, 0, keepdims=False), both
+
+
+def hidden_gather(x, after=None):
     far = flip(x, "hidden", 2)
+    if after is not None:
+        far = behind(far, after)
     return [x, far, flip(x, "hidden", 1), flip(far, "hidden", 1)]
 
 
@@ -85,32 +87,29 @@
     return jnp.where(seen & (first == second), 0.0, NEVER)
 
 
-def pack_kernel(in_ref, out_ref, gains_ref, *rest):
+def pack_kernel(in_ref, out_ref, *rest):
     o_ref = rest[-1]
-    o_ref[...] = jnp.zeros_like(o_ref)
     width = out_ref.shape[1]
     for c in range(3):
         o_ref[:, c * width : (c + 1) * width] = in_ref[c].astype(BF)
-    wide = round_up(3 * width, 128)
-    o_ref[:, wide : wide + width] = out_ref[...].astype(BF)
-    o_ref[:, wide + width : wide + width + 3] = gains_ref[...].astype(BF)
-
-
-def pack(attn_in, attn_out, gains, ready):
+    o_ref[:, 3 * width :] = out_ref[...].astype(BF)
+
+
+def pack(attn_in, attn_out, ready):
     rows, width = attn_out.shape
     return pl.pallas_call(
         pack_kernel,
-        in_specs=[WHOLE] * 3 + [ANY] * len(ready),
+        in_specs=[WHOLE] * 2 + [ANY] * len(ready),
         out_specs=WHOLE,
-        out_shape=jax.ShapeDtypeStruct((rows, round_up(round_up(3 * width, 128) + width + 3, 128)), BF),
+        out_shape=jax.ShapeDtypeStruct((rows, 4 * width), BF),
         name="pack",
-    )(attn_in.transpose(1, 0, 2), attn_out, gains, *ready)
+    )(attn_in.transpose(1, 0, 2), attn_out, *ready)
 
 
 def attend_kernel(rows_ref, w_ref, segr_ref, segc_ref, *rest):
     qkv_ref, o_ref, part_ref = rest[-3:]
     pieces, seq, width = o_ref.shape
-    wide = round_up(3 * width, 128)
+    wide = 3 * width
     factor = jnp.asarray(HD**-0.5, BF)
     heads = [(p, c) for p in range(pieces) for c in range(0, width, HD)]
     for p in range(pieces):
@@ -160,7 +159,7 @@
 def attend_back_kernel(branch_ref, w_ref, qkv_ref, segr_ref, segc_ref, *rest):
     d_ref, part_ref, g_ref, dk_acc, dv_acc = rest[-5:]
     pieces, seq, width = g_ref.shape
-    wide = round_up(3 * width, 128)
+    wide = 3 * width
     scale = HD**-0.5
     factor = jnp.asarray(scale, BF)
     heads = [(p, c) for p in range(pieces) for c in range(0, width, HD)]
@@ -404,6 +403,34 @@
     return x * below, below + x * jnp.exp(-square) * 0.3989422804014327
 
 
+def expert_kernel(rows_ref, *refs):
+    w_refs, out_ref, active_refs, slope_refs = refs[:4], refs[4], refs[5:9], refs[9:]
+    rows = rows_ref[...]
+    total = None
+    for w_ref, active_ref, slope_ref in zip(w_refs, active_refs, slope_refs, strict=True):
+        value, slope_ref[...] = gelu_and_slope(dot(rows, w_ref[0]))
+        active = value.astype(BF)
+        active_ref[...] = active
+        product = dot(active, w_ref[1])
+        total = product if total is None else total + product
+    out_ref[...] = total.astype(BF)
+
+
+def expert(rows, weights):
+    hidden = jax.ShapeDtypeStruct((rows.shape[0], weights[0].shape[2]), BF)
+    slope = jax.ShapeDtypeStruct(hidden.shape, F32)
+    out, *rest = pl.pallas_call(
+        expert_kernel,
+        in_specs=[WHOLE] * 5,
+        out_specs=[WHOLE] * 9,
+        out_shape=[jax.ShapeDtypeStruct(rows.shape, BF)] + [hidden] * 4 + [slope] * 4,
+        compiler_params=pltpu.CompilerParams(vmem_limit_bytes=VMEM),
+        cost_estimate=SHORT,
+        name="expert",
+    )(rows, *weights)
+    return out, rest[:4], rest[4:]
+
+
 def expert_back_kernel(grad_ref, *refs):
     w_refs, slope_refs, refs = refs[:4], refs[4:8], refs[8:]
     out_ref, d_refs = refs[-5], refs[-4:]
@@ -646,7 +673,7 @@
         total = product if total is None else total + product
     part = out_refs[0].shape[0]
     for q in range(2):
-        out_refs[q][...] = total[q * part : (q + 1) * part]
+        out_refs[q][...] = total[q * part : (q + 1) * part].astype(out_refs[q].dtype)
 
 
 def table_grad(ds, rows, padded, which, ready):
@@ -663,7 +690,7 @@
         + [pl.BlockSpec(r.shape, lambda j: (0, 0)) for r in rows]
         + [ANY] * len(ready),
         out_specs=[pl.BlockSpec((part, width), lambda j: (j, 0))] * 2,
-        out_shape=[jax.ShapeDtypeStruct((padded, width), F32)] * 2,
+        out_shape=[jax.ShapeDtypeStruct((padded, width), t) for t in (F32, BF)],
         compiler_params=pltpu.CompilerParams(vmem_limit_bytes=VMEM),
         cost_estimate=pl.CostEstimate(
             flops=4 * padded * width * sum(d.shape[1] for d in ds),
@@ -801,17 +828,22 @@
         ),
         axis=1,
     )
+    own_gains = norm_gains.astype(BF).astype(F32).T.reshape(1, 3 * own_rows)
+    own_gains = jnp.pad(own_gains, ((0, 0), (0, round_up(3 * own_rows, 128) - 3 * own_rows)))
     asked = jnp.concatenate(
         [
-            wanted.reshape(n_expert, slots),
-            jnp.broadcast_to(overflow.astype(jnp.int32), (n_expert, 128 - slots)),
+            wanted.reshape(n_expert, slots).astype(F32),
+            jnp.broadcast_to(overflow.astype(F32), (n_expert, 128 - slots)),
+            jnp.broadcast_to(own_gains, (n_expert, own_gains.shape[1])),
         ],
         axis=1,
     )
 
     asked = lax.all_to_all(asked, "expert", split_axis=0, concat_axis=0, tiled=True)
-    any_overflow = jnp.max(asked[:, slots:]) > 0
-    asked_rows = asked[:, :slots].reshape(n_expert * slots)
+    any_overflow = jnp.max(asked[:, slots:128]) > 0
+    asked_rows = asked[:, :slots].astype(jnp.int32).reshape(n_expert * slots)
+    gain_full = asked[:, 128 : 128 + 3 * own_rows].reshape(n_expert, 3, own_rows)
+    gain_full = gain_full.transpose(1, 0, 2).reshape(3, model_width)
 
     capacity = 3 * tok_count // (2 * n_expert)
     quarter = capacity // n_hidden
@@ -828,13 +860,10 @@
 
     asked_rows = jnp.where(any_overflow, -1, asked_rows)
     table_own, answer = cast_pick(asked_rows, embed_table, padded)
-    wide = round_up(3 * head_width, 128)
-    packed = pack(attn_in, attn_out, norm_gains, (asked_rows,))
+    packed = pack(attn_in, attn_out, (asked_rows,))
     packed = jnp.stack([packed, flip(packed, "hidden", 2)])
     packed = lax.all_gather(packed, "expert", axis=1, tiled=True)
-    gain_full = packed[0, :, wide + head_width : wide + head_width + 3].astype(F32).T
     weights_own = jnp.stack([expert_in[0], expert_out[0]]).astype(BF)
-    weights_y = far_flip(weights_own, "hidden", 2)
 
     n_all = n_expert * n_hidden
     own_shard = e_index * n_hidden + h_index
@@ -878,34 +907,32 @@
 
     fill_hot = hot_rows(fill_place, rows_dev)
 
-    def to_expert(rows_in):
+    def to_expert(rows_in, after=None):
         block = dot(fill_hot, rows_in).astype(BF)
+        if after is not None:
+            block = behind(block, after)
         return lax.all_to_all(block, "expert", split_axis=0, concat_axis=0, tiled=True)
 
-    def from_expert(rows_in):
+    def from_expert(rows_in, after=None):
         block = lax.all_to_all(rows_in, "expert", split_axis=0, concat_axis=0, tiled=True)
-        return hidden_gather(block.reshape(rows_dev, model_width))
-
+        return hidden_gather(block.reshape(rows_dev, model_width), after)
+
+    received = to_expert(normed_two)
+    weights_y, _ = far_flip(weights_own, "hidden", 2, received[0, 0])
     expert_w = [
         weights_own,
         weights_y,
         flip(weights_own, "hidden", 1),
         flip(weights_y, "hidden", 1),
     ]
-    received = to_expert(normed_two)
-    active, slope = [None] * 4, [None] * 4
-    expert_sum = 0.0
-    for p in (0, 2, 1, 3):
-        value, slope[p] = gelu_and_slope(dot(received, expert_w[p][0]))
-        active[p] = value.astype(BF)
-        expert_sum = expert_sum + dot(active[p], expert_w[p][1])
+    expert_result, active, slope = expert(received, expert_w)
     after_moe, final_rows = pick_norm(
-        (pick_place, *from_expert(expert_sum.astype(BF))),
+        (pick_place, *from_expert(expert_result)),
         after_attn,
         gain_full[2:3],
     )
 
-    slice_x = far_flip(table_own, "expert", 1, final_rows[0, 0])
+    slice_x, _ = far_flip(table_own, "expert", 1, final_rows[0, 0])
     slices = [table_own, slice_x, flip(table_own, "hidden", 1), flip(slice_x, "hidden", 1)]
     table_t = turned(slices)
     part = part_rows(padded)
@@ -942,18 +969,18 @@
         row_of = target % vocab_rows
         column = (row_of // part) * (4 * part) + (away_e + 2 * away_h) * part + row_of % part
         columns.append(jnp.where(mine, column, -1)[None, :])
-    head_rows = [jnp.concatenate([own_part, other_part])]
+    head_rows, onward = [jnp.concatenate([own_part, other_part])], []
     powers, stats = [], []
+    for k, far in enumerate(far_rows, 1):
+        onward.append(behind(far, table_t[0, 0].astype(F32)) if k > 1 else far)
+        head_rows.append(jnp.concatenate([onward[-1], flip(onward[-1], "hidden", 2)]))
     for k in range(0, n_far, 2):
-        for far in far_rows[max(k - 1, 0) : k + 1]:
-            far = behind(far, stats[-1][0, 0]) if stats else far
-            head_rows.append(jnp.concatenate([far, flip(far, "hidden", 2)]))
         one, two, stat = head_logits(
             slices,
             jnp.concatenate(head_rows[k : k + 2]),
             jnp.concatenate(columns[k : k + 2], axis=1),
             vocab_rows,
-            () if k else (table_t,),
+            () if k else (table_t, *onward[1:]),
         )
         powers.append((one, two))
         stats += [stat[:3, :half], stat[:3, half:]]
@@ -991,7 +1018,8 @@
                 gathered = flip(on_y[-1], "expert", 2 * k).astype(F32)
             d_parts[k] = gathered
     d_quarter = sum(d_parts)
-    d_four = hidden_gather(d_quarter.astype(BF))
+    d_quarter = d_quarter.astype(BF)
+    d_four = hidden_gather(d_quarter)
     quarter_h = jnp.array([0, 2, 1, 3], jnp.int32)
 
     d_gain_three, d_result, d_after_moe = norm_back(
@@ -1001,30 +1029,30 @@
         pick="blocks",
     )
     d_across = table_grad(d_logits, group_rows, padded, (1, 3), (d_result,))
-    across_x = (d_across[0] + flip(d_across[1], "hidden", 1)).astype(BF)
-    grad_in = to_expert(d_result)
-    d_received, *d_pre = expert_back(grad_in, expert_w, slope, (across_x,))
+    across_x = (d_across[0] + flip(d_across[1], "hidden", 1).astype(F32)).astype(BF)
+    grad_in = to_expert(d_result, across_x[0, 0].astype(F32))
+    d_received, *d_pre = expert_back(grad_in, expert_w, slope, ())
     d_w = [
         jnp.stack([dot(received, d_pre[p], 0, 0), dot(active[p], grad_in, 0, 0)]) for p in range(4)
     ]
     d_same = table_grad(d_logits, group_rows, padded, (0, 2), (d_received,))
 
-    d_base = (
-        d_same[0] + flip(d_same[1], "hidden", 1) + far_flip(across_x, "expert", 1).astype(F32)
-    )
+    base_x, both_x = far_flip(across_x, "expert", 1)
+    d_base = d_same[0] + flip(d_same[1], "hidden", 1).astype(F32) + base_x.astype(F32)
 
     w_near = flip(d_w[3], "hidden", 1), flip(d_w[2], "hidden", 1)
     w_sent = (d_w[1] + w_near[0]).astype(BF)
-    w_far = far_flip(w_sent, "hidden", 2)
+    w_far, _ = far_flip(w_sent, "hidden", 2)
     d_gain_two, d_branch, d_after_attn = norm_back(
         after_attn,
         gain_full[1:2],
-        (pick_place, *from_expert(d_received)),
+        (pick_place, *from_expert(d_received, d_same[0][0, 0])),
         d_after_moe,
         pick="rows",
-    )
-
-    d_qkv, d_norm_part = attend_back(d_branch, packed, qkv, segment, (w_sent,))
+        ready=(w_sent,),
+    )
+
+    d_qkv, d_norm_part = attend_back(d_branch, packed, qkv, segment, (both_x,))
     d_gain_one, d_high, d_low = norm_back(
         embedded,
         gain_full[0:1],
@@ -1105,7 +1133,12 @@
         attn_out, attn_out_first, attn_out_second, g_attn_out * clip_scale, RATE_MATRIX, DECAY
     )
     expert_in_up = adam_step(
-        expert_in, expert_in_first, expert_in_second, g_expert_in * clip_scale, RATE_MATRIX, DECAY
+        expert_in,
+        expert_in_first,
+        expert_in_second,
+        g_expert_in * clip_scale,
+        RATE_MATRIX,
+        DECAY,
     )
     expert_out_up = adam_step(
         expert_out,

time: 747 us -> 732 us (0.980)
  matrix products: 47.7 us -> 20.2 us
  Pallas kernels: 252 us -> 265 us
  starting transfers between devices: 64.6 us -> 52.8 us
  blocking collectives: 72 us -> 82.5 us
  other arithmetic: 81.9 us -> 89.4 us
    dot_general x20 -> x12, matrix products: 47.7 us -> 20.2 us  [dot(): lax.dot_general(a, b, (((ca,), (cb,)), ((), ())), preferred_element_type=...]
    ppermute x43, waiting for transfers between devices: 95 us -> 79 us  [flip(): lax.ppermute(x, axis, [(j, j ^ k) for j in range(lax.axis_size(axis))])]
    all_gather x4, waiting for transfers between devices: 12.7 us -> 27.7 us  [far_flip(): both = lax.all_gather(x, axis, axis_index_groups=pairs)]
    pallas_call x1 -> x2, Pallas kernels: 1.81 us -> 16.6 us  [the longest x1 14.7 us: expert(): pl.pallas_call(expert_kernel, in_specs=[WHOLE] * 5, out_specs=[WHOLE] * 9...]
    all_to_all x0 -> x1, blocking collectives: none -> 13.6 us  [on_device(): lax.all_to_all(asked, 'expert', split_axis=0, concat_axis=0, tiled=True)]
    all_to_all x1, waiting for transfers between devices: 0.01 us -> 11.2 us  [to_expert(): lax.all_to_all(block, 'expert', split_axis=0, concat_axis=0, tiled=True)]
    all_gather x1, waiting for transfers between devices: 11.8 us -> 0.79 us  [on_device(): packed = lax.all_gather(packed, 'expert', axis=1, tiled=True)]
    all_gather x4, starting transfers between devices: 8.9 us -> 0.17 us  [far_flip(): both = lax.all_gather(x, axis, axis_index_groups=pairs)]
  transfers between devices with their start and end apart: 54 -> 53, of which waited for: 26 -> 27; matrix products, arithmetic and copies ran while one was open for 17% -> 13% of each run, Pallas kernels for 24% -> 23%
where the time goes in v3:
time: 732 us; the launch traced here: 721 us
  Pallas kernels  265 us (36%)
  waiting for transfers between devices  132 us (18%)
  other arithmetic  89.4 us (12%)
  blocking collectives  82.5 us (11%)
  starting transfers between devices  52.8 us (7%)
  local copies, waits for them, and re-layouts  50.4 us (7%)
  between operations  28.4 us (4%)
  matrix products  20.2 us (3%)
    ppermute x43, waiting for transfers between devices, flip(): lax.ppermute(x, axis, [(j, j ^ k) for j in range(lax.axis_size(axis))])  79 us
    pallas_call x3, Pallas kernels, head_back(): pl.pallas_call(head_back_kernel, grid=(steps,), in_specs=[pl.BlockSpec((w...  55.2 us
    all_to_all x2, blocking collectives, from_expert(): lax.all_to_all(rows_in, 'expert', split_axis=0, concat_axis=0, tiled=True)  42.3 us
    pallas_call x2, Pallas kernels, head_logits(): pl.pallas_call(partial(logits_kernel, real), grid=(steps,), in_specs=[pl....  36.9 us
    ppermute x43, starting transfers between devices, flip(): lax.ppermute(x, axis, [(j, j ^ k) for j in range(lax.axis_size(axis))])  33.1 us
    pallas_call x2, Pallas kernels, table_grad(): pl.pallas_call(partial(table_grad_kernel, len(ds)), grid=(padded // part,...  30.4 us
    all_gather x4, waiting for transfers between devices, far_flip(): both = lax.all_gather(x, axis, axis_index_groups=pairs)  27.7 us
    pallas_call x1, Pallas kernels, attend_back(): pl.pallas_call(attend_back_kernel, in_specs=[WHOLE] * 5 + [ANY] * len(rea...  26.3 us
  transfers between devices with their start and end apart: 53, of which 27 were waited for; matrix products, arithmetic and copies ran while one was open for 13% of the time, Pallas kernels for 23%

profile of v3, /device:TPU:0, one launch (start us, length us, event | category | flops | bytes accessed | tf_op | source)
XLA Modules:
  0.0 721.3 jit_solution(5235343328980422171)
XLA Ops:
  13.0 13.6 %all_to_all.77 = f32[8,1,512]{2,1,0:T(1,128)S(1)} all-to-all(f32[8,1,512]{2,1,0:T(1,128)S(1)} %all_to_all.49), channel_id=1, replica_groups=mesh['expert'=8,'hidden'=4] {'expert'}, dimensions={0} | all-to-all | bytes 32768 | tf_op jit(solution)/shard_map/all_to_all | solution.py:842
  42.3 6.8 cast_pick.1
  58.0 6.1 gather_fusion
  72.3 7.9 %collective-permute-done.4 = bf16[320,768]{1,0:T(8,128)(2,1)} collective-permute-done((bf16[320,768]{1,0:T(8,128)(2,1)S(1)}, bf16[320,768]{1,0:T(8,128)(2,1)}, u32[]{:S(2)}, u32[]{:S(2)}) %collective-permute-start.4) | collective-permute-done | bytes 491552 | tf_op jit(solution)/shard_map/ppermute | solution.py:31
  84.0 7.1 pick_norm.3
  91.9 14.4 %attend.1 = (bf16[2,1024,576]{2,1,0:T(8,128)(2,1)}, bf16[2,1024,192]{2,1,0:T(8,128)(2,1)}, f32[1024,768]{1,0:T(8,128)}) custom-call(bf16[1024,768]{1,0:T(8,128)(2,1)} %get-tuple-element.343.rows_ref, bf16[2,768,768]{2,1,0:T(8,128)(2,1)} %all-gather.11.cloned.1.call-done.w_ref, s32[1,1024]{1,0:T(1,128)} %segr_ref.3, s32[1024,1]{1,0:T(8,128)} %copy.181.segc_ref), custom_call_target="tpu_custom_call" | custom-call | flops 1024 | bytes 1024 | tf_op jit(solution)/shard_map/attend/pallas_call | solution.py:144
  106.9 5.2 collective-permute-done.8.refs_1_
  113.8 6.6 pick_norm.4
  132.3 11.2 %all-to-all-done.2 = bf16[8,48,768]{2,1,0:T(8,128)(2,1)S(1)} async-done(((bf16[8,48,768]{2,1,0:T(8,128)(2,1)}), bf16[8,48,768]{2,1,0:T(8,128)(2,1)S(1)}, u32[]{:S(2)}, u32[]{:S(2)}) %all-to-all-start.2) | async-done | bytes 589856 | tf_op jit(solution)/shard_map/all_to_all | solution.py:914
  145.3 9.9 %all-gather.13.cloned.1.call-done = bf16[2,2,768,768]{3,2,1,0:T(8,128)(2,1)} async-done(((bf16[1,2,768,768]{3,2,1,0:T(8,128)(2,1)}), bf16[2,2,768,768]{3,2,1,0:T(8,128)(2,1)}) %all-gather.13.cloned.1.call-update) | async-done | bytes 4718608 | tf_op jit(solution)/shard_map/all_gather | solution.py:40
  157.2 4.5 collective-permute-done.10.refs_3_
  163.1 14.7 %expert.1 = (bf16[384,768]{1,0:T(8,128)(2,1)}, bf16[384,768]{1,0:T(8,128)(2,1)}, bf16[384,768]{1,0:T(8,128)(2,1)}, bf16[384,768]{1,0:T(8,128)(2,1)}, bf16[384,76...) custom-call(bf16[384,768]{1,0:T(8,128)(2,1)} %bitcast.242, ...), custom_call_target="tpu_custom_call" | custom-call | flops 1024 | bytes 1024 | tf_op jit(solution)/shard_map/expert/pallas_call | solution.py:422
  177.8 22.9 %all_to_all.78 = bf16[8,48,768]{2,1,0:T(8,128)(2,1)S(1)} all-to-all(bf16[8,48,768]{2,1,0:T(8,128)(2,1)} %bitcast.274), channel_id=1, replica_groups=mesh['expert'=8,'hidden'=4] {'expert'}, dimensions={0} | all-to-all | bytes 1179648 | tf_op jit(solution)/shard_map/all_to_all | solution.py:917
  201.3 13.2 %collective-permute-done.11.refs_2_ = bf16[384,768]{1,0:T(8,128)(2,1)} collective-permute-done((bf16[384,768]{1,0:T(8,128)(2,1)S(1)}, bf16[384,768]{1,0:T(8,128)(2,1)}, u32[]{:S(2)}, u32[]{:S(2)}) %collective-permute-start.11) | collective-permute-done | bytes 589856 | tf_op jit(solution)/shard_map/ppermute | solution.py:31
  221.4 7.9 %pick_norm.5 = (f32[1024,768]{1,0:T(8,128)}, bf16[1024,768]{1,0:T(8,128)(2,1)}) custom-call(s32[1024,1]{1,0:T(8,128)} %fusion.42.refs_0_, bf16[384,768]{1,0:T(8,128)(2,1)} %bitcast.259, bf16[384,768]{1,0:T(8,128)(2,1)} %collective-permute-done.11.refs_2_, bf16[384,768]{1,0:T(8,128)(2,1)} %collective-permute-done.12.refs_3_, ...), custom_call_target="tpu_custom_call" | custom-call | flops 1024 | bytes 1024 | tf_op jit(solution)/shard_map/pick_norm/pallas_call | solution.py:294
  244.3 6.8 collective-permute-done.16
  256.0 5.2 collective-permute-done.17
  262.5 10.3 %turned.1.rest_0_.table_ref = bf16[768,6400]{1,0:T(8,128)(2,1)} custom-call(bf16[1600,768]{1,0:T(8,128)(2,1)} %get-tuple-element.724.a_ref, bf16[1600,768]{1,0:T(8,128)(2,1)} %dynamic-slice_bitcast_fusion.b_ref, bf16[1600,768]{1,0:T(8,128)(2,1)} %collective-permute-done.14.c_ref, bf16[1600,768]{1,0:T(8,128)(2,1)} %collective-permute-done.15.d_ref), custom_call_target="tpu_custom_call" | custom-call | bytes 29491200 | tf_op jit(solution)/shard_map/turned/pallas_call | solution.py:518
  279.7 18.5 %head_logits.2 = (f32[6400,1024]{1,0:T(8,128)}, f32[160,1024]{1,0:T(8,128)}, f32[8,1024]{1,0:T(8,128)}) custom-call(bf16[1600,768]{1,0:T(8,128)(2,1)} %get-tuple-element.724.a_ref, bf16[1600,768]{1,0:T(8,128)(2,1)} %dynamic-slice_bitcast_fusion.b_ref, bf16[1600,768]{1,0:T(8,128)(2,1)} %collective-permute-done.14.c_ref, ...), custom_call_target="tpu_custom_call" | custom-call | flops 20132659200 | bytes 26214400 | tf_op jit(solution)/shard_map/head_logits/pallas_call | solution.py:579
  301.4 18.5 %head_logits.3 = (f32[6400,1024]{1,0:T(8,128)}, f32[160,1024]{1,0:T(8,128)}, f32[8,1024]{1,0:T(8,128)}) custom-call(bf16[1600,768]{1,0:T(8,128)(2,1)} %get-tuple-element.724.a_ref, bf16[1600,768]{1,0:T(8,128)(2,1)} %dynamic-slice_bitcast_fusion.b_ref, bf16[1600,768]{1,0:T(8,128)(2,1)} %collective-permute-done.14.c_ref, ...), custom_call_target="tpu_custom_call" | custom-call | flops 20132659200 | bytes 26214400 | tf_op jit(solution)/shard_map/head_logits/pallas_call | solution.py:579
  332.3 24.7 %head_back.3 = (bf16[6400,1024]{1,0:T(8,128)(2,1)}, bf16[1024,768]{1,0:T(8,128)(2,1)}) custom-call(bf16[768,6400]{1,0:T(8,128)(2,1)} %turned.1.rest_0_.table_ref, f32[6400,1024]{1,0:T(8,128)} %get-tuple-element.353.power_ref, f32[160,1024]{1,0:T(8,128)} %get-tuple-element.354.peak_ref, s32[1,1024]{1,0:T(1,128)} %pad_add_fusion.1.col_ref, ...), custom_call_target="tpu_custom_call" | custom-call | flops 20132659200 | bytes 39321600 | tf_op jit(solution)/shard_map/head_back/pallas_call | solution.py:641
  360.9 15.3 %head_back.5 = (bf16[6400,512]{1,0:T(8,128)(2,1)}, bf16[512,768]{1,0:T(8,128)(2,1)}) custom-call(bf16[768,6400]{1,0:T(8,128)(2,1)} %turned.1.rest_0_.table_ref, f32[6400,1024]{1,0:T(8,128)} %get-tuple-element.349.power_ref, f32[160,1024]{1,0:T(8,128)} %get-tuple-element.350.peak_ref, s32[1,512]{1,0:T(1,128)} %copy-done.64, f32[8,512]{1,0:T(8,128)} %get-tuple-element.604.side_ref), custom_call_target="tpu_custom_call" | custom-call | flops 10066329600 | bytes 19660800 | tf_op jit(solution)/shard_map/head_back/pallas_call | solution.py:641
  386.5 15.2 %head_back.4 = (bf16[6400,512]{1,0:T(8,128)(2,1)}, bf16[512,768]{1,0:T(8,128)(2,1)}) custom-call(bf16[768,6400]{1,0:T(8,128)(2,1)} %turned.1.rest_0_.table_ref, f32[6400,1024]{1,0:T(8,128)} %get-tuple-element.349.power_ref, f32[160,1024]{1,0:T(8,128)} %get-tuple-element.350.peak_ref, s32[1,512]{1,0:T(1,128)} %copy-done.63, ...), custom_call_target="tpu_custom_call" | custom-call | flops 10066329600 | bytes 19660800 | tf_op jit(solution)/shard_map/head_back/pallas_call | solution.py:641
  404.2 6.7 collective-permute-done.34
  413.3 8.3 %collective-permute-done.36.refs_2_ = bf16[256,768]{1,0:T(8,128)(2,1)S(1)} collective-permute-done((bf16[256,768]{1,0:T(8,128)(2,1)S(1)}, bf16[256,768]{1,0:T(8,128)(2,1)S(1)}, u32[]{:S(2)}, u32[]{:S(2)}) %collective-permute-start.36) | collective-permute-done | bytes 393248 | tf_op jit(solution)/shard_map/ppermute | solution.py:31
  424.3 6.0 norm_back.3
  430.2 15.2 %table_grad.2 = (f32[1600,768]{1,0:T(8,128)}, bf16[1600,768]{1,0:T(8,128)(2,1)}) custom-call(bf16[6400,512]{1,0:T(8,128)(2,1)} %get-tuple-element.356.refs_0_.refs_1_, bf16[6400,512]{1,0:T(8,128)(2,1)} %get-tuple-element.356.refs_0_.refs_1_, bf16[6400,512]{1,0:T(8,128)(2,1)} %get-tuple-element.357.refs_2_.refs_3_, ...), custom_call_target="tpu_custom_call" | custom-call | flops 10066329600 | bytes 9830400 | tf_op jit(solution)/shard_map/table_grad/pallas_call | solution.py:686
  445.9 4.5 collective-permute-done.39
  457.5 21.5 %all_to_all.79 = bf16[8,48,768]{2,1,0:T(8,128)(2,1)S(1)} all-to-all(bf16[8,48,768]{2,1,0:T(8,128)(2,1)S(1)} %bitcast.275), channel_id=1, replica_groups=mesh['expert'=8,'hidden'=4] {'expert'}, dimensions={0} | all-to-all | bytes 1179648 | tf_op jit(solution)/shard_map/all_to_all | solution.py:914
  479.9 10.4 %expert_back.1 = (bf16[384,768]{1,0:T(8,128)(2,1)}, bf16[384,768]{1,0:T(8,128)(2,1)}, bf16[384,768]{1,0:T(8,128)(2,1)}, bf16[384,768]{1,0:T(8,128)(2,1)}, bf16[384,768]{1,0:T(8,128)(2,1)}) custom-call(bf16[384,768]{1,0:T(8,128)(2,1)} %bitcast.248, bf16[2,768,768]{2,1,0:T(8,128)(2,1)} %pad_maximum_fusion.2.refs_0_, bf16[2,768,768]{2,1,0:T(8,128)(2,1)} %copy-done.12, ...), custom_call_target="tpu_custom_call" | custom-call | flops 1024 | bytes 1024 | tf_op jit(solution)/shard_map/expert_back/pallas_call | solution.py:448
  495.7 19.4 %all_to_all.80 = bf16[8,48,768]{2,1,0:T(8,128)(2,1)S(1)} all-to-all(bf16[8,48,768]{2,1,0:T(8,128)(2,1)S(1)} %bitcast.263), channel_id=1, replica_groups=mesh['expert'=8,'hidden'=4] {'expert'}, dimensions={0} | all-to-all | bytes 1179648 | tf_op jit(solution)/shard_map/all_to_all | solution.py:917
  515.9 15.2 %table_grad.3 = (f32[1600,768]{1,0:T(8,128)}, bf16[1600,768]{1,0:T(8,128)(2,1)}) custom-call(bf16[6400,512]{1,0:T(8,128)(2,1)} %get-tuple-element.356.refs_0_.refs_1_, bf16[6400,512]{1,0:T(8,128)(2,1)} %get-tuple-element.356.refs_0_.refs_1_, bf16[6400,512]{1,0:T(8,128)(2,1)} %get-tuple-element.357.refs_2_.refs_3_, ...), custom_call_target="tpu_custom_call" | custom-call | flops 10066329600 | bytes 9830400 | tf_op jit(solution)/shard_map/table_grad/pallas_call | solution.py:686
  536.0 4.3 fusion.16.refs_6_
  541.2 9.4 %norm_back.4 = (f32[1,768]{1,0:T(1,128)}, bf16[1024,768]{1,0:T(8,128)(2,1)}, f32[1024,768]{1,0:T(8,128)}) custom-call(f32[1024,768]{1,0:T(8,128)} %get-tuple-element.345.refs_5_.x_ref, f32[1,768]{1,0:T(1,128)} %slice.292.refs_3_.gain_ref, s32[1024,1]{1,0:T(8,128)} %fusion.42.refs_0_, bf16[384,768]{1,0:T(8,128)(2,1)} %bitcast.262, ...), custom_call_target="tpu_custom_call" | custom-call | flops 1024 | bytes 1024 | tf_op jit(solution)/shard_map/norm_back/pallas_call | solution.py:365
  550.6 10.5 %all-gather.17.cloned.1.call-done = bf16[3200,768]{1,0:T(8,128)(2,1)} async-done(((bf16[1600,768]{1,0:T(8,128)(2,1)}), bf16[3200,768]{1,0:T(8,128)(2,1)}) %all-gather.17.cloned.1.call-update) | async-done | bytes 4915216 | tf_op jit(solution)/shard_map/all_gather | solution.py:40
  561.0 26.3 %attend_back.1 = (bf16[2,1024,576]{2,1,0:T(8,128)(2,1)}, f32[1024,768]{1,0:T(8,128)}) custom-call(bf16[1024,768]{1,0:T(8,128)(2,1)} %get-tuple-element.376.branch_ref, bf16[2,768,768]{2,1,0:T(8,128)(2,1)} %all-gather.11.cloned.1.call-done.w_ref, bf16[2,1024,576]{2,1,0:T(8,128)(2,1)} %get-tuple-element.377.qkv_ref, s32[1,1024]{1,0:T(1,128)} %segr_ref.3, ...), custom_call_target="tpu_custom_call" | custom-call | flops 1024 | bytes 1024 | tf_op jit(solution)/shard_map/attend_back/pallas_call | solution.py:208
  594.0 8.1 %norm_back.5 = (f32[1,768]{1,0:T(1,128)}, bf16[1024,768]{1,0:T(8,128)(2,1)}, bf16[1024,768]{1,0:T(8,128)(2,1)}) custom-call(f32[1024,768]{1,0:T(8,128)} %get-tuple-element.342.refs_2_.x_ref, f32[1,768]{1,0:T(1,128)} %slice.288.refs_5_.gain_ref, f32[1024,768]{1,0:T(8,128)} %get-tuple-element.378.refs_0_, f32[1024,768]{1,0:T(8,128)} %collective-permute-done.44.refs_1_, ...), custom_call_target="tpu_custom_call" | custom-call | flops 1024 | bytes 1024 | tf_op jit(solution)/shard_map/norm_back/pallas_call | solution.py:365
  608.4 4.1 all-to-all-start.6
  616.9 6.7 convert_add_fusion
  623.6 5.3 attn_grad.1
  631.2 4.3 all-to-all-start.7
  636.3 7.6 %finish.1 = (f32[1572,768]{1,0:T(8,128)}, f32[1,768]{1,0:T(1,128)}) custom-call(f32[1600,768]{1,0:T(8,128)} %get-tuple-element.383.base_ref, s32[1,320]{1,0:T(1,128)} %select_n.550.place_ref, bf16[320,768]{1,0:T(8,128)(2,1)} %bitcast.264), custom_call_target="tpu_custom_call" | custom-call | flops 1024 | bytes 1024 | tf_op jit(solution)/shard_map/finish/pallas_call | solution.py:728
  647.2 7.3 %all-gather.19.cloned.1.call-done = bf16[4,768,768]{2,1,0:T(8,128)(2,1)} async-done(((bf16[2,768,768]{2,1,0:T(8,128)(2,1)}), bf16[4,768,768]{2,1,0:T(8,128)(2,1)}) %all-gather.19.cloned.1.call-update) | async-done | bytes 4718608 | tf_op jit(solution)/shard_map/all_gather | solution.py:40
  654.5 7.8 %multiply_reduce_fusion = (f32[]{:T(128)}, f32[2,768,768]{2,1,0:T(8,128)}) fusion(bf16[2,2,768,768]{3,2,1,0:T(8,128)(2,1)} %bitcast.272, s32[]{:T(128)S(6)} %select_n.551, f32[2,768,768]{2,1,0:T(8,128)} %collective-permute-done.46, f32[1,768,768]{2,1,0:T(8,128)S(1)} %copy-done.15, f32[1,768,768]{2,1,0:T(8,128)} %convolution_bitcast_fusion.3), kind=kLoop, calls=%fused_computation.40 | loop fusion | flops 7077887 | bytes 16515080 | tf_op jit(solution)/shard_map/reduce_sum | solution.py:1115
  673.1 5.9 all-to-all-done.8
  679.1 5.0 all-gather.4
  689.5 14.0 %multiply_subtract_fusion = (f32[1572,768]{1,0:T(8,128)}, f32[1572,768]{1,0:T(8,128)}, f32[1572,768]{1,0:T(8,128)}) fusion(f32[1572,768]{1,0:T(8,128)} %x_ref.1, f32[1572,768]{1,0:T(8,128)} %get-tuple-element.394, f32[]{:T(128)S(6)} %min.3, f32[1572,768]{1,0:T(8,128)} %param.32, f32[1572,768]{1,0:T(8,128)} %param.33), kind=kLoop, calls=%fused_computation.32 | loop fusion | flops 19316736 | bytes 33804292 | tf_op jit(solution)/shard_map/sub | solution.py:755
  706.8 6.4 multiply_subtract_fusion.1
  (416 shorter events, 186.2 us)
Async XLA Ops:
  7.2 84.7 %all-gather.11.cloned.1.call-start = ((), (), s32[]{:S(2)}) async-start(), calls=%async_computation.9 | async-start | bytes 2654208 | tf_op jit(solution)/shard_map/all_gather | solution.py:865
  30.5 5.4 collective-permute-start.7
  49.1 18.7 %all-to-all-start.1 = ((bf16[8,40,768]{2,1,0:T(8,128)(2,1)}), bf16[8,40,768]{2,1,0:T(8,128)(2,1)S(1)}, u32[]{:S(2)}, u32[]{:S(2)}) async-start(bf16[8,40,768]{2,1,0:T(8,128)(2,1)} %bitcast.278), calls=%async_computation.1 | async-start | bytes 983040 | tf_op jit(solution)/shard_map/all_to_all | solution.py:872
  52.6 102.6 %all-gather.13.cloned.1.call-start = ((), (), s32[]{:S(2)}) async-start(), calls=%async_computation.10 | async-start | bytes 7077888 | tf_op jit(solution)/shard_map/all_gather | solution.py:40
  67.9 12.3 %collective-permute-start.4 = (bf16[320,768]{1,0:T(8,128)(2,1)S(1)}, bf16[320,768]{1,0:T(8,128)(2,1)}, u32[]{:S(2)}, u32[]{:S(2)}) collective-permute-start(bf16[320,768]{1,0:T(8,128)(2,1)S(1)} %bitcast.238), channel_id=1, source_target_pairs={{0,2},{1,3},{2,0},{3,1},{4,6},{5,7},{6,4},{7,5},{8,10},{9,11},{10,... | collective-permute-start | bytes 1474568 | tf_op jit(solution)/shard_map/ppermute | solution.py:31
  72.3 11.5 %collective-permute-start.5 = (bf16[320,768]{1,0:T(8,128)(2,1)S(1)}, bf16[320,768]{1,0:T(8,128)(2,1)}, u32[]{:S(2)}, u32[]{:S(2)}) collective-permute-start(bf16[320,768]{1,0:T(8,128)(2,1)S(1)} %bitcast.239), channel_id=1, source_target_pairs={{0,1},{1,0},{2,3},{3,2},{4,5},{5,4},{6,7},{7,6},{8,9},{9,8},{10,11... | collective-permute-start | bytes 1474568 | tf_op jit(solution)/shard_map/ppermute | solution.py:31
  106.2 5.9 collective-permute-start.8
  123.6 19.9 %all-to-all-start.2 = ((bf16[8,48,768]{2,1,0:T(8,128)(2,1)}), bf16[8,48,768]{2,1,0:T(8,128)(2,1)S(1)}, u32[]{:S(2)}, u32[]{:S(2)}) async-start(bf16[8,48,768]{2,1,0:T(8,128)(2,1)} %bitcast.273), calls=%async_computation.2 | async-start | bytes 1179648 | tf_op jit(solution)/shard_map/all_to_all | solution.py:914
  127.1 104.7 %all-gather.15.cloned.1.call-start = ((), (), s32[]{:S(2)}) async-start(), calls=%async_computation.11 | async-start | bytes 7372800 | tf_op jit(solution)/shard_map/all_gather | solution.py:40
  129.4 431.6 %all-gather.17.cloned.1.call-start = ((), (), s32[]{:S(2)}) async-start(), calls=%async_computation.12 | async-start | bytes 7372800 | tf_op jit(solution)/shard_map/all_gather | solution.py:40
  132.1 25.0 %collective-permute-start.9 = (bf16[2,768,768]{2,1,0:T(8,128)(2,1)}, bf16[2,768,768]{2,1,0:T(8,128)(2,1)}, u32[]{:S(2)}, u32[]{:S(2)}) collective-permute-start(bf16[2,768,768]{2,1,0:T(8,128)(2,1)} %pad_maximum_fusion.2.refs_0_), channel_id=1, source_target_pairs={{0,1},{1,0},{2,3},{3,2},{4,5},{5,4},{6,7},{7,6},{8,9},{9,8},{10,11... | collective-permute-start | bytes 7077896 | tf_op jit(solution)/shard_map/ppermute | solution.py:31
  200.7 13.8 %collective-permute-start.11 = (bf16[384,768]{1,0:T(8,128)(2,1)S(1)}, bf16[384,768]{1,0:T(8,128)(2,1)}, u32[]{:S(2)}, u32[]{:S(2)}) collective-permute-start(bf16[384,768]{1,0:T(8,128)(2,1)S(1)} %bitcast.257), channel_id=1, source_target_pairs={{0,2},{1,3},{2,0},{3,1},{4,6},{5,7},{6,4},{7,5},{8,10},{9,11},{10,... | collective-permute-start | bytes 1769480 | tf_op jit(solution)/shard_map/ppermute | solution.py:31
  201.3 20.0 %collective-permute-start.12 = (bf16[384,768]{1,0:T(8,128)(2,1)S(1)}, bf16[384,768]{1,0:T(8,128)(2,1)}, u32[]{:S(2)}, u32[]{:S(2)}) collective-permute-start(bf16[384,768]{1,0:T(8,128)(2,1)S(1)} %bitcast.258), channel_id=1, source_target_pairs={{0,1},{1,0},{2,3},{3,2},{4,5},{5,4},{6,7},{7,6},{8,9},{9,8},{10,11... | collective-permute-start | bytes 1769480 | tf_op jit(solution)/shard_map/ppermute | solution.py:31
  214.5 6.9 collective-permute-start.13
  214.5 48.0 %collective-permute-start.14 = (bf16[1600,768]{1,0:T(8,128)(2,1)S(1)}, bf16[1600,768]{1,0:T(8,128)(2,1)}, u32[]{:S(2)}, u32[]{:S(2)}) collective-permute-start(bf16[1600,768]{1,0:T(8,128)(2,1)S(1)} %copy-done.2), channel_id=1, source_target_pairs={{0,1},{1,0},{2,3},{3,2},{4,5},{5,4},{6,7},{7,6},{8,9},{9,8},{10,11... | collective-permute-start | bytes 7372808 | tf_op jit(solution)/shard_map/ppermute | solution.py:31
  235.1 27.4 %collective-permute-start.15 = (bf16[1600,768]{1,0:T(8,128)(2,1)}, bf16[1600,768]{1,0:T(8,128)(2,1)}, u32[]{:S(2)}, u32[]{:S(2)}) collective-permute-start(bf16[1600,768]{1,0:T(8,128)(2,1)} %dynamic-slice_bitcast_fusion.b_ref), channel_id=1, source_target_pairs={{0,1},{1,0},{2,3},{3,2},{4,5},{5,4},{6,7},{7,6},{8,9},{9,8},{10,11... | collective-permute-start | bytes 7372808 | tf_op jit(solution)/shard_map/ppermute | solution.py:31
  235.8 5.7 collective-permute-start.24
  237.9 4.6 collective-permute-start.23
  239.4 11.6 %collective-permute-start.16 = (bf16[256,768]{1,0:T(8,128)(2,1)S(1)}, bf16[256,768]{1,0:T(8,128)(2,1)S(1)}, u32[]{:S(2)}, u32[]{:S(2)}) collective-permute-start(bf16[256,768]{1,0:T(8,128)(2,1)S(1)} %get-tuple-element.567), channel_id=1, source_target_pairs={{0,8},{4,12},{8,0},{12,4},{16,24},{20,28},{24,16},{28,20},{1,9},{5... | collective-permute-start | bytes 1179656 | tf_op jit(solution)/shard_map/ppermute | solution.py:31
  241.6 10.1 %collective-permute-start.18 = (f32[2,512]{1,0:T(2,128)S(1)}, f32[2,512]{1,0:T(2,128)S(1)}, u32[]{:S(2)}, u32[]{:S(2)}) collective-permute-start(f32[2,512]{1,0:T(2,128)S(1)} %pad_maximum_fusion.15), channel_id=1, source_target_pairs={{0,8},{4,12},{8,0},{12,4},{16,24},{20,28},{24,16},{28,20},{1,9},{5... | collective-permute-start | bytes 12296 | tf_op jit(solution)/shard_map/ppermute | solution.py:31
  242.6 32.8 %collective-permute-start.20 = (bf16[256,768]{1,0:T(8,128)(2,1)S(1)}, bf16[256,768]{1,0:T(8,128)(2,1)S(1)}, u32[]{:S(2)}, u32[]{:S(2)}) collective-permute-start(bf16[256,768]{1,0:T(8,128)(2,1)S(1)} %get-tuple-element.567), channel_id=1, source_target_pairs={{0,24},{4,28},{8,16},{12,20},{16,8},{20,12},{24,0},{28,4},{1,25},{... | collective-permute-start | bytes 1179656 | tf_op jit(solution)/shard_map/ppermute | solution.py:31
  251.1 10.2 %collective-permute-start.17 = (bf16[256,768]{1,0:T(8,128)(2,1)S(1)}, bf16[256,768]{1,0:T(8,128)(2,1)S(1)}, u32[]{:S(2)}, u32[]{:S(2)}) collective-permute-start(bf16[256,768]{1,0:T(8,128)(2,1)S(1)} %collective-permute-done.16), channel_id=1, source_target_pairs={{0,2},{1,3},{2,0},{3,1},{4,6},{5,7},{6,4},{7,5},{8,10},{9,11},{10,... | collective-permute-start | bytes 1179656 | tf_op jit(solution)/shard_map/ppermute | solution.py:31
  252.9 26.0 %collective-permute-start.19 = (bf16[256,768]{1,0:T(8,128)(2,1)S(1)}, bf16[256,768]{1,0:T(8,128)(2,1)S(1)}, u32[]{:S(2)}, u32[]{:S(2)}) collective-permute-start(bf16[256,768]{1,0:T(8,128)(2,1)S(1)} %get-tuple-element.567), channel_id=1, source_target_pairs={{0,16},{4,20},{8,24},{12,28},{16,0},{20,4},{24,8},{28,12},{1,17},{... | collective-permute-start | bytes 1179656 | tf_op jit(solution)/shard_map/ppermute | solution.py:31
  275.4 23.6 %collective-permute-start.22 = (bf16[256,768]{1,0:T(8,128)(2,1)S(1)}, bf16[256,768]{1,0:T(8,128)(2,1)S(1)}, u32[]{:S(2)}, u32[]{:S(2)}) collective-permute-start(bf16[256,768]{1,0:T(8,128)(2,1)S(1)} %broadcast_select_fusion.1.rest_2_), channel_id=1, source_target_pairs={{0,2},{1,3},{2,0},{3,1},{4,6},{5,7},{6,4},{7,5},{8,10},{9,11},{10,... | collective-permute-start | bytes 1179656 | tf_op jit(solution)/shard_map/ppermute | solution.py:31
  279.0 20.0 %collective-permute-start.21 = (bf16[256,768]{1,0:T(8,128)(2,1)S(1)}, bf16[256,768]{1,0:T(8,128)(2,1)S(1)}, u32[]{:S(2)}, u32[]{:S(2)}) collective-permute-start(bf16[256,768]{1,0:T(8,128)(2,1)S(1)} %broadcast_select_fusion.2.rest_1_), channel_id=1, source_target_pairs={{0,2},{1,3},{2,0},{3,1},{4,6},{5,7},{6,4},{7,5},{8,10},{9,11},{10,... | collective-permute-start | bytes 1179656 | tf_op jit(solution)/shard_map/ppermute | solution.py:31
  324.7 5.7 collective-permute-start.28
  326.8 4.7 collective-permute-start.27
  358.2 20.7 %collective-permute-start.33 = (bf16[256,768]{1,0:T(8,128)(2,1)S(1)}, bf16[256,768]{1,0:T(8,128)(2,1)S(1)}, u32[]{:S(2)}, u32[]{:S(2)}) collective-permute-start(bf16[256,768]{1,0:T(8,128)(2,1)S(1)} %get-tuple-element.564), channel_id=1, source_target_pairs={{0,2},{1,3},{2,0},{3,1},{4,6},{5,7},{6,4},{7,5},{8,10},{9,11},{10,... | collective-permute-start | bytes 1179656 | tf_op jit(solution)/shard_map/ppermute | solution.py:31
  359.6 19.2 %collective-permute-start.29 = (bf16[256,768]{1,0:T(8,128)(2,1)S(1)}, bf16[256,768]{1,0:T(8,128)(2,1)S(1)}, u32[]{:S(2)}, u32[]{:S(2)}) collective-permute-start(bf16[256,768]{1,0:T(8,128)(2,1)S(1)} %get-tuple-element.565), channel_id=1, source_target_pairs={{0,2},{1,3},{2,0},{3,1},{4,6},{5,7},{6,4},{7,5},{8,10},{9,11},{10,... | collective-permute-start | bytes 1179656 | tf_op jit(solution)/shard_map/ppermute | solution.py:31
  377.4 7.8 %collective-permute-start.31 = (bf16[256,768]{1,0:T(8,128)(2,1)S(1)}, bf16[256,768]{1,0:T(8,128)(2,1)S(1)}, u32[]{:S(2)}, u32[]{:S(2)}) collective-permute-start(bf16[256,768]{1,0:T(8,128)(2,1)S(1)} %slice.343), channel_id=1, source_target_pairs={{0,2},{1,3},{2,0},{3,1},{4,6},{5,7},{6,4},{7,5},{8,10},{9,11},{10,... | collective-permute-start | bytes 1179656 | tf_op jit(solution)/shard_map/ppermute | solution.py:31
  379.0 25.1 %collective-permute-start.35 = (bf16[256,768]{1,0:T(8,128)(2,1)S(1)}, bf16[256,768]{1,0:T(8,128)(2,1)S(1)}, u32[]{:S(2)}, u32[]{:S(2)}) collective-permute-start(bf16[256,768]{1,0:T(8,128)(2,1)S(1)} %get-tuple-element.563.rest_0_), channel_id=1, source_target_pairs={{0,24},{4,28},{8,16},{12,20},{16,8},{20,12},{24,0},{28,4},{1,25},{... | collective-permute-start | bytes 1179656 | tf_op jit(solution)/shard_map/ppermute | solution.py:31
  380.9 30.0 %collective-permute-start.34 = (bf16[256,768]{1,0:T(8,128)(2,1)S(1)}, bf16[256,768]{1,0:T(8,128)(2,1)S(1)}, u32[]{:S(2)}, u32[]{:S(2)}) collective-permute-start(bf16[256,768]{1,0:T(8,128)(2,1)S(1)} %get-tuple-element.562), channel_id=1, source_target_pairs={{0,16},{4,20},{8,24},{12,28},{16,0},{20,4},{24,8},{28,12},{1,17},{... | collective-permute-start | bytes 1179656 | tf_op jit(solution)/shard_map/ppermute | solution.py:31
  385.3 25.6 %collective-permute-start.32 = (bf16[256,768]{1,0:T(8,128)(2,1)S(1)}, bf16[256,768]{1,0:T(8,128)(2,1)S(1)}, u32[]{:S(2)}, u32[]{:S(2)}) collective-permute-start(bf16[256,768]{1,0:T(8,128)(2,1)S(1)} %add_convert_fusion.3), channel_id=1, source_target_pairs={{0,8},{4,12},{8,0},{12,4},{16,24},{20,28},{24,16},{28,20},{1,9},{5... | collective-permute-start | bytes 1179656 | tf_op jit(solution)/shard_map/ppermute | solution.py:31
  402.7 8.2 %collective-permute-start.30 = (bf16[256,768]{1,0:T(8,128)(2,1)S(1)}, bf16[256,768]{1,0:T(8,128)(2,1)S(1)}, u32[]{:S(2)}, u32[]{:S(2)}) collective-permute-start(bf16[256,768]{1,0:T(8,128)(2,1)S(1)} %slice.341), channel_id=1, source_target_pairs={{0,2},{1,3},{2,0},{3,1},{4,6},{5,7},{6,4},{7,5},{8,10},{9,11},{10,... | collective-permute-start | bytes 1179656 | tf_op jit(solution)/shard_map/ppermute | solution.py:31
  412.1 9.5 %collective-permute-start.36 = (bf16[256,768]{1,0:T(8,128)(2,1)S(1)}, bf16[256,768]{1,0:T(8,128)(2,1)S(1)}, u32[]{:S(2)}, u32[]{:S(2)}) collective-permute-start(bf16[256,768]{1,0:T(8,128)(2,1)S(1)} %add_convert_fusion.1.refs_1_), channel_id=1, source_target_pairs={{0,2},{1,3},{2,0},{3,1},{4,6},{5,7},{6,4},{7,5},{8,10},{9,11},{10,... | collective-permute-start | bytes 1179656 | tf_op jit(solution)/shard_map/ppermute | solution.py:31
  413.3 10.0 %collective-permute-start.37 = (bf16[256,768]{1,0:T(8,128)(2,1)S(1)}, bf16[256,768]{1,0:T(8,128)(2,1)S(1)}, u32[]{:S(2)}, u32[]{:S(2)}) collective-permute-start(bf16[256,768]{1,0:T(8,128)(2,1)S(1)} %add_convert_fusion.1.refs_1_), channel_id=1, source_target_pairs={{0,1},{1,0},{2,3},{3,2},{4,5},{5,4},{6,7},{7,6},{8,9},{9,8},{10,11... | collective-permute-start | bytes 1179656 | tf_op jit(solution)/shard_map/ppermute | solution.py:31
  445.4 5.0 collective-permute-start.39
  494.7 41.3 %collective-permute-start.43 = (f32[2,768,768]{2,1,0:T(8,128)}, f32[2,768,768]{2,1,0:T(8,128)}, u32[]{:S(2)}, u32[]{:S(2)}) collective-permute-start(f32[2,768,768]{2,1,0:T(8,128)} %pad_maximum_fusion), channel_id=1, source_target_pairs={{0,1},{1,0},{2,3},{3,2},{4,5},{5,4},{6,7},{7,6},{8,9},{9,8},{10,11... | collective-permute-start | bytes 14155784 | tf_op jit(solution)/shard_map/ppermute | solution.py:31
  494.7 159.8 %all-gather.19.cloned.1.call-start = ((), (), s32[]{:S(2)}) async-start(), calls=%async_computation.13 | async-start | bytes 7077888 | tf_op jit(solution)/shard_map/all_gather | solution.py:40
  515.1 19.5 %collective-permute-start.40 = (bf16[384,768]{1,0:T(8,128)(2,1)S(1)}, bf16[384,768]{1,0:T(8,128)(2,1)S(1)}, u32[]{:S(2)}, u32[]{:S(2)}) collective-permute-start(bf16[384,768]{1,0:T(8,128)(2,1)S(1)} %bitcast.260), channel_id=1, source_target_pairs={{0,2},{1,3},{2,0},{3,1},{4,6},{5,7},{6,4},{7,5},{8,10},{9,11},{10,... | collective-permute-start | bytes 1769480 | tf_op jit(solution)/shard_map/ppermute | solution.py:31
  534.5 5.9 collective-permute-start.41
  534.6 5.7 collective-permute-start.42
  587.3 6.6 collective-permute-start.44
  588.0 28.9 %collective-permute-start.45 = (bf16[1600,768]{1,0:T(8,128)(2,1)}, bf16[1600,768]{1,0:T(8,128)(2,1)}, u32[]{:S(2)}, u32[]{:S(2)}) collective-permute-start(bf16[1600,768]{1,0:T(8,128)(2,1)} %get-tuple-element.382), channel_id=1, source_target_pairs={{0,1},{1,0},{2,3},{3,2},{4,5},{5,4},{6,7},{7,6},{8,9},{9,8},{10,11... | collective-permute-start | bytes 7372808 | tf_op jit(solution)/shard_map/ppermute | solution.py:31
  592.6 54.6 %collective-permute-start.46 = (f32[2,768,768]{2,1,0:T(8,128)}, f32[2,768,768]{2,1,0:T(8,128)}, u32[]{:S(2)}, u32[]{:S(2)}) collective-permute-start(f32[2,768,768]{2,1,0:T(8,128)} %pad_maximum_fusion.1), channel_id=1, source_target_pairs={{0,1},{1,0},{2,3},{3,2},{4,5},{5,4},{6,7},{7,6},{8,9},{9,8},{10,11... | collective-permute-start | bytes 14155784 | tf_op jit(solution)/shard_map/ppermute | solution.py:31
  608.4 22.8 %all-to-all-start.6 = ((bf16[8,56,768]{2,1,0:T(8,128)(2,1)}), bf16[8,56,768]{2,1,0:T(8,128)(2,1)S(1)}, u32[]{:S(2)}, u32[]{:S(2)}) async-start(bf16[8,56,768]{2,1,0:T(8,128)(2,1)} %fusion.31), calls=%async_computation.6 | async-start | bytes 1376256 | tf_op jit(solution)/shard_map/all_to_all | solution.py:1084
  631.2 32.7 %all-to-all-start.7 = ((bf16[8,96,768]{2,1,0:T(8,128)(2,1)}), bf16[8,96,768]{2,1,0:T(8,128)(2,1)}, u32[]{:S(2)}, u32[]{:S(2)}) async-start(bf16[8,96,768]{2,1,0:T(8,128)(2,1)} %bitcast.256), calls=%async_computation.7 | async-start | bytes 2359296 | tf_op jit(solution)/shard_map/all_to_all | solution.py:1074
  668.6 10.4 %all-to-all-start.8 = ((f32[8,1,128]{2,1,0:T(1,128)}), f32[8,1,128]{2,1,0:T(1,128)S(1)}, u32[]{:S(2)}, u32[]{:S(2)}) async-start(f32[8,1,128]{2,1,0:T(1,128)} %broadcast_in_dim.151), calls=%async_computation.8 | async-start | bytes 8192 | tf_op jit(solution)/shard_map/all_to_all | solution.py:1120
  (78 other events, 889.6 us)
Sparse Core Ops, SparseCore 0:
  37.7 54.1 all-gather.10
  94.0 61.1 all-gather.12
  156.8 71.1 all-gather.14
  494.8 66.1 all-gather.16
  592.8 61.6 all-gather.18

commit v4 on v3

--- a/solution.py
+++ b/solution.py
@@ -1033,16 +1033,15 @@
     grad_in = to_expert(d_result, across_x[0, 0].astype(F32))
     d_received, *d_pre = expert_back(grad_in, expert_w, slope, ())
     d_w = [
-        jnp.stack([dot(received, d_pre[p], 0, 0), dot(active[p], grad_in, 0, 0)]) for p in range(4)
+        (dot(received, d_pre[p], 0, 0), dot(active[p], grad_in, 0, 0)) for p in range(4)
     ]
     d_same = table_grad(d_logits, group_rows, padded, (0, 2), (d_received,))
 
     base_x, both_x = far_flip(across_x, "expert", 1)
     d_base = d_same[0] + flip(d_same[1], "hidden", 1).astype(F32) + base_x.astype(F32)
 
-    w_near = flip(d_w[3], "hidden", 1), flip(d_w[2], "hidden", 1)
-    w_sent = (d_w[1] + w_near[0]).astype(BF)
-    w_far, _ = far_flip(w_sent, "hidden", 2)
+    w_near = flip(d_w[3], "hidden", 1), flip(jnp.stack(d_w[2]), "hidden", 1)
+    w_sent = jnp.stack([d_w[1][i] + w_near[0][i] for i in range(2)]).astype(BF)
     d_gain_two, d_branch, d_after_attn = norm_back(
         after_attn,
         gain_full[1:2],
@@ -1105,7 +1104,8 @@
     g_attn_out = g_attn[:, 3 * head_width :]
     g_gains = jnp.sum(got[:, slots : slots + 2, : 3 * own_rows].astype(F32), axis=(0, 1))
     g_gains = g_gains.reshape(3, own_rows).T
-    g_expert = d_w[0] + w_near[1] + w_far.astype(F32)
+    w_far, _ = far_flip(w_sent, "hidden", 2, table_squares[0, 0])
+    g_expert = jnp.stack(d_w[0]) + w_near[1] + w_far.astype(F32)
     g_expert_in = g_expert[0][None]
     g_expert_out = g_expert[1][None]
 

time: 732 us -> 723 us (0.988)
  blocking collectives: 82.5 us -> 63.4 us
    all_to_all x2 -> x1, blocking collectives: 42.3 us -> 22.9 us  [from_expert(): lax.all_to_all(rows_in, 'expert', split_axis=0, concat_axis=0, tiled=True)]
    all_gather x4, waiting for transfers between devices: 27.7 us -> 14.3 us  [far_flip(): both = lax.all_gather(x, axis, axis_index_groups=pairs)]
    all_to_all x0 -> x1, waiting for transfers between devices: none -> 13 us  [from_expert(): lax.all_to_all(rows_in, 'expert', split_axis=0, concat_axis=0, tiled=True)]
    ppermute x43 -> x44, starting transfers between devices: 33.1 us -> 33.7 us  [flip(): lax.ppermute(x, axis, [(j, j ^ k) for j in range(lax.axis_size(axis))])]
    unnamed x157 -> x159, local copies, waits for them, and re-layouts: 16.3 us -> 15.8 us
    ppermute x43 -> x44, waiting for transfers between devices: 79 us -> 79.1 us  [flip(): lax.ppermute(x, axis, [(j, j ^ k) for j in range(lax.axis_size(axis))])]
  transfers between devices with their start and end apart: 53 -> 55, of which waited for: 27 -> 27; matrix products, arithmetic and copies ran while one was open for 13% -> 15% of each run, Pallas kernels for 23% -> 24%
where the time goes in v4:
time: 723 us; the launch traced here: 713 us
  Pallas kernels  266 us (37%)
  waiting for transfers between devices  133 us (18%)
  other arithmetic  87 us (12%)
  blocking collectives  63.4 us (9%)
  starting transfers between devices  56.1 us (8%)
  local copies, waits for them, and re-layouts  51.9 us (7%)
  between operations  29.7 us (4%)
  matrix products  26.1 us (4%)
    ppermute x44, waiting for transfers between devices, flip(): lax.ppermute(x, axis, [(j, j ^ k) for j in range(lax.axis_size(axis))])  79.1 us
    pallas_call x3, Pallas kernels, head_back(): pl.pallas_call(head_back_kernel, grid=(steps,), in_specs=[pl.BlockSpec((w...  55.3 us
    pallas_call x2, Pallas kernels, head_logits(): pl.pallas_call(partial(logits_kernel, real), grid=(steps,), in_specs=[pl....  36.9 us
    ppermute x44, starting transfers between devices, flip(): lax.ppermute(x, axis, [(j, j ^ k) for j in range(lax.axis_size(axis))])  33.7 us
    pallas_call x2, Pallas kernels, table_grad(): pl.pallas_call(partial(table_grad_kernel, len(ds)), grid=(padded // part,...  30.4 us
    pallas_call x1, Pallas kernels, attend_back(): pl.pallas_call(attend_back_kernel, in_specs=[WHOLE] * 5 + [ANY] * len(rea...  26.2 us
    dot_general x12, matrix products, dot(): lax.dot_general(a, b, (((ca,), (cb,)), ((), ())), preferred_element_type=...  26.1 us
    pallas_call x3, Pallas kernels, norm_back(): pl.pallas_call(partial(norm_back_kernel, scale, len(gradients), pick, has...  23.7 us
  transfers between devices with their start and end apart: 55, of which 27 were waited for; matrix products, arithmetic and copies ran while one was open for 15% of the time, Pallas kernels for 24%

profile of v4, /device:TPU:0, one launch (start us, length us, event | category | flops | bytes accessed | tf_op | source)
XLA Modules:
  0.0 712.6 jit_solution(7913262559603068501)
XLA Ops:
  13.0 13.6 %all_to_all.77 = f32[8,1,512]{2,1,0:T(1,128)S(1)} all-to-all(f32[8,1,512]{2,1,0:T(1,128)S(1)} %all_to_all.49), channel_id=1, replica_groups=mesh['expert'=8,'hidden'=4] {'expert'}, dimensions={0} | all-to-all | bytes 32768 | tf_op jit(solution)/shard_map/all_to_all | solution.py:842
  32.1 3.8 collective-permute-done.7
  42.3 6.8 cast_pick.1
  58.0 6.1 gather_fusion
  64.1 3.7 all-to-all-done.1
  72.3 7.9 %collective-permute-done.4 = bf16[320,768]{1,0:T(8,128)(2,1)} collective-permute-done((bf16[320,768]{1,0:T(8,128)(2,1)S(1)}, bf16[320,768]{1,0:T(8,128)(2,1)}, u32[]{:S(2)}, u32[]{:S(2)}) %collective-permute-start.4) | collective-permute-done | bytes 491552 | tf_op jit(solution)/shard_map/ppermute | solution.py:31
  84.0 7.1 pick_norm.3
  91.8 14.4 %attend.1 = (bf16[2,1024,576]{2,1,0:T(8,128)(2,1)}, bf16[2,1024,192]{2,1,0:T(8,128)(2,1)}, f32[1024,768]{1,0:T(8,128)}) custom-call(bf16[1024,768]{1,0:T(8,128)(2,1)} %get-tuple-element.343.rows_ref, bf16[2,768,768]{2,1,0:T(8,128)(2,1)} %all-gather.10.cloned.1.call-done.w_ref, s32[1,1024]{1,0:T(1,128)} %segr_ref.3, s32[1024,1]{1,0:T(8,128)} %copy.181.segc_ref), custom_call_target="tpu_custom_call" | custom-call | flops 1024 | bytes 1024 | tf_op jit(solution)/shard_map/attend/pallas_call | solution.py:144
  106.9 5.2 collective-permute-done.8.refs_1_
  113.7 6.7 pick_norm.4
  132.4 11.2 %all-to-all-done.2 = bf16[8,48,768]{2,1,0:T(8,128)(2,1)S(1)} async-done(((bf16[8,48,768]{2,1,0:T(8,128)(2,1)}), bf16[8,48,768]{2,1,0:T(8,128)(2,1)S(1)}, u32[]{:S(2)}, u32[]{:S(2)}) %all-to-all-start.2) | async-done | bytes 589856 | tf_op jit(solution)/shard_map/all_to_all | solution.py:914
  145.5 9.8 %all-gather.12.cloned.1.call-done = bf16[2,2,768,768]{3,2,1,0:T(8,128)(2,1)} async-done(((bf16[1,2,768,768]{3,2,1,0:T(8,128)(2,1)}), bf16[2,2,768,768]{3,2,1,0:T(8,128)(2,1)}) %all-gather.12.cloned.1.call-update) | async-done | bytes 4718608 | tf_op jit(solution)/shard_map/all_gather | solution.py:40
  157.2 4.5 collective-permute-done.10.refs_3_
  163.1 14.7 %expert.1 = (bf16[384,768]{1,0:T(8,128)(2,1)}, bf16[384,768]{1,0:T(8,128)(2,1)}, bf16[384,768]{1,0:T(8,128)(2,1)}, bf16[384,768]{1,0:T(8,128)(2,1)}, bf16[384,76...) custom-call(bf16[384,768]{1,0:T(8,128)(2,1)} %bitcast.238, ...), custom_call_target="tpu_custom_call" | custom-call | flops 1024 | bytes 1024 | tf_op jit(solution)/shard_map/expert/pallas_call | solution.py:422
  177.8 22.9 %all_to_all.78 = bf16[8,48,768]{2,1,0:T(8,128)(2,1)S(1)} all-to-all(bf16[8,48,768]{2,1,0:T(8,128)(2,1)} %bitcast.273), channel_id=1, replica_groups=mesh['expert'=8,'hidden'=4] {'expert'}, dimensions={0} | all-to-all | bytes 1179648 | tf_op jit(solution)/shard_map/all_to_all | solution.py:917
  201.4 13.2 %collective-permute-done.11.refs_2_ = bf16[384,768]{1,0:T(8,128)(2,1)} collective-permute-done((bf16[384,768]{1,0:T(8,128)(2,1)S(1)}, bf16[384,768]{1,0:T(8,128)(2,1)}, u32[]{:S(2)}, u32[]{:S(2)}) %collective-permute-start.11) | collective-permute-done | bytes 589856 | tf_op jit(solution)/shard_map/ppermute | solution.py:31
  221.4 7.9 %pick_norm.5 = (f32[1024,768]{1,0:T(8,128)}, bf16[1024,768]{1,0:T(8,128)(2,1)}) custom-call(s32[1024,1]{1,0:T(8,128)} %fusion.41.refs_0_, bf16[384,768]{1,0:T(8,128)(2,1)} %bitcast.262, bf16[384,768]{1,0:T(8,128)(2,1)} %collective-permute-done.11.refs_2_, bf16[384,768]{1,0:T(8,128)(2,1)} %collective-permute-done.12.refs_3_, ...), custom_call_target="tpu_custom_call" | custom-call | flops 1024 | bytes 1024 | tf_op jit(solution)/shard_map/pick_norm/pallas_call | solution.py:294
  244.3 6.8 collective-permute-done.16
  256.1 5.2 collective-permute-done.17
  262.5 10.3 %turned.1.rest_0_.table_ref = bf16[768,6400]{1,0:T(8,128)(2,1)} custom-call(bf16[1600,768]{1,0:T(8,128)(2,1)} %get-tuple-element.724.a_ref, bf16[1600,768]{1,0:T(8,128)(2,1)} %dynamic-slice_bitcast_fusion.b_ref, bf16[1600,768]{1,0:T(8,128)(2,1)} %collective-permute-done.14.c_ref, bf16[1600,768]{1,0:T(8,128)(2,1)} %collective-permute-done.15.d_ref), custom_call_target="tpu_custom_call" | custom-call | bytes 29491200 | tf_op jit(solution)/shard_map/turned/pallas_call | solution.py:518
  279.8 18.5 %head_logits.2 = (f32[6400,1024]{1,0:T(8,128)}, f32[160,1024]{1,0:T(8,128)}, f32[8,1024]{1,0:T(8,128)}) custom-call(bf16[1600,768]{1,0:T(8,128)(2,1)} %get-tuple-element.724.a_ref, bf16[1600,768]{1,0:T(8,128)(2,1)} %dynamic-slice_bitcast_fusion.b_ref, bf16[1600,768]{1,0:T(8,128)(2,1)} %collective-permute-done.14.c_ref, ...), custom_call_target="tpu_custom_call" | custom-call | flops 20132659200 | bytes 26214400 | tf_op jit(solution)/shard_map/head_logits/pallas_call | solution.py:579
  301.4 18.4 %head_logits.3 = (f32[6400,1024]{1,0:T(8,128)}, f32[160,1024]{1,0:T(8,128)}, f32[8,1024]{1,0:T(8,128)}) custom-call(bf16[1600,768]{1,0:T(8,128)(2,1)} %get-tuple-element.724.a_ref, bf16[1600,768]{1,0:T(8,128)(2,1)} %dynamic-slice_bitcast_fusion.b_ref, bf16[1600,768]{1,0:T(8,128)(2,1)} %collective-permute-done.14.c_ref, ...), custom_call_target="tpu_custom_call" | custom-call | flops 20132659200 | bytes 26214400 | tf_op jit(solution)/shard_map/head_logits/pallas_call | solution.py:579
  332.3 24.8 %head_back.3 = (bf16[6400,1024]{1,0:T(8,128)(2,1)}, bf16[1024,768]{1,0:T(8,128)(2,1)}) custom-call(bf16[768,6400]{1,0:T(8,128)(2,1)} %turned.1.rest_0_.table_ref, f32[6400,1024]{1,0:T(8,128)} %get-tuple-element.353.power_ref, f32[160,1024]{1,0:T(8,128)} %get-tuple-element.354.peak_ref, s32[1,1024]{1,0:T(1,128)} %pad_add_fusion.1.col_ref, ...), custom_call_target="tpu_custom_call" | custom-call | flops 20132659200 | bytes 39321600 | tf_op jit(solution)/shard_map/head_back/pallas_call | solution.py:641
  361.0 15.3 %head_back.5 = (bf16[6400,512]{1,0:T(8,128)(2,1)}, bf16[512,768]{1,0:T(8,128)(2,1)}) custom-call(bf16[768,6400]{1,0:T(8,128)(2,1)} %turned.1.rest_0_.table_ref, f32[6400,1024]{1,0:T(8,128)} %get-tuple-element.349.power_ref, f32[160,1024]{1,0:T(8,128)} %get-tuple-element.350.peak_ref, s32[1,512]{1,0:T(1,128)} %copy-done.65, f32[8,512]{1,0:T(8,128)} %get-tuple-element.604.side_ref), custom_call_target="tpu_custom_call" | custom-call | flops 10066329600 | bytes 19660800 | tf_op jit(solution)/shard_map/head_back/pallas_call | solution.py:641
  386.6 15.2 %head_back.4 = (bf16[6400,512]{1,0:T(8,128)(2,1)}, bf16[512,768]{1,0:T(8,128)(2,1)}) custom-call(bf16[768,6400]{1,0:T(8,128)(2,1)} %turned.1.rest_0_.table_ref, f32[6400,1024]{1,0:T(8,128)} %get-tuple-element.349.power_ref, f32[160,1024]{1,0:T(8,128)} %get-tuple-element.350.peak_ref, s32[1,512]{1,0:T(1,128)} %copy-done.64, ...), custom_call_target="tpu_custom_call" | custom-call | flops 10066329600 | bytes 19660800 | tf_op jit(solution)/shard_map/head_back/pallas_call | solution.py:641
  404.2 6.7 collective-permute-done.34
  413.3 8.4 %collective-permute-done.36.refs_2_ = bf16[256,768]{1,0:T(8,128)(2,1)S(1)} collective-permute-done((bf16[256,768]{1,0:T(8,128)(2,1)S(1)}, bf16[256,768]{1,0:T(8,128)(2,1)S(1)}, u32[]{:S(2)}, u32[]{:S(2)}) %collective-permute-start.36) | collective-permute-done | bytes 393248 | tf_op jit(solution)/shard_map/ppermute | solution.py:31
  424.3 6.0 norm_back.3
  430.3 15.2 %table_grad.2 = (f32[1600,768]{1,0:T(8,128)}, bf16[1600,768]{1,0:T(8,128)(2,1)}) custom-call(bf16[6400,512]{1,0:T(8,128)(2,1)} %get-tuple-element.356.refs_0_.refs_1_, bf16[6400,512]{1,0:T(8,128)(2,1)} %get-tuple-element.356.refs_0_.refs_1_, bf16[6400,512]{1,0:T(8,128)(2,1)} %get-tuple-element.357.refs_2_.refs_3_, ...), custom_call_target="tpu_custom_call" | custom-call | flops 10066329600 | bytes 9830400 | tf_op jit(solution)/shard_map/table_grad/pallas_call | solution.py:686
  445.9 4.5 collective-permute-done.39
  450.4 4.4 add_convert_fusion
  458.3 21.6 %all_to_all.79 = bf16[8,48,768]{2,1,0:T(8,128)(2,1)S(1)} all-to-all(bf16[8,48,768]{2,1,0:T(8,128)(2,1)S(1)} %bitcast.274), channel_id=1, replica_groups=mesh['expert'=8,'hidden'=4] {'expert'}, dimensions={0} | all-to-all | bytes 1179648 | tf_op jit(solution)/shard_map/all_to_all | solution.py:914
  482.1 10.4 %expert_back.1 = (bf16[384,768]{1,0:T(8,128)(2,1)}, bf16[384,768]{1,0:T(8,128)(2,1)}, bf16[384,768]{1,0:T(8,128)(2,1)}, bf16[384,768]{1,0:T(8,128)(2,1)}, bf16[384,768]{1,0:T(8,128)(2,1)}) custom-call(bf16[384,768]{1,0:T(8,128)(2,1)} %bitcast.244, bf16[2,768,768]{2,1,0:T(8,128)(2,1)} %pad_maximum_fusion.1.refs_0_, bf16[2,768,768]{2,1,0:T(8,128)(2,1)} %copy-done.12, ...), custom_call_target="tpu_custom_call" | custom-call | flops 1024 | bytes 1024 | tf_op jit(solution)/shard_map/expert_back/pallas_call | solution.py:448
  499.9 13.0 %all-to-all-done.5 = bf16[8,48,768]{2,1,0:T(8,128)(2,1)S(1)} async-done(((bf16[8,48,768]{2,1,0:T(8,128)(2,1)}), bf16[8,48,768]{2,1,0:T(8,128)(2,1)S(1)}, u32[]{:S(2)}, u32[]{:S(2)}) %all-to-all-start.5) | async-done | bytes 589856 | tf_op jit(solution)/shard_map/all_to_all | solution.py:917
  513.8 15.2 %table_grad.3 = (f32[1600,768]{1,0:T(8,128)}, bf16[1600,768]{1,0:T(8,128)(2,1)}) custom-call(bf16[6400,512]{1,0:T(8,128)(2,1)} %get-tuple-element.356.refs_0_.refs_1_, bf16[6400,512]{1,0:T(8,128)(2,1)} %get-tuple-element.356.refs_0_.refs_1_, bf16[6400,512]{1,0:T(8,128)(2,1)} %get-tuple-element.357.refs_2_.refs_3_, ...), custom_call_target="tpu_custom_call" | custom-call | flops 10066329600 | bytes 9830400 | tf_op jit(solution)/shard_map/table_grad/pallas_call | solution.py:686
  540.1 9.4 %norm_back.4 = (f32[1,768]{1,0:T(1,128)}, bf16[1024,768]{1,0:T(8,128)(2,1)}, f32[1024,768]{1,0:T(8,128)}) custom-call(f32[1024,768]{1,0:T(8,128)} %get-tuple-element.345.refs_5_.x_ref, f32[1,768]{1,0:T(1,128)} %slice.295.refs_3_.gain_ref, s32[1024,1]{1,0:T(8,128)} %fusion.41.refs_0_, bf16[384,768]{1,0:T(8,128)(2,1)} %bitcast.259, ...), custom_call_target="tpu_custom_call" | custom-call | flops 1024 | bytes 1024 | tf_op jit(solution)/shard_map/norm_back/pallas_call | solution.py:365
  549.5 26.2 %attend_back.1 = (bf16[2,1024,576]{2,1,0:T(8,128)(2,1)}, f32[1024,768]{1,0:T(8,128)}) custom-call(bf16[1024,768]{1,0:T(8,128)(2,1)} %get-tuple-element.376.branch_ref, bf16[2,768,768]{2,1,0:T(8,128)(2,1)} %all-gather.10.cloned.1.call-done.w_ref, bf16[2,1024,576]{2,1,0:T(8,128)(2,1)} %get-tuple-element.377.qkv_ref, s32[1,1024]{1,0:T(1,128)} %segr_ref.3, ...), custom_call_target="tpu_custom_call" | custom-call | flops 1024 | bytes 1024 | tf_op jit(solution)/shard_map/attend_back/pallas_call | solution.py:208
  585.2 8.4 %norm_back.5 = (f32[1,768]{1,0:T(1,128)}, bf16[1024,768]{1,0:T(8,128)(2,1)}, bf16[1024,768]{1,0:T(8,128)(2,1)}) custom-call(f32[1024,768]{1,0:T(8,128)} %get-tuple-element.342.refs_2_.x_ref, f32[1,768]{1,0:T(1,128)} %slice.291.refs_5_.gain_ref, f32[1024,768]{1,0:T(8,128)} %get-tuple-element.378.refs_0_, f32[1024,768]{1,0:T(8,128)} %collective-permute-done.45.refs_1_, ...), custom_call_target="tpu_custom_call" | custom-call | flops 1024 | bytes 1024 | tf_op jit(solution)/shard_map/norm_back/pallas_call | solution.py:365
  608.0 6.7 convert_add_fusion
  614.7 5.3 attn_grad.1
  622.4 4.3 all-to-all-start.7
  627.5 7.6 %finish.1 = (f32[1572,768]{1,0:T(8,128)}, f32[1,768]{1,0:T(1,128)}) custom-call(f32[1600,768]{1,0:T(8,128)} %get-tuple-element.383.base_ref, s32[1,320]{1,0:T(1,128)} %select_n.553.place_ref, bf16[320,768]{1,0:T(8,128)(2,1)} %bitcast.264), custom_call_target="tpu_custom_call" | custom-call | flops 1024 | bytes 1024 | tf_op jit(solution)/shard_map/finish/pallas_call | solution.py:728
  640.9 4.5 all-gather.14.cloned.1.call-done
  645.4 7.7 %multiply_reduce_fusion = (f32[]{:T(128)}, f32[2,768,768]{2,1,0:T(8,128)}) fusion(bf16[2,2,768,768]{3,2,1,0:T(8,128)(2,1)} %all-gather.14.cloned.1.call-done, s32[]{:T(128)S(6)} %select_n.555, f32[2,768,768]{2,1,0:T(8,128)} %collective-permute-done.47, f32[1,768,768]{2,1,0:T(8,128)S(1)} %copy-done.16, f32[1,768,768]{2,1,0:T(8,128)} %convolution_bitcast_fusion.3), kind=kLoop, calls=%fused_computation.37 | loop fusion | flops 7077887 | bytes 16515080 | tf_op jit(solution)/shard_map/reduce_sum | solution.py:1115
  664.2 5.9 all-to-all-done.8
  670.1 5.3 all-gather.3
  680.8 13.7 %multiply_subtract_fusion = (f32[1572,768]{1,0:T(8,128)}, f32[1572,768]{1,0:T(8,128)}, f32[1572,768]{1,0:T(8,128)}) fusion(f32[1572,768]{1,0:T(8,128)} %x_ref.1, f32[1572,768]{1,0:T(8,128)} %get-tuple-element.394, f32[]{:T(128)S(6)} %min.3, f32[1572,768]{1,0:T(8,128)} %param.32, f32[1572,768]{1,0:T(8,128)} %param.33), kind=kLoop, calls=%fused_computation.32 | loop fusion | flops 19316736 | bytes 33804292 | tf_op jit(solution)/shard_map/sub | solution.py:755
  698.1 6.4 multiply_subtract_fusion.1
  (422 shorter events, 192.1 us)
Async XLA Ops:
  7.2 84.6 %all-gather.10.cloned.1.call-start = ((), (), s32[]{:S(2)}) async-start(), calls=%async_computation.9 | async-start | bytes 2654208 | tf_op jit(solution)/shard_map/all_gather | solution.py:865
  30.5 5.4 collective-permute-start.7
  49.1 18.7 %all-to-all-start.1 = ((bf16[8,40,768]{2,1,0:T(8,128)(2,1)}), bf16[8,40,768]{2,1,0:T(8,128)(2,1)S(1)}, u32[]{:S(2)}, u32[]{:S(2)}) async-start(bf16[8,40,768]{2,1,0:T(8,128)(2,1)} %bitcast.277), calls=%async_computation.1 | async-start | bytes 983040 | tf_op jit(solution)/shard_map/all_to_all | solution.py:872
  52.6 102.6 %all-gather.12.cloned.1.call-start = ((), (), s32[]{:S(2)}) async-start(), calls=%async_computation.10 | async-start | bytes 7077888 | tf_op jit(solution)/shard_map/all_gather | solution.py:40
  67.9 12.3 %collective-permute-start.4 = (bf16[320,768]{1,0:T(8,128)(2,1)S(1)}, bf16[320,768]{1,0:T(8,128)(2,1)}, u32[]{:S(2)}, u32[]{:S(2)}) collective-permute-start(bf16[320,768]{1,0:T(8,128)(2,1)S(1)} %bitcast.234), channel_id=1, source_target_pairs={{0,2},{1,3},{2,0},{3,1},{4,6},{5,7},{6,4},{7,5},{8,10},{9,11},{10,... | collective-permute-start | bytes 1474568 | tf_op jit(solution)/shard_map/ppermute | solution.py:31
  72.3 11.5 %collective-permute-start.5 = (bf16[320,768]{1,0:T(8,128)(2,1)S(1)}, bf16[320,768]{1,0:T(8,128)(2,1)}, u32[]{:S(2)}, u32[]{:S(2)}) collective-permute-start(bf16[320,768]{1,0:T(8,128)(2,1)S(1)} %bitcast.235), channel_id=1, source_target_pairs={{0,1},{1,0},{2,3},{3,2},{4,5},{5,4},{6,7},{7,6},{8,9},{9,8},{10,11... | collective-permute-start | bytes 1474568 | tf_op jit(solution)/shard_map/ppermute | solution.py:31
  106.2 5.9 collective-permute-start.8
  123.7 19.9 %all-to-all-start.2 = ((bf16[8,48,768]{2,1,0:T(8,128)(2,1)}), bf16[8,48,768]{2,1,0:T(8,128)(2,1)S(1)}, u32[]{:S(2)}, u32[]{:S(2)}) async-start(bf16[8,48,768]{2,1,0:T(8,128)(2,1)} %bitcast.272), calls=%async_computation.2 | async-start | bytes 1179648 | tf_op jit(solution)/shard_map/all_to_all | solution.py:914
  127.2 104.6 %all-gather.16.cloned.1.call-start = ((), (), s32[]{:S(2)}) async-start(), calls=%async_computation.12 | async-start | bytes 7372800 | tf_op jit(solution)/shard_map/all_gather | solution.py:40
  129.5 420.0 %all-gather.18.cloned.1.call-start = ((), (), s32[]{:S(2)}) async-start(), calls=%async_computation.13 | async-start | bytes 7372800 | tf_op jit(solution)/shard_map/all_gather | solution.py:40
  132.2 24.9 %collective-permute-start.9 = (bf16[2,768,768]{2,1,0:T(8,128)(2,1)}, bf16[2,768,768]{2,1,0:T(8,128)(2,1)}, u32[]{:S(2)}, u32[]{:S(2)}) collective-permute-start(bf16[2,768,768]{2,1,0:T(8,128)(2,1)} %pad_maximum_fusion.1.refs_0_), channel_id=1, source_target_pairs={{0,1},{1,0},{2,3},{3,2},{4,5},{5,4},{6,7},{7,6},{8,9},{9,8},{10,11... | collective-permute-start | bytes 7077896 | tf_op jit(solution)/shard_map/ppermute | solution.py:31
  200.7 13.8 %collective-permute-start.11 = (bf16[384,768]{1,0:T(8,128)(2,1)S(1)}, bf16[384,768]{1,0:T(8,128)(2,1)}, u32[]{:S(2)}, u32[]{:S(2)}) collective-permute-start(bf16[384,768]{1,0:T(8,128)(2,1)S(1)} %bitcast.260), channel_id=1, source_target_pairs={{0,2},{1,3},{2,0},{3,1},{4,6},{5,7},{6,4},{7,5},{8,10},{9,11},{10,... | collective-permute-start | bytes 1769480 | tf_op jit(solution)/shard_map/ppermute | solution.py:31
  201.4 20.0 %collective-permute-start.12 = (bf16[384,768]{1,0:T(8,128)(2,1)S(1)}, bf16[384,768]{1,0:T(8,128)(2,1)}, u32[]{:S(2)}, u32[]{:S(2)}) collective-permute-start(bf16[384,768]{1,0:T(8,128)(2,1)S(1)} %bitcast.261), channel_id=1, source_target_pairs={{0,1},{1,0},{2,3},{3,2},{4,5},{5,4},{6,7},{7,6},{8,9},{9,8},{10,11... | collective-permute-start | bytes 1769480 | tf_op jit(solution)/shard_map/ppermute | solution.py:31
  214.5 6.9 collective-permute-start.13
  214.5 48.0 %collective-permute-start.14 = (bf16[1600,768]{1,0:T(8,128)(2,1)S(1)}, bf16[1600,768]{1,0:T(8,128)(2,1)}, u32[]{:S(2)}, u32[]{:S(2)}) collective-permute-start(bf16[1600,768]{1,0:T(8,128)(2,1)S(1)} %copy-done.2), channel_id=1, source_target_pairs={{0,1},{1,0},{2,3},{3,2},{4,5},{5,4},{6,7},{7,6},{8,9},{9,8},{10,11... | collective-permute-start | bytes 7372808 | tf_op jit(solution)/shard_map/ppermute | solution.py:31
  235.1 27.4 %collective-permute-start.15 = (bf16[1600,768]{1,0:T(8,128)(2,1)}, bf16[1600,768]{1,0:T(8,128)(2,1)}, u32[]{:S(2)}, u32[]{:S(2)}) collective-permute-start(bf16[1600,768]{1,0:T(8,128)(2,1)} %dynamic-slice_bitcast_fusion.b_ref), channel_id=1, source_target_pairs={{0,1},{1,0},{2,3},{3,2},{4,5},{5,4},{6,7},{7,6},{8,9},{9,8},{10,11... | collective-permute-start | bytes 7372808 | tf_op jit(solution)/shard_map/ppermute | solution.py:31
  235.8 5.7 collective-permute-start.24
  239.4 11.6 %collective-permute-start.16 = (bf16[256,768]{1,0:T(8,128)(2,1)S(1)}, bf16[256,768]{1,0:T(8,128)(2,1)S(1)}, u32[]{:S(2)}, u32[]{:S(2)}) collective-permute-start(bf16[256,768]{1,0:T(8,128)(2,1)S(1)} %get-tuple-element.567), channel_id=1, source_target_pairs={{0,8},{4,12},{8,0},{12,4},{16,24},{20,28},{24,16},{28,20},{1,9},{5... | collective-permute-start | bytes 1179656 | tf_op jit(solution)/shard_map/ppermute | solution.py:31
  241.6 10.1 %collective-permute-start.18 = (f32[2,512]{1,0:T(2,128)S(1)}, f32[2,512]{1,0:T(2,128)S(1)}, u32[]{:S(2)}, u32[]{:S(2)}) collective-permute-start(f32[2,512]{1,0:T(2,128)S(1)} %pad_maximum_fusion.16), channel_id=1, source_target_pairs={{0,8},{4,12},{8,0},{12,4},{16,24},{20,28},{24,16},{28,20},{1,9},{5... | collective-permute-start | bytes 12296 | tf_op jit(solution)/shard_map/ppermute | solution.py:31
  242.6 32.8 %collective-permute-start.20 = (bf16[256,768]{1,0:T(8,128)(2,1)S(1)}, bf16[256,768]{1,0:T(8,128)(2,1)S(1)}, u32[]{:S(2)}, u32[]{:S(2)}) collective-permute-start(bf16[256,768]{1,0:T(8,128)(2,1)S(1)} %get-tuple-element.567), channel_id=1, source_target_pairs={{0,24},{4,28},{8,16},{12,20},{16,8},{20,12},{24,0},{28,4},{1,25},{... | collective-permute-start | bytes 1179656 | tf_op jit(solution)/shard_map/ppermute | solution.py:31
  251.1 10.2 %collective-permute-start.17 = (bf16[256,768]{1,0:T(8,128)(2,1)S(1)}, bf16[256,768]{1,0:T(8,128)(2,1)S(1)}, u32[]{:S(2)}, u32[]{:S(2)}) collective-permute-start(bf16[256,768]{1,0:T(8,128)(2,1)S(1)} %collective-permute-done.16), channel_id=1, source_target_pairs={{0,2},{1,3},{2,0},{3,1},{4,6},{5,7},{6,4},{7,5},{8,10},{9,11},{10,... | collective-permute-start | bytes 1179656 | tf_op jit(solution)/shard_map/ppermute | solution.py:31
  253.0 26.0 %collective-permute-start.19 = (bf16[256,768]{1,0:T(8,128)(2,1)S(1)}, bf16[256,768]{1,0:T(8,128)(2,1)S(1)}, u32[]{:S(2)}, u32[]{:S(2)}) collective-permute-start(bf16[256,768]{1,0:T(8,128)(2,1)S(1)} %get-tuple-element.567), channel_id=1, source_target_pairs={{0,16},{4,20},{8,24},{12,28},{16,0},{20,4},{24,8},{28,12},{1,17},{... | collective-permute-start | bytes 1179656 | tf_op jit(solution)/shard_map/ppermute | solution.py:31
  275.4 23.6 %collective-permute-start.22 = (bf16[256,768]{1,0:T(8,128)(2,1)S(1)}, bf16[256,768]{1,0:T(8,128)(2,1)S(1)}, u32[]{:S(2)}, u32[]{:S(2)}) collective-permute-start(bf16[256,768]{1,0:T(8,128)(2,1)S(1)} %broadcast_select_fusion.1.rest_2_), channel_id=1, source_target_pairs={{0,2},{1,3},{2,0},{3,1},{4,6},{5,7},{6,4},{7,5},{8,10},{9,11},{10,... | collective-permute-start | bytes 1179656 | tf_op jit(solution)/shard_map/ppermute | solution.py:31
  279.0 20.0 %collective-permute-start.21 = (bf16[256,768]{1,0:T(8,128)(2,1)S(1)}, bf16[256,768]{1,0:T(8,128)(2,1)S(1)}, u32[]{:S(2)}, u32[]{:S(2)}) collective-permute-start(bf16[256,768]{1,0:T(8,128)(2,1)S(1)} %broadcast_select_fusion.2.rest_1_), channel_id=1, source_target_pairs={{0,2},{1,3},{2,0},{3,1},{4,6},{5,7},{6,4},{7,5},{8,10},{9,11},{10,... | collective-permute-start | bytes 1179656 | tf_op jit(solution)/shard_map/ppermute | solution.py:31
  324.6 5.7 collective-permute-start.28
  358.2 20.6 %collective-permute-start.33 = (bf16[256,768]{1,0:T(8,128)(2,1)S(1)}, bf16[256,768]{1,0:T(8,128)(2,1)S(1)}, u32[]{:S(2)}, u32[]{:S(2)}) collective-permute-start(bf16[256,768]{1,0:T(8,128)(2,1)S(1)} %get-tuple-element.564), channel_id=1, source_target_pairs={{0,2},{1,3},{2,0},{3,1},{4,6},{5,7},{6,4},{7,5},{8,10},{9,11},{10,... | collective-permute-start | bytes 1179656 | tf_op jit(solution)/shard_map/ppermute | solution.py:31
  359.7 19.2 %collective-permute-start.29 = (bf16[256,768]{1,0:T(8,128)(2,1)S(1)}, bf16[256,768]{1,0:T(8,128)(2,1)S(1)}, u32[]{:S(2)}, u32[]{:S(2)}) collective-permute-start(bf16[256,768]{1,0:T(8,128)(2,1)S(1)} %get-tuple-element.565), channel_id=1, source_target_pairs={{0,2},{1,3},{2,0},{3,1},{4,6},{5,7},{6,4},{7,5},{8,10},{9,11},{10,... | collective-permute-start | bytes 1179656 | tf_op jit(solution)/shard_map/ppermute | solution.py:31
  377.4 7.8 %collective-permute-start.31 = (bf16[256,768]{1,0:T(8,128)(2,1)S(1)}, bf16[256,768]{1,0:T(8,128)(2,1)S(1)}, u32[]{:S(2)}, u32[]{:S(2)}) collective-permute-start(bf16[256,768]{1,0:T(8,128)(2,1)S(1)} %slice.346), channel_id=1, source_target_pairs={{0,2},{1,3},{2,0},{3,1},{4,6},{5,7},{6,4},{7,5},{8,10},{9,11},{10,... | collective-permute-start | bytes 1179656 | tf_op jit(solution)/shard_map/ppermute | solution.py:31
  379.1 25.1 %collective-permute-start.35 = (bf16[256,768]{1,0:T(8,128)(2,1)S(1)}, bf16[256,768]{1,0:T(8,128)(2,1)S(1)}, u32[]{:S(2)}, u32[]{:S(2)}) collective-permute-start(bf16[256,768]{1,0:T(8,128)(2,1)S(1)} %get-tuple-element.563.rest_0_), channel_id=1, source_target_pairs={{0,24},{4,28},{8,16},{12,20},{16,8},{20,12},{24,0},{28,4},{1,25},{... | collective-permute-start | bytes 1179656 | tf_op jit(solution)/shard_map/ppermute | solution.py:31
  380.9 30.0 %collective-permute-start.34 = (bf16[256,768]{1,0:T(8,128)(2,1)S(1)}, bf16[256,768]{1,0:T(8,128)(2,1)S(1)}, u32[]{:S(2)}, u32[]{:S(2)}) collective-permute-start(bf16[256,768]{1,0:T(8,128)(2,1)S(1)} %get-tuple-element.562), channel_id=1, source_target_pairs={{0,16},{4,20},{8,24},{12,28},{16,0},{20,4},{24,8},{28,12},{1,17},{... | collective-permute-start | bytes 1179656 | tf_op jit(solution)/shard_map/ppermute | solution.py:31
  385.4 25.5 %collective-permute-start.32 = (bf16[256,768]{1,0:T(8,128)(2,1)S(1)}, bf16[256,768]{1,0:T(8,128)(2,1)S(1)}, u32[]{:S(2)}, u32[]{:S(2)}) collective-permute-start(bf16[256,768]{1,0:T(8,128)(2,1)S(1)} %add_convert_fusion.5), channel_id=1, source_target_pairs={{0,8},{4,12},{8,0},{12,4},{16,24},{20,28},{24,16},{28,20},{1,9},{5... | collective-permute-start | bytes 1179656 | tf_op jit(solution)/shard_map/ppermute | solution.py:31
  402.8 8.1 %collective-permute-start.30 = (bf16[256,768]{1,0:T(8,128)(2,1)S(1)}, bf16[256,768]{1,0:T(8,128)(2,1)S(1)}, u32[]{:S(2)}, u32[]{:S(2)}) collective-permute-start(bf16[256,768]{1,0:T(8,128)(2,1)S(1)} %slice.344), channel_id=1, source_target_pairs={{0,2},{1,3},{2,0},{3,1},{4,6},{5,7},{6,4},{7,5},{8,10},{9,11},{10,... | collective-permute-start | bytes 1179656 | tf_op jit(solution)/shard_map/ppermute | solution.py:31
  412.2 9.5 %collective-permute-start.36 = (bf16[256,768]{1,0:T(8,128)(2,1)S(1)}, bf16[256,768]{1,0:T(8,128)(2,1)S(1)}, u32[]{:S(2)}, u32[]{:S(2)}) collective-permute-start(bf16[256,768]{1,0:T(8,128)(2,1)S(1)} %add_convert_fusion.3.refs_1_), channel_id=1, source_target_pairs={{0,2},{1,3},{2,0},{3,1},{4,6},{5,7},{6,4},{7,5},{8,10},{9,11},{10,... | collective-permute-start | bytes 1179656 | tf_op jit(solution)/shard_map/ppermute | solution.py:31
  413.3 10.0 %collective-permute-start.37 = (bf16[256,768]{1,0:T(8,128)(2,1)S(1)}, bf16[256,768]{1,0:T(8,128)(2,1)S(1)}, u32[]{:S(2)}, u32[]{:S(2)}) collective-permute-start(bf16[256,768]{1,0:T(8,128)(2,1)S(1)} %add_convert_fusion.3.refs_1_), channel_id=1, source_target_pairs={{0,1},{1,0},{2,3},{3,2},{4,5},{5,4},{6,7},{7,6},{8,9},{9,8},{10,11... | collective-permute-start | bytes 1179656 | tf_op jit(solution)/shard_map/ppermute | solution.py:31
  445.5 5.0 collective-permute-start.39
  482.1 50.1 %collective-permute-start.44 = (f32[768,768]{1,0:T(8,128)}, f32[768,768]{1,0:T(8,128)}, u32[]{:S(2)}, u32[]{:S(2)}) collective-permute-start(f32[768,768]{1,0:T(8,128)} %fusion.117), channel_id=1, source_target_pairs={{0,1},{1,0},{2,3},{3,2},{4,5},{5,4},{6,7},{7,6},{8,9},{9,8},{10,11... | collective-permute-start | bytes 7077896 | tf_op jit(solution)/shard_map/ppermute | solution.py:31
  492.5 20.3 %all-to-all-start.5 = ((bf16[8,48,768]{2,1,0:T(8,128)(2,1)}), bf16[8,48,768]{2,1,0:T(8,128)(2,1)S(1)}, u32[]{:S(2)}, u32[]{:S(2)}) async-start(bf16[8,48,768]{2,1,0:T(8,128)(2,1)} %bitcast.263), calls=%async_computation.5 | async-start | bytes 1179648 | tf_op jit(solution)/shard_map/all_to_all | solution.py:917
  496.0 149.4 %all-gather.14.cloned.1.call-start = ((), (), s32[]{:S(2)}) async-start(), calls=%async_computation.11 | async-start | bytes 7077888 | tf_op jit(solution)/shard_map/all_gather | solution.py:40
  499.4 35.4 %collective-permute-start.43 = (f32[768,768]{1,0:T(8,128)}, f32[768,768]{1,0:T(8,128)}, u32[]{:S(2)}, u32[]{:S(2)}) collective-permute-start(f32[768,768]{1,0:T(8,128)} %fusion.116), channel_id=1, source_target_pairs={{0,1},{1,0},{2,3},{3,2},{4,5},{5,4},{6,7},{7,6},{8,9},{9,8},{10,11... | collective-permute-start | bytes 7077896 | tf_op jit(solution)/shard_map/ppermute | solution.py:31
  512.9 18.7 %collective-permute-start.40 = (bf16[384,768]{1,0:T(8,128)(2,1)S(1)}, bf16[384,768]{1,0:T(8,128)(2,1)S(1)}, u32[]{:S(2)}, u32[]{:S(2)}) collective-permute-start(bf16[384,768]{1,0:T(8,128)(2,1)S(1)} %bitcast.257), channel_id=1, source_target_pairs={{0,2},{1,3},{2,0},{3,1},{4,6},{5,7},{6,4},{7,5},{8,10},{9,11},{10,... | collective-permute-start | bytes 1769480 | tf_op jit(solution)/shard_map/ppermute | solution.py:31
  531.5 7.6 %collective-permute-start.41 = (bf16[384,768]{1,0:T(8,128)(2,1)S(1)}, bf16[384,768]{1,0:T(8,128)(2,1)S(1)}, u32[]{:S(2)}, u32[]{:S(2)}) collective-permute-start(bf16[384,768]{1,0:T(8,128)(2,1)S(1)} %bitcast.258), channel_id=1, source_target_pairs={{0,1},{1,0},{2,3},{3,2},{4,5},{5,4},{6,7},{7,6},{8,9},{9,8},{10,11... | collective-permute-start | bytes 1769480 | tf_op jit(solution)/shard_map/ppermute | solution.py:31
  531.6 7.4 %collective-permute-start.42 = (bf16[384,768]{1,0:T(8,128)(2,1)S(1)}, bf16[384,768]{1,0:T(8,128)(2,1)S(1)}, u32[]{:S(2)}, u32[]{:S(2)}) collective-permute-start(bf16[384,768]{1,0:T(8,128)(2,1)S(1)} %broadcast_select_fusion.refs_2_), channel_id=1, source_target_pairs={{0,1},{1,0},{2,3},{3,2},{4,5},{5,4},{6,7},{7,6},{8,9},{9,8},{10,11... | collective-permute-start | bytes 1769480 | tf_op jit(solution)/shard_map/ppermute | solution.py:31
  575.8 9.4 %collective-permute-start.45 = (f32[1024,768]{1,0:T(8,128)}, f32[1024,768]{1,0:T(8,128)}, u32[]{:S(2)}, u32[]{:S(2)}) collective-permute-start(f32[1024,768]{1,0:T(8,128)} %get-tuple-element.378.refs_0_), channel_id=1, source_target_pairs={{0,1},{1,0},{2,3},{3,2},{4,5},{5,4},{6,7},{7,6},{8,9},{9,8},{10,11... | collective-permute-start | bytes 9437192 | tf_op jit(solution)/shard_map/ppermute | solution.py:31
  576.5 31.5 %collective-permute-start.46 = (bf16[1600,768]{1,0:T(8,128)(2,1)}, bf16[1600,768]{1,0:T(8,128)(2,1)}, u32[]{:S(2)}, u32[]{:S(2)}) collective-permute-start(bf16[1600,768]{1,0:T(8,128)(2,1)} %get-tuple-element.382), channel_id=1, source_target_pairs={{0,1},{1,0},{2,3},{3,2},{4,5},{5,4},{6,7},{7,6},{8,9},{9,8},{10,11... | collective-permute-start | bytes 7372808 | tf_op jit(solution)/shard_map/ppermute | solution.py:31
  582.1 58.8 %collective-permute-start.47 = (f32[2,768,768]{2,1,0:T(8,128)}, f32[2,768,768]{2,1,0:T(8,128)}, u32[]{:S(2)}, u32[]{:S(2)}) collective-permute-start(f32[2,768,768]{2,1,0:T(8,128)} %pad_maximum_fusion), channel_id=1, source_target_pairs={{0,1},{1,0},{2,3},{3,2},{4,5},{5,4},{6,7},{7,6},{8,9},{9,8},{10,11... | collective-permute-start | bytes 14155784 | tf_op jit(solution)/shard_map/ppermute | solution.py:31
  599.8 22.5 %all-to-all-start.6 = ((bf16[8,56,768]{2,1,0:T(8,128)(2,1)}), bf16[8,56,768]{2,1,0:T(8,128)(2,1)S(1)}, u32[]{:S(2)}, u32[]{:S(2)}) async-start(bf16[8,56,768]{2,1,0:T(8,128)(2,1)} %fusion.30), calls=%async_computation.6 | async-start | bytes 1376256 | tf_op jit(solution)/shard_map/all_to_all | solution.py:1083
  622.4 32.9 %all-to-all-start.7 = ((bf16[8,96,768]{2,1,0:T(8,128)(2,1)}), bf16[8,96,768]{2,1,0:T(8,128)(2,1)}, u32[]{:S(2)}, u32[]{:S(2)}) async-start(bf16[8,96,768]{2,1,0:T(8,128)(2,1)} %bitcast.256), calls=%async_computation.7 | async-start | bytes 2359296 | tf_op jit(solution)/shard_map/all_to_all | solution.py:1073
  660.1 10.0 %all-to-all-start.8 = ((f32[8,1,128]{2,1,0:T(1,128)}), f32[8,1,128]{2,1,0:T(1,128)S(1)}, u32[]{:S(2)}, u32[]{:S(2)}) async-start(f32[8,1,128]{2,1,0:T(1,128)} %broadcast_in_dim.151), calls=%async_computation.8 | async-start | bytes 8192 | tf_op jit(solution)/shard_map/all_to_all | solution.py:1120
  (81 other events, 883.6 us)
Sparse Core Ops, SparseCore 0:
  37.7 54.0 all-gather.9
  93.9 61.2 all-gather.11
  156.8 71.1 all-gather.15
  455.0 76.1 all-gather.17
  584.0 61.4 all-gather.13

commit v5 on v4

--- a/solution.py
+++ b/solution.py
@@ -894,7 +894,7 @@
     )[1]
     place_all = jnp.where(any_overflow, token_at, place_all)
     embedded, normed_one = pick_norm(
-        (place_all, *answers), None, gain_full[0:1], embed_scale, ready=(fill_place, pick_place)
+        (place_all, *answers), None, gain_full[0:1], embed_scale, ready=(fill_place, pick_place[:, None])
     )
 
     qkv, attended, attn_part = attend(normed_one, packed, head_width, segment, ())

time: 723 us -> 720 us (level)
  transfers between devices with their start and end apart: 55 -> 55, of which waited for: 27 -> 28; matrix products, arithmetic and copies ran while one was open for 15% -> 15% of each run, Pallas kernels for 24% -> 24%
where the time goes in v5:
time: 720 us; the launch traced here: 709 us
  Pallas kernels  266 us (37%)
  waiting for transfers between devices  128 us (18%)
  other arithmetic  86.4 us (12%)
  blocking collectives  63.3 us (9%)
  starting transfers between devices  58.1 us (8%)
  local copies, waits for them, and re-layouts  51.9 us (7%)
  between operations  29.7 us (4%)
  matrix products  26 us (4%)
    ppermute x44, waiting for transfers between devices, flip(): lax.ppermute(x, axis, [(j, j ^ k) for j in range(lax.axis_size(axis))])  80.4 us
    pallas_call x3, Pallas kernels, head_back(): pl.pallas_call(head_back_kernel, grid=(steps,), in_specs=[pl.BlockSpec((w...  55.2 us
    pallas_call x2, Pallas kernels, head_logits(): pl.pallas_call(partial(logits_kernel, real), grid=(steps,), in_specs=[pl....  36.9 us
    ppermute x44, starting transfers between devices, flip(): lax.ppermute(x, axis, [(j, j ^ k) for j in range(lax.axis_size(axis))])  35.7 us
    pallas_call x2, Pallas kernels, table_grad(): pl.pallas_call(partial(table_grad_kernel, len(ds)), grid=(padded // part,...  30.4 us
    pallas_call x1, Pallas kernels, attend_back(): pl.pallas_call(attend_back_kernel, in_specs=[WHOLE] * 5 + [ANY] * len(rea...  26.3 us
    dot_general x12, matrix products, dot(): lax.dot_general(a, b, (((ca,), (cb,)), ((), ())), preferred_element_type=...  26 us
    pallas_call x3, Pallas kernels, norm_back(): pl.pallas_call(partial(norm_back_kernel, scale, len(gradients), pick, has...  23.6 us
  transfers between devices with their start and end apart: 55, of which 28 were waited for; matrix products, arithmetic and copies ran while one was open for 15% of the time, Pallas kernels for 24%

profile of v5, /device:TPU:0, one launch (start us, length us, event | category | flops | bytes accessed | tf_op | source)
XLA Modules:
  0.0 709.4 jit_solution(15298916365065597845)
XLA Ops:
  13.0 13.6 %all_to_all.77 = f32[8,1,512]{2,1,0:T(1,128)S(1)} all-to-all(f32[8,1,512]{2,1,0:T(1,128)S(1)} %all_to_all.49), channel_id=1, replica_groups=mesh['expert'=8,'hidden'=4] {'expert'}, dimensions={0} | all-to-all | bytes 32768 | tf_op jit(solution)/shard_map/all_to_all | solution.py:842
  32.1 3.8 collective-permute-done.7
  42.3 6.8 cast_pick.1
  58.0 6.1 gather_fusion
  72.2 8.0 %collective-permute-done.4 = bf16[320,768]{1,0:T(8,128)(2,1)} collective-permute-done((bf16[320,768]{1,0:T(8,128)(2,1)S(1)}, bf16[320,768]{1,0:T(8,128)(2,1)}, u32[]{:S(2)}, u32[]{:S(2)}) %collective-permute-start.4) | collective-permute-done | bytes 491552 | tf_op jit(solution)/shard_map/ppermute | solution.py:31
  89.2 7.1 pick_norm.3
  96.3 14.5 %attend.1 = (bf16[2,1024,576]{2,1,0:T(8,128)(2,1)}, bf16[2,1024,192]{2,1,0:T(8,128)(2,1)}, f32[1024,768]{1,0:T(8,128)}) custom-call(bf16[1024,768]{1,0:T(8,128)(2,1)} %get-tuple-element.343.rows_ref, bf16[2,768,768]{2,1,0:T(8,128)(2,1)} %all-gather.10.cloned.1.call-done.w_ref, s32[1,1024]{1,0:T(1,128)} %segr_ref.3, s32[1024,1]{1,0:T(8,128)} %copy.191.segc_ref), custom_call_target="tpu_custom_call" | custom-call | flops 1024 | bytes 1024 | tf_op jit(solution)/shard_map/attend/pallas_call | solution.py:144
  112.1 4.8 collective-permute-done.8.refs_1_
  118.6 6.7 pick_norm.4
  137.4 11.2 %all-to-all-done.2 = bf16[8,48,768]{2,1,0:T(8,128)(2,1)S(1)} async-done(((bf16[8,48,768]{2,1,0:T(8,128)(2,1)}), bf16[8,48,768]{2,1,0:T(8,128)(2,1)S(1)}, u32[]{:S(2)}, u32[]{:S(2)}) %all-to-all-start.2) | async-done | bytes 589856 | tf_op jit(solution)/shard_map/all_to_all | solution.py:914
  150.5 4.7 all-gather.12.cloned.1.call-done
  157.1 4.5 collective-permute-done.10.refs_3_
  163.0 14.7 %expert.1 = (bf16[384,768]{1,0:T(8,128)(2,1)}, bf16[384,768]{1,0:T(8,128)(2,1)}, bf16[384,768]{1,0:T(8,128)(2,1)}, bf16[384,768]{1,0:T(8,128)(2,1)}, bf16[384,76...) custom-call(bf16[384,768]{1,0:T(8,128)(2,1)} %bitcast.238, ...), custom_call_target="tpu_custom_call" | custom-call | flops 1024 | bytes 1024 | tf_op jit(solution)/shard_map/expert/pallas_call | solution.py:422
  177.7 22.9 %all_to_all.78 = bf16[8,48,768]{2,1,0:T(8,128)(2,1)S(1)} all-to-all(bf16[8,48,768]{2,1,0:T(8,128)(2,1)} %bitcast.273), channel_id=1, replica_groups=mesh['expert'=8,'hidden'=4] {'expert'}, dimensions={0} | all-to-all | bytes 1179648 | tf_op jit(solution)/shard_map/all_to_all | solution.py:917
  201.3 13.2 %collective-permute-done.11.refs_2_ = bf16[384,768]{1,0:T(8,128)(2,1)} collective-permute-done((bf16[384,768]{1,0:T(8,128)(2,1)S(1)}, bf16[384,768]{1,0:T(8,128)(2,1)}, u32[]{:S(2)}, u32[]{:S(2)}) %collective-permute-start.11) | collective-permute-done | bytes 589856 | tf_op jit(solution)/shard_map/ppermute | solution.py:31
  217.6 7.9 %pick_norm.5 = (f32[1024,768]{1,0:T(8,128)}, bf16[1024,768]{1,0:T(8,128)(2,1)}) custom-call(s32[1024,1]{1,0:T(8,128)} %fusion.41.refs_7_.refs_0_, bf16[384,768]{1,0:T(8,128)(2,1)} %bitcast.262, bf16[384,768]{1,0:T(8,128)(2,1)} %collective-permute-done.11.refs_2_, bf16[384,768]{1,0:T(8,128)(2,1)} %collective-permute-done.12.refs_3_, ...), custom_call_target="tpu_custom_call" | custom-call | flops 1024 | bytes 1024 | tf_op jit(solution)/shard_map/pick_norm/pallas_call | solution.py:294
  241.3 6.7 collective-permute-done.16
  254.3 4.1 collective-permute-done.17
  259.6 10.4 %turned.1.rest_0_.table_ref = bf16[768,6400]{1,0:T(8,128)(2,1)} custom-call(bf16[1600,768]{1,0:T(8,128)(2,1)} %get-tuple-element.723.a_ref, bf16[1600,768]{1,0:T(8,128)(2,1)} %dynamic-slice_bitcast_fusion.b_ref, bf16[1600,768]{1,0:T(8,128)(2,1)} %collective-permute-done.14.c_ref, bf16[1600,768]{1,0:T(8,128)(2,1)} %collective-permute-done.15.d_ref), custom_call_target="tpu_custom_call" | custom-call | bytes 29491200 | tf_op jit(solution)/shard_map/turned/pallas_call | solution.py:518
  277.4 18.5 %head_logits.2 = (f32[6400,1024]{1,0:T(8,128)}, f32[160,1024]{1,0:T(8,128)}, f32[8,1024]{1,0:T(8,128)}) custom-call(bf16[1600,768]{1,0:T(8,128)(2,1)} %get-tuple-element.723.a_ref, bf16[1600,768]{1,0:T(8,128)(2,1)} %dynamic-slice_bitcast_fusion.b_ref, bf16[1600,768]{1,0:T(8,128)(2,1)} %collective-permute-done.14.c_ref, ...), custom_call_target="tpu_custom_call" | custom-call | flops 20132659200 | bytes 26214400 | tf_op jit(solution)/shard_map/head_logits/pallas_call | solution.py:579
  299.0 18.4 %head_logits.3 = (f32[6400,1024]{1,0:T(8,128)}, f32[160,1024]{1,0:T(8,128)}, f32[8,1024]{1,0:T(8,128)}) custom-call(bf16[1600,768]{1,0:T(8,128)(2,1)} %get-tuple-element.723.a_ref, bf16[1600,768]{1,0:T(8,128)(2,1)} %dynamic-slice_bitcast_fusion.b_ref, bf16[1600,768]{1,0:T(8,128)(2,1)} %collective-permute-done.14.c_ref, ...), custom_call_target="tpu_custom_call" | custom-call | flops 20132659200 | bytes 26214400 | tf_op jit(solution)/shard_map/head_logits/pallas_call | solution.py:579
  330.5 24.7 %head_back.3 = (bf16[6400,1024]{1,0:T(8,128)(2,1)}, bf16[1024,768]{1,0:T(8,128)(2,1)}) custom-call(bf16[768,6400]{1,0:T(8,128)(2,1)} %turned.1.rest_0_.table_ref, f32[6400,1024]{1,0:T(8,128)} %get-tuple-element.353.power_ref, f32[160,1024]{1,0:T(8,128)} %get-tuple-element.354.peak_ref, s32[1,1024]{1,0:T(1,128)} %pad_add_fusion.1.col_ref, ...), custom_call_target="tpu_custom_call" | custom-call | flops 20132659200 | bytes 39321600 | tf_op jit(solution)/shard_map/head_back/pallas_call | solution.py:641
  359.1 15.3 %head_back.5 = (bf16[6400,512]{1,0:T(8,128)(2,1)}, bf16[512,768]{1,0:T(8,128)(2,1)}) custom-call(bf16[768,6400]{1,0:T(8,128)(2,1)} %turned.1.rest_0_.table_ref, f32[6400,1024]{1,0:T(8,128)} %get-tuple-element.349.power_ref, f32[160,1024]{1,0:T(8,128)} %get-tuple-element.350.peak_ref, s32[1,512]{1,0:T(1,128)} %copy-done.65, f32[8,512]{1,0:T(8,128)} %get-tuple-element.603.side_ref), custom_call_target="tpu_custom_call" | custom-call | flops 10066329600 | bytes 19660800 | tf_op jit(solution)/shard_map/head_back/pallas_call | solution.py:641
  379.1 4.3 collective-permute-done.31
  384.7 15.2 %head_back.4 = (bf16[6400,512]{1,0:T(8,128)(2,1)}, bf16[512,768]{1,0:T(8,128)(2,1)}) custom-call(bf16[768,6400]{1,0:T(8,128)(2,1)} %turned.1.rest_0_.table_ref, f32[6400,1024]{1,0:T(8,128)} %get-tuple-element.349.power_ref, f32[160,1024]{1,0:T(8,128)} %get-tuple-element.350.peak_ref, s32[1,512]{1,0:T(1,128)} %copy-done.64, ...), custom_call_target="tpu_custom_call" | custom-call | flops 10066329600 | bytes 19660800 | tf_op jit(solution)/shard_map/head_back/pallas_call | solution.py:641
  401.7 6.5 collective-permute-done.34
  410.8 7.8 %collective-permute-done.36.refs_2_ = bf16[256,768]{1,0:T(8,128)(2,1)S(1)} collective-permute-done((bf16[256,768]{1,0:T(8,128)(2,1)S(1)}, bf16[256,768]{1,0:T(8,128)(2,1)S(1)}, u32[]{:S(2)}, u32[]{:S(2)}) %collective-permute-start.36) | collective-permute-done | bytes 393248 | tf_op jit(solution)/shard_map/ppermute | solution.py:31
  421.1 6.0 norm_back.3
  427.1 15.2 %table_grad.2 = (f32[1600,768]{1,0:T(8,128)}, bf16[1600,768]{1,0:T(8,128)(2,1)}) custom-call(bf16[6400,512]{1,0:T(8,128)(2,1)} %get-tuple-element.356.refs_0_.refs_1_, bf16[6400,512]{1,0:T(8,128)(2,1)} %get-tuple-element.356.refs_0_.refs_1_, bf16[6400,512]{1,0:T(8,128)(2,1)} %get-tuple-element.357.refs_2_.refs_3_, ...), custom_call_target="tpu_custom_call" | custom-call | flops 10066329600 | bytes 9830400 | tf_op jit(solution)/shard_map/table_grad/pallas_call | solution.py:686
  442.8 4.5 collective-permute-done.39
  447.3 4.4 add_convert_fusion
  455.2 21.4 %all_to_all.79 = bf16[8,48,768]{2,1,0:T(8,128)(2,1)S(1)} all-to-all(bf16[8,48,768]{2,1,0:T(8,128)(2,1)S(1)} %bitcast.274), channel_id=1, replica_groups=mesh['expert'=8,'hidden'=4] {'expert'}, dimensions={0} | all-to-all | bytes 1179648 | tf_op jit(solution)/shard_map/all_to_all | solution.py:914
  478.8 10.4 %expert_back.1 = (bf16[384,768]{1,0:T(8,128)(2,1)}, bf16[384,768]{1,0:T(8,128)(2,1)}, bf16[384,768]{1,0:T(8,128)(2,1)}, bf16[384,768]{1,0:T(8,128)(2,1)}, bf16[384,768]{1,0:T(8,128)(2,1)}) custom-call(bf16[384,768]{1,0:T(8,128)(2,1)} %bitcast.244, bf16[2,768,768]{2,1,0:T(8,128)(2,1)} %pad_maximum_fusion.1.refs_0_, bf16[2,768,768]{2,1,0:T(8,128)(2,1)} %copy-done.12, ...), custom_call_target="tpu_custom_call" | custom-call | flops 1024 | bytes 1024 | tf_op jit(solution)/shard_map/expert_back/pallas_call | solution.py:448
  496.6 13.0 %all-to-all-done.5 = bf16[8,48,768]{2,1,0:T(8,128)(2,1)S(1)} async-done(((bf16[8,48,768]{2,1,0:T(8,128)(2,1)}), bf16[8,48,768]{2,1,0:T(8,128)(2,1)S(1)}, u32[]{:S(2)}, u32[]{:S(2)}) %all-to-all-start.5) | async-done | bytes 589856 | tf_op jit(solution)/shard_map/all_to_all | solution.py:917
  510.6 15.2 %table_grad.3 = (f32[1600,768]{1,0:T(8,128)}, bf16[1600,768]{1,0:T(8,128)(2,1)}) custom-call(bf16[6400,512]{1,0:T(8,128)(2,1)} %get-tuple-element.356.refs_0_.refs_1_, bf16[6400,512]{1,0:T(8,128)(2,1)} %get-tuple-element.356.refs_0_.refs_1_, bf16[6400,512]{1,0:T(8,128)(2,1)} %get-tuple-element.357.refs_2_.refs_3_, ...), custom_call_target="tpu_custom_call" | custom-call | flops 10066329600 | bytes 9830400 | tf_op jit(solution)/shard_map/table_grad/pallas_call | solution.py:686
  536.9 9.4 %norm_back.4 = (f32[1,768]{1,0:T(1,128)}, bf16[1024,768]{1,0:T(8,128)(2,1)}, f32[1024,768]{1,0:T(8,128)}) custom-call(f32[1024,768]{1,0:T(8,128)} %get-tuple-element.345.refs_5_.x_ref, f32[1,768]{1,0:T(1,128)} %slice.295.refs_3_.gain_ref, s32[1024,1]{1,0:T(8,128)} %fusion.41.refs_7_.refs_0_, bf16[384,768]{1,0:T(8,128)(2,1)} %bitcast.259, ...), custom_call_target="tpu_custom_call" | custom-call | flops 1024 | bytes 1024 | tf_op jit(solution)/shard_map/norm_back/pallas_call | solution.py:365
  546.4 26.3 %attend_back.1 = (bf16[2,1024,576]{2,1,0:T(8,128)(2,1)}, f32[1024,768]{1,0:T(8,128)}) custom-call(bf16[1024,768]{1,0:T(8,128)(2,1)} %get-tuple-element.376.branch_ref, bf16[2,768,768]{2,1,0:T(8,128)(2,1)} %all-gather.10.cloned.1.call-done.w_ref, bf16[2,1024,576]{2,1,0:T(8,128)(2,1)} %get-tuple-element.377.qkv_ref, s32[1,1024]{1,0:T(1,128)} %segr_ref.3, ...), custom_call_target="tpu_custom_call" | custom-call | flops 1024 | bytes 1024 | tf_op jit(solution)/shard_map/attend_back/pallas_call | solution.py:208
  582.0 8.3 %norm_back.5 = (f32[1,768]{1,0:T(1,128)}, bf16[1024,768]{1,0:T(8,128)(2,1)}, bf16[1024,768]{1,0:T(8,128)(2,1)}) custom-call(f32[1024,768]{1,0:T(8,128)} %get-tuple-element.342.refs_2_.x_ref, f32[1,768]{1,0:T(1,128)} %slice.291.refs_5_.gain_ref, f32[1024,768]{1,0:T(8,128)} %get-tuple-element.378.refs_0_, f32[1024,768]{1,0:T(8,128)} %collective-permute-done.45.refs_1_, ...), custom_call_target="tpu_custom_call" | custom-call | flops 1024 | bytes 1024 | tf_op jit(solution)/shard_map/norm_back/pallas_call | solution.py:365
  604.8 6.7 convert_add_fusion
  611.5 5.3 attn_grad.1
  619.2 4.3 all-to-all-start.7
  624.3 7.6 %finish.1 = (f32[1572,768]{1,0:T(8,128)}, f32[1,768]{1,0:T(1,128)}) custom-call(f32[1600,768]{1,0:T(8,128)} %get-tuple-element.383.base_ref, s32[1,320]{1,0:T(1,128)} %select_n.557.place_ref, bf16[320,768]{1,0:T(8,128)(2,1)} %bitcast.264), custom_call_target="tpu_custom_call" | custom-call | flops 1024 | bytes 1024 | tf_op jit(solution)/shard_map/finish/pallas_call | solution.py:728
  637.7 4.4 all-gather.14.cloned.1.call-done
  642.1 7.7 %multiply_reduce_fusion = (f32[]{:T(128)}, f32[2,768,768]{2,1,0:T(8,128)}) fusion(bf16[2,2,768,768]{3,2,1,0:T(8,128)(2,1)} %all-gather.14.cloned.1.call-done, s32[]{:T(128)S(6)} %select_n.559, f32[2,768,768]{2,1,0:T(8,128)} %collective-permute-done.47, f32[1,768,768]{2,1,0:T(8,128)S(1)} %copy-done.16, f32[1,768,768]{2,1,0:T(8,128)} %convolution_bitcast_fusion.3), kind=kLoop, calls=%fused_computation.37 | loop fusion | flops 7077887 | bytes 16515080 | tf_op jit(solution)/shard_map/reduce_sum | solution.py:1115
  661.0 5.9 all-to-all-done.8
  666.9 5.3 all-gather.3
  677.6 13.7 %multiply_subtract_fusion = (f32[1572,768]{1,0:T(8,128)}, f32[1572,768]{1,0:T(8,128)}, f32[1572,768]{1,0:T(8,128)}) fusion(f32[1572,768]{1,0:T(8,128)} %x_ref.1, f32[1572,768]{1,0:T(8,128)} %get-tuple-element.394, f32[]{:T(128)S(6)} %min.3, f32[1572,768]{1,0:T(8,128)} %param.32, f32[1572,768]{1,0:T(8,128)} %param.33), kind=kLoop, calls=%fused_computation.32 | loop fusion | flops 19316736 | bytes 33804292 | tf_op jit(solution)/shard_map/sub | solution.py:755
  694.9 6.4 multiply_subtract_fusion.1
  (421 shorter events, 196.0 us)
Async XLA Ops:
  7.2 89.1 %all-gather.10.cloned.1.call-start = ((), (), s32[]{:S(2)}) async-start(), calls=%async_computation.9 | async-start | bytes 2654208 | tf_op jit(solution)/shard_map/all_gather | solution.py:865
  30.5 5.4 collective-permute-start.7
  49.1 18.7 %all-to-all-start.1 = ((bf16[8,40,768]{2,1,0:T(8,128)(2,1)}), bf16[8,40,768]{2,1,0:T(8,128)(2,1)S(1)}, u32[]{:S(2)}, u32[]{:S(2)}) async-start(bf16[8,40,768]{2,1,0:T(8,128)(2,1)} %bitcast.277), calls=%async_computation.1 | async-start | bytes 983040 | tf_op jit(solution)/shard_map/all_to_all | solution.py:872
  52.6 102.6 %all-gather.12.cloned.1.call-start = ((), (), s32[]{:S(2)}) async-start(), calls=%async_computation.10 | async-start | bytes 7077888 | tf_op jit(solution)/shard_map/all_gather | solution.py:40
  67.9 12.3 %collective-permute-start.4 = (bf16[320,768]{1,0:T(8,128)(2,1)S(1)}, bf16[320,768]{1,0:T(8,128)(2,1)}, u32[]{:S(2)}, u32[]{:S(2)}) collective-permute-start(bf16[320,768]{1,0:T(8,128)(2,1)S(1)} %bitcast.234), channel_id=1, source_target_pairs={{0,2},{1,3},{2,0},{3,1},{4,6},{5,7},{6,4},{7,5},{8,10},{9,11},{10,... | collective-permute-start | bytes 1474568 | tf_op jit(solution)/shard_map/ppermute | solution.py:31
  72.1 16.8 %collective-permute-start.5 = (bf16[320,768]{1,0:T(8,128)(2,1)S(1)}, bf16[320,768]{1,0:T(8,128)(2,1)}, u32[]{:S(2)}, u32[]{:S(2)}) collective-permute-start(bf16[320,768]{1,0:T(8,128)(2,1)S(1)} %bitcast.235), channel_id=1, source_target_pairs={{0,1},{1,0},{2,3},{3,2},{4,5},{5,4},{6,7},{7,6},{8,9},{9,8},{10,11... | collective-permute-start | bytes 1474568 | tf_op jit(solution)/shard_map/ppermute | solution.py:31
  80.2 8.8 %collective-permute-start.6 = (bf16[320,768]{1,0:T(8,128)(2,1)}, bf16[320,768]{1,0:T(8,128)(2,1)}, u32[]{:S(2)}, u32[]{:S(2)}) collective-permute-start(bf16[320,768]{1,0:T(8,128)(2,1)} %collective-permute-done.4), channel_id=1, source_target_pairs={{0,1},{1,0},{2,3},{3,2},{4,5},{5,4},{6,7},{7,6},{8,9},{9,8},{10,11... | collective-permute-start | bytes 1474568 | tf_op jit(solution)/shard_map/ppermute | solution.py:31
  110.8 6.1 collective-permute-start.8
  128.5 20.2 %all-to-all-start.2 = ((bf16[8,48,768]{2,1,0:T(8,128)(2,1)}), bf16[8,48,768]{2,1,0:T(8,128)(2,1)S(1)}, u32[]{:S(2)}, u32[]{:S(2)}) async-start(bf16[8,48,768]{2,1,0:T(8,128)(2,1)} %bitcast.272), calls=%async_computation.2 | async-start | bytes 1179648 | tf_op jit(solution)/shard_map/all_to_all | solution.py:914
  132.2 95.8 %all-gather.16.cloned.1.call-start = ((), (), s32[]{:S(2)}) async-start(), calls=%async_computation.12 | async-start | bytes 7372800 | tf_op jit(solution)/shard_map/all_gather | solution.py:40
  134.5 411.9 %all-gather.18.cloned.1.call-start = ((), (), s32[]{:S(2)}) async-start(), calls=%async_computation.13 | async-start | bytes 7372800 | tf_op jit(solution)/shard_map/all_gather | solution.py:40
  137.2 19.9 %collective-permute-start.9 = (bf16[2,768,768]{2,1,0:T(8,128)(2,1)}, bf16[2,768,768]{2,1,0:T(8,128)(2,1)}, u32[]{:S(2)}, u32[]{:S(2)}) collective-permute-start(bf16[2,768,768]{2,1,0:T(8,128)(2,1)} %pad_maximum_fusion.1.refs_0_), channel_id=1, source_target_pairs={{0,1},{1,0},{2,3},{3,2},{4,5},{5,4},{6,7},{7,6},{8,9},{9,8},{10,11... | collective-permute-start | bytes 7077896 | tf_op jit(solution)/shard_map/ppermute | solution.py:31
  200.7 13.8 %collective-permute-start.11 = (bf16[384,768]{1,0:T(8,128)(2,1)S(1)}, bf16[384,768]{1,0:T(8,128)(2,1)}, u32[]{:S(2)}, u32[]{:S(2)}) collective-permute-start(bf16[384,768]{1,0:T(8,128)(2,1)S(1)} %bitcast.260), channel_id=1, source_target_pairs={{0,2},{1,3},{2,0},{3,1},{4,6},{5,7},{6,4},{7,5},{8,10},{9,11},{10,... | collective-permute-start | bytes 1769480 | tf_op jit(solution)/shard_map/ppermute | solution.py:31
  201.3 14.4 %collective-permute-start.12 = (bf16[384,768]{1,0:T(8,128)(2,1)S(1)}, bf16[384,768]{1,0:T(8,128)(2,1)}, u32[]{:S(2)}, u32[]{:S(2)}) collective-permute-start(bf16[384,768]{1,0:T(8,128)(2,1)S(1)} %bitcast.261), channel_id=1, source_target_pairs={{0,1},{1,0},{2,3},{3,2},{4,5},{5,4},{6,7},{7,6},{8,9},{9,8},{10,11... | collective-permute-start | bytes 1769480 | tf_op jit(solution)/shard_map/ppermute | solution.py:31
  214.5 45.1 %collective-permute-start.14 = (bf16[1600,768]{1,0:T(8,128)(2,1)S(1)}, bf16[1600,768]{1,0:T(8,128)(2,1)}, u32[]{:S(2)}, u32[]{:S(2)}) collective-permute-start(bf16[1600,768]{1,0:T(8,128)(2,1)S(1)} %copy-done.2), channel_id=1, source_target_pairs={{0,1},{1,0},{2,3},{3,2},{4,5},{5,4},{6,7},{7,6},{8,9},{9,8},{10,11... | collective-permute-start | bytes 7372808 | tf_op jit(solution)/shard_map/ppermute | solution.py:31
  231.4 28.3 %collective-permute-start.15 = (bf16[1600,768]{1,0:T(8,128)(2,1)}, bf16[1600,768]{1,0:T(8,128)(2,1)}, u32[]{:S(2)}, u32[]{:S(2)}) collective-permute-start(bf16[1600,768]{1,0:T(8,128)(2,1)} %dynamic-slice_bitcast_fusion.b_ref), channel_id=1, source_target_pairs={{0,1},{1,0},{2,3},{3,2},{4,5},{5,4},{6,7},{7,6},{8,9},{9,8},{10,11... | collective-permute-start | bytes 7372808 | tf_op jit(solution)/shard_map/ppermute | solution.py:31
  232.2 5.7 collective-permute-start.24
  236.6 11.4 %collective-permute-start.16 = (bf16[256,768]{1,0:T(8,128)(2,1)S(1)}, bf16[256,768]{1,0:T(8,128)(2,1)S(1)}, u32[]{:S(2)}, u32[]{:S(2)}) collective-permute-start(bf16[256,768]{1,0:T(8,128)(2,1)S(1)} %get-tuple-element.567), channel_id=1, source_target_pairs={{0,8},{4,12},{8,0},{12,4},{16,24},{20,28},{24,16},{28,20},{1,9},{5... | collective-permute-start | bytes 1179656 | tf_op jit(solution)/shard_map/ppermute | solution.py:31
  238.0 11.5 %collective-permute-start.18 = (f32[2,512]{1,0:T(2,128)S(1)}, f32[2,512]{1,0:T(2,128)S(1)}, u32[]{:S(2)}, u32[]{:S(2)}) collective-permute-start(f32[2,512]{1,0:T(2,128)S(1)} %pad_maximum_fusion.16), channel_id=1, source_target_pairs={{0,8},{4,12},{8,0},{12,4},{16,24},{20,28},{24,16},{28,20},{1,9},{5... | collective-permute-start | bytes 12296 | tf_op jit(solution)/shard_map/ppermute | solution.py:31
  240.0 32.5 %collective-permute-start.20 = (bf16[256,768]{1,0:T(8,128)(2,1)S(1)}, bf16[256,768]{1,0:T(8,128)(2,1)S(1)}, u32[]{:S(2)}, u32[]{:S(2)}) collective-permute-start(bf16[256,768]{1,0:T(8,128)(2,1)S(1)} %get-tuple-element.567), channel_id=1, source_target_pairs={{0,24},{4,28},{8,16},{12,20},{16,8},{20,12},{24,0},{28,4},{1,25},{... | collective-permute-start | bytes 1179656 | tf_op jit(solution)/shard_map/ppermute | solution.py:31
  247.9 10.4 %collective-permute-start.17 = (bf16[256,768]{1,0:T(8,128)(2,1)S(1)}, bf16[256,768]{1,0:T(8,128)(2,1)S(1)}, u32[]{:S(2)}, u32[]{:S(2)}) collective-permute-start(bf16[256,768]{1,0:T(8,128)(2,1)S(1)} %collective-permute-done.16), channel_id=1, source_target_pairs={{0,2},{1,3},{2,0},{3,1},{4,6},{5,7},{6,4},{7,5},{8,10},{9,11},{10,... | collective-permute-start | bytes 1179656 | tf_op jit(solution)/shard_map/ppermute | solution.py:31
  250.7 25.1 %collective-permute-start.19 = (bf16[256,768]{1,0:T(8,128)(2,1)S(1)}, bf16[256,768]{1,0:T(8,128)(2,1)S(1)}, u32[]{:S(2)}, u32[]{:S(2)}) collective-permute-start(bf16[256,768]{1,0:T(8,128)(2,1)S(1)} %get-tuple-element.567), channel_id=1, source_target_pairs={{0,16},{4,20},{8,24},{12,28},{16,0},{20,4},{24,8},{28,12},{1,17},{... | collective-permute-start | bytes 1179656 | tf_op jit(solution)/shard_map/ppermute | solution.py:31
  272.6 24.1 %collective-permute-start.22 = (bf16[256,768]{1,0:T(8,128)(2,1)S(1)}, bf16[256,768]{1,0:T(8,128)(2,1)S(1)}, u32[]{:S(2)}, u32[]{:S(2)}) collective-permute-start(bf16[256,768]{1,0:T(8,128)(2,1)S(1)} %broadcast_select_fusion.1.rest_2_), channel_id=1, source_target_pairs={{0,2},{1,3},{2,0},{3,1},{4,6},{5,7},{6,4},{7,5},{8,10},{9,11},{10,... | collective-permute-start | bytes 1179656 | tf_op jit(solution)/shard_map/ppermute | solution.py:31
  275.8 20.8 %collective-permute-start.21 = (bf16[256,768]{1,0:T(8,128)(2,1)S(1)}, bf16[256,768]{1,0:T(8,128)(2,1)S(1)}, u32[]{:S(2)}, u32[]{:S(2)}) collective-permute-start(bf16[256,768]{1,0:T(8,128)(2,1)S(1)} %broadcast_select_fusion.2.rest_1_), channel_id=1, source_target_pairs={{0,2},{1,3},{2,0},{3,1},{4,6},{5,7},{6,4},{7,5},{8,10},{9,11},{10,... | collective-permute-start | bytes 1179656 | tf_op jit(solution)/shard_map/ppermute | solution.py:31
  322.3 5.7 collective-permute-start.28
  356.4 20.0 %collective-permute-start.33 = (bf16[256,768]{1,0:T(8,128)(2,1)S(1)}, bf16[256,768]{1,0:T(8,128)(2,1)S(1)}, u32[]{:S(2)}, u32[]{:S(2)}) collective-permute-start(bf16[256,768]{1,0:T(8,128)(2,1)S(1)} %get-tuple-element.564), channel_id=1, source_target_pairs={{0,2},{1,3},{2,0},{3,1},{4,6},{5,7},{6,4},{7,5},{8,10},{9,11},{10,... | collective-permute-start | bytes 1179656 | tf_op jit(solution)/shard_map/ppermute | solution.py:31
  357.1 19.2 %collective-permute-start.29 = (bf16[256,768]{1,0:T(8,128)(2,1)S(1)}, bf16[256,768]{1,0:T(8,128)(2,1)S(1)}, u32[]{:S(2)}, u32[]{:S(2)}) collective-permute-start(bf16[256,768]{1,0:T(8,128)(2,1)S(1)} %get-tuple-element.565), channel_id=1, source_target_pairs={{0,2},{1,3},{2,0},{3,1},{4,6},{5,7},{6,4},{7,5},{8,10},{9,11},{10,... | collective-permute-start | bytes 1179656 | tf_op jit(solution)/shard_map/ppermute | solution.py:31
  375.6 7.8 %collective-permute-start.31 = (bf16[256,768]{1,0:T(8,128)(2,1)S(1)}, bf16[256,768]{1,0:T(8,128)(2,1)S(1)}, u32[]{:S(2)}, u32[]{:S(2)}) collective-permute-start(bf16[256,768]{1,0:T(8,128)(2,1)S(1)} %slice.346), channel_id=1, source_target_pairs={{0,2},{1,3},{2,0},{3,1},{4,6},{5,7},{6,4},{7,5},{8,10},{9,11},{10,... | collective-permute-start | bytes 1179656 | tf_op jit(solution)/shard_map/ppermute | solution.py:31
  376.5 25.1 %collective-permute-start.35 = (bf16[256,768]{1,0:T(8,128)(2,1)S(1)}, bf16[256,768]{1,0:T(8,128)(2,1)S(1)}, u32[]{:S(2)}, u32[]{:S(2)}) collective-permute-start(bf16[256,768]{1,0:T(8,128)(2,1)S(1)} %get-tuple-element.563.rest_0_), channel_id=1, source_target_pairs={{0,24},{4,28},{8,16},{12,20},{16,8},{20,12},{24,0},{28,4},{1,25},{... | collective-permute-start | bytes 1179656 | tf_op jit(solution)/shard_map/ppermute | solution.py:31
  377.8 30.4 %collective-permute-start.34 = (bf16[256,768]{1,0:T(8,128)(2,1)S(1)}, bf16[256,768]{1,0:T(8,128)(2,1)S(1)}, u32[]{:S(2)}, u32[]{:S(2)}) collective-permute-start(bf16[256,768]{1,0:T(8,128)(2,1)S(1)} %get-tuple-element.562), channel_id=1, source_target_pairs={{0,16},{4,20},{8,24},{12,28},{16,0},{20,4},{24,8},{28,12},{1,17},{... | collective-permute-start | bytes 1179656 | tf_op jit(solution)/shard_map/ppermute | solution.py:31
  383.5 24.7 %collective-permute-start.32 = (bf16[256,768]{1,0:T(8,128)(2,1)S(1)}, bf16[256,768]{1,0:T(8,128)(2,1)S(1)}, u32[]{:S(2)}, u32[]{:S(2)}) collective-permute-start(bf16[256,768]{1,0:T(8,128)(2,1)S(1)} %add_convert_fusion.5), channel_id=1, source_target_pairs={{0,8},{4,12},{8,0},{12,4},{16,24},{20,28},{24,16},{28,20},{1,9},{5... | collective-permute-start | bytes 1179656 | tf_op jit(solution)/shard_map/ppermute | solution.py:31
  400.9 7.8 %collective-permute-start.30 = (bf16[256,768]{1,0:T(8,128)(2,1)S(1)}, bf16[256,768]{1,0:T(8,128)(2,1)S(1)}, u32[]{:S(2)}, u32[]{:S(2)}) collective-permute-start(bf16[256,768]{1,0:T(8,128)(2,1)S(1)} %slice.344), channel_id=1, source_target_pairs={{0,2},{1,3},{2,0},{3,1},{4,6},{5,7},{6,4},{7,5},{8,10},{9,11},{10,... | collective-permute-start | bytes 1179656 | tf_op jit(solution)/shard_map/ppermute | solution.py:31
  410.0 8.5 %collective-permute-start.36 = (bf16[256,768]{1,0:T(8,128)(2,1)S(1)}, bf16[256,768]{1,0:T(8,128)(2,1)S(1)}, u32[]{:S(2)}, u32[]{:S(2)}) collective-permute-start(bf16[256,768]{1,0:T(8,128)(2,1)S(1)} %add_convert_fusion.3.refs_1_), channel_id=1, source_target_pairs={{0,2},{1,3},{2,0},{3,1},{4,6},{5,7},{6,4},{7,5},{8,10},{9,11},{10,... | collective-permute-start | bytes 1179656 | tf_op jit(solution)/shard_map/ppermute | solution.py:31
  410.8 9.4 %collective-permute-start.37 = (bf16[256,768]{1,0:T(8,128)(2,1)S(1)}, bf16[256,768]{1,0:T(8,128)(2,1)S(1)}, u32[]{:S(2)}, u32[]{:S(2)}) collective-permute-start(bf16[256,768]{1,0:T(8,128)(2,1)S(1)} %add_convert_fusion.3.refs_1_), channel_id=1, source_target_pairs={{0,1},{1,0},{2,3},{3,2},{4,5},{5,4},{6,7},{7,6},{8,9},{9,8},{10,11... | collective-permute-start | bytes 1179656 | tf_op jit(solution)/shard_map/ppermute | solution.py:31
  442.3 5.0 collective-permute-start.39
  478.8 50.2 %collective-permute-start.44 = (f32[768,768]{1,0:T(8,128)}, f32[768,768]{1,0:T(8,128)}, u32[]{:S(2)}, u32[]{:S(2)}) collective-permute-start(f32[768,768]{1,0:T(8,128)} %fusion.120), channel_id=1, source_target_pairs={{0,1},{1,0},{2,3},{3,2},{4,5},{5,4},{6,7},{7,6},{8,9},{9,8},{10,11... | collective-permute-start | bytes 7077896 | tf_op jit(solution)/shard_map/ppermute | solution.py:31
  489.2 20.4 %all-to-all-start.5 = ((bf16[8,48,768]{2,1,0:T(8,128)(2,1)}), bf16[8,48,768]{2,1,0:T(8,128)(2,1)S(1)}, u32[]{:S(2)}, u32[]{:S(2)}) async-start(bf16[8,48,768]{2,1,0:T(8,128)(2,1)} %bitcast.263), calls=%async_computation.5 | async-start | bytes 1179648 | tf_op jit(solution)/shard_map/all_to_all | solution.py:917
  492.7 149.4 %all-gather.14.cloned.1.call-start = ((), (), s32[]{:S(2)}) async-start(), calls=%async_computation.11 | async-start | bytes 7077888 | tf_op jit(solution)/shard_map/all_gather | solution.py:40
  496.1 35.5 %collective-permute-start.43 = (f32[768,768]{1,0:T(8,128)}, f32[768,768]{1,0:T(8,128)}, u32[]{:S(2)}, u32[]{:S(2)}) collective-permute-start(f32[768,768]{1,0:T(8,128)} %fusion.119), channel_id=1, source_target_pairs={{0,1},{1,0},{2,3},{3,2},{4,5},{5,4},{6,7},{7,6},{8,9},{9,8},{10,11... | collective-permute-start | bytes 7077896 | tf_op jit(solution)/shard_map/ppermute | solution.py:31
  509.6 18.9 %collective-permute-start.40 = (bf16[384,768]{1,0:T(8,128)(2,1)S(1)}, bf16[384,768]{1,0:T(8,128)(2,1)S(1)}, u32[]{:S(2)}, u32[]{:S(2)}) collective-permute-start(bf16[384,768]{1,0:T(8,128)(2,1)S(1)} %bitcast.257), channel_id=1, source_target_pairs={{0,2},{1,3},{2,0},{3,1},{4,6},{5,7},{6,4},{7,5},{8,10},{9,11},{10,... | collective-permute-start | bytes 1769480 | tf_op jit(solution)/shard_map/ppermute | solution.py:31
  528.3 7.6 %collective-permute-start.41 = (bf16[384,768]{1,0:T(8,128)(2,1)S(1)}, bf16[384,768]{1,0:T(8,128)(2,1)S(1)}, u32[]{:S(2)}, u32[]{:S(2)}) collective-permute-start(bf16[384,768]{1,0:T(8,128)(2,1)S(1)} %bitcast.258), channel_id=1, source_target_pairs={{0,1},{1,0},{2,3},{3,2},{4,5},{5,4},{6,7},{7,6},{8,9},{9,8},{10,11... | collective-permute-start | bytes 1769480 | tf_op jit(solution)/shard_map/ppermute | solution.py:31
  528.5 7.4 %collective-permute-start.42 = (bf16[384,768]{1,0:T(8,128)(2,1)S(1)}, bf16[384,768]{1,0:T(8,128)(2,1)S(1)}, u32[]{:S(2)}, u32[]{:S(2)}) collective-permute-start(bf16[384,768]{1,0:T(8,128)(2,1)S(1)} %broadcast_select_fusion.refs_2_), channel_id=1, source_target_pairs={{0,1},{1,0},{2,3},{3,2},{4,5},{5,4},{6,7},{7,6},{8,9},{9,8},{10,11... | collective-permute-start | bytes 1769480 | tf_op jit(solution)/shard_map/ppermute | solution.py:31
  572.6 9.4 %collective-permute-start.45 = (f32[1024,768]{1,0:T(8,128)}, f32[1024,768]{1,0:T(8,128)}, u32[]{:S(2)}, u32[]{:S(2)}) collective-permute-start(f32[1024,768]{1,0:T(8,128)} %get-tuple-element.378.refs_0_), channel_id=1, source_target_pairs={{0,1},{1,0},{2,3},{3,2},{4,5},{5,4},{6,7},{7,6},{8,9},{9,8},{10,11... | collective-permute-start | bytes 9437192 | tf_op jit(solution)/shard_map/ppermute | solution.py:31
  573.4 31.4 %collective-permute-start.46 = (bf16[1600,768]{1,0:T(8,128)(2,1)}, bf16[1600,768]{1,0:T(8,128)(2,1)}, u32[]{:S(2)}, u32[]{:S(2)}) collective-permute-start(bf16[1600,768]{1,0:T(8,128)(2,1)} %get-tuple-element.382), channel_id=1, source_target_pairs={{0,1},{1,0},{2,3},{3,2},{4,5},{5,4},{6,7},{7,6},{8,9},{9,8},{10,11... | collective-permute-start | bytes 7372808 | tf_op jit(solution)/shard_map/ppermute | solution.py:31
  579.0 58.7 %collective-permute-start.47 = (f32[2,768,768]{2,1,0:T(8,128)}, f32[2,768,768]{2,1,0:T(8,128)}, u32[]{:S(2)}, u32[]{:S(2)}) collective-permute-start(f32[2,768,768]{2,1,0:T(8,128)} %pad_maximum_fusion), channel_id=1, source_target_pairs={{0,1},{1,0},{2,3},{3,2},{4,5},{5,4},{6,7},{7,6},{8,9},{9,8},{10,11... | collective-permute-start | bytes 14155784 | tf_op jit(solution)/shard_map/ppermute | solution.py:31
  596.6 22.5 %all-to-all-start.6 = ((bf16[8,56,768]{2,1,0:T(8,128)(2,1)}), bf16[8,56,768]{2,1,0:T(8,128)(2,1)S(1)}, u32[]{:S(2)}, u32[]{:S(2)}) async-start(bf16[8,56,768]{2,1,0:T(8,128)(2,1)} %fusion.30), calls=%async_computation.6 | async-start | bytes 1376256 | tf_op jit(solution)/shard_map/all_to_all | solution.py:1083
  619.2 32.9 %all-to-all-start.7 = ((bf16[8,96,768]{2,1,0:T(8,128)(2,1)}), bf16[8,96,768]{2,1,0:T(8,128)(2,1)}, u32[]{:S(2)}, u32[]{:S(2)}) async-start(bf16[8,96,768]{2,1,0:T(8,128)(2,1)} %bitcast.256), calls=%async_computation.7 | async-start | bytes 2359296 | tf_op jit(solution)/shard_map/all_to_all | solution.py:1073
  656.9 10.0 %all-to-all-start.8 = ((f32[8,1,128]{2,1,0:T(1,128)}), f32[8,1,128]{2,1,0:T(1,128)S(1)}, u32[]{:S(2)}, u32[]{:S(2)}) async-start(f32[8,1,128]{2,1,0:T(1,128)} %broadcast_in_dim.152), calls=%async_computation.8 | async-start | bytes 8192 | tf_op jit(solution)/shard_map/all_to_all | solution.py:1120
  (81 other events, 872.9 us)
Sparse Core Ops, SparseCore 0:
  37.7 54.1 all-gather.9
  94.0 61.1 all-gather.11
  156.7 71.1 all-gather.15
  451.8 75.9 all-gather.17
  580.8 61.2 all-gather.13

commit v6 on v5

--- a/solution.py
+++ b/solution.py
@@ -378,6 +378,23 @@
     )(x, gain, *gradients, *((rest,) if has_rest else ()), *ready)
 
 
+def gathered_rows_kernel(place_ref, high_ref, low_ref, out_ref):
+    at = lax.broadcasted_iota(jnp.int32, (out_ref.shape[0], place_ref.shape[1]), 0)
+    hot = (at == place_ref[...]).astype(BF)
+    out_ref[...] = (dot(hot, high_ref[...]) + dot(hot, low_ref[...])).astype(BF)
+
+
+def gathered_rows(place, high, low, count):
+    return pl.pallas_call(
+        gathered_rows_kernel,
+        in_specs=[WHOLE] * 3,
+        out_specs=WHOLE,
+        out_shape=jax.ShapeDtypeStruct((count, high.shape[1]), BF),
+        compiler_params=pltpu.CompilerParams(vmem_limit_bytes=VMEM),
+        name="gathered_rows",
+    )(place[None, :], high, low)
+
+
 ERFC = (
     -1.26551223,
     1.00002368,
@@ -1063,8 +1080,7 @@
 
     attn_sent = attn_grad(normed_one, d_qkv, d_branch, attended, (d_high,))
 
-    row_hot = hot_rows(place_own, n_expert * slots)
-    d_rows = dot(row_hot, d_high) + dot(row_hot, d_low)
+    d_rows = gathered_rows(place_own, d_high, d_low, n_expert * slots)
     d_gains = jnp.concatenate([d_gain_one, d_gain_two, d_gain_three])
     d_gains = d_gains.reshape(3, n_expert, own_rows).transpose(1, 0, 2).reshape(n_expert, 1, -1)
     gains_high = lax.reduce_precision(d_gains, 8, 7)
@@ -1078,7 +1094,7 @@
         tiled=True,
     )
     sent = jnp.concatenate(
-        [d_rows.astype(BF).reshape(n_expert, slots, model_width), gains_two], axis=1
+        [d_rows.reshape(n_expert, slots, model_width), gains_two], axis=1
     )
     got = lax.all_to_all(sent, "expert", split_axis=0, concat_axis=0, tiled=True)
     got_rows = got[:, :slots].reshape(n_expert * slots, model_width)

time: 720 us -> 720 us (level)
    dot_general x12 -> x10, matrix products: 26 us -> 20.5 us  [dot(): lax.dot_general(a, b, (((ca,), (cb,)), ((), ())), preferred_element_type=...]
  transfers between devices with their start and end apart: 55 -> 55, of which waited for: 28 -> 28; matrix products, arithmetic and copies ran while one was open for 15% -> 14% of each run, Pallas kernels for 24% -> 25%
where the time goes in v6:
time: 720 us; the launch traced here: 709 us
  Pallas kernels  270 us (38%)
  waiting for transfers between devices  128 us (18%)
  other arithmetic  87.7 us (12%)
  blocking collectives  63 us (9%)
  starting transfers between devices  58.4 us (8%)
  local copies, waits for them, and re-layouts  52.2 us (7%)
  between operations  29.7 us (4%)
  matrix products  20.5 us (3%)
    ppermute x44, waiting for transfers between devices, flip(): lax.ppermute(x, axis, [(j, j ^ k) for j in range(lax.axis_size(axis))])  80.4 us
    pallas_call x3, Pallas kernels, head_back(): pl.pallas_call(head_back_kernel, grid=(steps,), in_specs=[pl.BlockSpec((w...  55.2 us
    pallas_call x2, Pallas kernels, head_logits(): pl.pallas_call(partial(logits_kernel, real), grid=(steps,), in_specs=[pl....  36.9 us
    ppermute x44, starting transfers between devices, flip(): lax.ppermute(x, axis, [(j, j ^ k) for j in range(lax.axis_size(axis))])  35.7 us
    pallas_call x2, Pallas kernels, table_grad(): pl.pallas_call(partial(table_grad_kernel, len(ds)), grid=(padded // part,...  30.4 us
    pallas_call x1, Pallas kernels, attend_back(): pl.pallas_call(attend_back_kernel, in_specs=[WHOLE] * 5 + [ANY] * len(rea...  26.2 us
    pallas_call x3, Pallas kernels, norm_back(): pl.pallas_call(partial(norm_back_kernel, scale, len(gradients), pick, has...  23.6 us
    all_to_all x1, blocking collectives, from_expert(): lax.all_to_all(rows_in, 'expert', split_axis=0, concat_axis=0, tiled=True)  22.9 us
  transfers between devices with their start and end apart: 55, of which 28 were waited for; matrix products, arithmetic and copies ran while one was open for 14% of the time, Pallas kernels for 25%

profile of v6, /device:TPU:0, one launch (start us, length us, event | category | flops | bytes accessed | tf_op | source)
XLA Modules:
  0.0 709.3 jit_solution(17732664292715874148)
XLA Ops:
  13.0 13.6 %all_to_all.77 = f32[8,1,512]{2,1,0:T(1,128)S(1)} all-to-all(f32[8,1,512]{2,1,0:T(1,128)S(1)} %all_to_all.49), channel_id=1, replica_groups=mesh['expert'=8,'hidden'=4] {'expert'}, dimensions={0} | all-to-all | bytes 32768 | tf_op jit(solution)/shard_map/all_to_all | solution.py:859
  42.3 6.8 cast_pick.1
  58.0 6.1 gather_fusion
  72.2 8.0 %collective-permute-done.4 = bf16[320,768]{1,0:T(8,128)(2,1)} collective-permute-done((bf16[320,768]{1,0:T(8,128)(2,1)S(1)}, bf16[320,768]{1,0:T(8,128)(2,1)}, u32[]{:S(2)}, u32[]{:S(2)}) %collective-permute-start.4) | collective-permute-done | bytes 491552 | tf_op jit(solution)/shard_map/ppermute | solution.py:31
  89.2 7.1 pick_norm.3
  96.3 14.5 %attend.1 = (bf16[2,1024,576]{2,1,0:T(8,128)(2,1)}, bf16[2,1024,192]{2,1,0:T(8,128)(2,1)}, f32[1024,768]{1,0:T(8,128)}) custom-call(bf16[1024,768]{1,0:T(8,128)(2,1)} %get-tuple-element.343.rows_ref, bf16[2,768,768]{2,1,0:T(8,128)(2,1)} %all-gather.10.cloned.1.call-done.w_ref, s32[1,1024]{1,0:T(1,128)} %segr_ref.3, s32[1024,1]{1,0:T(8,128)} %copy.191.segc_ref), custom_call_target="tpu_custom_call" | custom-call | flops 1024 | bytes 1024 | tf_op jit(solution)/shard_map/attend/pallas_call | solution.py:144
  112.1 4.8 collective-permute-done.8.refs_1_
  118.6 6.7 pick_norm.4
  137.4 11.2 %all-to-all-done.2 = bf16[8,48,768]{2,1,0:T(8,128)(2,1)S(1)} async-done(((bf16[8,48,768]{2,1,0:T(8,128)(2,1)}), bf16[8,48,768]{2,1,0:T(8,128)(2,1)S(1)}, u32[]{:S(2)}, u32[]{:S(2)}) %all-to-all-start.2) | async-done | bytes 589856 | tf_op jit(solution)/shard_map/all_to_all | solution.py:931
  150.5 4.7 all-gather.12.cloned.1.call-done
  157.1 4.5 collective-permute-done.10.refs_3_
  163.0 14.7 %expert.1 = (bf16[384,768]{1,0:T(8,128)(2,1)}, bf16[384,768]{1,0:T(8,128)(2,1)}, bf16[384,768]{1,0:T(8,128)(2,1)}, bf16[384,768]{1,0:T(8,128)(2,1)}, bf16[384,76...) custom-call(bf16[384,768]{1,0:T(8,128)(2,1)} %bitcast.236, ...), custom_call_target="tpu_custom_call" | custom-call | flops 1024 | bytes 1024 | tf_op jit(solution)/shard_map/expert/pallas_call | solution.py:439
  177.7 22.9 %all_to_all.78 = bf16[8,48,768]{2,1,0:T(8,128)(2,1)S(1)} all-to-all(bf16[8,48,768]{2,1,0:T(8,128)(2,1)} %bitcast.272), channel_id=1, replica_groups=mesh['expert'=8,'hidden'=4] {'expert'}, dimensions={0} | all-to-all | bytes 1179648 | tf_op jit(solution)/shard_map/all_to_all | solution.py:934
  201.3 13.2 %collective-permute-done.11.refs_2_ = bf16[384,768]{1,0:T(8,128)(2,1)} collective-permute-done((bf16[384,768]{1,0:T(8,128)(2,1)S(1)}, bf16[384,768]{1,0:T(8,128)(2,1)}, u32[]{:S(2)}, u32[]{:S(2)}) %collective-permute-start.11) | collective-permute-done | bytes 589856 | tf_op jit(solution)/shard_map/ppermute | solution.py:31
  217.6 7.9 %pick_norm.5 = (f32[1024,768]{1,0:T(8,128)}, bf16[1024,768]{1,0:T(8,128)(2,1)}) custom-call(s32[1024,1]{1,0:T(8,128)} %fusion.37.refs_7_.refs_0_, bf16[384,768]{1,0:T(8,128)(2,1)} %bitcast.260, bf16[384,768]{1,0:T(8,128)(2,1)} %collective-permute-done.11.refs_2_, bf16[384,768]{1,0:T(8,128)(2,1)} %collective-permute-done.12.refs_3_, ...), custom_call_target="tpu_custom_call" | custom-call | flops 1024 | bytes 1024 | tf_op jit(solution)/shard_map/pick_norm/pallas_call | solution.py:294
  241.3 6.7 collective-permute-done.16
  254.3 4.1 collective-permute-done.17
  259.6 10.4 %turned.1.rest_0_.table_ref = bf16[768,6400]{1,0:T(8,128)(2,1)} custom-call(bf16[1600,768]{1,0:T(8,128)(2,1)} %get-tuple-element.723.a_ref, bf16[1600,768]{1,0:T(8,128)(2,1)} %dynamic-slice_bitcast_fusion.b_ref, bf16[1600,768]{1,0:T(8,128)(2,1)} %collective-permute-done.14.c_ref, bf16[1600,768]{1,0:T(8,128)(2,1)} %collective-permute-done.15.d_ref), custom_call_target="tpu_custom_call" | custom-call | bytes 29491200 | tf_op jit(solution)/shard_map/turned/pallas_call | solution.py:535
  277.4 18.5 %head_logits.2 = (f32[6400,1024]{1,0:T(8,128)}, f32[160,1024]{1,0:T(8,128)}, f32[8,1024]{1,0:T(8,128)}) custom-call(bf16[1600,768]{1,0:T(8,128)(2,1)} %get-tuple-element.723.a_ref, bf16[1600,768]{1,0:T(8,128)(2,1)} %dynamic-slice_bitcast_fusion.b_ref, bf16[1600,768]{1,0:T(8,128)(2,1)} %collective-permute-done.14.c_ref, ...), custom_call_target="tpu_custom_call" | custom-call | flops 20132659200 | bytes 26214400 | tf_op jit(solution)/shard_map/head_logits/pallas_call | solution.py:596
  299.0 18.4 %head_logits.3 = (f32[6400,1024]{1,0:T(8,128)}, f32[160,1024]{1,0:T(8,128)}, f32[8,1024]{1,0:T(8,128)}) custom-call(bf16[1600,768]{1,0:T(8,128)(2,1)} %get-tuple-element.723.a_ref, bf16[1600,768]{1,0:T(8,128)(2,1)} %dynamic-slice_bitcast_fusion.b_ref, bf16[1600,768]{1,0:T(8,128)(2,1)} %collective-permute-done.14.c_ref, ...), custom_call_target="tpu_custom_call" | custom-call | flops 20132659200 | bytes 26214400 | tf_op jit(solution)/shard_map/head_logits/pallas_call | solution.py:596
  330.5 24.7 %head_back.3 = (bf16[6400,1024]{1,0:T(8,128)(2,1)}, bf16[1024,768]{1,0:T(8,128)(2,1)}) custom-call(bf16[768,6400]{1,0:T(8,128)(2,1)} %turned.1.rest_0_.table_ref, f32[6400,1024]{1,0:T(8,128)} %get-tuple-element.353.power_ref, f32[160,1024]{1,0:T(8,128)} %get-tuple-element.354.peak_ref, s32[1,1024]{1,0:T(1,128)} %pad_add_fusion.1.col_ref, ...), custom_call_target="tpu_custom_call" | custom-call | flops 20132659200 | bytes 39321600 | tf_op jit(solution)/shard_map/head_back/pallas_call | solution.py:658
  359.1 15.3 %head_back.5 = (bf16[6400,512]{1,0:T(8,128)(2,1)}, bf16[512,768]{1,0:T(8,128)(2,1)}) custom-call(bf16[768,6400]{1,0:T(8,128)(2,1)} %turned.1.rest_0_.table_ref, f32[6400,1024]{1,0:T(8,128)} %get-tuple-element.349.power_ref, f32[160,1024]{1,0:T(8,128)} %get-tuple-element.350.peak_ref, s32[1,512]{1,0:T(1,128)} %copy-done.65, f32[8,512]{1,0:T(8,128)} %get-tuple-element.603.side_ref), custom_call_target="tpu_custom_call" | custom-call | flops 10066329600 | bytes 19660800 | tf_op jit(solution)/shard_map/head_back/pallas_call | solution.py:658
  379.1 4.3 collective-permute-done.31
  384.7 15.2 %head_back.4 = (bf16[6400,512]{1,0:T(8,128)(2,1)}, bf16[512,768]{1,0:T(8,128)(2,1)}) custom-call(bf16[768,6400]{1,0:T(8,128)(2,1)} %turned.1.rest_0_.table_ref, f32[6400,1024]{1,0:T(8,128)} %get-tuple-element.349.power_ref, f32[160,1024]{1,0:T(8,128)} %get-tuple-element.350.peak_ref, s32[1,512]{1,0:T(1,128)} %copy-done.64, ...), custom_call_target="tpu_custom_call" | custom-call | flops 10066329600 | bytes 19660800 | tf_op jit(solution)/shard_map/head_back/pallas_call | solution.py:658
  401.7 6.5 collective-permute-done.34
  410.8 7.8 %collective-permute-done.36.refs_2_ = bf16[256,768]{1,0:T(8,128)(2,1)S(1)} collective-permute-done((bf16[256,768]{1,0:T(8,128)(2,1)S(1)}, bf16[256,768]{1,0:T(8,128)(2,1)S(1)}, u32[]{:S(2)}, u32[]{:S(2)}) %collective-permute-start.36) | collective-permute-done | bytes 393248 | tf_op jit(solution)/shard_map/ppermute | solution.py:31
  421.1 6.0 norm_back.3
  427.1 15.2 %table_grad.2 = (f32[1600,768]{1,0:T(8,128)}, bf16[1600,768]{1,0:T(8,128)(2,1)}) custom-call(bf16[6400,512]{1,0:T(8,128)(2,1)} %get-tuple-element.356.refs_0_.refs_1_, bf16[6400,512]{1,0:T(8,128)(2,1)} %get-tuple-element.356.refs_0_.refs_1_, bf16[6400,512]{1,0:T(8,128)(2,1)} %get-tuple-element.357.refs_2_.refs_3_, ...), custom_call_target="tpu_custom_call" | custom-call | flops 10066329600 | bytes 9830400 | tf_op jit(solution)/shard_map/table_grad/pallas_call | solution.py:703
  442.8 4.5 collective-permute-done.39
  447.3 4.4 add_convert_fusion
  455.2 21.4 %all_to_all.79 = bf16[8,48,768]{2,1,0:T(8,128)(2,1)S(1)} all-to-all(bf16[8,48,768]{2,1,0:T(8,128)(2,1)S(1)} %bitcast.273), channel_id=1, replica_groups=mesh['expert'=8,'hidden'=4] {'expert'}, dimensions={0} | all-to-all | bytes 1179648 | tf_op jit(solution)/shard_map/all_to_all | solution.py:931
  478.8 10.4 %expert_back.1 = (bf16[384,768]{1,0:T(8,128)(2,1)}, bf16[384,768]{1,0:T(8,128)(2,1)}, bf16[384,768]{1,0:T(8,128)(2,1)}, bf16[384,768]{1,0:T(8,128)(2,1)}, bf16[384,768]{1,0:T(8,128)(2,1)}) custom-call(bf16[384,768]{1,0:T(8,128)(2,1)} %bitcast.242, bf16[2,768,768]{2,1,0:T(8,128)(2,1)} %pad_maximum_fusion.1.refs_0_, bf16[2,768,768]{2,1,0:T(8,128)(2,1)} %copy-done.12, ...), custom_call_target="tpu_custom_call" | custom-call | flops 1024 | bytes 1024 | tf_op jit(solution)/shard_map/expert_back/pallas_call | solution.py:465
  496.6 13.0 %all-to-all-done.5 = bf16[8,48,768]{2,1,0:T(8,128)(2,1)S(1)} async-done(((bf16[8,48,768]{2,1,0:T(8,128)(2,1)}), bf16[8,48,768]{2,1,0:T(8,128)(2,1)S(1)}, u32[]{:S(2)}, u32[]{:S(2)}) %all-to-all-start.5) | async-done | bytes 589856 | tf_op jit(solution)/shard_map/all_to_all | solution.py:934
  510.6 15.2 %table_grad.3 = (f32[1600,768]{1,0:T(8,128)}, bf16[1600,768]{1,0:T(8,128)(2,1)}) custom-call(bf16[6400,512]{1,0:T(8,128)(2,1)} %get-tuple-element.356.refs_0_.refs_1_, bf16[6400,512]{1,0:T(8,128)(2,1)} %get-tuple-element.356.refs_0_.refs_1_, bf16[6400,512]{1,0:T(8,128)(2,1)} %get-tuple-element.357.refs_2_.refs_3_, ...), custom_call_target="tpu_custom_call" | custom-call | flops 10066329600 | bytes 9830400 | tf_op jit(solution)/shard_map/table_grad/pallas_call | solution.py:703
  536.9 9.4 %norm_back.4 = (f32[1,768]{1,0:T(1,128)}, bf16[1024,768]{1,0:T(8,128)(2,1)}, f32[1024,768]{1,0:T(8,128)}) custom-call(f32[1024,768]{1,0:T(8,128)} %get-tuple-element.345.refs_5_.x_ref, f32[1,768]{1,0:T(1,128)} %slice.295.refs_3_.gain_ref, s32[1024,1]{1,0:T(8,128)} %fusion.37.refs_7_.refs_0_, bf16[384,768]{1,0:T(8,128)(2,1)} %bitcast.257, ...), custom_call_target="tpu_custom_call" | custom-call | flops 1024 | bytes 1024 | tf_op jit(solution)/shard_map/norm_back/pallas_call | solution.py:365
  546.4 26.2 %attend_back.1 = (bf16[2,1024,576]{2,1,0:T(8,128)(2,1)}, f32[1024,768]{1,0:T(8,128)}) custom-call(bf16[1024,768]{1,0:T(8,128)(2,1)} %get-tuple-element.376.branch_ref, bf16[2,768,768]{2,1,0:T(8,128)(2,1)} %all-gather.10.cloned.1.call-done.w_ref, bf16[2,1024,576]{2,1,0:T(8,128)(2,1)} %get-tuple-element.377.qkv_ref, s32[1,1024]{1,0:T(1,128)} %segr_ref.3, ...), custom_call_target="tpu_custom_call" | custom-call | flops 1024 | bytes 1024 | tf_op jit(solution)/shard_map/attend_back/pallas_call | solution.py:208
  581.6 8.2 %norm_back.5 = (f32[1,768]{1,0:T(1,128)}, bf16[1024,768]{1,0:T(8,128)(2,1)}, bf16[1024,768]{1,0:T(8,128)(2,1)}) custom-call(f32[1024,768]{1,0:T(8,128)} %get-tuple-element.342.refs_2_.x_ref, f32[1,768]{1,0:T(1,128)} %slice.291.refs_5_.gain_ref, f32[1024,768]{1,0:T(8,128)} %get-tuple-element.378.refs_0_, f32[1024,768]{1,0:T(8,128)} %collective-permute-done.45.refs_1_, ...), custom_call_target="tpu_custom_call" | custom-call | flops 1024 | bytes 1024 | tf_op jit(solution)/shard_map/norm_back/pallas_call | solution.py:365
  590.8 4.0 gathered_rows.1
  605.1 6.7 convert_add_fusion
  611.8 5.3 attn_grad.1
  619.4 4.3 all-to-all-start.7
  624.5 7.6 %finish.1 = (f32[1572,768]{1,0:T(8,128)}, f32[1,768]{1,0:T(1,128)}) custom-call(f32[1600,768]{1,0:T(8,128)} %get-tuple-element.383.base_ref, s32[1,320]{1,0:T(1,128)} %select_n.557.place_ref, bf16[320,768]{1,0:T(8,128)(2,1)} %bitcast.263), custom_call_target="tpu_custom_call" | custom-call | flops 1024 | bytes 1024 | tf_op jit(solution)/shard_map/finish/pallas_call | solution.py:745
  640.4 7.7 %multiply_reduce_fusion = (f32[]{:T(128)}, f32[2,768,768]{2,1,0:T(8,128)}) fusion(bf16[2,2,768,768]{3,2,1,0:T(8,128)(2,1)} %all-gather.14.cloned.1.call-done, s32[]{:T(128)S(6)} %select_n.559, f32[2,768,768]{2,1,0:T(8,128)} %collective-permute-done.47, f32[1,768,768]{2,1,0:T(8,128)S(1)} %copy-done.16, f32[1,768,768]{2,1,0:T(8,128)} %convolution_bitcast_fusion.3), kind=kLoop, calls=%fused_computation.37 | loop fusion | flops 7077887 | bytes 16515080 | tf_op jit(solution)/shard_map/reduce_sum | solution.py:1131
  648.1 4.1 all-to-all-done.7
  661.1 5.9 all-to-all-done.8
  667.1 5.0 all-gather.3
  677.5 14.0 %multiply_subtract_fusion = (f32[1572,768]{1,0:T(8,128)}, f32[1572,768]{1,0:T(8,128)}, f32[1572,768]{1,0:T(8,128)}) fusion(f32[1572,768]{1,0:T(8,128)} %x_ref.1, f32[1572,768]{1,0:T(8,128)} %get-tuple-element.394, f32[]{:T(128)S(6)} %min.3, f32[1572,768]{1,0:T(8,128)} %param.32, f32[1572,768]{1,0:T(8,128)} %param.33), kind=kLoop, calls=%fused_computation.32 | loop fusion | flops 19316736 | bytes 33804292 | tf_op jit(solution)/shard_map/sub | solution.py:772
  694.8 6.4 multiply_subtract_fusion.1
  (420 shorter events, 196.0 us)
Async XLA Ops:
  7.2 89.1 %all-gather.10.cloned.1.call-start = ((), (), s32[]{:S(2)}) async-start(), calls=%async_computation.9 | async-start | bytes 2654208 | tf_op jit(solution)/shard_map/all_gather | solution.py:882
  30.5 5.4 collective-permute-start.7
  49.1 18.7 %all-to-all-start.1 = ((bf16[8,40,768]{2,1,0:T(8,128)(2,1)}), bf16[8,40,768]{2,1,0:T(8,128)(2,1)S(1)}, u32[]{:S(2)}, u32[]{:S(2)}) async-start(bf16[8,40,768]{2,1,0:T(8,128)(2,1)} %bitcast.275), calls=%async_computation.1 | async-start | bytes 983040 | tf_op jit(solution)/shard_map/all_to_all | solution.py:889
  52.6 102.6 %all-gather.12.cloned.1.call-start = ((), (), s32[]{:S(2)}) async-start(), calls=%async_computation.10 | async-start | bytes 7077888 | tf_op jit(solution)/shard_map/all_gather | solution.py:40
  67.9 12.3 %collective-permute-start.4 = (bf16[320,768]{1,0:T(8,128)(2,1)S(1)}, bf16[320,768]{1,0:T(8,128)(2,1)}, u32[]{:S(2)}, u32[]{:S(2)}) collective-permute-start(bf16[320,768]{1,0:T(8,128)(2,1)S(1)} %bitcast.232), channel_id=1, source_target_pairs={{0,2},{1,3},{2,0},{3,1},{4,6},{5,7},{6,4},{7,5},{8,10},{9,11},{10,... | collective-permute-start | bytes 1474568 | tf_op jit(solution)/shard_map/ppermute | solution.py:31
  72.1 16.8 %collective-permute-start.5 = (bf16[320,768]{1,0:T(8,128)(2,1)S(1)}, bf16[320,768]{1,0:T(8,128)(2,1)}, u32[]{:S(2)}, u32[]{:S(2)}) collective-permute-start(bf16[320,768]{1,0:T(8,128)(2,1)S(1)} %bitcast.233), channel_id=1, source_target_pairs={{0,1},{1,0},{2,3},{3,2},{4,5},{5,4},{6,7},{7,6},{8,9},{9,8},{10,11... | collective-permute-start | bytes 1474568 | tf_op jit(solution)/shard_map/ppermute | solution.py:31
  80.2 8.8 %collective-permute-start.6 = (bf16[320,768]{1,0:T(8,128)(2,1)}, bf16[320,768]{1,0:T(8,128)(2,1)}, u32[]{:S(2)}, u32[]{:S(2)}) collective-permute-start(bf16[320,768]{1,0:T(8,128)(2,1)} %collective-permute-done.4), channel_id=1, source_target_pairs={{0,1},{1,0},{2,3},{3,2},{4,5},{5,4},{6,7},{7,6},{8,9},{9,8},{10,11... | collective-permute-start | bytes 1474568 | tf_op jit(solution)/shard_map/ppermute | solution.py:31
  110.8 6.1 collective-permute-start.8
  128.5 20.2 %all-to-all-start.2 = ((bf16[8,48,768]{2,1,0:T(8,128)(2,1)}), bf16[8,48,768]{2,1,0:T(8,128)(2,1)S(1)}, u32[]{:S(2)}, u32[]{:S(2)}) async-start(bf16[8,48,768]{2,1,0:T(8,128)(2,1)} %bitcast.271), calls=%async_computation.2 | async-start | bytes 1179648 | tf_op jit(solution)/shard_map/all_to_all | solution.py:931
  132.2 95.8 %all-gather.16.cloned.1.call-start = ((), (), s32[]{:S(2)}) async-start(), calls=%async_computation.12 | async-start | bytes 7372800 | tf_op jit(solution)/shard_map/all_gather | solution.py:40
  134.5 411.9 %all-gather.18.cloned.1.call-start = ((), (), s32[]{:S(2)}) async-start(), calls=%async_computation.13 | async-start | bytes 7372800 | tf_op jit(solution)/shard_map/all_gather | solution.py:40
  137.2 19.9 %collective-permute-start.9 = (bf16[2,768,768]{2,1,0:T(8,128)(2,1)}, bf16[2,768,768]{2,1,0:T(8,128)(2,1)}, u32[]{:S(2)}, u32[]{:S(2)}) collective-permute-start(bf16[2,768,768]{2,1,0:T(8,128)(2,1)} %pad_maximum_fusion.1.refs_0_), channel_id=1, source_target_pairs={{0,1},{1,0},{2,3},{3,2},{4,5},{5,4},{6,7},{7,6},{8,9},{9,8},{10,11... | collective-permute-start | bytes 7077896 | tf_op jit(solution)/shard_map/ppermute | solution.py:31
  200.7 13.8 %collective-permute-start.11 = (bf16[384,768]{1,0:T(8,128)(2,1)S(1)}, bf16[384,768]{1,0:T(8,128)(2,1)}, u32[]{:S(2)}, u32[]{:S(2)}) collective-permute-start(bf16[384,768]{1,0:T(8,128)(2,1)S(1)} %bitcast.258), channel_id=1, source_target_pairs={{0,2},{1,3},{2,0},{3,1},{4,6},{5,7},{6,4},{7,5},{8,10},{9,11},{10,... | collective-permute-start | bytes 1769480 | tf_op jit(solution)/shard_map/ppermute | solution.py:31
  201.3 14.4 %collective-permute-start.12 = (bf16[384,768]{1,0:T(8,128)(2,1)S(1)}, bf16[384,768]{1,0:T(8,128)(2,1)}, u32[]{:S(2)}, u32[]{:S(2)}) collective-permute-start(bf16[384,768]{1,0:T(8,128)(2,1)S(1)} %bitcast.259), channel_id=1, source_target_pairs={{0,1},{1,0},{2,3},{3,2},{4,5},{5,4},{6,7},{7,6},{8,9},{9,8},{10,11... | collective-permute-start | bytes 1769480 | tf_op jit(solution)/shard_map/ppermute | solution.py:31
  214.5 45.1 %collective-permute-start.14 = (bf16[1600,768]{1,0:T(8,128)(2,1)S(1)}, bf16[1600,768]{1,0:T(8,128)(2,1)}, u32[]{:S(2)}, u32[]{:S(2)}) collective-permute-start(bf16[1600,768]{1,0:T(8,128)(2,1)S(1)} %copy-done.2), channel_id=1, source_target_pairs={{0,1},{1,0},{2,3},{3,2},{4,5},{5,4},{6,7},{7,6},{8,9},{9,8},{10,11... | collective-permute-start | bytes 7372808 | tf_op jit(solution)/shard_map/ppermute | solution.py:31
  231.4 28.3 %collective-permute-start.15 = (bf16[1600,768]{1,0:T(8,128)(2,1)}, bf16[1600,768]{1,0:T(8,128)(2,1)}, u32[]{:S(2)}, u32[]{:S(2)}) collective-permute-start(bf16[1600,768]{1,0:T(8,128)(2,1)} %dynamic-slice_bitcast_fusion.b_ref), channel_id=1, source_target_pairs={{0,1},{1,0},{2,3},{3,2},{4,5},{5,4},{6,7},{7,6},{8,9},{9,8},{10,11... | collective-permute-start | bytes 7372808 | tf_op jit(solution)/shard_map/ppermute | solution.py:31
  232.2 5.7 collective-permute-start.24
  236.6 11.4 %collective-permute-start.16 = (bf16[256,768]{1,0:T(8,128)(2,1)S(1)}, bf16[256,768]{1,0:T(8,128)(2,1)S(1)}, u32[]{:S(2)}, u32[]{:S(2)}) collective-permute-start(bf16[256,768]{1,0:T(8,128)(2,1)S(1)} %get-tuple-element.567), channel_id=1, source_target_pairs={{0,8},{4,12},{8,0},{12,4},{16,24},{20,28},{24,16},{28,20},{1,9},{5... | collective-permute-start | bytes 1179656 | tf_op jit(solution)/shard_map/ppermute | solution.py:31
  238.0 11.5 %collective-permute-start.18 = (f32[2,512]{1,0:T(2,128)S(1)}, f32[2,512]{1,0:T(2,128)S(1)}, u32[]{:S(2)}, u32[]{:S(2)}) collective-permute-start(f32[2,512]{1,0:T(2,128)S(1)} %pad_maximum_fusion.16), channel_id=1, source_target_pairs={{0,8},{4,12},{8,0},{12,4},{16,24},{20,28},{24,16},{28,20},{1,9},{5... | collective-permute-start | bytes 12296 | tf_op jit(solution)/shard_map/ppermute | solution.py:31
  240.0 32.5 %collective-permute-start.20 = (bf16[256,768]{1,0:T(8,128)(2,1)S(1)}, bf16[256,768]{1,0:T(8,128)(2,1)S(1)}, u32[]{:S(2)}, u32[]{:S(2)}) collective-permute-start(bf16[256,768]{1,0:T(8,128)(2,1)S(1)} %get-tuple-element.567), channel_id=1, source_target_pairs={{0,24},{4,28},{8,16},{12,20},{16,8},{20,12},{24,0},{28,4},{1,25},{... | collective-permute-start | bytes 1179656 | tf_op jit(solution)/shard_map/ppermute | solution.py:31
  247.9 10.4 %collective-permute-start.17 = (bf16[256,768]{1,0:T(8,128)(2,1)S(1)}, bf16[256,768]{1,0:T(8,128)(2,1)S(1)}, u32[]{:S(2)}, u32[]{:S(2)}) collective-permute-start(bf16[256,768]{1,0:T(8,128)(2,1)S(1)} %collective-permute-done.16), channel_id=1, source_target_pairs={{0,2},{1,3},{2,0},{3,1},{4,6},{5,7},{6,4},{7,5},{8,10},{9,11},{10,... | collective-permute-start | bytes 1179656 | tf_op jit(solution)/shard_map/ppermute | solution.py:31
  250.7 25.1 %collective-permute-start.19 = (bf16[256,768]{1,0:T(8,128)(2,1)S(1)}, bf16[256,768]{1,0:T(8,128)(2,1)S(1)}, u32[]{:S(2)}, u32[]{:S(2)}) collective-permute-start(bf16[256,768]{1,0:T(8,128)(2,1)S(1)} %get-tuple-element.567), channel_id=1, source_target_pairs={{0,16},{4,20},{8,24},{12,28},{16,0},{20,4},{24,8},{28,12},{1,17},{... | collective-permute-start | bytes 1179656 | tf_op jit(solution)/shard_map/ppermute | solution.py:31
  272.6 24.1 %collective-permute-start.22 = (bf16[256,768]{1,0:T(8,128)(2,1)S(1)}, bf16[256,768]{1,0:T(8,128)(2,1)S(1)}, u32[]{:S(2)}, u32[]{:S(2)}) collective-permute-start(bf16[256,768]{1,0:T(8,128)(2,1)S(1)} %broadcast_select_fusion.1.rest_2_), channel_id=1, source_target_pairs={{0,2},{1,3},{2,0},{3,1},{4,6},{5,7},{6,4},{7,5},{8,10},{9,11},{10,... | collective-permute-start | bytes 1179656 | tf_op jit(solution)/shard_map/ppermute | solution.py:31
  275.8 20.8 %collective-permute-start.21 = (bf16[256,768]{1,0:T(8,128)(2,1)S(1)}, bf16[256,768]{1,0:T(8,128)(2,1)S(1)}, u32[]{:S(2)}, u32[]{:S(2)}) collective-permute-start(bf16[256,768]{1,0:T(8,128)(2,1)S(1)} %broadcast_select_fusion.2.rest_1_), channel_id=1, source_target_pairs={{0,2},{1,3},{2,0},{3,1},{4,6},{5,7},{6,4},{7,5},{8,10},{9,11},{10,... | collective-permute-start | bytes 1179656 | tf_op jit(solution)/shard_map/ppermute | solution.py:31
  322.3 5.7 collective-permute-start.28
  356.4 20.0 %collective-permute-start.33 = (bf16[256,768]{1,0:T(8,128)(2,1)S(1)}, bf16[256,768]{1,0:T(8,128)(2,1)S(1)}, u32[]{:S(2)}, u32[]{:S(2)}) collective-permute-start(bf16[256,768]{1,0:T(8,128)(2,1)S(1)} %get-tuple-element.564), channel_id=1, source_target_pairs={{0,2},{1,3},{2,0},{3,1},{4,6},{5,7},{6,4},{7,5},{8,10},{9,11},{10,... | collective-permute-start | bytes 1179656 | tf_op jit(solution)/shard_map/ppermute | solution.py:31
  357.1 19.2 %collective-permute-start.29 = (bf16[256,768]{1,0:T(8,128)(2,1)S(1)}, bf16[256,768]{1,0:T(8,128)(2,1)S(1)}, u32[]{:S(2)}, u32[]{:S(2)}) collective-permute-start(bf16[256,768]{1,0:T(8,128)(2,1)S(1)} %get-tuple-element.565), channel_id=1, source_target_pairs={{0,2},{1,3},{2,0},{3,1},{4,6},{5,7},{6,4},{7,5},{8,10},{9,11},{10,... | collective-permute-start | bytes 1179656 | tf_op jit(solution)/shard_map/ppermute | solution.py:31
  375.6 7.8 %collective-permute-start.31 = (bf16[256,768]{1,0:T(8,128)(2,1)S(1)}, bf16[256,768]{1,0:T(8,128)(2,1)S(1)}, u32[]{:S(2)}, u32[]{:S(2)}) collective-permute-start(bf16[256,768]{1,0:T(8,128)(2,1)S(1)} %slice.346), channel_id=1, source_target_pairs={{0,2},{1,3},{2,0},{3,1},{4,6},{5,7},{6,4},{7,5},{8,10},{9,11},{10,... | collective-permute-start | bytes 1179656 | tf_op jit(solution)/shard_map/ppermute | solution.py:31
  376.5 25.1 %collective-permute-start.35 = (bf16[256,768]{1,0:T(8,128)(2,1)S(1)}, bf16[256,768]{1,0:T(8,128)(2,1)S(1)}, u32[]{:S(2)}, u32[]{:S(2)}) collective-permute-start(bf16[256,768]{1,0:T(8,128)(2,1)S(1)} %get-tuple-element.563.rest_0_), channel_id=1, source_target_pairs={{0,24},{4,28},{8,16},{12,20},{16,8},{20,12},{24,0},{28,4},{1,25},{... | collective-permute-start | bytes 1179656 | tf_op jit(solution)/shard_map/ppermute | solution.py:31
  377.8 30.4 %collective-permute-start.34 = (bf16[256,768]{1,0:T(8,128)(2,1)S(1)}, bf16[256,768]{1,0:T(8,128)(2,1)S(1)}, u32[]{:S(2)}, u32[]{:S(2)}) collective-permute-start(bf16[256,768]{1,0:T(8,128)(2,1)S(1)} %get-tuple-element.562), channel_id=1, source_target_pairs={{0,16},{4,20},{8,24},{12,28},{16,0},{20,4},{24,8},{28,12},{1,17},{... | collective-permute-start | bytes 1179656 | tf_op jit(solution)/shard_map/ppermute | solution.py:31
  383.5 24.7 %collective-permute-start.32 = (bf16[256,768]{1,0:T(8,128)(2,1)S(1)}, bf16[256,768]{1,0:T(8,128)(2,1)S(1)}, u32[]{:S(2)}, u32[]{:S(2)}) collective-permute-start(bf16[256,768]{1,0:T(8,128)(2,1)S(1)} %add_convert_fusion.5), channel_id=1, source_target_pairs={{0,8},{4,12},{8,0},{12,4},{16,24},{20,28},{24,16},{28,20},{1,9},{5... | collective-permute-start | bytes 1179656 | tf_op jit(solution)/shard_map/ppermute | solution.py:31
  400.9 7.8 %collective-permute-start.30 = (bf16[256,768]{1,0:T(8,128)(2,1)S(1)}, bf16[256,768]{1,0:T(8,128)(2,1)S(1)}, u32[]{:S(2)}, u32[]{:S(2)}) collective-permute-start(bf16[256,768]{1,0:T(8,128)(2,1)S(1)} %slice.344), channel_id=1, source_target_pairs={{0,2},{1,3},{2,0},{3,1},{4,6},{5,7},{6,4},{7,5},{8,10},{9,11},{10,... | collective-permute-start | bytes 1179656 | tf_op jit(solution)/shard_map/ppermute | solution.py:31
  410.0 8.5 %collective-permute-start.36 = (bf16[256,768]{1,0:T(8,128)(2,1)S(1)}, bf16[256,768]{1,0:T(8,128)(2,1)S(1)}, u32[]{:S(2)}, u32[]{:S(2)}) collective-permute-start(bf16[256,768]{1,0:T(8,128)(2,1)S(1)} %add_convert_fusion.3.refs_1_), channel_id=1, source_target_pairs={{0,2},{1,3},{2,0},{3,1},{4,6},{5,7},{6,4},{7,5},{8,10},{9,11},{10,... | collective-permute-start | bytes 1179656 | tf_op jit(solution)/shard_map/ppermute | solution.py:31
  410.8 9.4 %collective-permute-start.37 = (bf16[256,768]{1,0:T(8,128)(2,1)S(1)}, bf16[256,768]{1,0:T(8,128)(2,1)S(1)}, u32[]{:S(2)}, u32[]{:S(2)}) collective-permute-start(bf16[256,768]{1,0:T(8,128)(2,1)S(1)} %add_convert_fusion.3.refs_1_), channel_id=1, source_target_pairs={{0,1},{1,0},{2,3},{3,2},{4,5},{5,4},{6,7},{7,6},{8,9},{9,8},{10,11... | collective-permute-start | bytes 1179656 | tf_op jit(solution)/shard_map/ppermute | solution.py:31
  442.3 5.0 collective-permute-start.39
  478.8 50.2 %collective-permute-start.44 = (f32[768,768]{1,0:T(8,128)}, f32[768,768]{1,0:T(8,128)}, u32[]{:S(2)}, u32[]{:S(2)}) collective-permute-start(f32[768,768]{1,0:T(8,128)} %fusion.116), channel_id=1, source_target_pairs={{0,1},{1,0},{2,3},{3,2},{4,5},{5,4},{6,7},{7,6},{8,9},{9,8},{10,11... | collective-permute-start | bytes 7077896 | tf_op jit(solution)/shard_map/ppermute | solution.py:31
  489.2 20.4 %all-to-all-start.5 = ((bf16[8,48,768]{2,1,0:T(8,128)(2,1)}), bf16[8,48,768]{2,1,0:T(8,128)(2,1)S(1)}, u32[]{:S(2)}, u32[]{:S(2)}) async-start(bf16[8,48,768]{2,1,0:T(8,128)(2,1)} %bitcast.261), calls=%async_computation.5 | async-start | bytes 1179648 | tf_op jit(solution)/shard_map/all_to_all | solution.py:934
  492.7 147.7 %all-gather.14.cloned.1.call-start = ((), (), s32[]{:S(2)}) async-start(), calls=%async_computation.11 | async-start | bytes 7077888 | tf_op jit(solution)/shard_map/all_gather | solution.py:40
  496.1 35.5 %collective-permute-start.43 = (f32[768,768]{1,0:T(8,128)}, f32[768,768]{1,0:T(8,128)}, u32[]{:S(2)}, u32[]{:S(2)}) collective-permute-start(f32[768,768]{1,0:T(8,128)} %fusion.115), channel_id=1, source_target_pairs={{0,1},{1,0},{2,3},{3,2},{4,5},{5,4},{6,7},{7,6},{8,9},{9,8},{10,11... | collective-permute-start | bytes 7077896 | tf_op jit(solution)/shard_map/ppermute | solution.py:31
  509.6 18.9 %collective-permute-start.40 = (bf16[384,768]{1,0:T(8,128)(2,1)S(1)}, bf16[384,768]{1,0:T(8,128)(2,1)S(1)}, u32[]{:S(2)}, u32[]{:S(2)}) collective-permute-start(bf16[384,768]{1,0:T(8,128)(2,1)S(1)} %bitcast.255), channel_id=1, source_target_pairs={{0,2},{1,3},{2,0},{3,1},{4,6},{5,7},{6,4},{7,5},{8,10},{9,11},{10,... | collective-permute-start | bytes 1769480 | tf_op jit(solution)/shard_map/ppermute | solution.py:31
  528.3 7.6 %collective-permute-start.41 = (bf16[384,768]{1,0:T(8,128)(2,1)S(1)}, bf16[384,768]{1,0:T(8,128)(2,1)S(1)}, u32[]{:S(2)}, u32[]{:S(2)}) collective-permute-start(bf16[384,768]{1,0:T(8,128)(2,1)S(1)} %bitcast.256), channel_id=1, source_target_pairs={{0,1},{1,0},{2,3},{3,2},{4,5},{5,4},{6,7},{7,6},{8,9},{9,8},{10,11... | collective-permute-start | bytes 1769480 | tf_op jit(solution)/shard_map/ppermute | solution.py:31
  528.5 7.4 %collective-permute-start.42 = (bf16[384,768]{1,0:T(8,128)(2,1)S(1)}, bf16[384,768]{1,0:T(8,128)(2,1)S(1)}, u32[]{:S(2)}, u32[]{:S(2)}) collective-permute-start(bf16[384,768]{1,0:T(8,128)(2,1)S(1)} %broadcast_select_fusion.refs_2_), channel_id=1, source_target_pairs={{0,1},{1,0},{2,3},{3,2},{4,5},{5,4},{6,7},{7,6},{8,9},{9,8},{10,11... | collective-permute-start | bytes 1769480 | tf_op jit(solution)/shard_map/ppermute | solution.py:31
  572.6 9.0 %collective-permute-start.45 = (f32[1024,768]{1,0:T(8,128)}, f32[1024,768]{1,0:T(8,128)}, u32[]{:S(2)}, u32[]{:S(2)}) collective-permute-start(f32[1024,768]{1,0:T(8,128)} %get-tuple-element.378.refs_0_), channel_id=1, source_target_pairs={{0,1},{1,0},{2,3},{3,2},{4,5},{5,4},{6,7},{7,6},{8,9},{9,8},{10,11... | collective-permute-start | bytes 9437192 | tf_op jit(solution)/shard_map/ppermute | solution.py:31
  572.7 32.4 %collective-permute-start.46 = (bf16[1600,768]{1,0:T(8,128)(2,1)}, bf16[1600,768]{1,0:T(8,128)(2,1)}, u32[]{:S(2)}, u32[]{:S(2)}) collective-permute-start(bf16[1600,768]{1,0:T(8,128)(2,1)} %get-tuple-element.382), channel_id=1, source_target_pairs={{0,1},{1,0},{2,3},{3,2},{4,5},{5,4},{6,7},{7,6},{8,9},{9,8},{10,11... | collective-permute-start | bytes 7372808 | tf_op jit(solution)/shard_map/ppermute | solution.py:31
  577.3 60.7 %collective-permute-start.47 = (f32[2,768,768]{2,1,0:T(8,128)}, f32[2,768,768]{2,1,0:T(8,128)}, u32[]{:S(2)}, u32[]{:S(2)}) collective-permute-start(f32[2,768,768]{2,1,0:T(8,128)} %pad_maximum_fusion), channel_id=1, source_target_pairs={{0,1},{1,0},{2,3},{3,2},{4,5},{5,4},{6,7},{7,6},{8,9},{9,8},{10,11... | collective-permute-start | bytes 14155784 | tf_op jit(solution)/shard_map/ppermute | solution.py:31
  596.7 22.7 %all-to-all-start.6 = ((bf16[8,56,768]{2,1,0:T(8,128)(2,1)}), bf16[8,56,768]{2,1,0:T(8,128)(2,1)S(1)}, u32[]{:S(2)}, u32[]{:S(2)}) async-start(bf16[8,56,768]{2,1,0:T(8,128)(2,1)} %fusion.28), calls=%async_computation.6 | async-start | bytes 1376256 | tf_op jit(solution)/shard_map/all_to_all | solution.py:1099
  619.4 32.8 %all-to-all-start.7 = ((bf16[8,96,768]{2,1,0:T(8,128)(2,1)}), bf16[8,96,768]{2,1,0:T(8,128)(2,1)}, u32[]{:S(2)}, u32[]{:S(2)}) async-start(bf16[8,96,768]{2,1,0:T(8,128)(2,1)} %bitcast.254), calls=%async_computation.7 | async-start | bytes 2359296 | tf_op jit(solution)/shard_map/all_to_all | solution.py:1089
  657.0 10.0 %all-to-all-start.8 = ((f32[8,1,128]{2,1,0:T(1,128)}), f32[8,1,128]{2,1,0:T(1,128)S(1)}, u32[]{:S(2)}, u32[]{:S(2)}) async-start(f32[8,1,128]{2,1,0:T(1,128)} %broadcast_in_dim.151), calls=%async_computation.8 | async-start | bytes 8192 | tf_op jit(solution)/shard_map/all_to_all | solution.py:1136
  (81 other events, 845.6 us)
Sparse Core Ops, SparseCore 0:
  37.7 54.1 all-gather.9
  94.0 61.1 all-gather.11
  156.7 71.1 all-gather.15
  451.8 75.9 all-gather.17
  579.1 61.2 all-gather.13
